TPU v7x, 32 devices: a whole 2x2x4 slice. The times are simulated.
32 devices in a mesh: grp: 8 (over z, x), hd: 4 (over y, core).
Axes of the slice: x: 2, y: 2, z: 4, core: 2. Of those that a mesh axis runs over, the one named last changes fastest.
Arguments:
- radar_tokens: bfloat16 [16384, 768], P(('grp', 'hd')), may hold values from -6 to 6
- optic_tokens: bfloat16 [16384, 768], P(('grp', 'hd')), may hold values from -6 to 6
- tile_lengths: int32 [8, 4, 3], P('grp'), may hold values from 0 to 400, as said below
- norm_gains: float32 [3, 768], replicated, may hold values from 0.5 to 1.5
- norm_shifts: float32 [3, 768], replicated, may hold values from -3 to 3
- self_qkv: bfloat16 [768, 2304], replicated, may hold values from -0.21875 to 0.21875
- self_out: bfloat16 [768, 768], replicated, may hold values from -0.4375 to 0.4375
- cross_query: bfloat16 [768, 768], replicated, may hold values from -0.21875 to 0.21875
- cross_keyval: bfloat16 [768, 1536], replicated, may hold values from -0.21875 to 0.21875
- cross_out: bfloat16 [768, 768], replicated, may hold values from -0.875 to 0.875
- hidden_in: bfloat16 [768, 3072], replicated, may hold values from -0.21875 to 0.21875
- hidden_out: bfloat16 [3072, 768], replicated, may hold values from -0.109375 to 0.109375
- proj_biases: float32 [3, 768], replicated, may hold values from -3 to 3
- hidden_bias: float32 [3072], replicated, may hold values from -3 to 3
- cotangent: bfloat16 [16384, 768], P(('grp', 'hd')), may hold values from -6 to 6
Outputs:
- layer_output: bfloat16 [16384, 768], P(('grp', 'hd'))
- radar_grad: float32 [16384, 768], P(('grp', 'hd'))
- optic_grad: float32 [16384, 768], P(('grp', 'hd'))
- self_qkv_grad: float32 [768, 2304], P('hd')
- self_out_grad: float32 [768, 768], P('hd')
- cross_query_grad: float32 [768, 768], P('hd')
- cross_keyval_grad: float32 [768, 1536], P('hd')
- cross_out_grad: float32 [768, 768], P('hd')
- hidden_in_grad: float32 [768, 3072], P('hd')
- hidden_out_grad: float32 [3072, 768], P('hd')
- norm_gains_grad: float32 [3, 768], P(None, 'hd')
- norm_shifts_grad: float32 [3, 768], P(None, 'hd')
- proj_biases_grad: float32 [3, 768], P(None, 'hd')
- hidden_bias_grad: float32 [3072], P('hd')
Inputs may be any that keep to these rules, and one draw needn't show every extreme that they name: `tile_lengths`: each device's 3 slots hold the patch counts of its tiles, each 144, 225 or 400, from the first slot on, then zeros; every device holds at least one tile, its counts sum to at most 512, and the first tile of the first device has 400 patches.
All inputs are finite; a program needn't handle non-finite values.
Results may differ from a plain program's by a relative error of at most 0.02.
Values may be sent and summed in bfloat16 or wider, within the bound.
No kernel may reach another device: no remote copies, remote signals or barrier semaphores. Data moves between devices by JAX's collectives and lax.ppermute only.
A program may use at most 192 MiB of HBM per device.

v0:
```python
import math

import jax
import jax.numpy as jnp
from jax import lax
from jax.sharding import PartitionSpec as P

HEADS = 12
HDIM = 64
SIDE_A = 12
SIDE_B = 15
SIDE_C = 20


epsilon = 1e-06
masked_score = -1e30


def layer_norm(values, norm_gain, norm_shift):
    average = jnp.mean(values, axis=-1, keepdims=True)
    centred = values - average
    variance = jnp.mean(centred * centred, axis=-1, keepdims=True)
    return centred * lax.rsqrt(variance + epsilon) * norm_gain + norm_shift


def gelu_exact(values):
    return jax.nn.gelu(values, approximate=False)


def inner_rows(left, right):
    return lax.dot_general(
        left, right, (((0,), (0,)), ((), ())), preferred_element_type=jnp.float32
    )


def times_transpose(left, right):
    return lax.dot_general(
        left, right, (((1,), (1,)), ((), ())), preferred_element_type=jnp.float32
    )


def tile_layout(lengths, local_rows):
    tile_end = jnp.cumsum(lengths, dtype=jnp.int32)
    starts = tile_end - lengths
    position = jnp.arange(local_rows, dtype=jnp.int32)
    segment = jnp.sum(
        (position[:, None] >= tile_end[None, :]).astype(jnp.int32), axis=1, dtype=jnp.int32
    )
    slots = jnp.arange(lengths.shape[0], dtype=jnp.int32)
    onehot = (segment[:, None] == slots[None, :]).astype(jnp.int32)
    tile_start = jnp.sum(onehot * starts[None, :], axis=1, dtype=jnp.int32)
    extent = jnp.sum(onehot * lengths[None, :], axis=1, dtype=jnp.int32)
    offset = position - tile_start
    tile_side = jnp.where(
        extent == SIDE_A * SIDE_A, SIDE_A, jnp.where(extent == SIDE_B * SIDE_B, SIDE_B, SIDE_C)
    ).astype(jnp.int32)
    is_valid = segment < lengths.shape[0]
    row_pos = jnp.where(is_valid, offset // tile_side, 0)
    col_pos = jnp.where(is_valid, offset % tile_side, 0)
    return (segment, row_pos, col_pos, is_valid)


def head_slopes(first_head, head_count):
    index = (first_head + jnp.arange(head_count, dtype=jnp.int32)).astype(jnp.float32)
    return jnp.exp2(-(index + 1.0) * (8.0 / HEADS))


def alibi_bias(slopes, rows_query, cols_query, rows_key, cols_key):
    delta_row = (rows_query[:, None] - rows_key[None, :]).astype(jnp.float32)
    delta_col = (cols_query[:, None] - cols_key[None, :]).astype(jnp.float32)
    distance = jnp.sqrt(delta_row * delta_row + delta_col * delta_col)
    return -slopes[:, None, None] * distance[None]


def block_scores(query_blk, key_heads, seg_src, row_src, col_src, slopes, with_bias):
    scores = jnp.einsum(
        "qhd,khd->hqk", query_blk, key_heads, preferred_element_type=jnp.float32
    ) * HDIM ** (-0.5)
    if with_bias:
        scores = scores + alibi_bias(slopes, row_src, col_src, row_src, col_src)
    same_tile = seg_src[:, None] == seg_src[None, :]
    return jnp.where(same_tile[None], scores, masked_score)


def attention_forward(queries, key_rows, value_rows, layout, slopes, head_count, with_bias):
    segment, row_pos, col_pos = layout
    sources, source_rows = segment.shape
    block_rows = math.gcd(source_rows, 512)
    block_count = source_rows // block_rows
    starts = jnp.arange(block_count, dtype=jnp.int32) * block_rows
    columns = queries.shape[1]

    def per_source(operands):
        query_src, key_src, value_src, seg_src, row_src, col_src = operands
        key_heads = key_src.reshape(source_rows, head_count, -1)
        value_heads = value_src.reshape(source_rows, head_count, -1)

        def per_block(row_start):
            query_blk = query_src.reshape(block_rows, head_count, -1)
            scores = block_scores(
                query_blk, key_heads, seg_src, row_src, col_src, slopes, with_bias
            )
            row_max = jnp.max(scores, axis=-1, keepdims=True)
            weights_exp = jnp.exp(scores - row_max)
            row_total = jnp.sum(weights_exp, axis=-1, keepdims=True)
            prob_low = (weights_exp / row_total).astype(jnp.bfloat16)
            attended = jnp.einsum(
                "hqk,khd->qhd", prob_low, value_heads, preferred_element_type=jnp.float32
            )
            return (
                attended.reshape(block_rows, -1).astype(jnp.bfloat16),
                row_max + jnp.log(row_total),
            )

        attended, logsums = lax.map(per_block, starts)
        return (attended.reshape(source_rows, -1), logsums)

    attended, logsums = lax.map(
        per_source,
        (
            queries.reshape(sources, source_rows, columns),
            key_rows.reshape(sources, source_rows, columns),
            value_rows.reshape(sources, source_rows, columns),
            segment,
            row_pos,
            col_pos,
        ),
    )
    return (attended.reshape(sources * source_rows, columns), logsums)


def attention_backward(
    queries, key_rows, value_rows, grad_out, logsums, layout, slopes, head_count, with_bias
):
    segment, row_pos, col_pos = layout
    sources, source_rows = segment.shape
    block_rows = math.gcd(source_rows, 512)
    block_count = source_rows // block_rows
    starts = jnp.arange(block_count, dtype=jnp.int32) * block_rows
    columns = queries.shape[1]
    scale = HDIM ** (-0.5)

    def per_source(operands):
        query_src, key_src, value_src, grad_src, logsum_src, seg_src, row_src, col_src = operands
        key_heads = key_src.reshape(source_rows, head_count, -1)
        value_heads = value_src.reshape(source_rows, head_count, -1)

        def per_block(carry, inputs):
            key_acc, value_acc = carry
            row_start, logsum_blk = inputs
            query_blk = query_src.reshape(block_rows, head_count, -1)
            grad_blk = grad_src.reshape(block_rows, head_count, -1)
            scores = block_scores(
                query_blk, key_heads, seg_src, row_src, col_src, slopes, with_bias
            )
            probs_blk = jnp.exp(scores - logsum_blk)
            grad_prob = jnp.einsum(
                "qhd,khd->hqk", grad_blk, value_heads, preferred_element_type=jnp.float32
            )
            inner = jnp.sum(probs_blk * grad_prob, axis=-1, keepdims=True)
            grad_score = (probs_blk * (grad_prob - inner)).astype(jnp.bfloat16)
            grad_query = (
                jnp.einsum(
                    "hqk,khd->qhd", grad_score, key_heads, preferred_element_type=jnp.float32
                )
                * scale
            )
            key_acc = (
                key_acc
                + jnp.einsum(
                    "hqk,qhd->khd", grad_score, query_blk, preferred_element_type=jnp.float32
                )
                * scale
            )
            value_acc = value_acc + jnp.einsum(
                "hqk,qhd->khd",
                probs_blk.astype(jnp.bfloat16),
                grad_blk,
                preferred_element_type=jnp.float32,
            )
            return ((key_acc, value_acc), grad_query.reshape(block_rows, -1).astype(jnp.bfloat16))

        zero_heads = jnp.zeros(key_heads.shape, jnp.float32)
        (key_acc, value_acc), grad_queries = lax.scan(
            per_block, (zero_heads, zero_heads), (starts, logsum_src)
        )
        return (
            grad_queries.reshape(source_rows, -1),
            key_acc.reshape(source_rows, -1).astype(jnp.bfloat16),
            value_acc.reshape(source_rows, -1).astype(jnp.bfloat16),
        )

    grad_queries, grad_keys, grad_values = lax.map(
        per_source,
        (
            queries.reshape(sources, source_rows, columns),
            key_rows.reshape(sources, source_rows, columns),
            value_rows.reshape(sources, source_rows, columns),
            grad_out.reshape(sources, source_rows, columns),
            logsums,
            segment,
            row_pos,
            col_pos,
        ),
    )
    total_rows = sources * source_rows
    return (
        grad_queries.reshape(total_rows, columns),
        grad_keys.reshape(total_rows, columns),
        grad_values.reshape(total_rows, columns),
    )


def on_device(
    radar_tokens,
    optic_tokens,
    tile_lengths,
    norm_gains,
    norm_shifts,
    self_qkv,
    self_out,
    cross_query,
    cross_keyval,
    cross_out,
    hidden_in,
    hidden_out,
    proj_biases,
    hidden_bias,
    cotangent,
):
    local_rows, model_width = radar_tokens.shape
    group_size = lax.axis_size("hd")
    head_group = lax.axis_index("hd")
    heads_here = HEADS // group_size

    def layout_of(lengths_row):
        return tile_layout(lengths_row, local_rows)

    segment_all, row_all, col_all, valid_all = jax.vmap(layout_of)(tile_lengths[0])
    own_valid = lax.dynamic_index_in_dim(valid_all, head_group, 0, keepdims=False)
    radar_wide = radar_tokens.astype(jnp.float32)
    normed_one, norm_back_one = jax.vjp(layer_norm, radar_wide, norm_gains[0], norm_shifts[0])
    normed_one_low = normed_one.astype(jnp.bfloat16)
    packed = jnp.dot(normed_one_low, self_qkv, preferred_element_type=jnp.float32)
    queries = packed[:, :model_width].astype(jnp.bfloat16)
    key_rows = packed[:, model_width : 2 * model_width].astype(jnp.bfloat16)
    value_rows = packed[:, 2 * model_width :].astype(jnp.bfloat16)
    optic_packed = jnp.dot(optic_tokens, cross_keyval, preferred_element_type=jnp.float32)
    optic_keys = optic_packed[:, :model_width].astype(jnp.bfloat16)
    optic_values = optic_packed[:, model_width:].astype(jnp.bfloat16)
    queries, key_rows, value_rows, optic_keys, optic_values = (
        lax.all_to_all(queries, "hd", split_axis=1, concat_axis=0, tiled=True),
        lax.all_to_all(key_rows, "hd", split_axis=1, concat_axis=0, tiled=True),
        lax.all_to_all(value_rows, "hd", split_axis=1, concat_axis=0, tiled=True),
        lax.all_to_all(optic_keys, "hd", split_axis=1, concat_axis=0, tiled=True),
        lax.all_to_all(optic_values, "hd", split_axis=1, concat_axis=0, tiled=True),
    )
    layout = (segment_all, row_all, col_all)
    first_head = head_group * heads_here
    slopes = head_slopes(first_head, heads_here)
    self_heads, self_logsums = attention_forward(
        queries, key_rows, value_rows, layout, slopes, heads_here, True
    )
    self_tokens = lax.all_to_all(self_heads, "hd", split_axis=0, concat_axis=1, tiled=True)
    residual_one = radar_wide + (
        jnp.dot(self_tokens, self_out, preferred_element_type=jnp.float32) + proj_biases[0]
    )
    normed_two, norm_back_two = jax.vjp(layer_norm, residual_one, norm_gains[1], norm_shifts[1])
    normed_two_low = normed_two.astype(jnp.bfloat16)
    cross_queries = jnp.dot(normed_two_low, cross_query, preferred_element_type=jnp.float32).astype(
        jnp.bfloat16
    )
    cross_queries = lax.all_to_all(cross_queries, "hd", split_axis=1, concat_axis=0, tiled=True)
    cross_result, cross_logsums = attention_forward(
        cross_queries, optic_keys, optic_values, layout, slopes, heads_here, False
    )
    cross_tokens = lax.all_to_all(cross_result, "hd", split_axis=0, concat_axis=1, tiled=True)
    residual_two = residual_one + (
        jnp.dot(cross_tokens, cross_out, preferred_element_type=jnp.float32) + proj_biases[1]
    )
    normed_three, norm_back_three = jax.vjp(layer_norm, residual_two, norm_gains[2], norm_shifts[2])
    normed_three_low = normed_three.astype(jnp.bfloat16)
    hidden_pre = (
        jnp.dot(normed_three_low, hidden_in, preferred_element_type=jnp.float32) + hidden_bias
    )
    activated, gelu_back = jax.vjp(gelu_exact, hidden_pre)
    activated_low = activated.astype(jnp.bfloat16)
    final = jnp.where(
        own_valid[:, None],
        residual_two
        + (jnp.dot(activated_low, hidden_out, preferred_element_type=jnp.float32) + proj_biases[2]),
        0.0,
    )
    layer_output = final.astype(jnp.bfloat16)
    grad_final = jnp.where(own_valid[:, None], cotangent.astype(jnp.float32), 0.0)
    grad_final_low = grad_final.astype(jnp.bfloat16)
    grad_hidden_out = inner_rows(activated_low, grad_final_low)
    grad_out_bias = jnp.sum(grad_final, axis=0)
    (grad_pre,) = gelu_back(times_transpose(grad_final_low, hidden_out))
    grad_pre_low = grad_pre.astype(jnp.bfloat16)
    grad_hidden_in = inner_rows(normed_three_low, grad_pre_low)
    grad_hidden_bias = jnp.sum(grad_pre_low.astype(jnp.float32), axis=0)
    grad_two_part, gain_three, shift_three = norm_back_three(
        times_transpose(grad_pre_low, hidden_in)
    )
    grad_two = grad_final + grad_two_part
    grad_cross_low = grad_two.astype(jnp.bfloat16)
    grad_cross_out = inner_rows(cross_tokens, grad_cross_low)
    grad_cross_bias = jnp.sum(grad_cross_low.astype(jnp.float32), axis=0)
    grad_cross_att = times_transpose(grad_cross_low, cross_out).astype(jnp.bfloat16)
    grad_cross_att = lax.all_to_all(grad_cross_att, "hd", split_axis=1, concat_axis=0, tiled=True)
    grad_cross_queries, grad_optic_keys, grad_optic_values = attention_backward(
        cross_queries,
        optic_keys,
        optic_values,
        grad_cross_att,
        cross_logsums,
        layout,
        slopes,
        heads_here,
        False,
    )
    grad_cross_queries, grad_optic_keys, grad_optic_values = (
        lax.all_to_all(grad_cross_queries, "hd", split_axis=0, concat_axis=1, tiled=True),
        lax.all_to_all(grad_optic_keys, "hd", split_axis=0, concat_axis=1, tiled=True),
        lax.all_to_all(grad_optic_values, "hd", split_axis=0, concat_axis=1, tiled=True),
    )
    grad_cross_query = inner_rows(normed_two_low, grad_cross_queries)
    optic_grads = jnp.concatenate((grad_optic_keys, grad_optic_values), axis=1)
    grad_cross_keyval = inner_rows(optic_tokens, optic_grads)
    optic_grad = times_transpose(optic_grads, cross_keyval)
    grad_one_part, gain_two, shift_two = norm_back_two(
        times_transpose(grad_cross_queries, cross_query)
    )
    grad_one = grad_two + grad_one_part
    grad_self_low = grad_one.astype(jnp.bfloat16)
    grad_self_out = inner_rows(self_tokens, grad_self_low)
    grad_self_bias = jnp.sum(grad_self_low.astype(jnp.float32), axis=0)
    grad_self_att = times_transpose(grad_self_low, self_out).astype(jnp.bfloat16)
    grad_self_att = lax.all_to_all(grad_self_att, "hd", split_axis=1, concat_axis=0, tiled=True)
    grad_queries, grad_keys, grad_values = attention_backward(
        queries, key_rows, value_rows, grad_self_att, self_logsums, layout, slopes, heads_here, True
    )
    grad_queries, grad_keys, grad_values = (
        lax.all_to_all(grad_queries, "hd", split_axis=0, concat_axis=1, tiled=True),
        lax.all_to_all(grad_keys, "hd", split_axis=0, concat_axis=1, tiled=True),
        lax.all_to_all(grad_values, "hd", split_axis=0, concat_axis=1, tiled=True),
    )
    packed_grads = jnp.concatenate((grad_queries, grad_keys, grad_values), axis=1)
    grad_self_qkv = inner_rows(normed_one_low, packed_grads)
    grad_zero_part, gain_one, shift_one = norm_back_one(times_transpose(packed_grads, self_qkv))
    radar_grad = grad_one + grad_zero_part
    gain_grads = jnp.stack((gain_one, gain_two, gain_three))
    shift_grads = jnp.stack((shift_one, shift_two, shift_three))
    bias_grads = jnp.stack((grad_self_bias, grad_cross_bias, grad_out_bias))
    summed = (
        lax.psum_scatter(
            grad_self_qkv.astype(jnp.bfloat16), "hd", scatter_dimension=0, tiled=True
        ).astype(jnp.float32),
        lax.psum_scatter(
            grad_self_out.astype(jnp.bfloat16), "hd", scatter_dimension=0, tiled=True
        ).astype(jnp.float32),
        lax.psum_scatter(
            grad_cross_query.astype(jnp.bfloat16), "hd", scatter_dimension=0, tiled=True
        ).astype(jnp.float32),
        lax.psum_scatter(
            grad_cross_keyval.astype(jnp.bfloat16), "hd", scatter_dimension=0, tiled=True
        ).astype(jnp.float32),
        lax.psum_scatter(
            grad_cross_out.astype(jnp.bfloat16), "hd", scatter_dimension=0, tiled=True
        ).astype(jnp.float32),
        lax.psum_scatter(
            gain_grads.astype(jnp.bfloat16), "hd", scatter_dimension=1, tiled=True
        ).astype(jnp.float32),
        lax.psum_scatter(
            shift_grads.astype(jnp.bfloat16), "hd", scatter_dimension=1, tiled=True
        ).astype(jnp.float32),
        lax.psum_scatter(
            bias_grads.astype(jnp.bfloat16), "hd", scatter_dimension=1, tiled=True
        ).astype(jnp.float32),
        lax.psum_scatter(
            grad_hidden_in.astype(jnp.bfloat16), "hd", scatter_dimension=0, tiled=True
        ).astype(jnp.float32),
        lax.psum_scatter(
            grad_hidden_out.astype(jnp.bfloat16), "hd", scatter_dimension=0, tiled=True
        ).astype(jnp.float32),
        lax.psum_scatter(
            grad_hidden_bias.astype(jnp.bfloat16), "hd", scatter_dimension=0, tiled=True
        ).astype(jnp.float32),
    )
    summed = lax.psum(
        (
            summed[0],
            summed[1],
            summed[2],
            summed[3],
            summed[4],
            summed[5],
            summed[6],
            summed[7],
            summed[8],
            summed[9],
            summed[10],
        ),
        "grp",
    )
    (
        qkv_part,
        self_out_part,
        cross_query_part,
        cross_keyval_part,
        cross_out_part,
        gain_part,
        shift_part,
        bias_part,
        hidden_in_part,
        hidden_out_part,
        hidden_bias_part,
    ) = summed
    return (
        layer_output,
        radar_grad,
        optic_grad,
        qkv_part,
        self_out_part,
        cross_query_part,
        cross_keyval_part,
        cross_out_part,
        hidden_in_part,
        hidden_out_part,
        gain_part,
        shift_part,
        bias_part,
        hidden_bias_part,
    )


def solution(mesh):
    placed = (
        P(("grp", "hd"), None),
        P(("grp", "hd"), None),
        P("grp", None, None),
        P(),
        P(),
        P(),
        P(),
        P(),
        P(),
        P(),
        P(),
        P(),
        P(),
        P(),
        P(("grp", "hd"), None),
    )
    return jax.shard_map(
        on_device,
        mesh=mesh,
        in_specs=placed,
        out_specs=(
            P(("grp", "hd"), None),
            P(("grp", "hd"), None),
            P(("grp", "hd"), None),
            P("hd", None),
            P("hd", None),
            P("hd", None),
            P("hd", None),
            P("hd", None),
            P("hd", None),
            P("hd", None),
            P(None, "hd"),
            P(None, "hd"),
            P(None, "hd"),
            P("hd"),
        ),
        check_vma=False,
    )
```

profile of v0, /device:TPU:0, one launch (start us, length us, event | category | flops | bytes accessed | tf_op | source)
XLA Modules:
  0.0 1151.6 jit_solution(8885405016040366465)
XLA Ops:
  18.8 4.4 all-to-all-start
  25.4 10.0 all-to-all-done
  35.5 4.2 all-to-all-start.1
  42.9 8.5 all-to-all-done.1
  51.4 4.2 all-to-all-start.2
  58.1 9.1 all-to-all-done.2
  68.8 28.0 %while.60 = (s32[]{:T(128)}, bf16[4,512,192]{1,2,0:T(8,128)(2,1)}, f32[4,1,3,512,1]{3,2,4,1,0:T(4,128)}, bf16[4,512,192]{1,2,0:T(8,128)(2,1)}, s32[4,512]{1,0:T(...) while((s32[]{:T(128)}, bf16[4,512,192]{1,2,0:T(8,128)(2,1)}, ...), condition=%wide.region_9.10_spmd.clone, body=%wide.region_6.9_spmd.clone.sunk | while | flops 211384848 | bytes 14488729 | solution.py:118
  96.8 4.2 all-to-all-start.3
  107.9 4.9 all-to-all-done.3
  112.7 4.2 all-to-all-start.4
  124.4 4.3 all-to-all-done.4
  128.7 4.2 all-to-all-start.6
  144.6 4.4 all-to-all-start.5
  149.0 11.7 %all-to-all-done.5 = bf16[512,4,192]{0,2,1:T(8,128)(2,1)} async-done(((bf16[512,4,192]{0,2,1:T(8,128)(2,1)}), bf16[512,4,192]{0,2,1:T(8,128)(2,1)}, u32[]{:S(2)}, u32[]{:S(2)}) %all-to-all-start.5) | async-done | bytes 786464 | tf_op jit(solution)/shard_map/all_to_all | solution.py:273
  162.3 24.4 %while.52 = (s32[]{:T(128)}, bf16[4,512,192]{1,2,0:T(8,128)(2,1)}, f32[4,1,3,512,1]{3,2,4,1,0:T(4,128)}, bf16[4,512,192]{1,2,0:T(8,128)(2,1)}, s32[4,512]{1,0:T(...) while((s32[]{:T(128)}, bf16[4,512,192]{1,2,0:T(8,128)(2,1)}, ...), condition=%wide.region_15.16_spmd, body=%wide.region_12.15_spmd.sunk | while | flops 211122688 | bytes 12903521 | solution.py:118
  186.7 4.2 all-to-all-start.7
  192.1 10.5 all-to-all-done.7
  206.1 20.6 %multiply_convert_fusion.2 = (bf16[512,3072]{1,0:T(8,128)(2,1)}, f32[512,3072]{1,0:T(8,128)}, f32[512,3072]{1,0:T(8,128)}) fusion(f32[3072]{0:T(1024)} %param.36, bf16[768,3072]{1,0:T(8,128)(2,1)} %param.33, f32[512,768]{1,0:T(8,128)S(1)} %get-tuple-element.764, f32[768]{0:T(1024)S(1)} %copy-done.42, f32[768]{0:T(1024)S(1)} %copy-done.30, ...), kind=kOutput, calls=%fused_computation.82 | convolution fusion | flops 2521694208 | bytes 22042624 | tf_op jit(solution)/shard_map/dot_general | solution.py:284
  226.8 9.3 fusion.84
  236.1 5.4 multiply_reduce_fusion.2
  249.2 12.9 %all-to-all-start.8 = ((bf16[512,4,192]{0,2,1:T(8,128)(2,1)}), bf16[512,4,192]{0,2,1:T(8,128)(2,1)}, u32[]{:S(2)}, u32[]{:S(2)}) async-start(bf16[512,4,192]{0,2,1:T(8,128)(2,1)} %bitcast.320), calls=%async_computation.8 | async-start | bytes 1572864 | tf_op jit(solution)/shard_map/all_to_all | solution.py:311
  262.1 11.5 all-to-all-done.8
  276.4 41.6 %while.53 = (s32[]{:T(128)}, bf16[4,512,192]{1,2,0:T(8,128)(2,1)}, bf16[4,512,192]{1,2,0:T(8,128)(2,1)}, bf16[4,512,192]{1,2,0:T(8,128)(2,1)}, bf16[4,512,192]{1...) while((s32[]{:T(128)}, bf16[4,512,192]{1,2,0:T(8,128)(2,1)}, ...), condition=%wide.region_22.23_spmd, body=%wide.region_20.22_spmd.sunk | while | flops 511146496 | bytes 28873860 | solution.py:193
  318.0 15.1 %all_to_all.256 = bf16[4,512,192]{1,2,0:T(8,128)(2,1)S(1)} all-to-all(bf16[4,512,192]{1,2,0:T(8,128)(2,1)} %get-tuple-element.497), channel_id=1, replica_groups=mesh['grp'=8,'hd'=4] {'hd'}, dimensions={0} | all-to-all | bytes 1572864 | tf_op jit(solution)/shard_map/all_to_all | solution.py:324
  333.2 4.0 multiply_reduce_fusion.3
  344.4 15.9 %all_to_all.257 = bf16[512,4,192]{0,2,1:T(8,128)(2,1)} all-to-all(bf16[512,4,192]{0,2,1:T(8,128)(2,1)} %bitcast.321), channel_id=1, replica_groups=mesh['grp'=8,'hd'=4] {'hd'}, dimensions={1} | all-to-all | bytes 1572864 | tf_op jit(solution)/shard_map/all_to_all | solution.py:340
  363.1 50.8 %while.61 = (s32[]{:T(128)}, bf16[4,512,192]{1,2,0:T(8,128)(2,1)}, bf16[4,512,192]{1,2,0:T(8,128)(2,1)}, bf16[4,512,192]{1,2,0:T(8,128)(2,1)}, bf16[4,512,192]{1...) while((s32[]{:T(128)}, bf16[4,512,192]{1,2,0:T(8,128)(2,1)}, ...), condition=%wide.region_27.28_spmd.clone, body=%wide.region_25.27_spmd.clone.sunk | while | flops 514554368 | bytes 30983360 | solution.py:193
  414.0 4.5 all-to-all-start.11
  420.9 9.4 all-to-all-done.11
  430.2 4.2 all-to-all-start.12
  437.7 9.5 all-to-all-done.12
  447.2 4.2 all-to-all-start.13
  455.1 8.0 all-to-all-done.13
  463.1 5.9 fusion.73
  483.7 16.3 %all_to_all.258 = bf16[4,512,192]{1,2,0:T(8,128)(2,1)S(1)} all-to-all(bf16[4,512,192]{1,2,0:T(8,128)(2,1)} %get-tuple-element.502), channel_id=1, replica_groups=mesh['grp'=8,'hd'=4] {'hd'}, dimensions={0} | all-to-all | bytes 1572864 | tf_op jit(solution)/shard_map/all_to_all | solution.py:325
  500.1 15.1 %all_to_all.259 = bf16[4,512,192]{1,2,0:T(8,128)(2,1)S(1)} all-to-all(bf16[4,512,192]{1,2,0:T(8,128)(2,1)} %get-tuple-element.503), channel_id=1, replica_groups=mesh['grp'=8,'hd'=4] {'hd'}, dimensions={0} | all-to-all | bytes 1572864 | tf_op jit(solution)/shard_map/all_to_all | solution.py:326
  518.8 4.3 copy.113
  523.8 5.9 convolution_convert_fusion.2
  530.4 7.6 convolution_convert_fusion.1
  538.7 7.2 convolution_convert_fusion
  547.7 6.6 all-reduce
  555.7 7.7 select_convert_fusion
  573.7 4.2 reduce-scatter.21.cloned.1.call-done
  577.9 36.4 %reduce-scatter.31.cloned.1.call-done = bf16[192,1536]{1,0:T(8,128)(2,1)} async-done(((bf16[768,1536]{1,0:T(8,128)(2,1)}), bf16[192,1536]{1,0:T(8,128)(2,1)}) %reduce-scatter.31.cloned.1.call-update) | async-done | bytes 589840
  616.5 40.8 %reduce-scatter.19.cloned.1.call-done = bf16[192,2304]{1,0:T(8,128)(2,1)} async-done(((bf16[768,2304]{1,0:T(8,128)(2,1)}), bf16[192,2304]{1,0:T(8,128)(2,1)}) %reduce-scatter.19.cloned.1.call-update) | async-done | bytes 884752 | tf_op jit(solution)/shard_map/reduce_scatter | solution.py:357
  657.3 50.6 %reduce-scatter.27.cloned.1.call-done = bf16[192,3072]{1,0:T(8,128)(2,1)} async-done(((bf16[768,3072]{1,0:T(8,128)(2,1)}), bf16[192,3072]{1,0:T(8,128)(2,1)}) %reduce-scatter.27.cloned.1.call-update) | async-done | bytes 1179664 | tf_op jit(solution)/shard_map/reduce_scatter | solution.py:381
  707.9 50.3 %reduce-scatter.29.cloned.1.call-done = bf16[768,768]{1,0:T(8,128)(2,1)} async-done(((bf16[3072,768]{1,0:T(8,128)(2,1)}), bf16[768,768]{1,0:T(8,128)(2,1)}) %reduce-scatter.29.cloned.1.call-update) | async-done | bytes 1179664 | tf_op jit(solution)/shard_map/reduce_scatter | solution.py:384
  758.1 383.3 %all-reduce.3 = (f32[192,2304]{1,0:T(8,128)}, f32[192,768]{1,0:T(8,128)}, f32[192,768]{1,0:T(8,128)}, f32[192,1536]{0,1:T(8,128)}, f32[192,768]{1,0:T(8,128)}, /...) all-reduce(bf16[192,2304]{1,0:T(8,128)(2,1)} %reduce-scatter.19.clo, ...), channel_id=1, replica_groups=mesh['grp'=8,'hd'=4] {'grp'}, use_global_device_ids=true, to_apply=%region_31.32 | all-reduce | flops 2361792 | bytes 14172288 | tf_op jit(solution)/shard_map/psum | solution.py:391
  (450 shorter events, 265.5 us)
Async XLA Ops:
  8.7 6.3 copy-start.17
  18.8 20.9 %copy-start.41 = (s32[1,4,3]{1,0,2:T(1,128)S(1)}, s32[1,4,3]{1,0,2:T(1,128)}, u32[]{:S(2)}) copy-start(s32[1,4,3]{1,0,2:T(1,128)} %param.25) | copy-start | bytes 148
  18.8 16.7 %all-to-all-start = ((bf16[512,4,192]{0,2,1:T(8,128)(2,1)}), bf16[512,4,192]{0,2,1:T(8,128)(2,1)}, u32[]{:S(2)}, u32[]{:S(2)}) async-start(bf16[512,4,192]{0,2,1:T(8,128)(2,1)} %bitcast.319), calls=%async_computation | async-start | bytes 1572864 | tf_op jit(solution)/shard_map/all_to_all | solution.py:254
  35.5 15.9 %all-to-all-start.1 = ((bf16[512,4,192]{0,2,1:T(8,128)(2,1)}), bf16[512,4,192]{0,2,1:T(8,128)(2,1)}, u32[]{:S(2)}, u32[]{:S(2)}) async-start(bf16[512,4,192]{0,2,1:T(8,128)(2,1)} %bitcast.317), calls=%async_computation.1 | async-start | bytes 1572864 | tf_op jit(solution)/shard_map/all_to_all | solution.py:252
  51.4 15.9 %all-to-all-start.2 = ((bf16[512,4,192]{0,2,1:T(8,128)(2,1)}), bf16[512,4,192]{0,2,1:T(8,128)(2,1)}, u32[]{:S(2)}, u32[]{:S(2)}) async-start(bf16[512,4,192]{0,2,1:T(8,128)(2,1)} %bitcast.314), calls=%async_computation.2 | async-start | bytes 1572864 | tf_op jit(solution)/shard_map/all_to_all | solution.py:253
  96.8 7.5 copy-start.14
  96.8 15.9 %all-to-all-start.3 = ((bf16[4,512,192]{1,2,0:T(8,128)(2,1)}), bf16[4,512,192]{1,2,0:T(8,128)(2,1)}, u32[]{:S(2)}, u32[]{:S(2)}) async-start(bf16[4,512,192]{1,2,0:T(8,128)(2,1)} %get-tuple-element.494), calls=%async_computation.3 | async-start | bytes 1572864 | tf_op jit(solution)/shard_map/all_to_all | solution.py:264
  112.7 15.9 %all-to-all-start.4 = ((bf16[512,4,192]{0,2,1:T(8,128)(2,1)}), bf16[512,4,192]{0,2,1:T(8,128)(2,1)}, u32[]{:S(2)}, u32[]{:S(2)}) async-start(bf16[512,4,192]{0,2,1:T(8,128)(2,1)} %bitcast.315), calls=%async_computation.4 | async-start | bytes 1572864 | tf_op jit(solution)/shard_map/all_to_all | solution.py:256
  124.4 212.8 %copy-start.19 = (f32[512]{0:T(512)}, f32[512]{0:T(512)S(1)}, u32[]{:S(2)}) copy-start(f32[512]{0:T(512)S(1)} %broadcast_multiply_fusion.1) | copy-start | bytes 6148
  128.7 15.9 %all-to-all-start.6 = ((bf16[512,4,192]{0,2,1:T(8,128)(2,1)}), bf16[512,4,192]{0,2,1:T(8,128)(2,1)}, u32[]{:S(2)}, u32[]{:S(2)}) async-start(bf16[512,4,192]{0,2,1:T(8,128)(2,1)} %bitcast.316), calls=%async_computation.6 | async-start | bytes 1572864 | tf_op jit(solution)/shard_map/all_to_all | solution.py:255
  144.6 16.2 %all-to-all-start.5 = ((bf16[512,4,192]{0,2,1:T(8,128)(2,1)}), bf16[512,4,192]{0,2,1:T(8,128)(2,1)}, u32[]{:S(2)}, u32[]{:S(2)}) async-start(bf16[512,4,192]{0,2,1:T(8,128)(2,1)} %bitcast.318), calls=%async_computation.5 | async-start | bytes 1572864 | tf_op jit(solution)/shard_map/all_to_all | solution.py:273
  186.7 15.9 %all-to-all-start.7 = ((bf16[4,512,192]{1,2,0:T(8,128)(2,1)}), bf16[4,512,192]{1,2,0:T(8,128)(2,1)}, u32[]{:S(2)}, u32[]{:S(2)}) async-start(bf16[4,512,192]{1,2,0:T(8,128)(2,1)} %get-tuple-element.495), calls=%async_computation.7 | async-start | bytes 1572864 | tf_op jit(solution)/shard_map/all_to_all | solution.py:277
  202.6 24.1 %slice-start.2 = ((s8[4718592]{0:T(1024)(128)(4,1)}), s8[4194304]{0:T(1024)(128)(4,1)S(1)}, s32[]{:S(2)}) async-start(s8[4718592]{0:T(1024)(128)(4,1)} %bitcast.346), calls=%async_computation.38 | async-start | bytes 8388608
  202.6 33.5 %slice-start = ((s8[4718592]{0:T(1024)(128)(4,1)}), s8[4194304]{0:T(1024)(128)(4,1)S(1)}, s32[]{:S(2)}) async-start(s8[4718592]{0:T(1024)(128)(4,1)} %bitcast.344), calls=%async_computation.36 | async-start | bytes 8388608
  205.7 35.9 %copy-start.7 = (f32[512,768]{1,0:T(8,128)}, f32[512,768]{1,0:T(8,128)S(1)}, u32[]{:S(2)}) copy-start(f32[512,768]{1,0:T(8,128)S(1)} %get-tuple-element.764) | copy-start | bytes 4718596
  205.7 35.8 %copy-start.20 = (f32[512]{0:T(512)}, f32[512]{0:T(512)S(1)}, u32[]{:S(2)}) copy-start(f32[512]{0:T(512)S(1)} %broadcast_multiply_fusion) | copy-start | bytes 6148
  206.0 35.5 %copy-start.36 = (f32[512]{0:T(512)}, f32[512]{0:T(512)S(1)}, u32[]{:S(2)}) copy-start(f32[512]{0:T(512)S(1)} %fusion.60) | copy-start | bytes 6148
  206.1 20.7 %copy-start.4 = (bf16[512,768]{1,0:T(8,128)(2,1)S(1)}, bf16[512,768]{1,0:T(8,128)(2,1)}, u32[]{:S(2)}) copy-start(bf16[512,768]{1,0:T(8,128)(2,1)} %param.37) | copy-start | bytes 2359300
  206.1 20.7 %copy-start.38 = (pred[512]{0:T(512)(128)(4,1)S(1)}, pred[512]{0:T(512)(128)(4,1)}, u32[]{:S(2)}) copy-start(pred[512]{0:T(512)(128)(4,1)} %dynamic-slice_reduce_fusion) | copy-start | bytes 1540
  206.1 20.7 %slice-start.3 = ((s8[4718592]{0:T(1024)(128)(4,1)}), s8[524288]{0:T(1024)(128)(4,1)S(1)}, s32[]{:S(2)}) async-start(s8[4718592]{0:T(1024)(128)(4,1)} %bitcast.346), calls=%async_computation.39 | async-start | bytes 1048576
  206.1 20.7 %copy-start.51 = (f32[3072]{0:T(1024)S(1)}, f32[3072]{0:T(1024)}, u32[]{:S(2)}) copy-start(f32[3072]{0:T(1024)} %param.36) | copy-start | bytes 36868
  206.1 30.0 %slice-start.1 = ((s8[4718592]{0:T(1024)(128)(4,1)}), s8[524288]{0:T(1024)(128)(4,1)S(1)}, s32[]{:S(2)}) async-start(s8[4718592]{0:T(1024)(128)(4,1)} %bitcast.344), calls=%async_computation.37 | async-start | bytes 1048576
  249.2 24.4 %all-to-all-start.8 = ((bf16[512,4,192]{0,2,1:T(8,128)(2,1)}), bf16[512,4,192]{0,2,1:T(8,128)(2,1)}, u32[]{:S(2)}, u32[]{:S(2)}) async-start(bf16[512,4,192]{0,2,1:T(8,128)(2,1)} %bitcast.320), calls=%async_computation.8 | async-start | bytes 1572864 | tf_op jit(solution)/shard_map/all_to_all | solution.py:311
  414.0 6.0 copy-start.37
  414.0 16.3 %all-to-all-start.11 = ((bf16[4,512,192]{1,2,0:T(8,128)(2,1)}), bf16[4,512,192]{1,2,0:T(8,128)(2,1)}, u32[]{:S(2)}, u32[]{:S(2)}) async-start(bf16[4,512,192]{1,2,0:T(8,128)(2,1)} %get-tuple-element.499), calls=%async_computation.11 | async-start | bytes 1572864 | tf_op jit(solution)/shard_map/all_to_all | solution.py:345
  418.5 147.4 %reduce-scatter.37.cloned.1.call-start = ((), (), s32[]{:S(2)}) async-start(), calls=%async_computation.35 | async-start | bytes 245760
  430.2 17.0 %all-to-all-start.12 = ((bf16[4,512,192]{1,2,0:T(8,128)(2,1)}), bf16[4,512,192]{1,2,0:T(8,128)(2,1)}, u32[]{:S(2)}, u32[]{:S(2)}) async-start(bf16[4,512,192]{1,2,0:T(8,128)(2,1)} %get-tuple-element.500), calls=%async_computation.12 | async-start | bytes 1572864 | tf_op jit(solution)/shard_map/all_to_all | solution.py:346
  434.4 17.0 %copy-start.46 = (bf16[768]{0:T(1024)(128)(2,1)S(1)}, bf16[768]{0:T(1024)(128)(2,1)}, u32[]{:S(2)}) copy-start(bf16[768]{0:T(1024)(128)(2,1)} %get-tuple-element.621) | copy-start | bytes 4612
  434.4 17.6 %copy-start.45 = (bf16[768]{0:T(1024)(128)(2,1)S(1)}, bf16[768]{0:T(1024)(128)(2,1)}, u32[]{:S(2)}) copy-start(bf16[768]{0:T(1024)(128)(2,1)} %get-tuple-element.614) | copy-start | bytes 4612
  434.4 28.7 %copy-start.16 = (f32[768]{0:T(1024)S(1)}, f32[768]{0:T(1024)}, u32[]{:S(2)}) copy-start(f32[768]{0:T(1024)} %copy-done.15) | copy-start | bytes 9220
  434.4 28.7 %copy-start.18 = (f32[512]{0:T(512)S(1)}, f32[512]{0:T(512)}, u32[]{:S(2)}) copy-start(f32[512]{0:T(512)} %copy-done.17) | copy-start | bytes 6148
  434.5 137.5 %reduce-scatter.25.cloned.1.call-start = ((), (), s32[]{:S(2)}) async-start(), calls=%async_computation.29 | async-start | bytes 1474560 | tf_op jit(solution)/shard_map/reduce_scatter | solution.py:369
  447.2 15.9 %all-to-all-start.13 = ((bf16[4,512,192]{1,2,0:T(8,128)(2,1)}), bf16[4,512,192]{1,2,0:T(8,128)(2,1)}, u32[]{:S(2)}, u32[]{:S(2)}) async-start(bf16[4,512,192]{1,2,0:T(8,128)(2,1)} %get-tuple-element.501), calls=%async_computation.13 | async-start | bytes 1572864 | tf_op jit(solution)/shard_map/all_to_all | solution.py:347
  451.4 120.5 %reduce-scatter.35.cloned.1.call-start = ((), (), s32[]{:S(2)}) async-start(), calls=%async_computation.34 | async-start | bytes 245760
  463.1 5.9 copy-start.32
  463.1 5.9 copy-start.33
  474.7 98.1 %reduce-scatter.33.cloned.1.call-start = ((), (), s32[]{:S(2)}) async-start(), calls=%async_computation.33 | async-start | bytes 245760
  476.3 97.3 %reduce-scatter.23.cloned.1.call-start = ((), (), s32[]{:S(2)}) async-start(), calls=%async_computation.28 | async-start | bytes 1474560 | tf_op jit(solution)/shard_map/reduce_scatter | solution.py:363
  480.2 97.8 %reduce-scatter.21.cloned.1.call-start = ((), (), s32[]{:S(2)}) async-start(), calls=%async_computation.27 | async-start | bytes 1474560 | tf_op jit(solution)/shard_map/reduce_scatter | solution.py:360
  483.7 130.6 %reduce-scatter.31.cloned.1.call-start = ((), (), s32[]{:S(2)}) async-start(), calls=%async_computation.32 | async-start | bytes 2949120
  483.7 32.3 %copy-start.50 = (bf16[512,768]{1,0:T(8,128)(2,1)S(1)}, bf16[512,768]{1,0:T(8,128)(2,1)}, u32[]{:S(2)}) copy-start(bf16[512,768]{1,0:T(8,128)(2,1)} %param.24) | copy-start | bytes 2359300
  500.1 15.1 %copy-start.9 = (bf16[4,512,192]{1,2,0:T(8,128)(2,1)}, bf16[4,512,192]{1,2,0:T(8,128)(2,1)S(1)}, u32[]{:S(2)}) copy-start(bf16[4,512,192]{1,2,0:T(8,128)(2,1)S(1)} %all_to_all.258) | copy-start | bytes 2359300
  523.1 134.2 %reduce-scatter.19.cloned.1.call-start = ((), (), s32[]{:S(2)}) async-start(), calls=%async_computation.26 | async-start | bytes 4423680 | tf_op jit(solution)/shard_map/reduce_scatter | solution.py:357
  529.8 178.1 %reduce-scatter.27.cloned.1.call-start = ((), (), s32[]{:S(2)}) async-start(), calls=%async_computation.30 | async-start | bytes 5898240 | tf_op jit(solution)/shard_map/reduce_scatter | solution.py:381
  538.0 220.1 %reduce-scatter.29.cloned.1.call-start = ((), (), s32[]{:S(2)}) async-start(), calls=%async_computation.31 | async-start | bytes 5898240 | tf_op jit(solution)/shard_map/reduce_scatter | solution.py:384
  555.7 7.7 copy-start.10
  555.7 7.7 copy-start.12
  555.7 7.7 copy-start.47
  (30 other events, 66.4 us)
Sparse Core Ops, SparseCore 0:
  422.4 23.2 reduce-scatter.36
  448.2 25.8 reduce-scatter.24
  477.3 20.7 reduce-scatter.34
  501.1 19.7 reduce-scatter.32
  523.5 25.7 reduce-scatter.22
  552.2 25.6 reduce-scatter.20
  581.2 33.0 reduce-scatter.30
  616.8 40.4 reduce-scatter.18
  660.0 47.8 reduce-scatter.26
  710.3 47.8 reduce-scatter.28
where the time goes:
time: 1160 us; the launch traced here: 1150 us
  blocking collectives  452 us (39%)
  waiting for transfers between devices  283 us (24%)
  matrix products  152 us (13%)
  local copies, waits for them, and re-layouts  142 us (12%)
  starting transfers between devices  60.5 us (5%)
  other arithmetic  45.2 us (4%)
  between operations  16 us (1%)
    psum x1, blocking collectives, on_device(): lax.psum((summed[0], summed[1], summed[2], summed[3], summed[4], summed[5...  383 us
    dynamic_slice x76, local copies, waits for them, and re-layouts, attention_forward(): lax.map(per_source, (queries.reshape(sources, source_rows, columns), key_...  54.8 us
    reduce_scatter x1, waiting for transfers between devices, on_device(): lax.psum_scatter(grad_hidden_in.astype(jnp.bfloat16), 'hd', scatter_dimen...  50.6 us
    reduce_scatter x1, waiting for transfers between devices, on_device(): lax.psum_scatter(grad_hidden_out.astype(jnp.bfloat16), 'hd', scatter_dime...  50.3 us
    reduce_scatter x1, waiting for transfers between devices, on_device(): lax.psum_scatter(grad_self_qkv.astype(jnp.bfloat16), 'hd', scatter_dimens...  40.8 us
    unnamed x14, waiting for transfers between devices  36.5 us
    dot_general x7, matrix products, inner_rows(): lax.dot_general(left, right, (((0,), (0,)), ((), ())), preferred_element_...  33.8 us
    dot_general x7, matrix products, times_transpose(): lax.dot_general(left, right, (((1,), (1,)), ((), ())), preferred_element_...  30.6 us
  transfers between devices with their start and end apart: 22, of which 17 were waited for; matrix products, arithmetic and copies ran while one was open for 10% of the time, Pallas kernels for 0%

commit v1 on v0

v1 whole, which is shorter than its diff:
```python
import functools
import math

import jax
import jax.numpy as jnp
import numpy as np
from jax import lax
from jax.experimental import pallas as pl
from jax.experimental.pallas import tpu as pltpu
from jax.sharding import PartitionSpec as P

HEADS = 12
HDIM = 64
SIDES = (12, 15, 20)
QUAD = 4
EPSILON = 1e-06
MASKED = -1e30
FAR = 1e33
F32 = jnp.float32
BF16 = jnp.bfloat16
VMEM_LIMIT = 56 * 1024 * 1024


def rows_in_use(local_rows, slots):
    counts = [0] + [side * side for side in SIDES]
    sums = {0}
    for _ in range(slots):
        sums = {a + b for a in sums for b in counts if a + b <= local_rows}
    return min(local_rows, -(-max(sums) // 16) * 16)


def dot_nn(left, right):
    return lax.dot_general(left, right, (((1,), (0,)), ((), ())), preferred_element_type=F32)


def dot_nt(left, right):
    return lax.dot_general(left, right, (((1,), (1,)), ((), ())), preferred_element_type=F32)


def norm_parts(values):
    average = jnp.mean(values, axis=-1, keepdims=True)
    centred = values - average
    variance = jnp.mean(centred * centred, axis=-1, keepdims=True)
    return centred, lax.rsqrt(variance + EPSILON)


def norm(values, gain, shift):
    centred, inverse = norm_parts(values)
    return centred * inverse * gain + shift


def norm_back(values, gain, grad):
    centred, inverse = norm_parts(values)
    unit = centred * inverse
    gain_grad = jnp.sum(grad * unit, axis=0, keepdims=True)
    shift_grad = jnp.sum(grad, axis=0, keepdims=True)
    scaled = grad * gain
    lift = jnp.mean(scaled, axis=-1, keepdims=True)
    tilt = jnp.mean(scaled * unit, axis=-1, keepdims=True)
    return inverse * (scaled - lift - unit * tilt), gain_grad, shift_grad


def layout_of(lens_ref, shape, dim):
    place = lax.broadcasted_iota(jnp.int32, shape, dim)
    count = [lens_ref[i] for i in range(3)]
    ends = [count[0], count[0] + count[1], count[0] + count[1] + count[2]]
    zero = jnp.zeros(shape, jnp.int32)
    segment = zero
    for end in ends:
        segment = segment + jnp.where(place >= end, 1, 0)
    sides = [
        jnp.where(c == SIDES[0] ** 2, SIDES[0], jnp.where(c == SIDES[1] ** 2, SIDES[1], SIDES[2]))
        for c in count
    ]
    start = jnp.where(segment == 0, 0, jnp.where(segment == 1, ends[0], ends[1]))
    side = jnp.where(segment == 0, sides[0], jnp.where(segment == 1, sides[1], sides[2])).astype(F32)
    offset = (place - start).astype(F32)
    row = jnp.floor((offset + 0.5) / side)
    col = offset - row * side
    valid = segment < 3
    return segment, jnp.where(valid, row, 0.0), jnp.where(valid, col, 0.0), valid


def gelu_parts(values):
    bell = jnp.exp(values * values * -0.5)
    size = jnp.abs(values) * math.sqrt(0.5)
    t = 1.0 / (1.0 + 0.3275911 * size)
    poly = t * (
        0.254829592
        + t * (-0.284496736 + t * (1.421413741 + t * (-1.453152027 + t * 1.061405429)))
    )
    tail = 0.5 * poly * bell
    below = jnp.where(values < 0, tail, 1.0 - tail)
    return values * below, below + values * bell * (1.0 / math.sqrt(2.0 * math.pi))


def whole(shape):
    return pl.BlockSpec(shape, lambda *_: (0,) * len(shape))


def smem():
    return pl.BlockSpec(memory_space=pltpu.SMEM)


def cols(rows, width, first=0):
    return pl.BlockSpec((rows, width), lambda j, *_: (0, first + j))


def rowblk(height, width, first=0):
    return pl.BlockSpec((height, width), lambda j, *_: (first + j, 0))


def params(**kw):
    return pltpu.CompilerParams(vmem_limit_bytes=VMEM_LIMIT, dimension_semantics=("arbitrary",), **kw)


def attend_quad(q, k, v, add_bias, probs_ref):
    lane = lax.broadcasted_iota(jnp.int32, q.shape, 1)
    scaled = q * jnp.asarray(HDIM**-0.5, BF16)
    v_t = v.T
    outs = []
    for h in range(QUAD):
        q_h = jnp.where(lane // HDIM == h, scaled, jnp.zeros_like(scaled))
        scores = add_bias(dot_nt(k, q_h), h)
        top = jnp.max(scores, axis=0, keepdims=True)
        weights = jnp.exp(scores - top)
        total = jnp.sum(weights, axis=0, keepdims=True)
        probs = (weights * (1.0 / total)).astype(BF16)
        probs_ref[h] = probs
        outs.append(dot_nn(v_t[h * HDIM : (h + 1) * HDIM], probs))
    return jnp.concatenate(outs, axis=0).astype(BF16).T


def self_forward_kernel(
    lens, slopes, radar, gain, shift, gain_next, shift_next, bias, wq, wk, wv, wo,
    n1, q_out, k_out, v_out, probs, att_out, resid, n2, dist,
):
    j = pl.program_id(0)
    rows = n1.shape[0]

    @pl.when(j == 0)
    def _():
        wide = radar[...].astype(F32)
        n1[...] = norm(wide, gain[...], shift[...]).astype(BF16)
        resid[...] = wide + bias[...]
        seg_k, row_k, col_k, _ = layout_of(lens, (rows, 1), 0)
        seg_q, row_q, col_q, _ = layout_of(lens, (1, rows), 1)
        dr = row_k - row_q
        dc = col_k - col_q
        dist[...] = jnp.where(seg_k == seg_q, jnp.sqrt(dr * dr + dc * dc), FAR)

    x = n1[...]
    q = dot_nn(x, wq[...]).astype(BF16)
    k = dot_nn(x, wk[...]).astype(BF16)
    v = dot_nn(x, wv[...]).astype(BF16)
    q_out[...] = q
    k_out[...] = k
    v_out[...] = v
    att = attend_quad(
        q, k, v, lambda s, h: s - slopes[j * QUAD + h] * dist[...], probs
    )
    att_out[...] = att
    resid[...] += dot_nn(att, wo[...])

    @pl.when(j == pl.num_programs(0) - 1)
    def _():
        n2[...] = norm(resid[...], gain_next[...], shift_next[...]).astype(BF16)


def cross_forward_kernel(
    lens, res_in, n_in, optic, gain_next, shift_next, bias, wq, wk, wv, wo,
    q_out, k_out, v_out, probs, att_out, resid, n3, mask,
):
    j = pl.program_id(0)
    rows = n_in.shape[0]

    @pl.when(j == 0)
    def _():
        resid[...] = res_in[...] + bias[...]
        seg_k = layout_of(lens, (rows, 1), 0)[0]
        seg_q = layout_of(lens, (1, rows), 1)[0]
        mask[...] = jnp.where(seg_k == seg_q, 0.0, MASKED)

    q = dot_nn(n_in[...], wq[...]).astype(BF16)
    k = dot_nn(optic[...], wk[...]).astype(BF16)
    v = dot_nn(optic[...], wv[...]).astype(BF16)
    q_out[...] = q
    k_out[...] = k
    v_out[...] = v
    att = attend_quad(q, k, v, lambda s, h: s + mask[...], probs)
    att_out[...] = att
    resid[...] += dot_nn(att, wo[...])

    @pl.when(j == pl.num_programs(0) - 1)
    def _():
        n3[...] = norm(resid[...], gain_next[...], shift_next[...]).astype(BF16)


def shaped(*shape, dtype=BF16):
    return jax.ShapeDtypeStruct(shape, dtype)


def self_forward(rows, lens, slopes, radar, gains, shifts, biases, w_qkv, w_out):
    d = radar.shape[1]
    wide = QUAD * HDIM
    steps = d // wide
    return pl.pallas_call(
        self_forward_kernel,
        grid=(steps,),
        in_specs=[
            smem(), smem(), whole((rows, d)),
            *[whole((1, d))] * 5,
            cols(d, wide), cols(d, wide, steps), cols(d, wide, 2 * steps), rowblk(wide, d),
        ],
        out_specs=[
            whole((rows, d)), cols(rows, wide), cols(rows, wide), cols(rows, wide),
            pl.BlockSpec((QUAD, rows, rows), lambda j: (j, 0, 0)),
            cols(rows, wide), whole((rows, d)), whole((rows, d)),
        ],
        out_shape=[
            shaped(rows, d), shaped(rows, d), shaped(rows, d), shaped(rows, d),
            shaped(HEADS, rows, rows), shaped(rows, d), shaped(rows, d, dtype=F32), shaped(rows, d),
        ],
        scratch_shapes=[pltpu.VMEM((rows, rows), F32)],
        compiler_params=params(),
        name="self_forward",
    )(lens, slopes, radar, gains[0:1], shifts[0:1], gains[1:2], shifts[1:2], biases[0:1],
      w_qkv, w_qkv, w_qkv, w_out)


def cross_forward(rows, lens, res_in, n_in, optic, gains, shifts, biases, w_q, w_kv, w_out):
    d = optic.shape[1]
    wide = QUAD * HDIM
    steps = d // wide
    return pl.pallas_call(
        cross_forward_kernel,
        grid=(steps,),
        in_specs=[
            smem(), whole((rows, d)), whole((rows, d)), whole((rows, d)),
            *[whole((1, d))] * 3,
            cols(d, wide), cols(d, wide), cols(d, wide, steps), rowblk(wide, d),
        ],
        out_specs=[
            cols(rows, wide), cols(rows, wide), cols(rows, wide),
            pl.BlockSpec((QUAD, rows, rows), lambda j: (j, 0, 0)),
            cols(rows, wide), whole((rows, d)), whole((rows, d)),
        ],
        out_shape=[
            shaped(rows, d), shaped(rows, d), shaped(rows, d),
            shaped(HEADS, rows, rows), shaped(rows, d), shaped(rows, d, dtype=F32), shaped(rows, d),
        ],
        scratch_shapes=[pltpu.VMEM((rows, rows), F32)],
        compiler_params=params(),
        name="cross_forward",
    )(lens, res_in, n_in, optic, gains[2:3], shifts[2:3], biases[1:2], w_q, w_kv, w_kv, w_out)


def place(meta, keep, send, grad, spot=None):
    first = meta[4] == 0
    part = grad.shape[0] // 8
    for y in range(2):
        for x in range(2):
            at = y * 4 + x
            low = grad[at * part : (at + 1) * part]
            high = grad[(at + 2) * part : (at + 3) * part]
            where_to = (y ^ meta[3]) * 2 + (x ^ meta[5])
            to = (where_to,) if spot is None else (where_to, slice(None), spot)
            keep[to] = jnp.where(first, low, high)
            send[to] = jnp.where(first, high, low)


def hidden_kernel(
    meta, res2, n3, cot, gain, bias, hb, win, wout,
    y_out, grad_two, dwin, dwin_s, dwout, dwout_s, dhb, gain_g, shift_g, bias_g,
    n3_t, gf, acc_y, acc_n,
):
    j = pl.program_id(0)
    rows = n3.shape[0]

    @pl.when(j == 0)
    def _():
        valid = layout_of(meta, (rows, 1), 0)[3]
        gf[...] = jnp.where(valid, cot[...], jnp.zeros_like(cot))
        n3_t[...] = n3[...].T
        acc_y[...] = jnp.zeros_like(acc_y)
        acc_n[...] = jnp.zeros_like(acc_n)

    act, slope = gelu_parts(dot_nn(n3[...], win[...]) + hb[...])
    act = act.astype(BF16)
    g_pre = (dot_nt(gf[...], wout[...]) * slope).astype(BF16)
    acc_y[...] += dot_nn(act, wout[...])
    acc_n[...] += dot_nt(g_pre, win[...])
    place(meta, dwin, dwin_s, dot_nn(n3_t[...], g_pre).astype(BF16))
    grad = dot_nn(act.T, gf[...]).astype(BF16)
    half = grad.shape[0] // 2
    mine = lax.rem(j, 2) == meta[4]

    def put(out):
        for x in range(2):
            out[x ^ meta[5]] = grad[x * half : (x + 1) * half]

    pl.when(mine)(lambda: put(dwout))
    pl.when(jnp.logical_not(mine))(lambda: put(dwout_s))
    dhb[...] = jnp.sum(g_pre.astype(F32), axis=0, keepdims=True)

    @pl.when(j == pl.num_programs(0) - 1)
    def _():
        valid = layout_of(meta, (rows, 1), 0)[3]
        y = jnp.where(valid, res2[...] + (acc_y[...] + bias[...]), 0.0)
        y_out[0:rows] = y.astype(BF16)
        if y_out.shape[0] > rows:
            y_out[rows:] = jnp.zeros((y_out.shape[0] - rows, y_out.shape[1]), BF16)
        part, g_gain, g_shift = norm_back(res2[...], gain[...], acc_n[...])
        wide = gf[...].astype(F32)
        grad_two[...] = wide + part
        gain_g[...] = g_gain
        shift_g[...] = g_shift
        bias_g[...] = jnp.sum(wide, axis=0, keepdims=True)


def hidden(rows, meta, res2, n3, cot, gains, biases, hb, win, wout):
    d = n3.shape[1]
    ff = win.shape[1]
    chunk = ff // 4
    vec = shaped(1, d, dtype=F32)
    eighth = shaped(4, d // 8, ff)
    wide = pl.BlockSpec((4, d // 8, chunk), lambda j, m: (0, 0, j))
    tall = pl.BlockSpec((2, ff // 8, d), lambda j, m: ((j // 2) ^ m[3], 0, 0))
    return pl.pallas_call(
        hidden_kernel,
        grid_spec=pltpu.PrefetchScalarGridSpec(
            num_scalar_prefetch=1,
            grid=(4,),
            in_specs=[
                whole((rows, d)), whole((rows, d)), whole((rows, d)),
                whole((1, d)), whole((1, d)), cols(1, chunk), cols(d, chunk), rowblk(chunk, d),
            ],
            out_specs=[
                whole((cot.shape[0], d)), whole((rows, d)), wide, wide, tall, tall,
                cols(1, chunk), whole((1, d)), whole((1, d)), whole((1, d)),
            ],
            scratch_shapes=[
                pltpu.VMEM((d, rows), BF16), pltpu.VMEM((rows, d), BF16),
                pltpu.VMEM((rows, d), F32), pltpu.VMEM((rows, d), F32),
            ],
        ),
        out_shape=[
            shaped(cot.shape[0], d), shaped(rows, d, dtype=F32), eighth, eighth,
            shaped(4, ff // 8, d), shaped(4, ff // 8, d),
            shaped(1, ff, dtype=F32), vec, vec, vec,
        ],
        compiler_params=params(),
        name="hidden",
    )(meta, res2, n3, cot, gains[2:3], biases[2:3], hb, win, wout)


def quad_back(q, k, v, att, g_att, probs):
    lane = lax.broadcasted_iota(jnp.int32, q.shape, 1)
    nil = jnp.zeros_like(q)
    g_t = g_att.T
    k_t = k.T
    inner = g_t.astype(F32) * att.T.astype(F32)
    dq_t, dk, dv = [], 0.0, 0.0
    for h in range(QUAD):
        part = slice(h * HDIM, (h + 1) * HDIM)
        mine = lane // HDIM == h
        delta = jnp.sum(inner[part], axis=0, keepdims=True)
        v_h = jnp.where(mine, v, nil)
        p = probs[h]
        g_scores = (p.astype(F32) * (dot_nn(v_h, g_t) - delta)).astype(BF16)
        dv = dv + dot_nn(p, jnp.where(mine, g_att, nil))
        dk = dk + dot_nn(g_scores, jnp.where(mine, q, nil))
        dq_t.append(dot_nn(k_t[part], g_scores))
    scale = HDIM**-0.5
    dq = (jnp.concatenate(dq_t, axis=0) * scale).astype(BF16).T
    return dq, (dk * scale).astype(BF16), dv.astype(BF16)


def cross_back_kernel(
    meta, grad_in, res1, n2, optic, q, k, v, att, probs, gain, wo, wq, wk, wv, att_all,
    grad_one, optic_g, keep, send, bias_g, gain_g, shift_g,
    gc, n2_t, op_t, acc,
):
    j = pl.program_id(0)
    rows, d = n2.shape
    wide = q.shape[1]

    @pl.when(j == 0)
    def _():
        low = grad_in[...].astype(BF16)
        gc[...] = low
        bias_g[...] = jnp.sum(low.astype(F32), axis=0, keepdims=True)
        n2_t[...] = n2[...].T
        op_t[...] = optic[...].T
        acc[...] = jnp.zeros_like(acc)
        optic_g[...] = jnp.zeros_like(optic_g)
        place(meta, keep, send, dot_nn(att_all[...].T, low).astype(BF16), slice(0, d))

    g_att = dot_nt(gc[...], wo[...]).astype(BF16)
    dq, dk, dv = quad_back(q[...], k[...], v[...], att[...], g_att, probs)

    def put(grad, first):
        spot = pl.ds(pl.multiple_of(first * d + j * wide, wide), wide)
        place(meta, keep, send, grad.astype(BF16), spot)

    put(dot_nn(n2_t[...], dq), 1)
    put(dot_nn(op_t[...], dk), 2)
    put(dot_nn(op_t[...], dv), 3)
    optic_g[0:rows] += dot_nt(dk, wk[...]) + dot_nt(dv, wv[...])
    acc[...] += dot_nt(dq, wq[...])

    @pl.when(j == pl.num_programs(0) - 1)
    def _():
        part, g_gain, g_shift = norm_back(res1[...], gain[...], acc[...])
        grad_one[...] = grad_in[...] + part
        gain_g[...] = g_gain
        shift_g[...] = g_shift


def cross_back(rows, meta, grad_in, res1, n2, optic, q, k, v, att, probs, gains, wo, wq, wkv):
    d = n2.shape[1]
    wide = QUAD * HDIM
    steps = d // wide
    vec = shaped(1, d, dtype=F32)
    eighth = (4, d // 8, 4 * d)
    return pl.pallas_call(
        cross_back_kernel,
        grid=(steps,),
        in_specs=[
            smem(), whole((rows, d)), whole((rows, d)), whole((rows, d)), whole((rows, d)),
            *[cols(rows, wide)] * 4,
            pl.BlockSpec((QUAD, rows, rows), lambda j: (j, 0, 0)),
            whole((1, d)), rowblk(wide, d), cols(d, wide), cols(d, wide), cols(d, wide, steps),
            whole((rows, d)),
        ],
        out_specs=[
            whole((rows, d)), whole((optic.shape[0], d)), whole(eighth), whole(eighth),
            whole((1, d)), whole((1, d)), whole((1, d)),
        ],
        out_shape=[
            shaped(rows, d, dtype=F32), shaped(optic.shape[0], d, dtype=F32),
            shaped(*eighth), shaped(*eighth), vec, vec, vec,
        ],
        scratch_shapes=[
            pltpu.VMEM((rows, d), BF16), pltpu.VMEM((d, rows), BF16),
            pltpu.VMEM((d, rows), BF16), pltpu.VMEM((rows, d), F32),
        ],
        compiler_params=params(),
        name="cross_back",
    )(meta, grad_in, res1, n2, optic, q, k, v, att, probs, gains[1:2], wo, wq, wkv, wkv, att)


def self_back_kernel(
    meta, grad_in, radar, n1, q, k, v, att, probs, gain, wo, wq, wk, wv, att_all,
    radar_g, keep, send, bias_g, gain_g, shift_g,
    gs, n1_t, acc,
):
    j = pl.program_id(0)
    rows, d = n1.shape
    wide = q.shape[1]

    @pl.when(j == 0)
    def _():
        low = grad_in[...].astype(BF16)
        gs[...] = low
        bias_g[...] = jnp.sum(low.astype(F32), axis=0, keepdims=True)
        n1_t[...] = n1[...].T
        acc[...] = jnp.zeros_like(acc)
        place(meta, keep, send, dot_nn(att_all[...].T, low).astype(BF16), slice(0, d))

    g_att = dot_nt(gs[...], wo[...]).astype(BF16)
    dq, dk, dv = quad_back(q[...], k[...], v[...], att[...], g_att, probs)

    def put(grad, first):
        spot = pl.ds(pl.multiple_of(first * d + j * wide, wide), wide)
        place(meta, keep, send, grad.astype(BF16), spot)

    put(dot_nn(n1_t[...], dq), 1)
    put(dot_nn(n1_t[...], dk), 2)
    put(dot_nn(n1_t[...], dv), 3)
    acc[...] += dot_nt(dq, wq[...]) + dot_nt(dk, wk[...]) + dot_nt(dv, wv[...])

    @pl.when(j == pl.num_programs(0) - 1)
    def _():
        part, g_gain, g_shift = norm_back(radar[...].astype(F32), gain[...], acc[...])
        radar_g[0:rows] = grad_in[...] + part
        if radar_g.shape[0] > rows:
            radar_g[rows:] = jnp.zeros((radar_g.shape[0] - rows, radar_g.shape[1]), F32)
        gain_g[...] = g_gain
        shift_g[...] = g_shift


def self_back(rows, meta, grad_in, radar, n1, q, k, v, att, probs, gains, wo, w_qkv):
    d = n1.shape[1]
    wide = QUAD * HDIM
    steps = d // wide
    vec = shaped(1, d, dtype=F32)
    eighth = (4, d // 8, 4 * d)
    return pl.pallas_call(
        self_back_kernel,
        grid=(steps,),
        in_specs=[
            smem(), whole((rows, d)), whole((rows, d)), whole((rows, d)),
            *[cols(rows, wide)] * 4,
            pl.BlockSpec((QUAD, rows, rows), lambda j: (j, 0, 0)),
            whole((1, d)), rowblk(wide, d),
            cols(d, wide), cols(d, wide, steps), cols(d, wide, 2 * steps), whole((rows, d)),
        ],
        out_specs=[
            whole((radar.shape[0], d)), whole(eighth), whole(eighth),
            whole((1, d)), whole((1, d)), whole((1, d)),
        ],
        out_shape=[
            shaped(radar.shape[0], d, dtype=F32), shaped(*eighth), shaped(*eighth), vec, vec, vec,
        ],
        scratch_shapes=[
            pltpu.VMEM((rows, d), BF16), pltpu.VMEM((d, rows), BF16), pltpu.VMEM((rows, d), F32),
        ],
        compiler_params=params(),
        name="self_back",
    )(meta, grad_in, radar, n1, q, k, v, att, probs, gains[0:1], wo, w_qkv, w_qkv, w_qkv, att)


def local_grads(
    meta, radar_tokens, optic_tokens, norm_gains, norm_shifts, self_qkv, self_out, cross_query,
    cross_keyval, cross_out, hidden_in, hidden_out, proj_biases, hidden_bias, cotangent,
):
    rows = rows_in_use(radar_tokens.shape[0], 3)
    slopes = jnp.asarray([2.0 ** (-8.0 * (h + 1) / HEADS) for h in range(HEADS)], F32)
    n1, q1, k1, v1, p1, att1, res1, n2 = self_forward(
        rows, meta, slopes, radar_tokens, norm_gains, norm_shifts, proj_biases, self_qkv, self_out
    )
    q2, k2, v2, p2, att2, res2, n3 = cross_forward(
        rows, meta, res1, n2, optic_tokens, norm_gains, norm_shifts, proj_biases,
        cross_query, cross_keyval, cross_out,
    )
    y, grad_two, dwin, dwin_s, dwout, dwout_s, dhb, gain3, shift3, bias3 = hidden(
        rows, meta, res2, n3, cotangent, norm_gains, proj_biases, hidden_bias[None], hidden_in,
        hidden_out,
    )
    grad_one, optic_g, cross, cross_s, bias2, gain2, shift2 = cross_back(
        rows, meta, grad_two, res1, n2, optic_tokens, q2, k2, v2, att2, p2, norm_gains,
        cross_out, cross_query, cross_keyval,
    )
    radar_g, own, own_s, bias1, gain1, shift1 = self_back(
        rows, meta, grad_one, radar_tokens, n1, q1, k1, v1, att1, p1, norm_gains, self_out, self_qkv
    )
    small = jnp.concatenate(
        [gain1, gain2, gain3, shift1, shift2, shift3, bias1, bias2, bias3, dhb.reshape(4, -1)]
    )
    big = ((dwin, dwin_s), (dwout, dwout_s), (cross, cross_s), (own, own_s))
    return y, radar_g, optic_g, big, small


def hop(values, perm):
    return lax.ppermute(values, ("grp", "hd"), perm)


def pairs(move):
    found = []
    for z in range(4):
        for x in range(2):
            for y in range(2):
                for c in range(2):
                    to = move(z, x, y, c)
                    if to is not None:
                        tz, tx, ty, tc = to
                        found.append(((z * 2 + x) * 4 + y * 2 + c, (tz * 2 + tx) * 4 + ty * 2 + tc))
    return found


ACROSS_CORE = pairs(lambda z, x, y, c: (z, x, y, 1 - c))
ACROSS_Y = pairs(lambda z, x, y, c: (z, x, 1 - y, c))
ACROSS_X = pairs(lambda z, x, y, c: (z, 1 - x, y, c))
INWARD = pairs(lambda z, x, y, c: {0: (1, x, y, c), 3: (2, x, y, c)}.get(z))
MIDDLE = pairs(lambda z, x, y, c: {1: (2, x, y, c), 2: (1, x, y, c)}.get(z))
OUTWARD = pairs(lambda z, x, y, c: {1: (0, x, y, c), 2: (3, x, y, c)}.get(z))


def add(*terms):
    total = terms[0].astype(F32)
    for term in terms[1:]:
        total = total + term.astype(F32)
    return total


def reduce_part(keep, send, at_x, at_edge):
    from_core = hop(send, ACROSS_CORE)
    to_y = add(keep[2:], from_core[2:]).astype(BF16)
    from_y = hop(to_y, ACROSS_Y)
    both = add(keep[:2], from_core[:2], from_y).astype(BF16)
    from_x = hop(both[1], ACROSS_X)
    mine = add(both[0], from_x).astype(BF16)
    inward = hop(mine, INWARD)
    inner = add(mine, inward).astype(BF16)
    crossed = hop(inner, MIDDLE)
    done = add(inner, crossed).astype(BF16)
    outward = hop(done, OUTWARD)
    done = jnp.where(at_edge, outward, done)
    other = hop(done, ACROSS_X)
    first = jnp.where(at_x == 0, done, other)
    second = jnp.where(at_x == 0, other, done)
    return jnp.concatenate([first, second], axis=0).astype(F32)


def reduce_anywhere(keep, send):
    parts = jnp.stack([keep.reshape(2, 2, *keep.shape[1:]), send.reshape(2, 2, *send.shape[1:])], axis=1)
    grad = parts.reshape(-1, keep.shape[-1])
    mine = lax.psum_scatter(grad, "hd", scatter_dimension=0, tiled=True)
    return lax.psum(mine.astype(F32), "grp")


def on_device(
    radar_tokens, optic_tokens, tile_lengths, norm_gains, norm_shifts, self_qkv, self_out,
    cross_query, cross_keyval, cross_out, hidden_in, hidden_out, proj_biases, hidden_bias, cotangent,
):
    d = radar_tokens.shape[1]
    known = lax.axis_size("grp") == 8 and lax.axis_size("hd") == 4
    at_hd = lax.axis_index("hd")
    at_grp = lax.axis_index("grp")
    lens = lax.dynamic_index_in_dim(tile_lengths[0], at_hd, 0, keepdims=False)
    if known:
        at_z, at_x = at_grp // 2, at_grp % 2
        at_edge = jnp.logical_or(at_z == 0, at_z == 3)
        spot = jnp.stack([at_hd // 2, at_hd % 2, at_x]).astype(jnp.int32)
    else:
        spot = jnp.zeros((3,), jnp.int32)
    meta = jnp.concatenate([lens, spot])
    layer_output, radar_grad, optic_grad, big, small = local_grads(
        meta, radar_tokens, optic_tokens, norm_gains, norm_shifts, self_qkv, self_out, cross_query,
        cross_keyval, cross_out, hidden_in, hidden_out, proj_biases, hidden_bias, cotangent,
    )
    if known:
        sums = [reduce_part(keep, send, at_x, at_edge) for keep, send in big]
    else:
        sums = [reduce_anywhere(keep, send) for keep, send in big]
    into, out, cross, own = sums
    small = lax.psum(small, ("grp", "hd"))
    vectors = lax.dynamic_slice_in_dim(small[:9], at_hd * (d // 4), d // 4, 1)
    hidden_part = lax.dynamic_index_in_dim(small[9:], at_hd, 0, keepdims=False)
    return (
        layer_output,
        radar_grad,
        optic_grad,
        own[:, d:],
        own[:, :d],
        cross[:, d : 2 * d],
        cross[:, 2 * d :],
        cross[:, :d],
        into,
        out,
        vectors[0:3],
        vectors[3:6],
        vectors[6:9],
        hidden_part,
    )


def solution(mesh):
    rows = P(("grp", "hd"), None)
    kept = P("hd", None)
    vector = P(None, "hd")
    return jax.shard_map(
        on_device,
        mesh=mesh,
        in_specs=(rows, rows, P("grp", None, None), *[P()] * 11, rows),
        out_specs=(rows, rows, rows, *[kept] * 7, vector, vector, vector, P("hd")),
        check_vma=False,
    )
```

time: 1160 us -> 392 us (0.34)
  blocking collectives: 452 us -> 44.9 us
  matrix products: 152 us -> 0 us
  local copies, waits for them, and re-layouts: 142 us -> 8.49 us
  waiting for transfers between devices: 283 us -> 174 us
  Pallas kernels: 0 us -> 102 us
  starting transfers between devices: 60.5 us -> 32.3 us
  other arithmetic: 45.2 us -> 20.8 us
  between operations: 16 us -> 1.68 us
    psum x1, blocking collectives: 383 us -> 44.9 us  [on_device(): small = lax.psum(small, ('grp', 'hd'))]
    ppermute x0 -> x28, waiting for transfers between devices: none -> 174 us  [hop(): return lax.ppermute(values, ('grp', 'hd'), perm)]
    dot_general x77 -> x0, matrix products: 152 us -> none  [the longest x7 33.8 us: inner_rows(): lax.dot_general(left, right, (((0,), (0,)), ((), ())), preferred_element_...]
    reduce_scatter x6 -> x0, waiting for transfers between devices: 146 us -> none  [the longest x1 50.6 us: on_device(): lax.psum_scatter(grad_hidden_in.astype(jnp.bfloat16), 'hd', scatter_dimen...]
    pallas_call x0 -> x5, Pallas kernels: none -> 102 us  [the longest x1 27.2 us: hidden(): pl.pallas_call(hidden_kernel, grid_spec=pltpu.PrefetchScalarGridSpec(num_...]
    all_to_all x12 -> x0, waiting for transfers between devices: 101 us -> none  [the longest x1 11.7 us: on_device(): lax.all_to_all(cross_queries, 'hd', split_axis=1, concat_axis=0, tiled=True)]
    all_to_all x4 -> x0, blocking collectives: 62.4 us -> none  [the longest x1 16.3 us: on_device(): lax.all_to_all(grad_optic_keys, 'hd', split_axis=0, concat_axis=1, tiled=...]
    all_to_all x12 -> x0, starting transfers between devices: 59.8 us -> none  [the longest x1 12.9 us: on_device(): lax.all_to_all(grad_cross_att, 'hd', split_axis=1, concat_axis=0, tiled=T...]
  transfers between devices with their start and end apart: 22 -> 28, of which waited for: 17 -> 15; matrix products, arithmetic and copies ran while one was open for 10% -> 6% of each run, Pallas kernels for 0% -> 0%
where the time goes in v1:
time: 392 us; the launch traced here: 385 us
  waiting for transfers between devices  174 us (44%)
  Pallas kernels  102 us (26%)
  blocking collectives  44.9 us (11%)
  starting transfers between devices  32.3 us (8%)
  other arithmetic  20.8 us (5%)
  local copies, waits for them, and re-layouts  8.49 us (2%)
    ppermute x28, waiting for transfers between devices, hop(): return lax.ppermute(values, ('grp', 'hd'), perm)  174 us
    psum x1, blocking collectives, on_device(): small = lax.psum(small, ('grp', 'hd'))  44.9 us
    ppermute x28, starting transfers between devices, hop(): return lax.ppermute(values, ('grp', 'hd'), perm)  32.3 us
    pallas_call x1, Pallas kernels, hidden(): pl.pallas_call(hidden_kernel, grid_spec=pltpu.PrefetchScalarGridSpec(num_...  27.2 us
    pallas_call x1, Pallas kernels, cross_back(): pl.pallas_call(cross_back_kernel, grid=(steps,), in_specs=[smem(), whole(...  22 us
    pallas_call x1, Pallas kernels, self_back(): pl.pallas_call(self_back_kernel, grid=(steps,), in_specs=[smem(), whole((...  21.2 us
    pallas_call x1, Pallas kernels, self_forward(): pl.pallas_call(self_forward_kernel, grid=(steps,), in_specs=[smem(), smem...  16.2 us
    pallas_call x1, Pallas kernels, cross_forward(): pl.pallas_call(cross_forward_kernel, grid=(steps,), in_specs=[smem(), who...  15.3 us
  transfers between devices with their start and end apart: 28, of which 15 were waited for; matrix products, arithmetic and copies ran while one was open for 6% of the time, Pallas kernels for 0%

profile of v1, /device:TPU:0, one launch (start us, length us, event | category | flops | bytes accessed | tf_op | source)
XLA Modules:
  0.0 384.6 jit_solution(10448200310845626312)
XLA Ops:
  0.7 1.4 fusion.7
  2.3 1.5 fusion.5
  4.4 16.2 %self_forward.1 = (bf16[464,768]{1,0:T(8,128)(2,1)}, bf16[464,768]{1,0:T(8,128)(2,1)}, bf16[464,768]{1,0:T(8,128)(2,1)}, bf16[464,768]{1,0:T(8,128)(2,1)}, bf16[...) custom-call(s32[6]{0:T(128)} %pad_add_fusion.lens.meta, ...), custom_call_target="tpu_custom_call" | custom-call | tf_op jit(solution)/shard_map/self_forward/pallas_call | solution.py:207
  20.6 15.3 %cross_forward.1 = (bf16[464,768]{1,0:T(8,128)(2,1)}, bf16[464,768]{1,0:T(8,128)(2,1)}, bf16[464,768]{1,0:T(8,128)(2,1)}, bf16[12,464,464]{2,1,0:T(8,128)(2,1)},...) custom-call(s32[6]{0:T(128)} %pad_add_fusion.lens.meta, ...), custom_call_target="tpu_custom_call" | custom-call | tf_op jit(solution)/shard_map/cross_forward/pallas_call | solution.py:235
  35.9 27.2 %hidden.1 = (bf16[512,768]{1,0:T(8,128)(2,1)}, f32[464,768]{1,0:T(8,128)}, bf16[4,96,3072]{2,1,0:T(8,128)(2,1)}, bf16[4,96,3072]{2,1,0:T(8,128)(2,1)}, bf16[4,38...) custom-call(s32[6]{0:T(128)} %pad_add_fusion.lens.meta, ...), custom_call_target="tpu_custom_call" | custom-call | tf_op jit(solution)/shard_map/hidden/pallas_call | solution.py:329
  63.1 22.0 %cross_back.1 = (f32[464,768]{1,0:T(8,128)}, f32[512,768]{1,0:T(8,128)}, bf16[4,96,3072]{2,1,0:T(8,128)(2,1)}, bf16[4,96,3072]{2,1,0:T(8,128)(2,1)}, f32[1,768]{...) custom-call(s32[6]{0:T(128)} %pad_add_fusion.lens.meta, f32[464,768]{1,0:T(8,128)} %get-tuple-element.57.grad_in, ...), custom_call_target="tpu_custom_call" | custom-call | tf_op jit(solution)/shard_map/cross_back/pallas_call | solution.py:426
  85.3 21.2 %self_back.1 = (f32[512,768]{1,0:T(8,128)}, bf16[4,96,3072]{2,1,0:T(8,128)(2,1)}, bf16[4,96,3072]{2,1,0:T(8,128)(2,1)}, f32[1,768]{1,0:T(1,128)}, f32[1,768]{1,0:T(1,128)}, /*index=5*/f32[1,768]{1,0:T(1,128)}) custom-call(s32[6]{0:T(128)} %pad_add_fusion.lens.meta, f32[464,768]{1,0:T(8,128)} %get-tuple-element.63.grad_in, bf16[512,768]{1,0:T(8,128)(2,1)} %radar.3, ...), custom_call_target="tpu_custom_call" | custom-call | tf_op jit(solution)/shard_map/self_back/pallas_call | solution.py:499
  109.7 44.9 %psum.7 = f32[13,768]{1,0:T(8,128)S(1)} all-reduce(f32[13,768]{1,0:T(8,128)S(1)} %concatenate.23), channel_id=1, replica_groups=mesh['grp'=8,'hd'=4] {'grp','hd'}, use_global_device_ids=true, to_apply=%region_0.1 | all-reduce | flops 9984 | bytes 79872 | tf_op jit(solution)/shard_map/psum | solution.py:638
  155.9 2.2 add_convert_fusion.7
  158.1 2.3 collective-permute-start.1
  160.4 1.7 add_convert_fusion.5
  162.4 1.7 add_convert_fusion.3
  164.1 1.9 collective-permute-start.15
  166.6 20.6 %collective-permute-done.1 = bf16[2,96,3072]{2,1,0:T(8,128)(2,1)S(1)} collective-permute-done((bf16[2,96,3072]{2,1,0:T(8,128)(2,1)S(1)}, bf16[2,96,3072]{2,1,0:T(8,128)(2,1)S(1)}, u32[]{:S(2)}, u32[]{:S(2)}) %collective-permute-start.1) | collective-permute-done | bytes 1179680 | tf_op jit(solution)/shard_map/ppermute | solution.py:556
  187.3 1.7 add_convert_fusion.6
  189.0 2.0 collective-permute-start.2
  191.1 21.5 %collective-permute-done.8 = bf16[2,96,3072]{2,1,0:T(8,128)(2,1)S(1)} collective-permute-done((bf16[2,96,3072]{2,1,0:T(8,128)(2,1)S(1)}, bf16[2,96,3072]{2,1,0:T(8,128)(2,1)S(1)}, u32[]{:S(2)}, u32[]{:S(2)}) %collective-permute-start.8) | collective-permute-done | bytes 1179680 | tf_op jit(solution)/shard_map/ppermute | solution.py:556
  212.6 1.7 add_convert_fusion.4
  214.3 2.0 collective-permute-start.9
  216.3 21.5 %collective-permute-done.15 = bf16[2,96,3072]{2,1,0:T(8,128)(2,1)S(1)} collective-permute-done((bf16[2,96,3072]{2,1,0:T(8,128)(2,1)S(1)}, bf16[2,96,3072]{2,1,0:T(8,128)(2,1)S(1)}, u32[]{:S(2)}, u32[]{:S(2)}) %collective-permute-start.15) | collective-permute-done | bytes 1179680 | tf_op jit(solution)/shard_map/ppermute | solution.py:556
  237.8 1.7 add_convert_fusion.2
  239.6 2.0 collective-permute-start.16
  241.6 19.3 %collective-permute-done.22 = bf16[2,384,768]{2,1,0:T(8,128)(2,1)S(1)} collective-permute-done((bf16[2,384,768]{2,1,0:T(8,128)(2,1)S(1)}, bf16[2,384,768]{2,1,0:T(8,128)(2,1)S(1)}, u32[]{:S(2)}, u32[]{:S(2)}) %collective-permute-start.22) | collective-permute-done | bytes 1179680 | tf_op jit(solution)/shard_map/ppermute | solution.py:556
  261.4 1.7 collective-permute-start.23
  263.3 2.4 collective-permute-start.3
  265.9 1.3 collective-permute-start.10
  267.4 1.3 collective-permute-start.17
  268.7 5.9 %collective-permute-done.23 = bf16[384,768]{1,0:T(8,128)(2,1)S(1)} collective-permute-done((bf16[384,768]{1,0:T(8,128)(2,1)S(1)}, bf16[384,768]{1,0:T(8,128)(2,1)S(1)}, u32[]{:S(2)}, u32[]{:S(2)}) %collective-permute-start.23) | collective-permute-done | bytes 589856 | tf_op jit(solution)/shard_map/ppermute | solution.py:556
  274.7 2.4 collective-permute-start.24
  277.1 2.3 collective-permute-done.3
  280.5 11.5 %collective-permute-done.10 = bf16[96,3072]{1,0:T(8,128)(2,1)S(1)} collective-permute-done((bf16[96,3072]{1,0:T(8,128)(2,1)S(1)}, bf16[96,3072]{1,0:T(8,128)(2,1)S(1)}, u32[]{:S(2)}, u32[]{:S(2)}) %collective-permute-start.10) | collective-permute-done | bytes 589856 | tf_op jit(solution)/shard_map/ppermute | solution.py:556
  292.9 11.8 %collective-permute-done.17 = bf16[96,3072]{1,0:T(8,128)(2,1)S(1)} collective-permute-done((bf16[96,3072]{1,0:T(8,128)(2,1)S(1)}, bf16[96,3072]{1,0:T(8,128)(2,1)S(1)}, u32[]{:S(2)}, u32[]{:S(2)}) %collective-permute-start.17) | collective-permute-done | bytes 589856 | tf_op jit(solution)/shard_map/ppermute | solution.py:556
  305.6 8.1 %collective-permute-done.24 = bf16[384,768]{1,0:T(8,128)(2,1)S(1)} collective-permute-done((bf16[384,768]{1,0:T(8,128)(2,1)S(1)}, bf16[384,768]{1,0:T(8,128)(2,1)S(1)}, u32[]{:S(2)}, u32[]{:S(2)}) %collective-permute-start.24) | collective-permute-done | bytes 589856 | tf_op jit(solution)/shard_map/ppermute | solution.py:556
  314.7 1.3 collective-permute-start.5
  316.1 1.3 collective-permute-start.12
  317.6 1.3 collective-permute-start.19
  319.0 1.3 collective-permute-start.26
  320.3 14.2 %collective-permute-done.5 = bf16[96,3072]{1,0:T(8,128)(2,1)S(1)} collective-permute-done((bf16[96,3072]{1,0:T(8,128)(2,1)S(1)}, bf16[96,3072]{1,0:T(8,128)(2,1)S(1)}, u32[]{:S(2)}, u32[]{:S(2)}) %collective-permute-start.5) | collective-permute-done | bytes 589856 | tf_op jit(solution)/shard_map/ppermute | solution.py:556
  335.3 11.9 %collective-permute-done.12 = bf16[96,3072]{1,0:T(8,128)(2,1)S(1)} collective-permute-done((bf16[96,3072]{1,0:T(8,128)(2,1)S(1)}, bf16[96,3072]{1,0:T(8,128)(2,1)S(1)}, u32[]{:S(2)}, u32[]{:S(2)}) %collective-permute-start.12) | collective-permute-done | bytes 589856 | tf_op jit(solution)/shard_map/ppermute | solution.py:556
  347.9 11.9 %collective-permute-done.19 = bf16[96,3072]{1,0:T(8,128)(2,1)S(1)} collective-permute-done((bf16[96,3072]{1,0:T(8,128)(2,1)S(1)}, bf16[96,3072]{1,0:T(8,128)(2,1)S(1)}, u32[]{:S(2)}, u32[]{:S(2)}) %collective-permute-start.19) | collective-permute-done | bytes 589856 | tf_op jit(solution)/shard_map/ppermute | solution.py:556
  360.6 7.2 %collective-permute-done.26 = bf16[384,768]{1,0:T(8,128)(2,1)S(1)} collective-permute-done((bf16[384,768]{1,0:T(8,128)(2,1)S(1)}, bf16[384,768]{1,0:T(8,128)(2,1)S(1)}, u32[]{:S(2)}, u32[]{:S(2)}) %collective-permute-start.26) | collective-permute-done | bytes 589856 | tf_op jit(solution)/shard_map/ppermute | solution.py:556
  369.6 4.0 %collective-permute-done.20 = bf16[96,3072]{1,0:T(8,128)(2,1)S(1)} collective-permute-done((bf16[96,3072]{1,0:T(8,128)(2,1)S(1)}, bf16[96,3072]{1,0:T(8,128)(2,1)S(1)}, u32[]{:S(2)}, u32[]{:S(2)}) %collective-permute-start.20) | collective-permute-done | bytes 589856 | tf_op jit(solution)/shard_map/ppermute | solution.py:556
  374.5 1.3 slice.179
  375.8 1.1 slice.184
  376.9 1.1 maximum_convert_fusion.4
  378.0 1.7 maximum_convert_fusion.2
  379.7 2.8 collective-permute-done.27
  382.5 1.6 maximum_convert_fusion.3
  (91 shorter events, 16.7 us)
Async XLA Ops:
  0.6 1.4 copy-start
  85.2 22.9 %copy-start.6 = (f32[1,3072]{1,0:T(1,128)S(1)}, f32[1,3072]{1,0:T(1,128)}, u32[]{:S(2)}) copy-start(f32[1,3072]{1,0:T(1,128)} %get-tuple-element.89) | copy-start | bytes 36868
  85.2 23.6 %copy-start.7 = (f32[1,768]{1,0:T(1,128)S(1)}, f32[1,768]{1,0:T(1,128)}, u32[]{:S(2)}) copy-start(f32[1,768]{1,0:T(1,128)} %get-tuple-element.82) | copy-start | bytes 9220
  85.2 23.6 %copy-start.8 = (f32[1,768]{1,0:T(1,128)S(1)}, f32[1,768]{1,0:T(1,128)}, u32[]{:S(2)}) copy-start(f32[1,768]{1,0:T(1,128)} %get-tuple-element.85) | copy-start | bytes 9220
  85.2 23.6 %copy-start.9 = (f32[1,768]{1,0:T(1,128)S(1)}, f32[1,768]{1,0:T(1,128)}, u32[]{:S(2)}) copy-start(f32[1,768]{1,0:T(1,128)} %get-tuple-element.88) | copy-start | bytes 9220
  85.2 23.6 %copy-start.10 = (f32[1,768]{1,0:T(1,128)S(1)}, f32[1,768]{1,0:T(1,128)}, u32[]{:S(2)}) copy-start(f32[1,768]{1,0:T(1,128)} %get-tuple-element.87) | copy-start | bytes 9220
  85.3 23.6 %copy-start.11 = (f32[1,768]{1,0:T(1,128)S(1)}, f32[1,768]{1,0:T(1,128)}, u32[]{:S(2)}) copy-start(f32[1,768]{1,0:T(1,128)} %get-tuple-element.81) | copy-start | bytes 9220
  85.3 23.6 %copy-start.12 = (f32[1,768]{1,0:T(1,128)S(1)}, f32[1,768]{1,0:T(1,128)}, u32[]{:S(2)}) copy-start(f32[1,768]{1,0:T(1,128)} %get-tuple-element.84) | copy-start | bytes 9220
  106.5 49.3 %collective-permute-start = (bf16[4,96,3072]{2,1,0:T(8,128)(2,1)}, bf16[4,96,3072]{2,1,0:T(8,128)(2,1)}, u32[]{:S(2)}, u32[]{:S(2)}) collective-permute-start(bf16[4,96,3072]{2,1,0:T(8,128)(2,1)} %get-tuple-element.73), channel_id=1, source_target_pairs={{0,1},{1,0},{2,3},{3,2},{4,5},{5,4},{6,7},{7,6},{8,9},{9,8},{10,11... | collective-permute-start | bytes 7077896 | tf_op jit(solution)/shard_map/ppermute | solution.py:556
  107.0 53.4 %collective-permute-start.7 = (bf16[4,96,3072]{2,1,0:T(8,128)(2,1)}, bf16[4,96,3072]{2,1,0:T(8,128)(2,1)}, u32[]{:S(2)}, u32[]{:S(2)}) collective-permute-start(bf16[4,96,3072]{2,1,0:T(8,128)(2,1)} %get-tuple-element.75), channel_id=1, source_target_pairs={{0,1},{1,0},{2,3},{3,2},{4,5},{5,4},{6,7},{7,6},{8,9},{9,8},{10,11... | collective-permute-start | bytes 7077896 | tf_op jit(solution)/shard_map/ppermute | solution.py:556
  107.1 55.2 %collective-permute-start.14 = (bf16[4,96,3072]{2,1,0:T(8,128)(2,1)}, bf16[4,96,3072]{2,1,0:T(8,128)(2,1)}, u32[]{:S(2)}, u32[]{:S(2)}) collective-permute-start(bf16[4,96,3072]{2,1,0:T(8,128)(2,1)} %get-tuple-element.77), channel_id=1, source_target_pairs={{0,1},{1,0},{2,3},{3,2},{4,5},{5,4},{6,7},{7,6},{8,9},{9,8},{10,11... | collective-permute-start | bytes 7077896 | tf_op jit(solution)/shard_map/ppermute | solution.py:556
  107.6 58.5 %collective-permute-start.21 = (bf16[4,384,768]{2,1,0:T(8,128)(2,1)}, bf16[4,384,768]{2,1,0:T(8,128)(2,1)S(1)}, u32[]{:S(2)}, u32[]{:S(2)}) collective-permute-start(bf16[4,384,768]{2,1,0:T(8,128)(2,1)} %get-tuple-element.79), channel_id=1, source_target_pairs={{0,1},{1,0},{2,3},{3,2},{4,5},{5,4},{6,7},{7,6},{8,9},{9,8},{10,11... | collective-permute-start | bytes 7077896 | tf_op jit(solution)/shard_map/ppermute | solution.py:556
  155.9 4.5 %copy-start.4 = (bf16[4,96,3072]{2,1,0:T(8,128)(2,1)S(1)}, bf16[4,96,3072]{2,1,0:T(8,128)(2,1)}, u32[]{:S(2)}) copy-start(bf16[4,96,3072]{2,1,0:T(8,128)(2,1)} %get-tuple-element.74) | copy-start | bytes 7077892
  158.1 29.2 %collective-permute-start.1 = (bf16[2,96,3072]{2,1,0:T(8,128)(2,1)S(1)}, bf16[2,96,3072]{2,1,0:T(8,128)(2,1)S(1)}, u32[]{:S(2)}, u32[]{:S(2)}) collective-permute-start(bf16[2,96,3072]{2,1,0:T(8,128)(2,1)S(1)} %add_convert_fusion.7), channel_id=1, source_target_pairs={{0,2},{1,3},{2,0},{3,1},{4,6},{5,7},{6,4},{7,5},{8,10},{9,11},{10,... | collective-permute-start | bytes 3538952 | tf_op jit(solution)/shard_map/ppermute | solution.py:556
  160.4 2.0 copy-start.3
  162.1 50.4 %collective-permute-start.8 = (bf16[2,96,3072]{2,1,0:T(8,128)(2,1)S(1)}, bf16[2,96,3072]{2,1,0:T(8,128)(2,1)S(1)}, u32[]{:S(2)}, u32[]{:S(2)}) collective-permute-start(bf16[2,96,3072]{2,1,0:T(8,128)(2,1)S(1)} %add_convert_fusion.5), channel_id=1, source_target_pairs={{0,2},{1,3},{2,0},{3,1},{4,6},{5,7},{6,4},{7,5},{8,10},{9,11},{10,... | collective-permute-start | bytes 3538952 | tf_op jit(solution)/shard_map/ppermute | solution.py:556
  162.4 3.6 copy-start.2
  164.1 73.7 %collective-permute-start.15 = (bf16[2,96,3072]{2,1,0:T(8,128)(2,1)S(1)}, bf16[2,96,3072]{2,1,0:T(8,128)(2,1)S(1)}, u32[]{:S(2)}, u32[]{:S(2)}) collective-permute-start(bf16[2,96,3072]{2,1,0:T(8,128)(2,1)S(1)} %add_convert_fusion.3), channel_id=1, source_target_pairs={{0,2},{1,3},{2,0},{3,1},{4,6},{5,7},{6,4},{7,5},{8,10},{9,11},{10,... | collective-permute-start | bytes 3538952 | tf_op jit(solution)/shard_map/ppermute | solution.py:556
  166.0 21.3 %copy-start.5 = (bf16[4,96,3072]{2,1,0:T(8,128)(2,1)S(1)}, bf16[4,96,3072]{2,1,0:T(8,128)(2,1)}, u32[]{:S(2)}) copy-start(bf16[4,96,3072]{2,1,0:T(8,128)(2,1)} %get-tuple-element.72) | copy-start | bytes 7077892
  166.3 94.5 %collective-permute-start.22 = (bf16[2,384,768]{2,1,0:T(8,128)(2,1)S(1)}, bf16[2,384,768]{2,1,0:T(8,128)(2,1)S(1)}, u32[]{:S(2)}, u32[]{:S(2)}) collective-permute-start(bf16[2,384,768]{2,1,0:T(8,128)(2,1)S(1)} %add_convert_fusion.1), channel_id=1, source_target_pairs={{0,2},{1,3},{2,0},{3,1},{4,6},{5,7},{6,4},{7,5},{8,10},{9,11},{10,... | collective-permute-start | bytes 3538952 | tf_op jit(solution)/shard_map/ppermute | solution.py:556
  189.0 74.1 %collective-permute-start.2 = (bf16[96,3072]{1,0:T(8,128)(2,1)S(1)}, bf16[96,3072]{1,0:T(8,128)(2,1)S(1)}, u32[]{:S(2)}, u32[]{:S(2)}) collective-permute-start(bf16[96,3072]{1,0:T(8,128)(2,1)S(1)} %slice_bitcast_fusion.6), channel_id=1, source_target_pairs={{0,4},{1,5},{2,6},{3,7},{4,0},{5,1},{6,2},{7,3},{8,12},{9,13},{10,... | collective-permute-start | bytes 1769480 | tf_op jit(solution)/shard_map/ppermute | solution.py:556
  214.3 51.4 %collective-permute-start.9 = (bf16[96,3072]{1,0:T(8,128)(2,1)S(1)}, bf16[96,3072]{1,0:T(8,128)(2,1)S(1)}, u32[]{:S(2)}, u32[]{:S(2)}) collective-permute-start(bf16[96,3072]{1,0:T(8,128)(2,1)S(1)} %slice_bitcast_fusion.4), channel_id=1, source_target_pairs={{0,4},{1,5},{2,6},{3,7},{4,0},{5,1},{6,2},{7,3},{8,12},{9,13},{10,... | collective-permute-start | bytes 1769480 | tf_op jit(solution)/shard_map/ppermute | solution.py:556
  239.6 27.6 %collective-permute-start.16 = (bf16[96,3072]{1,0:T(8,128)(2,1)S(1)}, bf16[96,3072]{1,0:T(8,128)(2,1)S(1)}, u32[]{:S(2)}, u32[]{:S(2)}) collective-permute-start(bf16[96,3072]{1,0:T(8,128)(2,1)S(1)} %slice_bitcast_fusion.2), channel_id=1, source_target_pairs={{0,4},{1,5},{2,6},{3,7},{4,0},{5,1},{6,2},{7,3},{8,12},{9,13},{10,... | collective-permute-start | bytes 1769480 | tf_op jit(solution)/shard_map/ppermute | solution.py:556
  261.4 13.2 %collective-permute-start.23 = (bf16[384,768]{1,0:T(8,128)(2,1)S(1)}, bf16[384,768]{1,0:T(8,128)(2,1)S(1)}, u32[]{:S(2)}, u32[]{:S(2)}) collective-permute-start(bf16[384,768]{1,0:T(8,128)(2,1)S(1)} %slice_bitcast_fusion), channel_id=1, source_target_pairs={{0,4},{1,5},{2,6},{3,7},{4,0},{5,1},{6,2},{7,3},{8,12},{9,13},{10,... | collective-permute-start | bytes 1769480 | tf_op jit(solution)/shard_map/ppermute | solution.py:556
  263.3 16.1 %collective-permute-start.3 = (bf16[96,3072]{1,0:T(8,128)(2,1)S(1)}, bf16[96,3072]{1,0:T(8,128)(2,1)S(1)}, u32[]{:S(2)}, u32[]{:S(2)}) collective-permute-start(bf16[96,3072]{1,0:T(8,128)(2,1)S(1)} %fusion.3), channel_id=1, source_target_pairs={{0,8},{1,9},{2,10},{3,11},{4,12},{5,13},{6,14},{7,15},{24,16},{25,... | collective-permute-start | bytes 1769480 | tf_op jit(solution)/shard_map/ppermute | solution.py:556
  265.9 26.2 %collective-permute-start.10 = (bf16[96,3072]{1,0:T(8,128)(2,1)S(1)}, bf16[96,3072]{1,0:T(8,128)(2,1)S(1)}, u32[]{:S(2)}, u32[]{:S(2)}) collective-permute-start(bf16[96,3072]{1,0:T(8,128)(2,1)S(1)} %fusion.2), channel_id=1, source_target_pairs={{0,8},{1,9},{2,10},{3,11},{4,12},{5,13},{6,14},{7,15},{24,16},{25,... | collective-permute-start | bytes 1769480 | tf_op jit(solution)/shard_map/ppermute | solution.py:556
  267.4 37.3 %collective-permute-start.17 = (bf16[96,3072]{1,0:T(8,128)(2,1)S(1)}, bf16[96,3072]{1,0:T(8,128)(2,1)S(1)}, u32[]{:S(2)}, u32[]{:S(2)}) collective-permute-start(bf16[96,3072]{1,0:T(8,128)(2,1)S(1)} %fusion.1), channel_id=1, source_target_pairs={{0,8},{1,9},{2,10},{3,11},{4,12},{5,13},{6,14},{7,15},{24,16},{25,... | collective-permute-start | bytes 1769480 | tf_op jit(solution)/shard_map/ppermute | solution.py:556
  274.7 38.9 %collective-permute-start.24 = (bf16[384,768]{1,0:T(8,128)(2,1)S(1)}, bf16[384,768]{1,0:T(8,128)(2,1)S(1)}, u32[]{:S(2)}, u32[]{:S(2)}) collective-permute-start(bf16[384,768]{1,0:T(8,128)(2,1)S(1)} %fusion), channel_id=1, source_target_pairs={{0,8},{1,9},{2,10},{3,11},{4,12},{5,13},{6,14},{7,15},{24,16},{25,... | collective-permute-start | bytes 1769480 | tf_op jit(solution)/shard_map/ppermute | solution.py:556
  279.6 34.9 %collective-permute-start.4 = (bf16[96,3072]{1,0:T(8,128)(2,1)S(1)}, bf16[96,3072]{1,0:T(8,128)(2,1)S(1)}, u32[]{:S(2)}, u32[]{:S(2)}) collective-permute-start(bf16[96,3072]{1,0:T(8,128)(2,1)S(1)} %add_convert_fusion.15), channel_id=1, source_target_pairs={{8,16},{9,17},{10,18},{11,19},{12,20},{13,21},{14,22},{15,23},{16,... | collective-permute-start | bytes 1769480 | tf_op jit(solution)/shard_map/ppermute | solution.py:556
  292.2 23.7 %collective-permute-start.11 = (bf16[96,3072]{1,0:T(8,128)(2,1)S(1)}, bf16[96,3072]{1,0:T(8,128)(2,1)S(1)}, u32[]{:S(2)}, u32[]{:S(2)}) collective-permute-start(bf16[96,3072]{1,0:T(8,128)(2,1)S(1)} %add_convert_fusion.13), channel_id=1, source_target_pairs={{8,16},{9,17},{10,18},{11,19},{12,20},{13,21},{14,22},{15,23},{16,... | collective-permute-start | bytes 1769480 | tf_op jit(solution)/shard_map/ppermute | solution.py:556
  304.9 12.6 %collective-permute-start.18 = (bf16[96,3072]{1,0:T(8,128)(2,1)S(1)}, bf16[96,3072]{1,0:T(8,128)(2,1)S(1)}, u32[]{:S(2)}, u32[]{:S(2)}) collective-permute-start(bf16[96,3072]{1,0:T(8,128)(2,1)S(1)} %add_convert_fusion.11), channel_id=1, source_target_pairs={{8,16},{9,17},{10,18},{11,19},{12,20},{13,21},{14,22},{15,23},{16,... | collective-permute-start | bytes 1769480 | tf_op jit(solution)/shard_map/ppermute | solution.py:556
  313.8 5.1 %collective-permute-start.25 = (bf16[384,768]{1,0:T(8,128)(2,1)S(1)}, bf16[384,768]{1,0:T(8,128)(2,1)S(1)}, u32[]{:S(2)}, u32[]{:S(2)}) collective-permute-start(bf16[384,768]{1,0:T(8,128)(2,1)S(1)} %add_convert_fusion.9), channel_id=1, source_target_pairs={{8,16},{9,17},{10,18},{11,19},{12,20},{13,21},{14,22},{15,23},{16,... | collective-permute-start | bytes 1769480 | tf_op jit(solution)/shard_map/ppermute | solution.py:556
  314.7 19.9 %collective-permute-start.5 = (bf16[96,3072]{1,0:T(8,128)(2,1)S(1)}, bf16[96,3072]{1,0:T(8,128)(2,1)S(1)}, u32[]{:S(2)}, u32[]{:S(2)}) collective-permute-start(bf16[96,3072]{1,0:T(8,128)(2,1)S(1)} %add_convert_fusion.14), channel_id=1, source_target_pairs={{8,0},{9,1},{10,2},{11,3},{12,4},{13,5},{14,6},{15,7},{16,24},{17,... | collective-permute-start | bytes 1769480 | tf_op jit(solution)/shard_map/ppermute | solution.py:556
  316.1 31.0 %collective-permute-start.12 = (bf16[96,3072]{1,0:T(8,128)(2,1)S(1)}, bf16[96,3072]{1,0:T(8,128)(2,1)S(1)}, u32[]{:S(2)}, u32[]{:S(2)}) collective-permute-start(bf16[96,3072]{1,0:T(8,128)(2,1)S(1)} %add_convert_fusion.12), channel_id=1, source_target_pairs={{8,0},{9,1},{10,2},{11,3},{12,4},{13,5},{14,6},{15,7},{16,24},{17,... | collective-permute-start | bytes 1769480 | tf_op jit(solution)/shard_map/ppermute | solution.py:556
  317.6 42.2 %collective-permute-start.19 = (bf16[96,3072]{1,0:T(8,128)(2,1)S(1)}, bf16[96,3072]{1,0:T(8,128)(2,1)S(1)}, u32[]{:S(2)}, u32[]{:S(2)}) collective-permute-start(bf16[96,3072]{1,0:T(8,128)(2,1)S(1)} %add_convert_fusion.10), channel_id=1, source_target_pairs={{8,0},{9,1},{10,2},{11,3},{12,4},{13,5},{14,6},{15,7},{16,24},{17,... | collective-permute-start | bytes 1769480 | tf_op jit(solution)/shard_map/ppermute | solution.py:556
  319.0 48.7 %collective-permute-start.26 = (bf16[384,768]{1,0:T(8,128)(2,1)S(1)}, bf16[384,768]{1,0:T(8,128)(2,1)S(1)}, u32[]{:S(2)}, u32[]{:S(2)}) collective-permute-start(bf16[384,768]{1,0:T(8,128)(2,1)S(1)} %add_convert_fusion.8), channel_id=1, source_target_pairs={{8,0},{9,1},{10,2},{11,3},{12,4},{13,5},{14,6},{15,7},{16,24},{17,... | collective-permute-start | bytes 1769480 | tf_op jit(solution)/shard_map/ppermute | solution.py:556
  334.6 34.3 %collective-permute-start.6 = (bf16[96,3072]{1,0:T(8,128)(2,1)S(1)}, bf16[96,3072]{1,0:T(8,128)(2,1)S(1)}, u32[]{:S(2)}, u32[]{:S(2)}) collective-permute-start(bf16[96,3072]{1,0:T(8,128)(2,1)S(1)} %broadcast_select_fusion.5), channel_id=1, source_target_pairs={{0,4},{1,5},{2,6},{3,7},{4,0},{5,1},{6,2},{7,3},{8,12},{9,13},{10,... | collective-permute-start | bytes 1769480 | tf_op jit(solution)/shard_map/ppermute | solution.py:556
  347.2 21.7 %collective-permute-start.13 = (bf16[96,3072]{1,0:T(8,128)(2,1)S(1)}, bf16[96,3072]{1,0:T(8,128)(2,1)S(1)}, u32[]{:S(2)}, u32[]{:S(2)}) collective-permute-start(bf16[96,3072]{1,0:T(8,128)(2,1)S(1)} %broadcast_select_fusion.4), channel_id=1, source_target_pairs={{0,4},{1,5},{2,6},{3,7},{4,0},{5,1},{6,2},{7,3},{8,12},{9,13},{10,... | collective-permute-start | bytes 1769480 | tf_op jit(solution)/shard_map/ppermute | solution.py:556
  359.9 13.7 %collective-permute-start.20 = (bf16[96,3072]{1,0:T(8,128)(2,1)S(1)}, bf16[96,3072]{1,0:T(8,128)(2,1)S(1)}, u32[]{:S(2)}, u32[]{:S(2)}) collective-permute-start(bf16[96,3072]{1,0:T(8,128)(2,1)S(1)} %broadcast_select_fusion.3), channel_id=1, source_target_pairs={{0,4},{1,5},{2,6},{3,7},{4,0},{5,1},{6,2},{7,3},{8,12},{9,13},{10,... | collective-permute-start | bytes 1769480 | tf_op jit(solution)/shard_map/ppermute | solution.py:556
  367.9 14.6 %collective-permute-start.27 = (bf16[384,768]{1,0:T(8,128)(2,1)S(1)}, bf16[384,768]{1,0:T(8,128)(2,1)S(1)}, u32[]{:S(2)}, u32[]{:S(2)}) collective-permute-start(bf16[384,768]{1,0:T(8,128)(2,1)S(1)} %broadcast_select_fusion), channel_id=1, source_target_pairs={{0,4},{1,5},{2,6},{3,7},{4,0},{5,1},{6,2},{7,3},{8,12},{9,13},{10,... | collective-permute-start | bytes 1769480 | tf_op jit(solution)/shard_map/ppermute | solution.py:556
  382.5 1.6 copy-start.1

commit v2 on v1

v2 whole, which is shorter than its diff:
```python
import functools
import math

import jax
import jax.numpy as jnp
import numpy as np
from jax import lax
from jax.experimental import pallas as pl
from jax.experimental.pallas import tpu as pltpu
from jax.sharding import PartitionSpec as P

HEADS = 12
HDIM = 64
SIDES = (12, 15, 20)
QUAD = 4
EPSILON = 1e-06
MASKED = -1e30
FAR = 1e33
F32 = jnp.float32
BF16 = jnp.bfloat16
VMEM_LIMIT = 24 * 1024 * 1024


def rows_in_use(local_rows, slots):
    counts = [0] + [side * side for side in SIDES]
    sums = {0}
    for _ in range(slots):
        sums = {a + b for a in sums for b in counts if a + b <= local_rows}
    return min(local_rows, -(-max(sums) // 16) * 16)


def dot_nn(left, right):
    return lax.dot_general(left, right, (((1,), (0,)), ((), ())), preferred_element_type=F32)


def dot_nt(left, right):
    return lax.dot_general(left, right, (((1,), (1,)), ((), ())), preferred_element_type=F32)


def norm_parts(values):
    average = jnp.mean(values, axis=-1, keepdims=True)
    centred = values - average
    variance = jnp.mean(centred * centred, axis=-1, keepdims=True)
    return centred, lax.rsqrt(variance + EPSILON)


def norm(values, gain, shift):
    centred, inverse = norm_parts(values)
    return centred * inverse * gain + shift


def norm_back(values, gain, grad):
    centred, inverse = norm_parts(values)
    unit = centred * inverse
    gain_grad = jnp.sum(grad * unit, axis=0, keepdims=True)
    shift_grad = jnp.sum(grad, axis=0, keepdims=True)
    scaled = grad * gain
    lift = jnp.mean(scaled, axis=-1, keepdims=True)
    tilt = jnp.mean(scaled * unit, axis=-1, keepdims=True)
    return inverse * (scaled - lift - unit * tilt), gain_grad, shift_grad


def own_counts(lens_ref):
    block = lax.axis_index("hd")
    return [lens_ref[0, block, i] for i in range(3)]


def layout_of(lens_ref, shape, dim):
    place = lax.broadcasted_iota(jnp.int32, shape, dim)
    count = own_counts(lens_ref)
    ends = [count[0], count[0] + count[1], count[0] + count[1] + count[2]]
    zero = jnp.zeros(shape, jnp.int32)
    segment = zero
    for end in ends:
        segment = segment + jnp.where(place >= end, 1, 0)
    sides = [
        jnp.where(c == SIDES[0] ** 2, SIDES[0], jnp.where(c == SIDES[1] ** 2, SIDES[1], SIDES[2]))
        for c in count
    ]
    start = jnp.where(segment == 0, 0, jnp.where(segment == 1, ends[0], ends[1]))
    side = jnp.where(segment == 0, sides[0], jnp.where(segment == 1, sides[1], sides[2])).astype(F32)
    offset = (place - start).astype(F32)
    row = jnp.floor((offset + 0.5) / side)
    col = offset - row * side
    valid = segment < 3
    return segment, jnp.where(valid, row, 0.0), jnp.where(valid, col, 0.0), valid


def gelu_parts(values):
    bell = jnp.exp(values * values * -0.5)
    size = jnp.abs(values) * math.sqrt(0.5)
    t = 1.0 / (1.0 + 0.3275911 * size)
    poly = t * (
        0.254829592
        + t * (-0.284496736 + t * (1.421413741 + t * (-1.453152027 + t * 1.061405429)))
    )
    tail = 0.5 * poly * bell
    below = jnp.where(values < 0, tail, 1.0 - tail)
    return values * below, below + values * bell * (1.0 / math.sqrt(2.0 * math.pi))


def whole(shape):
    return pl.BlockSpec(shape, lambda *_: (0,) * len(shape))


def smem():
    return pl.BlockSpec(memory_space=pltpu.SMEM)


def cols(rows, width, first=0):
    return pl.BlockSpec((rows, width), lambda j, *_: (0, first + j))


def rowblk(height, width, first=0):
    return pl.BlockSpec((height, width), lambda j, *_: (first + j, 0))


def cost(flops, moved):
    return pl.CostEstimate(flops=1, bytes_accessed=1, transcendentals=0)


def params(**kw):
    return pltpu.CompilerParams(vmem_limit_bytes=VMEM_LIMIT, dimension_semantics=("arbitrary",), **kw)


def attend_quad(q, k, v, add_bias, probs_ref):
    lane = lax.broadcasted_iota(jnp.int32, q.shape, 1)
    scaled = q * jnp.asarray(HDIM**-0.5, BF16)
    v_t = v.T
    outs = []
    for h in range(QUAD):
        q_h = jnp.where(lane // HDIM == h, scaled, jnp.zeros_like(scaled))
        scores = add_bias(dot_nt(k, q_h), h)
        top = jnp.max(scores, axis=0, keepdims=True)
        weights = jnp.exp(scores - top)
        total = jnp.sum(weights, axis=0, keepdims=True)
        probs = (weights * (1.0 / total)).astype(BF16)
        probs_ref[h] = probs
        outs.append(dot_nn(v_t[h * HDIM : (h + 1) * HDIM], probs))
    return jnp.concatenate(outs, axis=0).astype(BF16).T


def self_forward_kernel(
    lens, slopes, radar, cot, gains, shifts, biases, wq, wk, wv, wo,
    n1, q_out, k_out, v_out, probs, att_out, resid, n2, gf, dist,
):
    j = pl.program_id(0)
    rows = n1.shape[0]

    @pl.when(j == 0)
    def _():
        wide = radar[...].astype(F32)
        n1[...] = norm(wide, gains[0:1], shifts[0:1]).astype(BF16)
        resid[...] = wide + biases[0:1]
        seg_k, row_k, col_k, valid = layout_of(lens, (rows, 1), 0)
        gf[...] = jnp.where(valid, cot[...], jnp.zeros_like(cot))
        seg_q, row_q, col_q, _ = layout_of(lens, (1, rows), 1)
        dr = row_k - row_q
        dc = col_k - col_q
        dist[...] = jnp.where(seg_k == seg_q, jnp.sqrt(dr * dr + dc * dc), FAR)

    x = n1[...]
    q = dot_nn(x, wq[...]).astype(BF16)
    k = dot_nn(x, wk[...]).astype(BF16)
    v = dot_nn(x, wv[...]).astype(BF16)
    q_out[...] = q
    k_out[...] = k
    v_out[...] = v
    att = attend_quad(
        q, k, v, lambda s, h: s - slopes[j * QUAD + h] * dist[...], probs
    )
    att_out[...] = att
    resid[...] += dot_nn(att, wo[...])

    @pl.when(j == pl.num_programs(0) - 1)
    def _():
        n2[...] = norm(resid[...], gains[1:2], shifts[1:2]).astype(BF16)


def cross_forward_kernel(
    lens, res_in, n_in, optic, gains, shifts, biases, wq, wk, wv, wo,
    q_out, k_out, v_out, probs, att_out, resid, n3, mask,
):
    j = pl.program_id(0)
    rows = n_in.shape[0]

    @pl.when(j == 0)
    def _():
        resid[...] = res_in[...] + biases[1:2]
        seg_k = layout_of(lens, (rows, 1), 0)[0]
        seg_q = layout_of(lens, (1, rows), 1)[0]
        mask[...] = jnp.where(seg_k == seg_q, 0.0, MASKED)

    q = dot_nn(n_in[...], wq[...]).astype(BF16)
    k = dot_nn(optic[...], wk[...]).astype(BF16)
    v = dot_nn(optic[...], wv[...]).astype(BF16)
    q_out[...] = q
    k_out[...] = k
    v_out[...] = v
    att = attend_quad(q, k, v, lambda s, h: s + mask[...], probs)
    att_out[...] = att
    resid[...] += dot_nn(att, wo[...])

    @pl.when(j == pl.num_programs(0) - 1)
    def _():
        n3[...] = norm(resid[...], gains[2:3], shifts[2:3]).astype(BF16)


def shaped(*shape, dtype=BF16):
    return jax.ShapeDtypeStruct(shape, dtype)


def held(*shape, dtype=BF16):
    return pltpu.HBM(shape, dtype)


def far(*arrays):
    return [pltpu.with_memory_space_constraint(a, pltpu.HBM) for a in arrays]


def self_forward(rows, lens, slopes, radar, cot, gains, shifts, biases, w_qkv, w_out):
    d = radar.shape[1]
    wide = QUAD * HDIM
    steps = d // wide
    return pl.pallas_call(
        self_forward_kernel,
        grid=(steps,),
        in_specs=[
            smem(), smem(), whole((rows, d)), whole((rows, d)),
            *[whole((3, d))] * 3,
            cols(d, wide), cols(d, wide, steps), cols(d, wide, 2 * steps), rowblk(wide, d),
        ],
        out_specs=[
            whole((rows, d)), cols(rows, wide), cols(rows, wide), cols(rows, wide),
            pl.BlockSpec((QUAD, rows, rows), lambda j: (j, 0, 0)),
            cols(rows, wide), whole((rows, d)), whole((rows, d)), whole((rows, d)),
        ],
        out_shape=[
            held(rows, d), held(rows, d), held(rows, d), held(rows, d),
            held(HEADS, rows, rows), held(rows, d), shaped(rows, d, dtype=F32), shaped(rows, d), held(rows, d),
        ],
        scratch_shapes=[pltpu.VMEM((rows, rows), F32)],
        compiler_params=params(),
        cost_estimate=cost(8 * rows * d * d + 12 * HEADS * rows * rows * 128, 8 * d * d + HEADS * rows * rows * 2),
        name="self_forward",
    )(lens, slopes, *far(radar, cot, gains, shifts, biases),
      *far(w_qkv, w_qkv, w_qkv, w_out))


def cross_forward(rows, lens, res_in, n_in, optic, gains, shifts, biases, w_q, w_kv, w_out):
    d = optic.shape[1]
    wide = QUAD * HDIM
    steps = d // wide
    return pl.pallas_call(
        cross_forward_kernel,
        grid=(steps,),
        in_specs=[
            smem(), whole((rows, d)), whole((rows, d)), whole((rows, d)),
            *[whole((3, d))] * 3,
            cols(d, wide), cols(d, wide), cols(d, wide, steps), rowblk(wide, d),
        ],
        out_specs=[
            cols(rows, wide), cols(rows, wide), cols(rows, wide),
            pl.BlockSpec((QUAD, rows, rows), lambda j: (j, 0, 0)),
            cols(rows, wide), whole((rows, d)), whole((rows, d)),
        ],
        out_shape=[
            held(rows, d), held(rows, d), held(rows, d),
            held(HEADS, rows, rows), held(rows, d), shaped(rows, d, dtype=F32), shaped(rows, d),
        ],
        scratch_shapes=[pltpu.VMEM((rows, rows), F32)],
        compiler_params=params(),
        cost_estimate=cost(8 * rows * d * d + 12 * HEADS * rows * rows * 128, 8 * d * d + HEADS * rows * rows * 2),
        name="cross_forward",
    )(lens, res_in, n_in, *far(optic, gains, shifts, biases),
      *far(w_q, w_kv, w_kv, w_out))


def hidden_kernel(res2, n3, gf, gains, hb, win, wout, act_out, grad_two, vectors, acc):
    j = pl.program_id(0)

    @pl.when(j == 0)
    def _():
        acc[...] = jnp.zeros_like(acc)

    act, slope = gelu_parts(dot_nn(n3[...], win[...]) + hb[...])
    act_out[...] = act.astype(BF16)
    g_pre = (dot_nt(gf[...], wout[...]) * slope).astype(BF16)
    acc[...] += dot_nt(g_pre, win[...])
    vectors[pl.ds(j, 1)] = jnp.sum(g_pre.astype(F32), axis=0, keepdims=True)

    @pl.when(j == pl.num_programs(0) - 1)
    def _():
        part, g_gain, g_shift = norm_back(res2[...], gains[2:3], acc[...])
        wide = gf[...].astype(F32)
        grad_two[...] = wide + part
        vectors[4:5] = g_gain
        vectors[5:6] = g_shift
        vectors[6:7] = jnp.sum(wide, axis=0, keepdims=True)
        vectors[7:8] = jnp.zeros_like(g_gain)


def hidden(rows, res2, n3, gf, gains, hb, win, wout):
    d = n3.shape[1]
    ff = win.shape[1]
    chunk = ff // 4
    return pl.pallas_call(
        hidden_kernel,
        grid=(4,),
        in_specs=[
            whole((rows, d)), whole((rows, d)), whole((rows, d)),
            whole((3, d)), cols(1, chunk), cols(d, chunk), rowblk(chunk, d),
        ],
        out_specs=[cols(rows, chunk), whole((rows, d)), whole((8, d))],
        out_shape=[held(rows, ff), shaped(rows, d, dtype=F32), shaped(8, d, dtype=F32)],
        scratch_shapes=[pltpu.VMEM((rows, d), F32)],
        compiler_params=params(),
        cost_estimate=cost(6 * rows * d * ff, 4 * d * ff),
        name="hidden",
    )(*far(res2, n3, gf, gains, hb, win, wout))


def output_kernel(lens, act, res2, biases, wout, y_out, acc):
    j = pl.program_id(0)
    rows = act.shape[0]

    @pl.when(j == 0)
    def _():
        acc[...] = res2[...] + biases[2:3]

    acc[...] += dot_nn(act[...], wout[...])

    @pl.when(j == pl.num_programs(0) - 1)
    def _():
        valid = layout_of(lens, (rows, 1), 0)[3]
        y_out[0:rows] = jnp.where(valid, acc[...], 0.0).astype(BF16)
        if y_out.shape[0] > rows:
            y_out[rows:] = jnp.zeros((y_out.shape[0] - rows, y_out.shape[1]), BF16)


def output(rows, local_rows, lens, act, res2, biases, wout):
    ff, d = wout.shape
    chunk = ff // 2
    return pl.pallas_call(
        output_kernel,
        grid=(2,),
        in_specs=[smem(), cols(rows, chunk), whole((rows, d)), whole((3, d)), rowblk(chunk, d)],
        out_specs=whole((local_rows, d)),
        out_shape=held(local_rows, d),
        scratch_shapes=[pltpu.VMEM((rows, d), F32)],
        compiler_params=params(),
        cost_estimate=cost(2 * rows * d * ff, 2 * d * ff),
        name="output",
    )(lens, *far(act, res2, biases, wout))


def hidden_grads_kernel(blocks, meta, *refs):
    normed, grads = refs[:blocks], refs[blocks : 2 * blocks]
    hb_a, hb_b, win_a, win_b, wout_a, wout_b, dwin, dwout, acc_in, acc_out = refs[2 * blocks :]
    win = jnp.concatenate([win_a[...], win_b[...]], axis=1)
    wout = jnp.concatenate([wout_a[...], wout_b[...]], axis=0)
    hb = jnp.concatenate([hb_a[...], hb_b[...]], axis=1)
    for i in range(blocks):
        act, slope = gelu_parts(dot_nn(normed[i][...], win) + hb)
        g_pre = (dot_nt(grads[i][...], wout) * slope).astype(BF16)
        into = dot_nn(normed[i][...].T, g_pre)
        out = dot_nn(act.astype(BF16).T, grads[i][...])
        if i == 0:
            acc_in[...] = into
            acc_out[...] = out
        else:
            acc_in[...] += into
            acc_out[...] += out
    at_y, at_c, at_p = meta[0], meta[1], meta[3]
    piece = dwout.shape[2]
    for y in range(2):
        for p in range(2):
            at = (y * 2 + p) * piece
            dwout[y ^ at_y, p ^ at_p] = acc_out[at : at + piece].astype(BF16)
    piece = dwin.shape[3]
    for y in range(2):
        for c in range(2):
            for p in range(2):
                at = ((y * 2 + c) * 2 + p) * piece
                dwin[y ^ at_y, c ^ at_c, p ^ at_p] = acc_in[at : at + piece].astype(BF16)


def hidden_grads(rows, meta, normed, grads, hb, win, wout):
    d, ff = win.shape
    part = ff // 8
    blocks = len(normed)

    def wide(height, y):
        return pl.BlockSpec((height, part), lambda i, m: (0, y * 4 + m[1] * 2 + m[2]))

    def tall(y):
        return pl.BlockSpec((part, d), lambda i, m: (y * 4 + m[1] * 2 + m[2], 0))

    return pl.pallas_call(
        functools.partial(hidden_grads_kernel, blocks),
        grid_spec=pltpu.PrefetchScalarGridSpec(
            num_scalar_prefetch=1,
            grid=(1,),
            in_specs=[
                *[whole((rows, d))] * (2 * blocks),
                wide(1, 0), wide(1, 1), wide(d, 0), wide(d, 1), tall(0), tall(1),
            ],
            out_specs=[whole((2, 2, 2, d // 8, 2 * part)), whole((2, 2, part // 2, d))],
            scratch_shapes=[pltpu.VMEM((d, 2 * part), F32), pltpu.VMEM((2 * part, d), F32)],
        ),
        out_shape=[shaped(2, 2, 2, d // 8, 2 * part), shaped(2, 2, part // 2, d)],
        compiler_params=params(),
        cost_estimate=cost(16 * blocks * rows * d * part, 4 * blocks * rows * d + 4 * d * ff),
        name="hidden_grads",
    )(meta, *far(*normed, *grads, hb, hb, win, win, wout, wout))


def place(keep, send, bucket, grad, spot):
    at_hd, at_grp = lax.axis_index("hd"), lax.axis_index("grp")
    at_y, first = at_hd // 2, lax.rem(at_hd, 2) == 0
    at_x, at_p = lax.rem(at_grp, 2), lax.rem(at_grp // 2, 2)
    part = grad.shape[0] // 16
    for y in range(2):
        for x in range(2):
            for p in range(2):
                at = y * 8 + x * 2 + p
                low = grad[at * part : (at + 1) * part]
                high = grad[(at + 4) * part : (at + 5) * part]
                lead, other = (x ^ at_x, y ^ at_y) if bucket == 0 else (y ^ at_y, x ^ at_x)
                to = (bucket, lead, other, p ^ at_p, slice(None), spot)
                keep[to] = jnp.where(first, low, high)
                send[to] = jnp.where(first, high, low)


def quad_back(q, k, v, att, g_att, probs):
    lane = lax.broadcasted_iota(jnp.int32, q.shape, 1)
    nil = jnp.zeros_like(q)
    g_t = g_att.T
    k_t = k.T
    inner = g_t.astype(F32) * att.T.astype(F32)
    dq_t, dk, dv = [], 0.0, 0.0
    for h in range(QUAD):
        part = slice(h * HDIM, (h + 1) * HDIM)
        mine = lane // HDIM == h
        delta = jnp.sum(inner[part], axis=0, keepdims=True)
        v_h = jnp.where(mine, v, nil)
        p = probs[h]
        g_scores = (p.astype(F32) * (dot_nn(v_h, g_t) - delta)).astype(BF16)
        dv = dv + dot_nn(p, jnp.where(mine, g_att, nil))
        dk = dk + dot_nn(g_scores, jnp.where(mine, q, nil))
        dq_t.append(dot_nn(k_t[part], g_scores))
    scale = HDIM**-0.5
    dq = (jnp.concatenate(dq_t, axis=0) * scale).astype(BF16).T
    return dq, (dk * scale).astype(BF16), dv.astype(BF16)


def back_kernel(own_keys, grad_in, res, xq, xkv, q, k, v, att, att_all, probs, gains, wo, wq, *refs):
    refs = list(refs)
    keep, send, dk_out, dv_out, vectors = [refs.pop(0) for _ in range(5)]
    last_out = refs.pop(0)
    low, xq_t, xkv_t, acc = refs
    i = pl.program_id(0)
    d = xq.shape[1]
    wide = q.shape[1]

    @pl.when(i == 0)
    def _():
        low[...] = grad_in[...].astype(BF16)
        xq_t[...] = xq[...].T
        if not own_keys:
            xkv_t[...] = xkv[...].T
            acc[...] = jnp.zeros_like(acc)
        vectors[0:1] = jnp.sum(low[...].astype(F32), axis=0, keepdims=True)
        vectors[1:8] = jnp.zeros((7, d), F32)
        place(keep, send, 0, dot_nn(att_all[...].T, low[...]).astype(BF16), slice(0, d))

    g_att = dot_nt(low[...], wo[...]).astype(BF16)
    dq, dk, dv = quad_back(q[...], k[...], v[...], att[...], g_att, probs)
    dk_out[...] = dk
    dv_out[...] = dv
    source_t = xq_t if own_keys else xkv_t
    near = pl.ds(pl.multiple_of(i * wide, wide), wide)
    past = pl.ds(pl.multiple_of(d + i * wide, wide), wide)
    place(keep, send, 0, dot_nn(xq_t[...], dq).astype(BF16), past)
    place(keep, send, 1, dot_nn(source_t[...], dk).astype(BF16), near)
    place(keep, send, 1, dot_nn(source_t[...], dv).astype(BF16), past)
    if own_keys:
        last_out[...] = dq
    else:
        acc[...] += dot_nt(dq, wq[...])

        @pl.when(i == pl.num_programs(0) - 1)
        def _():
            part, g_gain, g_shift = norm_back(res[...], gains[1:2], acc[...])
            last_out[...] = grad_in[...] + part
            vectors[1:2] = g_gain
            vectors[2:3] = g_shift


def back(own_keys, rows, grad_in, res, xq, xkv, q, k, v, att, probs, gains, wo, wq):
    d = xq.shape[1]
    wide = QUAD * HDIM
    halves = (2, 2, 2, 2, d // 16, 2 * d)
    at = cols(rows, wide)
    full = whole((rows, d))
    if own_keys:
        res = gains
    return pl.pallas_call(
        functools.partial(back_kernel, own_keys),
        grid=(d // wide,),
        in_specs=[
            full, whole(res.shape), full, full, at, at, at, at, full,
            pl.BlockSpec((QUAD, rows, rows), lambda i: (i, 0, 0)),
            whole((3, d)), rowblk(wide, d), cols(d, wide),
        ],
        out_specs=[*[whole(halves)] * 2, at, at, whole((8, d)), at if own_keys else full],
        out_shape=[
            *[shaped(*halves)] * 2, held(rows, d), held(rows, d), shaped(8, d, dtype=F32),
            held(rows, d) if own_keys else shaped(rows, d, dtype=F32),
        ],
        scratch_shapes=[
            pltpu.VMEM((rows, d), BF16), pltpu.VMEM((d, rows), BF16),
            pltpu.VMEM((16, 128) if own_keys else (d, rows), BF16),
            pltpu.VMEM((8, 128) if own_keys else (rows, d), F32),
        ],
        compiler_params=params(),
        cost_estimate=cost(18 * rows * d * d + 24 * HEADS * rows * rows * 128, 16 * d * d),
        name="self_back" if own_keys else "cross_back",
    )(*far(grad_in, res, xq, xkv, q, k, v, att, att, probs, gains, wo, wq))


def through(parts, weights):
    total = None
    for i, part in enumerate(parts):
        d = part.shape[1]
        term = dot_nt(part[...], weights[:, i * d : (i + 1) * d])
        total = term if total is None else total + term
    return total


def store_padded(out, values):
    rows = values.shape[0]
    out[0:rows] = values
    if out.shape[0] > rows:
        out[rows:] = jnp.zeros((out.shape[0] - rows, out.shape[1]), out.dtype)


def optic_kernel(dk, dv, weights, out):
    store_padded(out, through([dk, dv], weights))


def optic(local_rows, dk, dv, weights):
    rows, d = dk.shape
    return pl.pallas_call(
        optic_kernel,
        in_specs=[whole(dk.shape), whole(dv.shape), whole(weights.shape)],
        out_specs=whole((local_rows, d)),
        out_shape=held(local_rows, d, dtype=F32),
        grid=(1,),
        compiler_params=params(),
        cost_estimate=cost(4 * rows * d * d, 4 * d * d),
        name="optic",
    )(*far(dk, dv, weights))


def radar_kernel(dq, dk, dv, weights, grad_in, radar, gains, hidden_vec, cross_vec, self_vec, out, vectors):
    total = through([dq, dk, dv], weights)
    part, g_gain, g_shift = norm_back(radar[...].astype(F32), gains[0:1], total)
    store_padded(out, grad_in[...] + part)
    vectors[0:1] = g_gain
    vectors[1:2] = cross_vec[1:2]
    vectors[2:3] = hidden_vec[4:5]
    vectors[3:4] = g_shift
    vectors[4:5] = cross_vec[2:3]
    vectors[5:6] = hidden_vec[5:6]
    vectors[6:7] = self_vec[0:1]
    vectors[7:8] = cross_vec[0:1]
    vectors[8:9] = hidden_vec[6:7]
    vectors[9:13] = hidden_vec[0:4]
    vectors[13:16] = jnp.zeros((3, out.shape[1]), F32)


def radar(local_rows, dq, dk, dv, weights, grad_in, tokens, gains, vectors):
    rows, d = dq.shape
    full = whole((rows, d))
    return pl.pallas_call(
        radar_kernel,
        grid=(1,),
        in_specs=[full, full, full, whole(weights.shape), full, full, whole((3, d)), *[whole((8, d))] * 3],
        out_specs=[whole((local_rows, d)), whole((16, d))],
        out_shape=[held(local_rows, d, dtype=F32), shaped(16, d, dtype=F32)],
        compiler_params=params(),
        cost_estimate=cost(6 * rows * d * d, 6 * d * d),
        name="radar",
    )(*far(dq, dk, dv, weights, grad_in, tokens, gains, *vectors))
def hop(values, perm):
    return lax.ppermute(values, ("grp", "hd"), perm)


def pairs(move):
    found = []
    for z in range(4):
        for x in range(2):
            for y in range(2):
                for c in range(2):
                    to = move(z, x, y, c)
                    if to is not None:
                        tz, tx, ty, tc = to
                        found.append(((z * 2 + x) * 4 + y * 2 + c, (tz * 2 + tx) * 4 + ty * 2 + tc))
    return found


ACROSS_CORE = pairs(lambda z, x, y, c: (z, x, y, 1 - c))
ACROSS_Y = pairs(lambda z, x, y, c: (z, x, 1 - y, c))
ACROSS_X = pairs(lambda z, x, y, c: (z, 1 - x, y, c))
ACROSS_P = pairs(lambda z, x, y, c: (z ^ 1, x, y, c))
ACROSS_Q = pairs(lambda z, x, y, c: (z ^ 2, x, y, c))
ACROSS_XP = pairs(lambda z, x, y, c: (z ^ 1, 1 - x, y, c))


def add(*terms):
    total = terms[0].astype(F32)
    for term in terms[1:]:
        total = total + term.astype(F32)
    return total.astype(terms[0].dtype)


def in_order(at, own, other):
    return jnp.where(at == 0, own, other), jnp.where(at == 0, other, own)


def tie(values):
    return list(lax.optimization_barrier(tuple(values)))


MOVES = {
    "C": ACROSS_CORE, "Y": ACROSS_Y, "Z": ACROSS_Y, "X": ACROSS_X, "P": ACROSS_P, "Q": ACROSS_Q,
    "A": ACROSS_P, "G": ACROSS_X, "D": ACROSS_XP, "W": ACROSS_Y, "V": ACROSS_X,
}


class Flow:
    def __init__(self, value):
        self.value, self.ends = value, {}

    def operand(self, stage):
        return self.value[1] if stage in ("Y", "P") else self.value

    def absorb(self, stage, got):
        if stage in ("Y", "P"):
            self.value = add(self.value[0], got)
        elif stage == "Q":
            self.value = add(self.value, got)
        else:
            self.ends[stage] = got

    def together(self, at_x, at_p):
        rows = [
            in_order(at_p, self.value, self.ends["A"]),
            in_order(at_p, self.ends["G"], self.ends["D"]),
        ]
        return in_order(at_x, jnp.stack(rows[0]), jnp.stack(rows[1]))


class InFlow(Flow):
    def operand(self, stage):
        if stage in ("Y", "Z"):
            return self.value[1, 1 if stage == "Y" else 0]
        if stage == "C":
            return self.value[1]
        return self.value[:, 1] if stage == "P" else self.value

    def absorb(self, stage, got):
        if stage == "Y":
            self.other = add(self.value[0, 1], got)
        elif stage == "Z":
            self.value = [add(self.value[0, 0], got), self.other]
        elif stage == "C":
            self.value = jnp.stack([self.value[0], got])
        elif stage == "P":
            self.value = add(self.value[:, 0], got)
        else:
            super().absorb(stage, got)


class RowFlow(Flow):
    def __init__(self, keep, send):
        super().__init__(None)
        self.keep, self.send, self.parts = keep, send, None

    def operand(self, stage):
        if stage == "C":
            return self.send
        if stage in "XYWV":
            return self.parts[int(stage in "WV")][1]
        if stage == "P" and self.value is None:
            self.value = jnp.stack(self.parts)
        return self.value[:, 1] if stage == "P" else self.value

    def absorb(self, stage, got):
        if stage == "C":
            self.parts = [[add(self.keep[b, i], got[b, i]) for i in range(2)] for b in range(2)]
        elif stage in "XYWV":
            b = int(stage in "WV")
            self.parts[b] = add(self.parts[b][0], got)
        elif stage == "P":
            self.value = add(self.value[:, 0], got)
        else:
            super().absorb(stage, got)


class Vectors(Flow):
    def operand(self, stage):
        return self.value

    def absorb(self, stage, got):
        self.value = self.value + got


def whole_rows(keep, send, bucket, at):
    at_y, at_c, at_x, at_p = at
    lead_at, other_at = (at_x, at_y) if bucket == 0 else (at_y, at_x)
    parts = jnp.stack(in_order(at_c, keep[bucket], send[bucket]))
    for axis, place_at in ((1, lead_at), (2, other_at), (3, at_p)):
        own, other = [lax.index_in_dim(parts, i, axis, keepdims=False) for i in range(2)]
        parts = jnp.stack(in_order(place_at, own, other), axis=axis)
    order = (2, 0, 1, 3, 4, 5) if bucket == 0 else (1, 0, 2, 3, 4, 5)
    return parts.transpose(order).reshape(-1, parts.shape[-1])


def summed_anywhere(grad):
    mine = lax.psum_scatter(grad, "hd", scatter_dimension=0, tiled=True)
    return lax.psum(mine.astype(F32), "grp")


class Plan:
    def __init__(self):
        self.flows, self.flying = {}, {}

    def begin(self, gate, *moves):
        sent = [self.flows[m[0]].operand(m[1]) for m in moves]
        gate, *sent = tie([gate, *sent])
        for m, operand in zip(moves, sent):
            self.flying[m] = hop(operand, MOVES[m[1]])
        return gate

    def end(self, gate, *moves):
        gate, *got = tie([gate, *[self.flying.pop(m) for m in moves]])
        for m, value in zip(moves, got):
            self.flows[m[0]].absorb(m[1], value)
        return gate


def on_device(
    radar_tokens, optic_tokens, tile_lengths, norm_gains, norm_shifts, self_qkv, self_out,
    cross_query, cross_keyval, cross_out, hidden_in, hidden_out, proj_biases, hidden_bias, cotangent,
):
    local_rows, d = radar_tokens.shape
    ff = hidden_in.shape[1]
    known = lax.axis_size("grp") == 8 and lax.axis_size("hd") == 4
    at_hd = lax.axis_index("hd")
    at_grp = lax.axis_index("grp")
    at_y, at_c, at_z, at_x = at_hd // 2, at_hd % 2, at_grp // 2, at_grp % 2
    at_p = at_z % 2
    rows = rows_in_use(local_rows, tile_lengths.shape[2])
    slopes = jnp.asarray([2.0 ** (-8.0 * (h + 1) / HEADS) for h in range(HEADS)], F32)
    hb = hidden_bias[None]

    n1, q1, k1, v1, p1, att1, res1, n2, gf = self_forward(
        rows, tile_lengths, slopes, radar_tokens, cotangent, norm_gains, norm_shifts, proj_biases, self_qkv, self_out
    )
    if known:
        n2, gf = tie([n2, gf])
        gf_x = hop(gf, ACROSS_X)
        gf_c = hop(gf, ACROSS_CORE)
    q2, k2, v2, p2, att2, res2, n3 = cross_forward(
        rows, tile_lengths, res1, n2, optic_tokens, norm_gains, norm_shifts, proj_biases,
        cross_query, cross_keyval, cross_out,
    )
    if known:
        n3, gf_x, gf_c, res2 = tie([n3, gf_x, gf_c, res2])
        gf_xc = hop(gf_x, ACROSS_CORE)
        n3_x = hop(n3, ACROSS_X)
        n3_c = hop(n3, ACROSS_CORE)
    act, grad_two, hidden_vec = hidden(rows, res2, n3, gf, norm_gains, hb, hidden_in, hidden_out)

    def cross_step(grad):
        return back(
            False, rows, grad, res1, n2, optic_tokens, q2, k2, v2, att2, p2, norm_gains, cross_out, cross_query
        )

    def self_step(grad):
        return back(True, rows, grad, None, n1, n1, q1, k1, v1, att1, p1, norm_gains, self_out, self_qkv)

    def radar_step(dq, grad):
        return radar(
            local_rows, dq, dk1, dv1, self_qkv, grad, radar_tokens, norm_gains, [hidden_vec, cross_vec, self_vec]
        )

    if known:
        meta = jnp.stack([at_y, at_c, at_x, at_p]).astype(jnp.int32)
        act, n3_x, n3_c, gf_x, gf_c, gf_xc, grad_two = tie([act, n3_x, n3_c, gf_x, gf_c, gf_xc, grad_two])
        n3_xc = hop(n3_x, ACROSS_CORE)
        dwin, dwout = hidden_grads(
            rows, meta, [n3, n3_x, n3_c, n3_xc], [gf, gf_x, gf_c, gf_xc], hb, hidden_in, hidden_out
        )
        plan = Plan()
        grad_two, dwin, dwout = tie([grad_two, dwin, dwout])
        plan.flows["o"], plan.flows["n"] = Flow(dwout), InFlow(dwin)

        grad_two = plan.begin(grad_two, "oY", "nY")
        keep, send, dk2, dv2, cross_vec, grad_one = cross_step(grad_two)
        act = plan.end(tie([act, grad_one])[0], "oY", "nY")
        plan.flows["a"] = RowFlow(keep, send)

        act = plan.begin(act, "aC", "nZ", "oP")
        layer_output = output(rows, local_rows, tile_lengths, act, res2, proj_biases, hidden_out)
        grad_one = plan.end(tie([grad_one, layer_output])[0], "aC", "nZ", "oP")

        grad_one = plan.begin(grad_one, "nC", "aX", "aW", "oQ")
        keep, send, dk1, dv1, self_vec, dq1 = self_step(grad_one)
        dq1 = plan.end(dq1, "nC", "aX", "aW", "oQ")
        plan.flows["c"] = RowFlow(keep, send)

        dq1 = plan.begin(dq1, "cC", "aY", "aV", "nP")
        radar_grad, small = radar_step(dq1, grad_one)
        dk2 = plan.end(tie([dk2, radar_grad])[0], "cC", "aY", "aV", "nP")
        plan.flows["s"] = Vectors(small)

        dk2 = plan.begin(dk2, "sC", "cX", "cW", "aP", "nQ")
        optic_grad = optic(local_rows, dk2, dv2, cross_keyval)
        gate = plan.end(optic_grad, "sC", "cX", "cW", "aP", "nQ")

        for stages in (
            ("sY", "cV", "cY", "oA", "oG", "oD", "aQ"),
            ("sX", "cP", "aA", "aG", "aD"),
            ("sP", "cQ", "nA", "nG", "nD"),
            ("sQ", "cA", "cG", "cD"),
        ):
            gate = plan.end(plan.begin(gate, *stages), *stages)
        optic_grad = gate

        done = {name: plan.flows[name].together(at_x, at_p) for name in "onac"}
        out_part = jnp.stack(done["o"]).reshape(-1, d).astype(F32)
        slices = [in_order(at_c, v[:, 0], v[:, 1]) for v in done["n"]]
        half = ff // 8
        in_part = jnp.concatenate(
            [
                slices[x][c][..., y * half : (y + 1) * half].reshape(-1, half)
                for y in range(2) for c in range(2) for x in range(2)
            ],
            axis=1,
        ).astype(F32)
        (cross_a, cross_b), (self_a, self_b) = [
            [jnp.stack([v[:, i] for v in done[name]]).reshape(-1, 2 * d).astype(F32) for i in range(2)] for name in "ac"
        ]
        small = plan.flows["s"].value
    else:
        into, out = [], []
        for c in range(2):
            for x in range(2):
                at = jnp.asarray([0, c, x, 0], jnp.int32)
                dwin, dwout = hidden_grads(rows, at, [n3], [gf], hb, hidden_in, hidden_out)
                into.append(jnp.stack([dwin[:, c], dwin[:, 1 - c]], axis=1).reshape(d, 2, ff // 8))
                out.append(dwout.reshape(2, ff // 8, d))
        in_part = summed_anywhere(jnp.stack(into, axis=2).reshape(d, ff))
        out_part = summed_anywhere(jnp.stack(out, axis=1).reshape(ff, d))
        cross_keep, cross_send, dk2, dv2, cross_vec, grad_one = cross_step(grad_two)
        self_keep, self_send, dk1, dv1, self_vec, dq1 = self_step(grad_one)
        radar_grad, small = radar_step(dq1, grad_one)
        optic_grad = optic(local_rows, dk2, dv2, cross_keyval)
        layer_output = output(rows, local_rows, tile_lengths, act, res2, proj_biases, hidden_out)
        at = (at_y, at_c, at_x, at_p)
        cross_a, cross_b = [summed_anywhere(whole_rows(cross_keep, cross_send, b, at)) for b in range(2)]
        self_a, self_b = [summed_anywhere(whole_rows(self_keep, self_send, b, at)) for b in range(2)]
        small = lax.psum(small, ("grp", "hd"))
    vectors = lax.dynamic_slice_in_dim(small[:9], at_hd * (d // 4), d // 4, 1)
    hidden_part = lax.dynamic_index_in_dim(small[9:13], at_hd, 0, keepdims=False)
    return (
        layer_output,
        radar_grad,
        optic_grad,
        jnp.concatenate([self_a[:, d:], self_b], axis=1),
        self_a[:, :d],
        cross_a[:, d:],
        cross_b,
        cross_a[:, :d],
        in_part,
        out_part,
        vectors[0:3],
        vectors[3:6],
        vectors[6:9],
        hidden_part,
    )


def solution(mesh):
    rows = P(("grp", "hd"), None)
    kept = P("hd", None)
    vector = P(None, "hd")
    return jax.shard_map(
        on_device,
        mesh=mesh,
        in_specs=(rows, rows, P("grp", None, None), *[P()] * 11, rows),
        out_specs=(rows, rows, rows, *[kept] * 7, vector, vector, vector, P("hd")),
        check_vma=False,
    )
```

time: 392 us -> 258 us (0.66); the launches traced: 385 us -> 257 us
  waiting for transfers between devices: 174 us -> 60.9 us
  blocking collectives: 44.9 us -> 0 us
  Pallas kernels: 102 us -> 125 us
  starting transfers between devices: 32.3 us -> 47.2 us
  other arithmetic: 20.8 us -> 13.5 us
    ppermute x28 -> x45, waiting for transfers between devices: 174 us -> 60.9 us  [hop(): return lax.ppermute(values, ('grp', 'hd'), perm)]
    psum x1 -> x0, blocking collectives: 44.9 us -> none  [on_device(): small = lax.psum(small, ('grp', 'hd'))]
    pallas_call x3 -> x7, Pallas kernels: 70.5 us -> 94.7 us  [the longest x2 34.5 us: back(): pl.pallas_call(functools.partial(back_kernel, own_keys), grid=(d // wide,...]
    ppermute x28 -> x45, starting transfers between devices: 32.3 us -> 47.2 us  [hop(): return lax.ppermute(values, ('grp', 'hd'), perm)]
    convert_element_type x24 -> x19, other arithmetic: 17 us -> 7.19 us  [the longest x13 2.22 us: add(): return total.astype(terms[0].dtype)]
    unnamed x26 -> x44, local copies, waits for them, and re-layouts: 0.18 us -> 5.41 us
  transfers between devices with their start and end apart: 28 -> 45, of which waited for: 15 -> 21; matrix products, arithmetic and copies ran while one was open for 6% -> 4% of each run, Pallas kernels for 0% -> 36%
where the time goes in v2:
time: 258 us; the launch traced here: 257 us
  Pallas kernels  125 us (48%)
  waiting for transfers between devices  60.9 us (24%)
  starting transfers between devices  47.2 us (18%)
  other arithmetic  13.5 us (5%)
  local copies, waits for them, and re-layouts  9.19 us (4%)
    ppermute x45, waiting for transfers between devices, hop(): return lax.ppermute(values, ('grp', 'hd'), perm)  60.9 us
    ppermute x45, starting transfers between devices, hop(): return lax.ppermute(values, ('grp', 'hd'), perm)  47.2 us
    pallas_call x2, Pallas kernels, back(): pl.pallas_call(functools.partial(back_kernel, own_keys), grid=(d // wide,...  34.5 us
    pallas_call x1, Pallas kernels, hidden(): pl.pallas_call(hidden_kernel, grid=(4,), in_specs=[whole((rows, d)), whol...  26 us
    pallas_call x1, Pallas kernels, hidden_grads(): pl.pallas_call(functools.partial(hidden_grads_kernel, blocks), grid_spec=...  16.7 us
    pallas_call x1, Pallas kernels, self_forward(): pl.pallas_call(self_forward_kernel, grid=(steps,), in_specs=[smem(), smem...  16 us
    pallas_call x1, Pallas kernels, cross_forward(): pl.pallas_call(cross_forward_kernel, grid=(steps,), in_specs=[smem(), who...  13.9 us
    pallas_call x1, Pallas kernels, radar(): pl.pallas_call(radar_kernel, grid=(1,), in_specs=[full, full, full, whole...  6.79 us
  transfers between devices with their start and end apart: 45, of which 21 were waited for; matrix products, arithmetic and copies ran while one was open for 4% of the time, Pallas kernels for 36%

profile of v2, /device:TPU:0, one launch (start us, length us, event | category | flops | bytes accessed | tf_op | source)
XLA Modules:
  0.0 256.9 jit_solution(2790186546698762687)
XLA Ops:
  2.1 16.0 %self_forward.1 = (bf16[464,768]{1,0:T(8,128)(2,1)}, bf16[464,768]{1,0:T(8,128)(2,1)}, bf16[464,768]{1,0:T(8,128)(2,1)}, bf16[464,768]{1,0:T(8,128)(2,1)}, bf16[...) custom-call(s32[1,4,3]{2,1,0:T(4,128)S(1)} %copy.32.lens, ...), custom_call_target="tpu_custom_call" | custom-call | flops 1 | bytes 1 | tf_op jit(solution)/shard_map/self_forward/pallas_call | solution.py:225
  18.0 3.0 %collective-permute-start = (bf16[464,768]{1,0:T(8,128)(2,1)}, bf16[464,768]{1,0:T(8,128)(2,1)S(1)}, u32[]{:S(2)}, u32[]{:S(2)}) collective-permute-start(bf16[464,768]{1,0:T(8,128)(2,1)} %get-tuple-element.169.gf.refs_4_), channel_id=1, source_target_pairs={{0,4},{1,5},{2,6},{3,7},{4,0},{5,1},{6,2},{7,3},{8,12},{9,13},{10,... | collective-permute-start | bytes 2138120 | tf_op jit(solution)/shard_map/ppermute | solution.py:597
  21.1 13.9 %cross_forward.1 = (bf16[464,768]{1,0:T(8,128)(2,1)}, bf16[464,768]{1,0:T(8,128)(2,1)}, bf16[464,768]{1,0:T(8,128)(2,1)}, bf16[12,464,464]{2,1,0:T(8,128)(2,1)},...) custom-call(s32[1,4,3]{2,1,0:T(4,128)S(1)} %copy.32.lens, ...), custom_call_target="tpu_custom_call" | custom-call | flops 1 | bytes 1 | tf_op jit(solution)/shard_map/cross_forward/pallas_call | solution.py:254
  37.2 1.8 collective-permute-start.2
  39.5 26.0 %hidden.1 = (bf16[464,3072]{1,0:T(8,128)(2,1)}, f32[464,768]{1,0:T(8,128)S(1)}, f32[8,768]{1,0:T(8,128)S(1)}) custom-call(f32[464,768]{1,0:T(8,128)} %copy-done.2, bf16[464,768]{1,0:T(8,128)(2,1)} %copy-done.4, bf16[464,768]{1,0:T(8,128)(2,1)} %get-tuple-element.169.gf.refs_4_, f32[3,768]{1,0:T(4,128)} %gains.11, f32[1,3072]{1,0:T(1,128)} %bitcast.220, ...), custom_call_target="tpu_custom_call" | custom-call | flops 1 | bytes 1 | tf_op jit(solution)/shard_map/hidden/pallas_call | solution.py:307
  67.6 2.0 collective-permute-done.5.refs_3_
  70.5 16.7 %hidden_grads.1 = (bf16[2,2,2,96,768]{4,3,2,1,0:T(8,128)(2,1)S(1)}, bf16[2,2,192,768]{3,2,1,0:T(8,128)(2,1)S(1)}) custom-call(s32[4]{0:T(128)S(1)} %pad_add_fusion.meta, bf16[464,768]{1,0:T(8,128)(2,1)} %copy-done.4, bf16[464,768]{1,0:T(8,128)(2,1)} %copy-done.12, bf16[464,768]{1,0:T(8,128)(2,1)} %copy-done.13, bf16[464,768]{1,0:T(8,128)(2,1)} %copy-done.15, ...), custom_call_target="tpu_custom_call" | custom-call | flops 1 | bytes 1 | tf_op jit(solution)/shard_map/hidden_grads/pallas_call | solution.py:399
  87.2 1.6 collective-permute-start.6
  89.3 17.9 %cross_back.1 = (bf16[2,2,2,2,48,1536]{5,4,3,2,1,0:T(8,128)(2,1)S(1)}, bf16[2,2,2,2,48,1536]{5,4,3,2,1,0:T(8,128)(2,1)S(1)}, bf16[464,768]{1,0:T(8,128)(2,1)}, b...) custom-call(f32[464,768]{1,0:T(8,128)} %copy-done.5, f32[464,768]{1,0:T(8,128)} %copy-done, ...), custom_call_target="tpu_custom_call" | custom-call | flops 1 | bytes 1 | tf_op jit(solution)/shard_map/cross_back/pallas_call | solution.py:508
  107.3 1.7 collective-permute-done.7
  109.3 1.6 collective-permute-start.9
  110.8 1.6 collective-permute-start.10
  112.4 6.2 %output.1 = bf16[512,768]{1,0:T(8,128)(2,1)} custom-call(s32[1,4,3]{2,1,0:T(4,128)S(1)} %copy.32.lens, bf16[464,3072]{1,0:T(8,128)(2,1)} %get-tuple-element.202.act, f32[464,768]{1,0:T(8,128)} %copy-done.2, f32[3,768]{1,0:T(4,128)} %biases.5, bf16[3072,768]{1,0:T(8,128)(2,1)} %wout.3), custom_call_target="tpu_custom_call" | custom-call | flops 1 | bytes 1 | tf_op jit(solution)/shard_map/output/pallas_call | solution.py:344
  118.7 1.2 collective-permute-done.10
  121.4 2.8 %collective-permute-start.14 = (bf16[192,768]{1,0:T(8,128)(2,1)S(1)}, bf16[192,768]{1,0:T(8,128)(2,1)S(1)}, u32[]{:S(2)}, u32[]{:S(2)}) collective-permute-start(bf16[192,768]{1,0:T(8,128)(2,1)S(1)} %fusion.21), channel_id=1, source_target_pairs={{0,16},{1,17},{2,18},{3,19},{4,20},{5,21},{6,22},{7,23},{8,24},{9,... | collective-permute-start | bytes 884744 | tf_op jit(solution)/shard_map/ppermute | solution.py:597
  124.2 16.6 %self_back.1 = (bf16[2,2,2,2,48,1536]{5,4,3,2,1,0:T(8,128)(2,1)S(1)}, bf16[2,2,2,2,48,1536]{5,4,3,2,1,0:T(8,128)(2,1)S(1)}, bf16[464,768]{1,0:T(8,128)(2,1)}, bf...) custom-call(f32[464,768]{1,0:T(8,128)} %copy-done.1, f32[3,768]{1,0:T(4,128)} %gains.11, ...), custom_call_target="tpu_custom_call" | custom-call | flops 1 | bytes 1 | tf_op jit(solution)/shard_map/self_back/pallas_call | solution.py:508
  141.7 1.5 collective-permute-start.16
  143.2 1.5 collective-permute-start.17
  144.7 1.6 collective-permute-start.18
  146.3 6.8 %radar.4 = (f32[512,768]{1,0:T(8,128)}, f32[16,768]{1,0:T(8,128)S(1)}) custom-call(bf16[464,768]{1,0:T(8,128)(2,1)} %get-tuple-element.230.dq, bf16[464,768]{1,0:T(8,128)(2,1)} %get-tuple-element.231.dk, bf16[464,768]{1,0:T(8,128)(2,1)} %get-tuple-element.232.dv, bf16[768,2304]{1,0:T(8,128)(2,1)} %weights.2, f32[464,768]{1,0:T(8,128)} %copy-done.1, ...), custom_call_target="tpu_custom_call" | custom-call | flops 1 | bytes 1 | tf_op jit(solution)/shard_map/radar/pallas_call | solution.py:586
  155.0 1.6 collective-permute-start.22
  157.0 4.6 %optic.3 = f32[512,768]{1,0:T(8,128)} custom-call(bf16[464,768]{1,0:T(8,128)(2,1)} %get-tuple-element.250.dk, bf16[464,768]{1,0:T(8,128)(2,1)} %get-tuple-element.251.dv, bf16[768,1536]{1,0:T(8,128)(2,1)} %weights.3), custom_call_target="tpu_custom_call" | custom-call | flops 1 | bytes 1 | tf_op jit(solution)/shard_map/optic/pallas_call | solution.py:554
  161.6 5.2 %collective-permute-done.22 = bf16[2,48,1536]{2,1,0:T(8,128)(2,1)S(1)} collective-permute-done((bf16[2,48,1536]{2,1,0:T(8,128)(2,1)S(1)}, bf16[2,48,1536]{2,1,0:T(8,128)(2,1)S(1)}, u32[]{:S(2)}, u32[]{:S(2)}) %collective-permute-start.22) | collective-permute-done | bytes 294944 | tf_op jit(solution)/shard_map/ppermute | solution.py:597
  166.8 4.2 %collective-permute-done.23 = bf16[2,96,768]{2,1,0:T(8,128)(2,1)S(1)} collective-permute-done((bf16[2,96,768]{2,1,0:T(8,128)(2,1)S(1)}, bf16[2,96,768]{2,1,0:T(8,128)(2,1)S(1)}, u32[]{:S(2)}, u32[]{:S(2)}) %collective-permute-start.23) | collective-permute-done | bytes 294944 | tf_op jit(solution)/shard_map/ppermute | solution.py:597
  171.6 1.4 collective-permute-start.25
  173.0 1.5 collective-permute-start.24
  175.7 1.4 collective-permute-done.24
  177.0 1.4 collective-permute-start.29
  178.5 3.1 %collective-permute-done.25 = bf16[2,48,1536]{2,1,0:T(8,128)(2,1)S(1)} collective-permute-done((bf16[2,48,1536]{2,1,0:T(8,128)(2,1)S(1)}, bf16[2,48,1536]{2,1,0:T(8,128)(2,1)S(1)}, u32[]{:S(2)}, u32[]{:S(2)}) %collective-permute-start.25) | collective-permute-done | bytes 294944 | tf_op jit(solution)/shard_map/ppermute | solution.py:597
  181.6 3.0 %collective-permute-start.30 = (bf16[2,48,1536]{2,1,0:T(8,128)(2,1)S(1)}, bf16[2,48,1536]{2,1,0:T(8,128)(2,1)S(1)}, u32[]{:S(2)}, u32[]{:S(2)}) collective-permute-start(bf16[2,48,1536]{2,1,0:T(8,128)(2,1)S(1)} %fusion.16), channel_id=1, source_target_pairs={{0,16},{1,17},{2,18},{3,19},{4,20},{5,21},{6,22},{7,23},{8,24},{9,... | collective-permute-start | bytes 884744 | tf_op jit(solution)/shard_map/ppermute | solution.py:597
  185.4 2.3 collective-permute-done.28
  187.7 3.2 %collective-permute-done.29 = bf16[192,768]{1,0:T(8,128)(2,1)} collective-permute-done((bf16[192,768]{1,0:T(8,128)(2,1)S(1)}, bf16[192,768]{1,0:T(8,128)(2,1)}, u32[]{:S(2)}, u32[]{:S(2)}) %collective-permute-start.29) | collective-permute-done | bytes 294944 | tf_op jit(solution)/shard_map/ppermute | solution.py:597
  190.9 2.6 %collective-permute-done.30 = bf16[2,48,1536]{2,1,0:T(8,128)(2,1)S(1)} collective-permute-done((bf16[2,48,1536]{2,1,0:T(8,128)(2,1)S(1)}, bf16[2,48,1536]{2,1,0:T(8,128)(2,1)S(1)}, u32[]{:S(2)}, u32[]{:S(2)}) %collective-permute-start.30) | collective-permute-done | bytes 294944 | tf_op jit(solution)/shard_map/ppermute | solution.py:597
  194.6 1.3 collective-permute-start.31
  195.9 2.0 collective-permute-start.33
  201.8 1.7 bitcast_convert_fusion
  203.5 1.7 collective-permute-done.32
  205.1 3.4 %collective-permute-done.33 = bf16[2,48,1536]{2,1,0:T(8,128)(2,1)S(1)} collective-permute-done((bf16[2,48,1536]{2,1,0:T(8,128)(2,1)S(1)}, bf16[2,48,1536]{2,1,0:T(8,128)(2,1)S(1)}, u32[]{:S(2)}, u32[]{:S(2)}) %collective-permute-start.33) | collective-permute-done | bytes 294944 | tf_op jit(solution)/shard_map/ppermute | solution.py:597
  208.5 9.9 %collective-permute-done.35 = bf16[2,48,1536]{2,1,0:T(8,128)(2,1)S(1)} collective-permute-done((bf16[2,48,1536]{2,1,0:T(8,128)(2,1)S(1)}, bf16[2,48,1536]{2,1,0:T(8,128)(2,1)S(1)}, u32[]{:S(2)}, u32[]{:S(2)}) %collective-permute-start.35) | collective-permute-done | bytes 294944 | tf_op jit(solution)/shard_map/ppermute | solution.py:597
  218.6 1.9 collective-permute-start.38
  222.9 1.2 bitcast_convert_fusion.1
  225.2 5.4 %collective-permute-done.37 = bf16[2,48,1536]{2,1,0:T(8,128)(2,1)S(1)} collective-permute-done((bf16[2,48,1536]{2,1,0:T(8,128)(2,1)S(1)}, bf16[2,48,1536]{2,1,0:T(8,128)(2,1)S(1)}, u32[]{:S(2)}, u32[]{:S(2)}) %collective-permute-start.37) | collective-permute-done | bytes 294944 | tf_op jit(solution)/shard_map/ppermute | solution.py:597
  231.1 6.7 %collective-permute-done.40 = bf16[2,96,768]{2,1,0:T(8,128)(2,1)S(1)} collective-permute-done((bf16[2,96,768]{2,1,0:T(8,128)(2,1)S(1)}, bf16[2,96,768]{2,1,0:T(8,128)(2,1)S(1)}, u32[]{:S(2)}, u32[]{:S(2)}) %collective-permute-start.40) | collective-permute-done | bytes 294944 | tf_op jit(solution)/shard_map/ppermute | solution.py:597
  237.8 4.2 %collective-permute-start.41 = (f32[16,768]{1,0:T(8,128)S(1)}, f32[16,768]{1,0:T(8,128)S(1)}, u32[]{:S(2)}, u32[]{:S(2)}) collective-permute-start(f32[16,768]{1,0:T(8,128)S(1)} %add.155), channel_id=1, source_target_pairs={{0,16},{1,17},{2,18},{3,19},{4,20},{5,21},{6,22},{7,23},{8,24},{9,... | collective-permute-start | bytes 147464 | tf_op jit(solution)/shard_map/ppermute | solution.py:597
  243.0 2.5 collective-permute-start.44
  246.3 1.7 convert_element_type.461
  248.7 3.6 %collective-permute-done.44 = bf16[2,48,1536]{2,1,0:T(8,128)(2,1)S(1)} collective-permute-done((bf16[2,48,1536]{2,1,0:T(8,128)(2,1)S(1)}, bf16[2,48,1536]{2,1,0:T(8,128)(2,1)S(1)}, u32[]{:S(2)}, u32[]{:S(2)}) %collective-permute-start.44) | collective-permute-done | bytes 294944 | tf_op jit(solution)/shard_map/ppermute | solution.py:597
  254.1 1.3 pad_maximum_fusion
  (170 shorter events, 29.7 us)
Async XLA Ops:
  18.0 17.0 %copy-start = (f32[464,768]{1,0:T(8,128)}, f32[464,768]{1,0:T(8,128)S(1)}, u32[]{:S(2)}) copy-start(f32[464,768]{1,0:T(8,128)S(1)} %get-tuple-element.164.res_in.res) | copy-start | bytes 4276228
  18.0 19.2 %collective-permute-start = (bf16[464,768]{1,0:T(8,128)(2,1)}, bf16[464,768]{1,0:T(8,128)(2,1)S(1)}, u32[]{:S(2)}, u32[]{:S(2)}) collective-permute-start(bf16[464,768]{1,0:T(8,128)(2,1)} %get-tuple-element.169.gf.refs_4_), channel_id=1, source_target_pairs={{0,4},{1,5},{2,6},{3,7},{4,0},{5,1},{6,2},{7,3},{8,12},{9,13},{10,... | collective-permute-start | bytes 2138120 | tf_op jit(solution)/shard_map/ppermute | solution.py:597
  21.1 16.2 %collective-permute-start.1 = (bf16[464,768]{1,0:T(8,128)(2,1)}, bf16[464,768]{1,0:T(8,128)(2,1)S(1)}, u32[]{:S(2)}, u32[]{:S(2)}) collective-permute-start(bf16[464,768]{1,0:T(8,128)(2,1)} %get-tuple-element.169.gf.refs_4_), channel_id=1, source_target_pairs={{0,1},{1,0},{2,3},{3,2},{4,5},{5,4},{6,7},{7,6},{8,9},{9,8},{10,11... | collective-permute-start | bytes 2138120 | tf_op jit(solution)/shard_map/ppermute | solution.py:597
  37.2 28.3 %copy-start.10 = (bf16[464,768]{1,0:T(8,128)(2,1)}, bf16[464,768]{1,0:T(8,128)(2,1)S(1)}, u32[]{:S(2)}) copy-start(bf16[464,768]{1,0:T(8,128)(2,1)S(1)} %collective-permute-done.refs_5_) | copy-start | bytes 2138116
  37.2 28.3 %copy-start.11 = (bf16[464,768]{1,0:T(8,128)(2,1)}, bf16[464,768]{1,0:T(8,128)(2,1)S(1)}, u32[]{:S(2)}) copy-start(bf16[464,768]{1,0:T(8,128)(2,1)S(1)} %collective-permute-done.1.refs_6_) | copy-start | bytes 2138116
  37.2 30.1 %collective-permute-start.2 = (bf16[464,768]{1,0:T(8,128)(2,1)S(1)}, bf16[464,768]{1,0:T(8,128)(2,1)S(1)}, u32[]{:S(2)}, u32[]{:S(2)}) collective-permute-start(bf16[464,768]{1,0:T(8,128)(2,1)S(1)} %get-tuple-element.172.n3.refs_0_), channel_id=1, source_target_pairs={{0,4},{1,5},{2,6},{3,7},{4,0},{5,1},{6,2},{7,3},{8,12},{9,13},{10,... | collective-permute-start | bytes 2138120 | tf_op jit(solution)/shard_map/ppermute | solution.py:597
  39.0 28.3 %collective-permute-start.3 = (bf16[464,768]{1,0:T(8,128)(2,1)S(1)}, bf16[464,768]{1,0:T(8,128)(2,1)S(1)}, u32[]{:S(2)}, u32[]{:S(2)}) collective-permute-start(bf16[464,768]{1,0:T(8,128)(2,1)S(1)} %get-tuple-element.172.n3.refs_0_), channel_id=1, source_target_pairs={{0,1},{1,0},{2,3},{3,2},{4,5},{5,4},{6,7},{7,6},{8,9},{9,8},{10,11... | collective-permute-start | bytes 2138120 | tf_op jit(solution)/shard_map/ppermute | solution.py:597
  39.0 28.3 %collective-permute-start.4 = (bf16[464,768]{1,0:T(8,128)(2,1)S(1)}, bf16[464,768]{1,0:T(8,128)(2,1)S(1)}, u32[]{:S(2)}, u32[]{:S(2)}) collective-permute-start(bf16[464,768]{1,0:T(8,128)(2,1)S(1)} %collective-permute-done.refs_5_), channel_id=1, source_target_pairs={{0,1},{1,0},{2,3},{3,2},{4,5},{5,4},{6,7},{7,6},{8,9},{9,8},{10,11... | collective-permute-start | bytes 2138120 | tf_op jit(solution)/shard_map/ppermute | solution.py:597
  67.3 2.2 collective-permute-start.5
  87.2 21.8 %collective-permute-start.6 = (bf16[2,192,768]{2,1,0:T(8,128)(2,1)S(1)}, bf16[2,192,768]{2,1,0:T(8,128)(2,1)S(1)}, u32[]{:S(2)}, u32[]{:S(2)}) collective-permute-start(bf16[2,192,768]{2,1,0:T(8,128)(2,1)S(1)} %slice_bitcast_fusion), channel_id=1, source_target_pairs={{0,2},{1,3},{2,0},{3,1},{4,6},{5,7},{6,4},{7,5},{8,10},{9,11},{10,... | collective-permute-start | bytes 1769480 | tf_op jit(solution)/shard_map/ppermute | solution.py:597
  88.8 20.2 %collective-permute-start.7 = (bf16[2,96,768]{2,1,0:T(8,128)(2,1)S(1)}, bf16[2,96,768]{2,1,0:T(8,128)(2,1)S(1)}, u32[]{:S(2)}, u32[]{:S(2)}) collective-permute-start(bf16[2,96,768]{2,1,0:T(8,128)(2,1)S(1)} %get-tuple-element.198), channel_id=1, source_target_pairs={{0,2},{1,3},{2,0},{3,1},{4,6},{5,7},{6,4},{7,5},{8,10},{9,11},{10,... | collective-permute-start | bytes 884744 | tf_op jit(solution)/shard_map/ppermute | solution.py:597
  109.2 10.8 %collective-permute-start.8 = (bf16[2,2,2,2,48,1536]{5,4,3,2,1,0:T(8,128)(2,1)S(1)}, bf16[2,2,2,2,48,1536]{5,4,3,2,1,0:T(8,128)(2,1)S(1)}, u32[]{:S(2)}, u32[]{:S(2)}) collective-permute-start(bf16[2,2,2,2,48,1536]{5,4,3,2,1,0:T(8,128)(2,1)S(1)} %get-tuple-element.204), channel_id=1, source_target_pairs={{0,1},{1,0},{2,3},{3,2},{4,5},{5,4},{6,7},{7,6},{8,9},{9,8},{10,11... | collective-permute-start | bytes 7077896 | tf_op jit(solution)/shard_map/ppermute | solution.py:597
  109.3 9.4 %collective-permute-start.9 = (bf16[2,96,768]{2,1,0:T(8,128)(2,1)S(1)}, bf16[2,96,768]{2,1,0:T(8,128)(2,1)S(1)}, u32[]{:S(2)}, u32[]{:S(2)}) collective-permute-start(bf16[2,96,768]{2,1,0:T(8,128)(2,1)S(1)} %get-tuple-element.205), channel_id=1, source_target_pairs={{0,2},{1,3},{2,0},{3,1},{4,6},{5,7},{6,4},{7,5},{8,10},{9,11},{10,... | collective-permute-start | bytes 884744 | tf_op jit(solution)/shard_map/ppermute | solution.py:597
  110.8 9.1 %collective-permute-start.10 = (bf16[192,768]{1,0:T(8,128)(2,1)S(1)}, bf16[192,768]{1,0:T(8,128)(2,1)S(1)}, u32[]{:S(2)}, u32[]{:S(2)}) collective-permute-start(bf16[192,768]{1,0:T(8,128)(2,1)S(1)} %slice_bitcast_fusion.18), channel_id=1, source_target_pairs={{0,8},{1,9},{2,10},{3,11},{4,12},{5,13},{6,14},{7,15},{8,0},{9,1},... | collective-permute-start | bytes 884744 | tf_op jit(solution)/shard_map/ppermute | solution.py:597
  120.5 20.3 %collective-permute-start.12 = (bf16[2,2,48,1536]{3,2,1,0:T(8,128)(2,1)S(1)}, bf16[2,2,48,1536]{3,2,1,0:T(8,128)(2,1)S(1)}, u32[]{:S(2)}, u32[]{:S(2)}) collective-permute-start(bf16[2,2,48,1536]{3,2,1,0:T(8,128)(2,1)S(1)} %get-tuple-element.221), channel_id=1, source_target_pairs={{0,4},{1,5},{2,6},{3,7},{4,0},{5,1},{6,2},{7,3},{8,12},{9,13},{10,... | collective-permute-start | bytes 1769480 | tf_op jit(solution)/shard_map/ppermute | solution.py:597
  121.0 19.7 %collective-permute-start.13 = (bf16[2,2,48,1536]{3,2,1,0:T(8,128)(2,1)S(1)}, bf16[2,2,48,1536]{3,2,1,0:T(8,128)(2,1)S(1)}, u32[]{:S(2)}, u32[]{:S(2)}) collective-permute-start(bf16[2,2,48,1536]{3,2,1,0:T(8,128)(2,1)S(1)} %get-tuple-element.222), channel_id=1, source_target_pairs={{0,2},{1,3},{2,0},{3,1},{4,6},{5,7},{6,4},{7,5},{8,10},{9,11},{10,... | collective-permute-start | bytes 1769480 | tf_op jit(solution)/shard_map/ppermute | solution.py:597
  121.4 19.3 %collective-permute-start.11 = (bf16[2,96,768]{2,1,0:T(8,128)(2,1)S(1)}, bf16[2,96,768]{2,1,0:T(8,128)(2,1)S(1)}, u32[]{:S(2)}, u32[]{:S(2)}) collective-permute-start(bf16[2,96,768]{2,1,0:T(8,128)(2,1)S(1)} %get-tuple-element.220), channel_id=1, source_target_pairs={{0,1},{1,0},{2,3},{3,2},{4,5},{5,4},{6,7},{7,6},{8,9},{9,8},{10,11... | collective-permute-start | bytes 884744 | tf_op jit(solution)/shard_map/ppermute | solution.py:597
  121.4 19.3 %collective-permute-start.14 = (bf16[192,768]{1,0:T(8,128)(2,1)S(1)}, bf16[192,768]{1,0:T(8,128)(2,1)S(1)}, u32[]{:S(2)}, u32[]{:S(2)}) collective-permute-start(bf16[192,768]{1,0:T(8,128)(2,1)S(1)} %fusion.21), channel_id=1, source_target_pairs={{0,16},{1,17},{2,18},{3,19},{4,20},{5,21},{6,22},{7,23},{8,24},{9,... | collective-permute-start | bytes 884744 | tf_op jit(solution)/shard_map/ppermute | solution.py:597
  141.4 11.9 %collective-permute-start.15 = (bf16[2,2,2,2,48,1536]{5,4,3,2,1,0:T(8,128)(2,1)S(1)}, bf16[2,2,2,2,48,1536]{5,4,3,2,1,0:T(8,128)(2,1)S(1)}, u32[]{:S(2)}, u32[]{:S(2)}) collective-permute-start(bf16[2,2,2,2,48,1536]{5,4,3,2,1,0:T(8,128)(2,1)S(1)} %get-tuple-element.239), channel_id=1, source_target_pairs={{0,1},{1,0},{2,3},{3,2},{4,5},{5,4},{6,7},{7,6},{8,9},{9,8},{10,11... | collective-permute-start | bytes 7077896 | tf_op jit(solution)/shard_map/ppermute | solution.py:597
  141.7 11.4 %collective-permute-start.16 = (bf16[2,48,1536]{2,1,0:T(8,128)(2,1)S(1)}, bf16[2,48,1536]{2,1,0:T(8,128)(2,1)S(1)}, u32[]{:S(2)}, u32[]{:S(2)}) collective-permute-start(bf16[2,48,1536]{2,1,0:T(8,128)(2,1)S(1)} %slice_bitcast_fusion.16), channel_id=1, source_target_pairs={{0,2},{1,3},{2,0},{3,1},{4,6},{5,7},{6,4},{7,5},{8,10},{9,11},{10,... | collective-permute-start | bytes 884744 | tf_op jit(solution)/shard_map/ppermute | solution.py:597
  143.2 9.9 %collective-permute-start.17 = (bf16[2,48,1536]{2,1,0:T(8,128)(2,1)S(1)}, bf16[2,48,1536]{2,1,0:T(8,128)(2,1)S(1)}, u32[]{:S(2)}, u32[]{:S(2)}) collective-permute-start(bf16[2,48,1536]{2,1,0:T(8,128)(2,1)S(1)} %slice_bitcast_fusion.15), channel_id=1, source_target_pairs={{0,4},{1,5},{2,6},{3,7},{4,0},{5,1},{6,2},{7,3},{8,12},{9,13},{10,... | collective-permute-start | bytes 884744 | tf_op jit(solution)/shard_map/ppermute | solution.py:597
  144.7 8.6 %collective-permute-start.18 = (bf16[2,96,768]{2,1,0:T(8,128)(2,1)S(1)}, bf16[2,96,768]{2,1,0:T(8,128)(2,1)S(1)}, u32[]{:S(2)}, u32[]{:S(2)}) collective-permute-start(bf16[2,96,768]{2,1,0:T(8,128)(2,1)S(1)} %fusion.33), channel_id=1, source_target_pairs={{0,8},{1,9},{2,10},{3,11},{4,12},{5,13},{6,14},{7,15},{8,0},{9,1},... | collective-permute-start | bytes 884744 | tf_op jit(solution)/shard_map/ppermute | solution.py:597
  153.9 17.0 %collective-permute-start.20 = (bf16[2,2,48,1536]{3,2,1,0:T(8,128)(2,1)S(1)}, bf16[2,2,48,1536]{3,2,1,0:T(8,128)(2,1)S(1)}, u32[]{:S(2)}, u32[]{:S(2)}) collective-permute-start(bf16[2,2,48,1536]{3,2,1,0:T(8,128)(2,1)S(1)} %get-tuple-element.253), channel_id=1, source_target_pairs={{0,4},{1,5},{2,6},{3,7},{4,0},{5,1},{6,2},{7,3},{8,12},{9,13},{10,... | collective-permute-start | bytes 1769480 | tf_op jit(solution)/shard_map/ppermute | solution.py:597
  154.5 16.4 %collective-permute-start.21 = (bf16[2,2,48,1536]{3,2,1,0:T(8,128)(2,1)S(1)}, bf16[2,2,48,1536]{3,2,1,0:T(8,128)(2,1)S(1)}, u32[]{:S(2)}, u32[]{:S(2)}) collective-permute-start(bf16[2,2,48,1536]{3,2,1,0:T(8,128)(2,1)S(1)} %get-tuple-element.254), channel_id=1, source_target_pairs={{0,2},{1,3},{2,0},{3,1},{4,6},{5,7},{6,4},{7,5},{8,10},{9,11},{10,... | collective-permute-start | bytes 1769480 | tf_op jit(solution)/shard_map/ppermute | solution.py:597
  155.0 11.7 %collective-permute-start.22 = (bf16[2,48,1536]{2,1,0:T(8,128)(2,1)S(1)}, bf16[2,48,1536]{2,1,0:T(8,128)(2,1)S(1)}, u32[]{:S(2)}, u32[]{:S(2)}) collective-permute-start(bf16[2,48,1536]{2,1,0:T(8,128)(2,1)S(1)} %fusion.31), channel_id=1, source_target_pairs={{0,8},{1,9},{2,10},{3,11},{4,12},{5,13},{6,14},{7,15},{8,0},{9,1},... | collective-permute-start | bytes 884744 | tf_op jit(solution)/shard_map/ppermute | solution.py:597
  156.6 14.3 %collective-permute-start.23 = (bf16[2,96,768]{2,1,0:T(8,128)(2,1)S(1)}, bf16[2,96,768]{2,1,0:T(8,128)(2,1)S(1)}, u32[]{:S(2)}, u32[]{:S(2)}) collective-permute-start(bf16[2,96,768]{2,1,0:T(8,128)(2,1)S(1)} %fusion.17), channel_id=1, source_target_pairs={{0,16},{1,17},{2,18},{3,19},{4,20},{5,21},{6,22},{7,23},{8,24},{9,... | collective-permute-start | bytes 884744 | tf_op jit(solution)/shard_map/ppermute | solution.py:597
  156.9 4.6 %collective-permute-start.19 = (f32[16,768]{1,0:T(8,128)S(1)}, f32[16,768]{1,0:T(8,128)S(1)}, u32[]{:S(2)}, u32[]{:S(2)}) collective-permute-start(f32[16,768]{1,0:T(8,128)S(1)} %get-tuple-element.252), channel_id=1, source_target_pairs={{0,1},{1,0},{2,3},{3,2},{4,5},{5,4},{6,7},{7,6},{8,9},{9,8},{10,11... | collective-permute-start | bytes 147464 | tf_op jit(solution)/shard_map/ppermute | solution.py:597
  171.6 10.1 %collective-permute-start.25 = (bf16[2,48,1536]{2,1,0:T(8,128)(2,1)S(1)}, bf16[2,48,1536]{2,1,0:T(8,128)(2,1)S(1)}, u32[]{:S(2)}, u32[]{:S(2)}) collective-permute-start(bf16[2,48,1536]{2,1,0:T(8,128)(2,1)S(1)} %slice_bitcast_fusion.12), channel_id=1, source_target_pairs={{0,4},{1,5},{2,6},{3,7},{4,0},{5,1},{6,2},{7,3},{8,12},{9,13},{10,... | collective-permute-start | bytes 884744 | tf_op jit(solution)/shard_map/ppermute | solution.py:597
  173.0 4.1 %collective-permute-start.24 = (f32[16,768]{1,0:T(8,128)S(1)}, f32[16,768]{1,0:T(8,128)S(1)}, u32[]{:S(2)}, u32[]{:S(2)}) collective-permute-start(f32[16,768]{1,0:T(8,128)S(1)} %add.141), channel_id=1, source_target_pairs={{0,2},{1,3},{2,0},{3,1},{4,6},{5,7},{6,4},{7,5},{8,10},{9,11},{10,... | collective-permute-start | bytes 147464 | tf_op jit(solution)/shard_map/ppermute | solution.py:597
  174.5 10.2 %collective-permute-start.26 = (bf16[2,48,1536]{2,1,0:T(8,128)(2,1)S(1)}, bf16[2,48,1536]{2,1,0:T(8,128)(2,1)S(1)}, u32[]{:S(2)}, u32[]{:S(2)}) collective-permute-start(bf16[2,48,1536]{2,1,0:T(8,128)(2,1)S(1)} %slice_bitcast_fusion.11), channel_id=1, source_target_pairs={{0,2},{1,3},{2,0},{3,1},{4,6},{5,7},{6,4},{7,5},{8,10},{9,11},{10,... | collective-permute-start | bytes 884744 | tf_op jit(solution)/shard_map/ppermute | solution.py:597
  175.0 10.4 %collective-permute-start.27 = (bf16[192,768]{1,0:T(8,128)(2,1)S(1)}, bf16[192,768]{1,0:T(8,128)(2,1)}, u32[]{:S(2)}, u32[]{:S(2)}) collective-permute-start(bf16[192,768]{1,0:T(8,128)(2,1)S(1)} %add_convert_fusion.11), channel_id=1, source_target_pairs={{0,8},{1,9},{2,10},{3,11},{4,12},{5,13},{6,14},{7,15},{8,0},{9,1},... | collective-permute-start | bytes 884744 | tf_op jit(solution)/shard_map/ppermute | solution.py:597
  175.0 12.7 %collective-permute-start.28 = (bf16[192,768]{1,0:T(8,128)(2,1)S(1)}, bf16[192,768]{1,0:T(8,128)(2,1)}, u32[]{:S(2)}, u32[]{:S(2)}) collective-permute-start(bf16[192,768]{1,0:T(8,128)(2,1)S(1)} %add_convert_fusion.11), channel_id=1, source_target_pairs={{0,4},{1,5},{2,6},{3,7},{4,0},{5,1},{6,2},{7,3},{8,12},{9,13},{10,... | collective-permute-start | bytes 884744 | tf_op jit(solution)/shard_map/ppermute | solution.py:597
  177.0 13.9 %collective-permute-start.29 = (bf16[192,768]{1,0:T(8,128)(2,1)S(1)}, bf16[192,768]{1,0:T(8,128)(2,1)}, u32[]{:S(2)}, u32[]{:S(2)}) collective-permute-start(bf16[192,768]{1,0:T(8,128)(2,1)S(1)} %add_convert_fusion.11), channel_id=1, source_target_pairs={{0,12},{1,13},{2,14},{3,15},{4,8},{5,9},{6,10},{7,11},{8,4},{9,5},... | collective-permute-start | bytes 884744 | tf_op jit(solution)/shard_map/ppermute | solution.py:597
  181.6 11.9 %collective-permute-start.30 = (bf16[2,48,1536]{2,1,0:T(8,128)(2,1)S(1)}, bf16[2,48,1536]{2,1,0:T(8,128)(2,1)S(1)}, u32[]{:S(2)}, u32[]{:S(2)}) collective-permute-start(bf16[2,48,1536]{2,1,0:T(8,128)(2,1)S(1)} %fusion.16), channel_id=1, source_target_pairs={{0,16},{1,17},{2,18},{3,19},{4,20},{5,21},{6,22},{7,23},{8,24},{9,... | collective-permute-start | bytes 884744 | tf_op jit(solution)/shard_map/ppermute | solution.py:597
  194.6 8.8 %collective-permute-start.31 = (f32[16,768]{1,0:T(8,128)S(1)}, f32[16,768]{1,0:T(8,128)S(1)}, u32[]{:S(2)}, u32[]{:S(2)}) collective-permute-start(f32[16,768]{1,0:T(8,128)S(1)} %add.148), channel_id=1, source_target_pairs={{0,4},{1,5},{2,6},{3,7},{4,0},{5,1},{6,2},{7,3},{8,12},{9,13},{10,... | collective-permute-start | bytes 147464 | tf_op jit(solution)/shard_map/ppermute | solution.py:597
  195.9 9.2 %collective-permute-start.32 = (bf16[2,48,1536]{2,1,0:T(8,128)(2,1)S(1)}, bf16[2,48,1536]{2,1,0:T(8,128)(2,1)S(1)}, u32[]{:S(2)}, u32[]{:S(2)}) collective-permute-start(bf16[2,48,1536]{2,1,0:T(8,128)(2,1)S(1)} %fusion.29), channel_id=1, source_target_pairs={{0,8},{1,9},{2,10},{3,11},{4,12},{5,13},{6,14},{7,15},{8,0},{9,1},... | collective-permute-start | bytes 884744 | tf_op jit(solution)/shard_map/ppermute | solution.py:597
  195.9 12.5 %collective-permute-start.33 = (bf16[2,48,1536]{2,1,0:T(8,128)(2,1)S(1)}, bf16[2,48,1536]{2,1,0:T(8,128)(2,1)S(1)}, u32[]{:S(2)}, u32[]{:S(2)}) collective-permute-start(bf16[2,48,1536]{2,1,0:T(8,128)(2,1)S(1)} %add_convert_fusion.10), channel_id=1, source_target_pairs={{0,8},{1,9},{2,10},{3,11},{4,12},{5,13},{6,14},{7,15},{8,0},{9,1},... | collective-permute-start | bytes 884744 | tf_op jit(solution)/shard_map/ppermute | solution.py:597
  198.0 10.5 %collective-permute-start.34 = (bf16[2,48,1536]{2,1,0:T(8,128)(2,1)S(1)}, bf16[2,48,1536]{2,1,0:T(8,128)(2,1)S(1)}, u32[]{:S(2)}, u32[]{:S(2)}) collective-permute-start(bf16[2,48,1536]{2,1,0:T(8,128)(2,1)S(1)} %add_convert_fusion.10), channel_id=1, source_target_pairs={{0,4},{1,5},{2,6},{3,7},{4,0},{5,1},{6,2},{7,3},{8,12},{9,13},{10,... | collective-permute-start | bytes 884744 | tf_op jit(solution)/shard_map/ppermute | solution.py:597
  198.7 19.6 %collective-permute-start.35 = (bf16[2,48,1536]{2,1,0:T(8,128)(2,1)S(1)}, bf16[2,48,1536]{2,1,0:T(8,128)(2,1)S(1)}, u32[]{:S(2)}, u32[]{:S(2)}) collective-permute-start(bf16[2,48,1536]{2,1,0:T(8,128)(2,1)S(1)} %add_convert_fusion.10), channel_id=1, source_target_pairs={{0,12},{1,13},{2,14},{3,15},{4,8},{5,9},{6,10},{7,11},{8,4},{9,5},... | collective-permute-start | bytes 884744 | tf_op jit(solution)/shard_map/ppermute | solution.py:597
  218.4 6.7 %collective-permute-start.36 = (f32[16,768]{1,0:T(8,128)S(1)}, f32[16,768]{1,0:T(8,128)S(1)}, u32[]{:S(2)}, u32[]{:S(2)}) collective-permute-start(f32[16,768]{1,0:T(8,128)S(1)} %add.152), channel_id=1, source_target_pairs={{0,8},{1,9},{2,10},{3,11},{4,12},{5,13},{6,14},{7,15},{8,0},{9,1},... | collective-permute-start | bytes 147464 | tf_op jit(solution)/shard_map/ppermute | solution.py:597
  218.5 12.1 %collective-permute-start.37 = (bf16[2,48,1536]{2,1,0:T(8,128)(2,1)S(1)}, bf16[2,48,1536]{2,1,0:T(8,128)(2,1)S(1)}, u32[]{:S(2)}, u32[]{:S(2)}) collective-permute-start(bf16[2,48,1536]{2,1,0:T(8,128)(2,1)S(1)} %fusion.13), channel_id=1, source_target_pairs={{0,16},{1,17},{2,18},{3,19},{4,20},{5,21},{6,22},{7,23},{8,24},{9,... | collective-permute-start | bytes 884744 | tf_op jit(solution)/shard_map/ppermute | solution.py:597
  218.6 12.4 %collective-permute-start.38 = (bf16[2,96,768]{2,1,0:T(8,128)(2,1)S(1)}, bf16[2,96,768]{2,1,0:T(8,128)(2,1)S(1)}, u32[]{:S(2)}, u32[]{:S(2)}) collective-permute-start(bf16[2,96,768]{2,1,0:T(8,128)(2,1)S(1)} %add_convert_fusion.9), channel_id=1, source_target_pairs={{0,8},{1,9},{2,10},{3,11},{4,12},{5,13},{6,14},{7,15},{8,0},{9,1},... | collective-permute-start | bytes 884744 | tf_op jit(solution)/shard_map/ppermute | solution.py:597
  220.5 10.5 %collective-permute-start.39 = (bf16[2,96,768]{2,1,0:T(8,128)(2,1)S(1)}, bf16[2,96,768]{2,1,0:T(8,128)(2,1)S(1)}, u32[]{:S(2)}, u32[]{:S(2)}) collective-permute-start(bf16[2,96,768]{2,1,0:T(8,128)(2,1)S(1)} %add_convert_fusion.9), channel_id=1, source_target_pairs={{0,4},{1,5},{2,6},{3,7},{4,0},{5,1},{6,2},{7,3},{8,12},{9,13},{10,... | collective-permute-start | bytes 884744 | tf_op jit(solution)/shard_map/ppermute | solution.py:597
  221.6 16.2 %collective-permute-start.40 = (bf16[2,96,768]{2,1,0:T(8,128)(2,1)S(1)}, bf16[2,96,768]{2,1,0:T(8,128)(2,1)S(1)}, u32[]{:S(2)}, u32[]{:S(2)}) collective-permute-start(bf16[2,96,768]{2,1,0:T(8,128)(2,1)S(1)} %add_convert_fusion.9), channel_id=1, source_target_pairs={{0,12},{1,13},{2,14},{3,15},{4,8},{5,9},{6,10},{7,11},{8,4},{9,5},... | collective-permute-start | bytes 884744 | tf_op jit(solution)/shard_map/ppermute | solution.py:597
  237.8 10.1 %collective-permute-start.41 = (f32[16,768]{1,0:T(8,128)S(1)}, f32[16,768]{1,0:T(8,128)S(1)}, u32[]{:S(2)}, u32[]{:S(2)}) collective-permute-start(f32[16,768]{1,0:T(8,128)S(1)} %add.155), channel_id=1, source_target_pairs={{0,16},{1,17},{2,18},{3,19},{4,20},{5,21},{6,22},{7,23},{8,24},{9,... | collective-permute-start | bytes 147464 | tf_op jit(solution)/shard_map/ppermute | solution.py:597
  242.0 6.7 %collective-permute-start.42 = (bf16[2,48,1536]{2,1,0:T(8,128)(2,1)S(1)}, bf16[2,48,1536]{2,1,0:T(8,128)(2,1)S(1)}, u32[]{:S(2)}, u32[]{:S(2)}) collective-permute-start(bf16[2,48,1536]{2,1,0:T(8,128)(2,1)S(1)} %add_convert_fusion.8), channel_id=1, source_target_pairs={{0,8},{1,9},{2,10},{3,11},{4,12},{5,13},{6,14},{7,15},{8,0},{9,1},... | collective-permute-start | bytes 884744 | tf_op jit(solution)/shard_map/ppermute | solution.py:597
  242.0 6.7 %collective-permute-start.43 = (bf16[2,48,1536]{2,1,0:T(8,128)(2,1)S(1)}, bf16[2,48,1536]{2,1,0:T(8,128)(2,1)S(1)}, u32[]{:S(2)}, u32[]{:S(2)}) collective-permute-start(bf16[2,48,1536]{2,1,0:T(8,128)(2,1)S(1)} %add_convert_fusion.8), channel_id=1, source_target_pairs={{0,4},{1,5},{2,6},{3,7},{4,0},{5,1},{6,2},{7,3},{8,12},{9,13},{10,... | collective-permute-start | bytes 884744 | tf_op jit(solution)/shard_map/ppermute | solution.py:597
  243.0 9.3 %collective-permute-start.44 = (bf16[2,48,1536]{2,1,0:T(8,128)(2,1)S(1)}, bf16[2,48,1536]{2,1,0:T(8,128)(2,1)S(1)}, u32[]{:S(2)}, u32[]{:S(2)}) collective-permute-start(bf16[2,48,1536]{2,1,0:T(8,128)(2,1)S(1)} %add_convert_fusion.8), channel_id=1, source_target_pairs={{0,12},{1,13},{2,14},{3,15},{4,8},{5,9},{6,10},{7,11},{8,4},{9,5},... | collective-permute-start | bytes 884744 | tf_op jit(solution)/shard_map/ppermute | solution.py:597
  (15 other events, 42.6 us)

commit v3 on v2

--- a/solution.py
+++ b/solution.py
@@ -99,12 +99,12 @@
     return values * below, below + values * bell * (1.0 / math.sqrt(2.0 * math.pi))
 
 
+def smem():
+    return pl.BlockSpec(memory_space=pltpu.SMEM)
+
+
 def whole(shape):
     return pl.BlockSpec(shape, lambda *_: (0,) * len(shape))
-
-
-def smem():
-    return pl.BlockSpec(memory_space=pltpu.SMEM)
 
 
 def cols(rows, width, first=0):
@@ -140,8 +140,15 @@
     return jnp.concatenate(outs, axis=0).astype(BF16).T
 
 
+def slope_of(group, h):
+    found = 0.0
+    for g in range(HEADS // QUAD):
+        found = jnp.where(group == g, 2.0 ** (-8.0 * (g * QUAD + h + 1) / HEADS), found)
+    return found
+
+
 def self_forward_kernel(
-    lens, slopes, radar, cot, gains, shifts, biases, wq, wk, wv, wo,
+    lens, radar, cot, gains, shifts, biases, wq, wk, wv, wo,
     n1, q_out, k_out, v_out, probs, att_out, resid, n2, gf, dist,
 ):
     j = pl.program_id(0)
@@ -167,7 +174,7 @@
     k_out[...] = k
     v_out[...] = v
     att = attend_quad(
-        q, k, v, lambda s, h: s - slopes[j * QUAD + h] * dist[...], probs
+        q, k, v, lambda s, h: s - slope_of(j, h) * dist[...], probs
     )
     att_out[...] = att
     resid[...] += dot_nn(att, wo[...])
@@ -218,7 +225,7 @@
     return [pltpu.with_memory_space_constraint(a, pltpu.HBM) for a in arrays]
 
 
-def self_forward(rows, lens, slopes, radar, cot, gains, shifts, biases, w_qkv, w_out):
+def self_forward(rows, lens, radar, cot, gains, shifts, biases, w_qkv, w_out):
     d = radar.shape[1]
     wide = QUAD * HDIM
     steps = d // wide
@@ -226,7 +233,7 @@
         self_forward_kernel,
         grid=(steps,),
         in_specs=[
-            smem(), smem(), whole((rows, d)), whole((rows, d)),
+            smem(), whole((rows, d)), whole((rows, d)),
             *[whole((3, d))] * 3,
             cols(d, wide), cols(d, wide, steps), cols(d, wide, 2 * steps), rowblk(wide, d),
         ],
@@ -243,7 +250,7 @@
         compiler_params=params(),
         cost_estimate=cost(8 * rows * d * d + 12 * HEADS * rows * rows * 128, 8 * d * d + HEADS * rows * rows * 2),
         name="self_forward",
-    )(lens, slopes, *far(radar, cot, gains, shifts, biases),
+    )(lens, *far(radar, cot, gains, shifts, biases),
       *far(w_qkv, w_qkv, w_qkv, w_out))
 
 
@@ -272,8 +279,7 @@
         compiler_params=params(),
         cost_estimate=cost(8 * rows * d * d + 12 * HEADS * rows * rows * 128, 8 * d * d + HEADS * rows * rows * 2),
         name="cross_forward",
-    )(lens, res_in, n_in, *far(optic, gains, shifts, biases),
-      *far(w_q, w_kv, w_kv, w_out))
+    )(lens, res_in, n_in, optic, gains, shifts, biases, w_q, w_kv, w_kv, w_out)
 
 
 def hidden_kernel(res2, n3, gf, gains, hb, win, wout, act_out, grad_two, vectors, acc):
@@ -312,12 +318,12 @@
             whole((3, d)), cols(1, chunk), cols(d, chunk), rowblk(chunk, d),
         ],
         out_specs=[cols(rows, chunk), whole((rows, d)), whole((8, d))],
-        out_shape=[held(rows, ff), shaped(rows, d, dtype=F32), shaped(8, d, dtype=F32)],
+        out_shape=[held(rows, ff), held(rows, d, dtype=F32), held(8, d, dtype=F32)],
         scratch_shapes=[pltpu.VMEM((rows, d), F32)],
         compiler_params=params(),
         cost_estimate=cost(6 * rows * d * ff, 4 * d * ff),
         name="hidden",
-    )(*far(res2, n3, gf, gains, hb, win, wout))
+    )(res2, n3, *far(gf), gains, hb, win, wout)
 
 
 def output_kernel(lens, act, res2, biases, wout, y_out, acc):
@@ -351,7 +357,7 @@
         compiler_params=params(),
         cost_estimate=cost(2 * rows * d * ff, 2 * d * ff),
         name="output",
-    )(lens, *far(act, res2, biases, wout))
+    )(lens, act, res2, biases, wout)
 
 
 def hidden_grads_kernel(blocks, meta, *refs):
@@ -426,7 +432,12 @@
                 at = y * 8 + x * 2 + p
                 low = grad[at * part : (at + 1) * part]
                 high = grad[(at + 4) * part : (at + 5) * part]
-                lead, other = (x ^ at_x, y ^ at_y) if bucket == 0 else (y ^ at_y, x ^ at_x)
+                ways = (x ^ at_x, y ^ at_y)
+                if isinstance(bucket, int):
+                    lead, other = ways[bucket], ways[1 - bucket]
+                else:
+                    lead = jnp.where(bucket == 0, ways[0], ways[1])
+                    other = jnp.where(bucket == 0, ways[1], ways[0])
                 to = (bucket, lead, other, p ^ at_p, slice(None), spot)
                 keep[to] = jnp.where(first, low, high)
                 send[to] = jnp.where(first, high, low)
@@ -454,11 +465,14 @@
     return dq, (dk * scale).astype(BF16), dv.astype(BF16)
 
 
-def back_kernel(own_keys, grad_in, res, xq, xkv, q, k, v, att, att_all, probs, gains, wo, wq, *refs):
-    refs = list(refs)
-    keep, send, dk_out, dv_out, vectors = [refs.pop(0) for _ in range(5)]
-    last_out = refs.pop(0)
-    low, xq_t, xkv_t, acc = refs
+def aligned(first, width):
+    return pl.ds(pl.multiple_of(first, 128), width)
+
+
+def cross_back_kernel(
+    grad_in, res, xq, xkv, q, k, v, att, att_all, probs, gains, wo, wq, att_self,
+    keep, send, dk_out, dv_out, vectors, grad_out, low, xq_t, xkv_t, acc,
+):
     i = pl.program_id(0)
     d = xq.shape[1]
     wide = q.shape[1]
@@ -467,66 +481,111 @@
     def _():
         low[...] = grad_in[...].astype(BF16)
         xq_t[...] = xq[...].T
-        if not own_keys:
-            xkv_t[...] = xkv[...].T
-            acc[...] = jnp.zeros_like(acc)
-        vectors[0:1] = jnp.sum(low[...].astype(F32), axis=0, keepdims=True)
-        vectors[1:8] = jnp.zeros((7, d), F32)
+        xkv_t[...] = xkv[...].T
+        acc[...] = jnp.zeros_like(acc)
         place(keep, send, 0, dot_nn(att_all[...].T, low[...]).astype(BF16), slice(0, d))
 
     g_att = dot_nt(low[...], wo[...]).astype(BF16)
     dq, dk, dv = quad_back(q[...], k[...], v[...], att[...], g_att, probs)
     dk_out[...] = dk
     dv_out[...] = dv
-    source_t = xq_t if own_keys else xkv_t
-    near = pl.ds(pl.multiple_of(i * wide, wide), wide)
-    past = pl.ds(pl.multiple_of(d + i * wide, wide), wide)
-    place(keep, send, 0, dot_nn(xq_t[...], dq).astype(BF16), past)
-    place(keep, send, 1, dot_nn(source_t[...], dk).astype(BF16), near)
-    place(keep, send, 1, dot_nn(source_t[...], dv).astype(BF16), past)
-    if own_keys:
-        last_out[...] = dq
-    else:
-        acc[...] += dot_nt(dq, wq[...])
-
-        @pl.when(i == pl.num_programs(0) - 1)
-        def _():
-            part, g_gain, g_shift = norm_back(res[...], gains[1:2], acc[...])
-            last_out[...] = grad_in[...] + part
-            vectors[1:2] = g_gain
-            vectors[2:3] = g_shift
-
-
-def back(own_keys, rows, grad_in, res, xq, xkv, q, k, v, att, probs, gains, wo, wq):
+    place(keep, send, 0, dot_nn(xq_t[...], dq).astype(BF16), aligned(d + i * wide, wide))
+    place(keep, send, 1, dot_nn(xkv_t[...], dk).astype(BF16), aligned(i * wide, wide))
+    place(keep, send, 1, dot_nn(xkv_t[...], dv).astype(BF16), aligned(d + i * wide, wide))
+    acc[...] += dot_nt(dq, wq[...])
+
+    @pl.when(i == pl.num_programs(0) - 1)
+    def _():
+        part, g_gain, g_shift = norm_back(res[...], gains[1:2], acc[...])
+        grad = grad_in[...] + part
+        grad_out[...] = grad
+        vectors[0:1] = jnp.sum(low[...].astype(F32), axis=0, keepdims=True)
+        vectors[1:2] = g_gain
+        vectors[2:3] = g_shift
+        grad_low = grad.astype(BF16)
+        vectors[3:4] = jnp.sum(grad_low.astype(F32), axis=0, keepdims=True)
+        vectors[4:8] = jnp.zeros((4, d), F32)
+        out = dot_nn(att_self[...].T, grad_low).astype(BF16)
+        place(keep, send, 0, out[:, : d // 2], slice(2 * d, 2 * d + d // 2))
+        place(keep, send, 1, out[:, d // 2 :], slice(2 * d, 2 * d + d // 2))
+
+
+def self_back_kernel(
+    grad_in, xq, q, k, v, att, probs, wo, keep, send, dk_out, dv_out, dq_out, low, xq_t,
+):
+    i = pl.program_id(0)
+    d = xq.shape[1]
+    wide = q.shape[1]
+
+    @pl.when(i == 0)
+    def _():
+        low[...] = grad_in[...].astype(BF16)
+        xq_t[...] = xq[...].T
+
+    g_att = dot_nt(low[...], wo[...]).astype(BF16)
+    dq, dk, dv = quad_back(q[...], k[...], v[...], att[...], g_att, probs)
+    dq_out[...] = dq
+    dk_out[...] = dk
+    dv_out[...] = dv
+    place(keep, send, 0, dot_nn(xq_t[...], dq).astype(BF16), aligned(i * wide, wide))
+    place(keep, send, 1, dot_nn(xq_t[...], dv).astype(BF16), aligned(i * wide, wide))
+    keys = dot_nn(xq_t[...], dk).astype(BF16)
+    half = wide // 2
+    for t in range(2):
+        piece = 2 * i + t
+        bucket = jnp.where(piece * half < d // 2, 0, 1)
+        at = d + piece * half - bucket * (d // 2)
+        place(keep, send, bucket, keys[:, t * half : (t + 1) * half], aligned(at, half))
+
+
+def cross_back(rows, grad_in, res, xq, xkv, q, k, v, att, probs, gains, wo, wq, att_self):
     d = xq.shape[1]
     wide = QUAD * HDIM
-    halves = (2, 2, 2, 2, d // 16, 2 * d)
+    halves = (2, 2, 2, 2, d // 16, 2 * d + d // 2)
     at = cols(rows, wide)
     full = whole((rows, d))
-    if own_keys:
-        res = gains
     return pl.pallas_call(
-        functools.partial(back_kernel, own_keys),
+        cross_back_kernel,
         grid=(d // wide,),
         in_specs=[
-            full, whole(res.shape), full, full, at, at, at, at, full,
+            full, full, full, full, at, at, at, at, full,
             pl.BlockSpec((QUAD, rows, rows), lambda i: (i, 0, 0)),
-            whole((3, d)), rowblk(wide, d), cols(d, wide),
-        ],
-        out_specs=[*[whole(halves)] * 2, at, at, whole((8, d)), at if own_keys else full],
+            whole((3, d)), rowblk(wide, d), cols(d, wide), full,
+        ],
+        out_specs=[*[whole(halves)] * 2, at, at, whole((8, d)), full],
         out_shape=[
-            *[shaped(*halves)] * 2, held(rows, d), held(rows, d), shaped(8, d, dtype=F32),
-            held(rows, d) if own_keys else shaped(rows, d, dtype=F32),
+            *[shaped(*halves)] * 2, held(rows, d), held(rows, d), held(8, d, dtype=F32), held(rows, d, dtype=F32),
         ],
         scratch_shapes=[
-            pltpu.VMEM((rows, d), BF16), pltpu.VMEM((d, rows), BF16),
-            pltpu.VMEM((16, 128) if own_keys else (d, rows), BF16),
-            pltpu.VMEM((8, 128) if own_keys else (rows, d), F32),
+            pltpu.VMEM((rows, d), BF16), pltpu.VMEM((d, rows), BF16), pltpu.VMEM((d, rows), BF16),
+            pltpu.VMEM((rows, d), F32),
         ],
         compiler_params=params(),
         cost_estimate=cost(18 * rows * d * d + 24 * HEADS * rows * rows * 128, 16 * d * d),
-        name="self_back" if own_keys else "cross_back",
-    )(*far(grad_in, res, xq, xkv, q, k, v, att, att, probs, gains, wo, wq))
+        name="cross_back",
+    )(grad_in, res, xq, xkv, q, k, v, att, att, *far(probs), gains, wo, wq, att_self)
+
+
+def self_back(rows, grad_in, xq, q, k, v, att, probs, wo):
+    d = xq.shape[1]
+    wide = QUAD * HDIM
+    halves = (2, 2, 2, 2, d // 16, d + d // 2)
+    at = cols(rows, wide)
+    full = whole((rows, d))
+    return pl.pallas_call(
+        self_back_kernel,
+        grid=(d // wide,),
+        in_specs=[
+            full, full, at, at, at, at,
+            pl.BlockSpec((QUAD, rows, rows), lambda i: (i, 0, 0)), rowblk(wide, d),
+        ],
+        out_specs=[*[whole(halves)] * 2, at, at, at],
+        out_shape=[*[shaped(*halves)] * 2, held(rows, d), held(rows, d), held(rows, d)],
+        scratch_shapes=[pltpu.VMEM((rows, d), BF16), pltpu.VMEM((d, rows), BF16)],
+        compiler_params=params(),
+        cost_estimate=cost(18 * rows * d * d + 24 * HEADS * rows * rows * 128, 16 * d * d),
+        name="self_back",
+    )(grad_in, xq, q, k, v, att, *far(probs), wo)
 
 
 def through(parts, weights):
@@ -560,10 +619,10 @@
         compiler_params=params(),
         cost_estimate=cost(4 * rows * d * d, 4 * d * d),
         name="optic",
-    )(*far(dk, dv, weights))
-
-
-def radar_kernel(dq, dk, dv, weights, grad_in, radar, gains, hidden_vec, cross_vec, self_vec, out, vectors):
+    )(*far(dk, dv), weights)
+
+
+def radar_kernel(dq, dk, dv, weights, grad_in, radar, gains, hidden_vec, cross_vec, out, vectors):
     total = through([dq, dk, dv], weights)
     part, g_gain, g_shift = norm_back(radar[...].astype(F32), gains[0:1], total)
     store_padded(out, grad_in[...] + part)
@@ -573,7 +632,7 @@
     vectors[3:4] = g_shift
     vectors[4:5] = cross_vec[2:3]
     vectors[5:6] = hidden_vec[5:6]
-    vectors[6:7] = self_vec[0:1]
+    vectors[6:7] = cross_vec[3:4]
     vectors[7:8] = cross_vec[0:1]
     vectors[8:9] = hidden_vec[6:7]
     vectors[9:13] = hidden_vec[0:4]
@@ -586,13 +645,13 @@
     return pl.pallas_call(
         radar_kernel,
         grid=(1,),
-        in_specs=[full, full, full, whole(weights.shape), full, full, whole((3, d)), *[whole((8, d))] * 3],
+        in_specs=[full, full, full, whole(weights.shape), full, full, whole((3, d)), *[whole((8, d))] * 2],
         out_specs=[whole((local_rows, d)), whole((16, d))],
         out_shape=[held(local_rows, d, dtype=F32), shaped(16, d, dtype=F32)],
         compiler_params=params(),
         cost_estimate=cost(6 * rows * d * d, 6 * d * d),
         name="radar",
-    )(*far(dq, dk, dv, weights, grad_in, tokens, gains, *vectors))
+    )(dq, dk, dv, weights, grad_in, tokens, gains, *vectors)
 def hop(values, perm):
     return lax.ppermute(values, ("grp", "hd"), perm)
 
@@ -636,12 +695,13 @@
 MOVES = {
     "C": ACROSS_CORE, "Y": ACROSS_Y, "Z": ACROSS_Y, "X": ACROSS_X, "P": ACROSS_P, "Q": ACROSS_Q,
     "A": ACROSS_P, "G": ACROSS_X, "D": ACROSS_XP, "W": ACROSS_Y, "V": ACROSS_X,
+    "B": ACROSS_P, "H": ACROSS_X,
 }
 
 
 class Flow:
-    def __init__(self, value):
-        self.value, self.ends = value, {}
+    def __init__(self, value, at_x, at_p):
+        self.value, self.ends, self.at_x, self.at_p = value, {}, at_x, at_p
 
     def operand(self, stage):
         return self.value[1] if stage in ("Y", "P") else self.value
@@ -651,15 +711,19 @@
             self.value = add(self.value[0], got)
         elif stage == "Q":
             self.value = add(self.value, got)
+        elif stage == "B":
+            self.value = jnp.stack(in_order(self.at_p, self.value, got))
         else:
             self.ends[stage] = got
 
-    def together(self, at_x, at_p):
+    def together(self):
+        if "H" in self.ends:
+            return in_order(self.at_x, self.value, self.ends["H"])
         rows = [
-            in_order(at_p, self.value, self.ends["A"]),
-            in_order(at_p, self.ends["G"], self.ends["D"]),
+            jnp.stack(in_order(self.at_p, self.value, self.ends["A"])),
+            jnp.stack(in_order(self.at_p, self.ends["G"], self.ends["D"])),
         ]
-        return in_order(at_x, jnp.stack(rows[0]), jnp.stack(rows[1]))
+        return in_order(self.at_x, *rows)
 
 
 class InFlow(Flow):
@@ -684,8 +748,8 @@
 
 
 class RowFlow(Flow):
-    def __init__(self, keep, send):
-        super().__init__(None)
+    def __init__(self, keep, send, at_x, at_p):
+        super().__init__(None, at_x, at_p)
         self.keep, self.send, self.parts = keep, send, None
 
     def operand(self, stage):
@@ -763,11 +827,10 @@
     at_y, at_c, at_z, at_x = at_hd // 2, at_hd % 2, at_grp // 2, at_grp % 2
     at_p = at_z % 2
     rows = rows_in_use(local_rows, tile_lengths.shape[2])
-    slopes = jnp.asarray([2.0 ** (-8.0 * (h + 1) / HEADS) for h in range(HEADS)], F32)
     hb = hidden_bias[None]
 
     n1, q1, k1, v1, p1, att1, res1, n2, gf = self_forward(
-        rows, tile_lengths, slopes, radar_tokens, cotangent, norm_gains, norm_shifts, proj_biases, self_qkv, self_out
+        rows, tile_lengths, radar_tokens, cotangent, norm_gains, norm_shifts, proj_biases, self_qkv, self_out
     )
     if known:
         n2, gf = tie([n2, gf])
@@ -785,17 +848,15 @@
     act, grad_two, hidden_vec = hidden(rows, res2, n3, gf, norm_gains, hb, hidden_in, hidden_out)
 
     def cross_step(grad):
-        return back(
-            False, rows, grad, res1, n2, optic_tokens, q2, k2, v2, att2, p2, norm_gains, cross_out, cross_query
+        return cross_back(
+            rows, grad, res1, n2, optic_tokens, q2, k2, v2, att2, p2, norm_gains, cross_out, cross_query, att1
         )
 
     def self_step(grad):
-        return back(True, rows, grad, None, n1, n1, q1, k1, v1, att1, p1, norm_gains, self_out, self_qkv)
+        return self_back(rows, grad, n1, q1, k1, v1, att1, p1, self_out)
 
     def radar_step(dq, grad):
-        return radar(
-            local_rows, dq, dk1, dv1, self_qkv, grad, radar_tokens, norm_gains, [hidden_vec, cross_vec, self_vec]
-        )
+        return radar(local_rows, dq, dk1, dv1, self_qkv, grad, radar_tokens, norm_gains, [hidden_vec, cross_vec])
 
     if known:
         meta = jnp.stack([at_y, at_c, at_x, at_p]).astype(jnp.int32)
@@ -806,41 +867,41 @@
         )
         plan = Plan()
         grad_two, dwin, dwout = tie([grad_two, dwin, dwout])
-        plan.flows["o"], plan.flows["n"] = Flow(dwout), InFlow(dwin)
+        plan.flows["o"], plan.flows["n"] = Flow(dwout, at_x, at_p), InFlow(dwin, at_x, at_p)
 
         grad_two = plan.begin(grad_two, "oY", "nY")
         keep, send, dk2, dv2, cross_vec, grad_one = cross_step(grad_two)
         act = plan.end(tie([act, grad_one])[0], "oY", "nY")
-        plan.flows["a"] = RowFlow(keep, send)
+        plan.flows["a"] = RowFlow(keep, send, at_x, at_p)
 
         act = plan.begin(act, "aC", "nZ", "oP")
         layer_output = output(rows, local_rows, tile_lengths, act, res2, proj_biases, hidden_out)
         grad_one = plan.end(tie([grad_one, layer_output])[0], "aC", "nZ", "oP")
 
-        grad_one = plan.begin(grad_one, "nC", "aX", "aW", "oQ")
-        keep, send, dk1, dv1, self_vec, dq1 = self_step(grad_one)
-        dq1 = plan.end(dq1, "nC", "aX", "aW", "oQ")
-        plan.flows["c"] = RowFlow(keep, send)
-
-        dq1 = plan.begin(dq1, "cC", "aY", "aV", "nP")
+        grad_one = plan.begin(grad_one, "oQ", "aX", "aW", "nC")
+        keep, send, dk1, dv1, dq1 = self_step(grad_one)
+        dq1 = plan.end(dq1, "oQ", "aX", "aW", "nC")
+        plan.flows["c"] = RowFlow(keep, send, at_x, at_p)
+
+        dq1 = plan.begin(dq1, "cC", "nP", "oB", "aY", "aV")
         radar_grad, small = radar_step(dq1, grad_one)
-        dk2 = plan.end(tie([dk2, radar_grad])[0], "cC", "aY", "aV", "nP")
-        plan.flows["s"] = Vectors(small)
-
-        dk2 = plan.begin(dk2, "sC", "cX", "cW", "aP", "nQ")
+        dk2 = plan.end(tie([dk2, radar_grad])[0], "cC", "nP", "oB", "aY", "aV")
+        plan.flows["s"] = Vectors(small, at_x, at_p)
+
+        dk2 = plan.begin(dk2, "nQ", "cX", "cW", "aP", "sC")
         optic_grad = optic(local_rows, dk2, dv2, cross_keyval)
-        gate = plan.end(optic_grad, "sC", "cX", "cW", "aP", "nQ")
+        gate = plan.end(optic_grad, "nQ", "cX", "cW", "aP", "sC")
 
         for stages in (
-            ("sY", "cV", "cY", "oA", "oG", "oD", "aQ"),
-            ("sX", "cP", "aA", "aG", "aD"),
-            ("sP", "cQ", "nA", "nG", "nD"),
-            ("sQ", "cA", "cG", "cD"),
+            ("cV", "aQ", "oH", "cY", "nB", "sY"),
+            ("cP", "nH", "aB", "sX"),
+            ("cQ", "aH", "sP"),
+            ("cG", "cD", "cA", "sQ"),
         ):
             gate = plan.end(plan.begin(gate, *stages), *stages)
         optic_grad = gate
 
-        done = {name: plan.flows[name].together(at_x, at_p) for name in "onac"}
+        done = {name: plan.flows[name].together() for name in "onac"}
         out_part = jnp.stack(done["o"]).reshape(-1, d).astype(F32)
         slices = [in_order(at_c, v[:, 0], v[:, 1]) for v in done["n"]]
         half = ff // 8
@@ -852,7 +913,7 @@
             axis=1,
         ).astype(F32)
         (cross_a, cross_b), (self_a, self_b) = [
-            [jnp.stack([v[:, i] for v in done[name]]).reshape(-1, 2 * d).astype(F32) for i in range(2)] for name in "ac"
+            [jnp.stack([v[:, i] for v in done[name]]).reshape(d // 4, -1).astype(F32) for i in range(2)] for name in "ac"
         ]
         small = plan.flows["s"].value
     else:
@@ -866,7 +927,7 @@
         in_part = summed_anywhere(jnp.stack(into, axis=2).reshape(d, ff))
         out_part = summed_anywhere(jnp.stack(out, axis=1).reshape(ff, d))
         cross_keep, cross_send, dk2, dv2, cross_vec, grad_one = cross_step(grad_two)
-        self_keep, self_send, dk1, dv1, self_vec, dq1 = self_step(grad_one)
+        self_keep, self_send, dk1, dv1, dq1 = self_step(grad_one)
         radar_grad, small = radar_step(dq1, grad_one)
         optic_grad = optic(local_rows, dk2, dv2, cross_keyval)
         layer_output = output(rows, local_rows, tile_lengths, act, res2, proj_biases, hidden_out)
@@ -880,10 +941,10 @@
         layer_output,
         radar_grad,
         optic_grad,
-        jnp.concatenate([self_a[:, d:], self_b], axis=1),
-        self_a[:, :d],
-        cross_a[:, d:],
-        cross_b,
+        jnp.concatenate([self_a, self_b[:, d:], self_b[:, :d]], axis=1),
+        jnp.concatenate([cross_a[:, 2 * d :], cross_b[:, 2 * d :]], axis=1),
+        cross_a[:, d : 2 * d],
+        cross_b[:, : 2 * d],
         cross_a[:, :d],
         in_part,
         out_part,

time: 258 us -> 254 us (0.984)
  Pallas kernels: 125 us -> 114 us
  other arithmetic: 13.5 us -> 18.8 us
  starting transfers between devices: 47.2 us -> 44.6 us
    convert_element_type x13, other arithmetic: 2.22 us -> 6.01 us  [add(): return total.astype(terms[0].dtype)]
    pallas_call x3, Pallas kernels: 50.4 us -> 47 us  [the longest x1 17.4 us: cross_back(): pl.pallas_call(cross_back_kernel, grid=(d // wide,), in_specs=[full, full...]
    pallas_call x1, Pallas kernels: 6.79 us -> 3.62 us  [radar(): pl.pallas_call(radar_kernel, grid=(1,), in_specs=[full, full, full, whole...]
    ppermute x45 -> x42, starting transfers between devices: 47.2 us -> 44.6 us  [hop(): return lax.ppermute(values, ('grp', 'hd'), perm)]
    ppermute x45 -> x42, waiting for transfers between devices: 60.9 us -> 63.1 us  [hop(): return lax.ppermute(values, ('grp', 'hd'), perm)]
    unnamed x44 -> x122, local copies, waits for them, and re-layouts: 5.41 us -> 3.25 us
  transfers between devices with their start and end apart: 45 -> 42, of which waited for: 21 -> 19; matrix products, arithmetic and copies ran while one was open for 4% -> 3% of each run, Pallas kernels for 36% -> 32%
where the time goes in v3:
time: 254 us; the launch traced here: 252 us
  Pallas kernels  114 us (45%)
  waiting for transfers between devices  63.1 us (25%)
  starting transfers between devices  44.6 us (18%)
  other arithmetic  18.8 us (7%)
  local copies, waits for them, and re-layouts  8.97 us (4%)
    ppermute x42, waiting for transfers between devices, hop(): return lax.ppermute(values, ('grp', 'hd'), perm)  63.1 us
    ppermute x42, starting transfers between devices, hop(): return lax.ppermute(values, ('grp', 'hd'), perm)  44.6 us
    pallas_call x1, Pallas kernels, hidden(): pl.pallas_call(hidden_kernel, grid=(4,), in_specs=[whole((rows, d)), whol...  25.2 us
    pallas_call x1, Pallas kernels, cross_back(): pl.pallas_call(cross_back_kernel, grid=(d // wide,), in_specs=[full, full...  17.4 us
    pallas_call x1, Pallas kernels, hidden_grads(): pl.pallas_call(functools.partial(hidden_grads_kernel, blocks), grid_spec=...  17 us
    pallas_call x1, Pallas kernels, self_forward(): pl.pallas_call(self_forward_kernel, grid=(steps,), in_specs=[smem(), whol...  16.1 us
    pallas_call x1, Pallas kernels, self_back(): pl.pallas_call(self_back_kernel, grid=(d // wide,), in_specs=[full, full,...  13.6 us
    pallas_call x1, Pallas kernels, cross_forward(): pl.pallas_call(cross_forward_kernel, grid=(steps,), in_specs=[smem(), who...  13 us
  transfers between devices with their start and end apart: 42, of which 19 were waited for; matrix products, arithmetic and copies ran while one was open for 3% of the time, Pallas kernels for 32%

profile of v3, /device:TPU:0, one launch (start us, length us, event | category | flops | bytes accessed | tf_op | source)
XLA Modules:
  0.0 251.5 jit_solution(12758496391895821865)
XLA Ops:
  1.5 16.1 %self_forward.1 = (bf16[464,768]{1,0:T(8,128)(2,1)}, bf16[464,768]{1,0:T(8,128)(2,1)}, bf16[464,768]{1,0:T(8,128)(2,1)}, bf16[464,768]{1,0:T(8,128)(2,1)}, bf16[...) custom-call(s32[1,4,3]{2,1,0:T(4,128)S(1)} %copy.31.lens, ...), custom_call_target="tpu_custom_call" | custom-call | flops 1 | bytes 1 | tf_op jit(solution)/shard_map/self_forward/pallas_call | solution.py:232
  17.7 3.0 %collective-permute-start = (bf16[464,768]{1,0:T(8,128)(2,1)}, bf16[464,768]{1,0:T(8,128)(2,1)S(1)}, u32[]{:S(2)}, u32[]{:S(2)}) collective-permute-start(bf16[464,768]{1,0:T(8,128)(2,1)} %get-tuple-element.162.gf.refs_4_), channel_id=1, source_target_pairs={{0,4},{1,5},{2,6},{3,7},{4,0},{5,1},{6,2},{7,3},{8,12},{9,13},{10,... | collective-permute-start | bytes 2138120 | tf_op jit(solution)/shard_map/ppermute | solution.py:656
  20.7 13.0 %cross_forward.1 = (bf16[464,768]{1,0:T(8,128)(2,1)}, bf16[464,768]{1,0:T(8,128)(2,1)}, bf16[464,768]{1,0:T(8,128)(2,1)}, bf16[12,464,464]{2,1,0:T(8,128)(2,1)},...) custom-call(s32[1,4,3]{2,1,0:T(4,128)S(1)} %copy.31.lens, ...), custom_call_target="tpu_custom_call" | custom-call | flops 1 | bytes 1 | tf_op jit(solution)/shard_map/cross_forward/pallas_call | solution.py:261
  33.8 3.1 %collective-permute-done.refs_5_ = bf16[464,768]{1,0:T(8,128)(2,1)S(1)} collective-permute-done((bf16[464,768]{1,0:T(8,128)(2,1)}, bf16[464,768]{1,0:T(8,128)(2,1)S(1)}, u32[]{:S(2)}, u32[]{:S(2)}) %collective-permute-start) | collective-permute-done | bytes 712736 | tf_op jit(solution)/shard_map/ppermute | solution.py:656
  36.8 1.8 collective-permute-start.2
  39.2 25.2 %hidden.1 = (bf16[464,3072]{1,0:T(8,128)(2,1)}, f32[464,768]{1,0:T(8,128)}, f32[8,768]{1,0:T(8,128)}) custom-call(f32[464,768]{1,0:T(8,128)S(1)} %get-tuple-element.164.res2, bf16[464,768]{1,0:T(8,128)(2,1)S(1)} %get-tuple-element.165.n3.refs_0_, bf16[464,768]{1,0:T(8,128)(2,1)} %get-tuple-element.162.gf.refs_4_, f32[3,768]{1,0:T(4,128)S(1)} %copy-done.34, ...), custom_call_target="tpu_custom_call" | custom-call | flops 1 | bytes 1 | tf_op jit(solution)/shard_map/hidden/pallas_call | solution.py:313
  66.3 2.4 collective-permute-done.5.refs_3_
  68.8 17.0 %hidden_grads.1 = (bf16[2,2,2,96,768]{4,3,2,1,0:T(8,128)(2,1)S(1)}, bf16[2,2,192,768]{3,2,1,0:T(8,128)(2,1)S(1)}) custom-call(s32[4]{0:T(128)S(1)} %pad_add_fusion.meta, bf16[464,768]{1,0:T(8,128)(2,1)} %copy-done.19, bf16[464,768]{1,0:T(8,128)(2,1)} %collective-permute-done.2.refs_1_, bf16[464,768]{1,0:T(8,128)(2,1)} %copy-done.48, ...), custom_call_target="tpu_custom_call" | custom-call | flops 1 | bytes 1 | tf_op jit(solution)/shard_map/hidden_grads/pallas_call | solution.py:405
  85.8 1.6 collective-permute-start.6
  88.0 17.4 %cross_back.1 = (bf16[2,2,2,2,48,1920]{5,4,3,2,1,0:T(8,128)(2,1)S(1)}, bf16[2,2,2,2,48,1920]{5,4,3,2,1,0:T(8,128)(2,1)S(1)}, bf16[464,768]{1,0:T(8,128)(2,1)}, b...) custom-call(f32[464,768]{1,0:T(8,128)S(1)} %copy-done.23, f32[464,768]{1,0:T(8,128)S(1)} %copy-done.6, ...), custom_call_target="tpu_custom_call" | custom-call | flops 1 | bytes 1 | tf_op jit(solution)/shard_map/cross_back/pallas_call | solution.py:547
  105.4 2.2 collective-permute-done.7
  107.9 1.6 collective-permute-start.9
  109.4 1.6 collective-permute-start.10
  111.0 4.4 %output.1 = bf16[512,768]{1,0:T(8,128)(2,1)} custom-call(s32[1,4,3]{2,1,0:T(4,128)S(1)} %copy.31.lens, bf16[464,3072]{1,0:T(8,128)(2,1)S(1)} %copy-done.15, f32[464,768]{1,0:T(8,128)S(1)} %copy-done.4, f32[3,768]{1,0:T(4,128)S(1)} %copy-done.36, bf16[3072,768]{1,0:T(8,128)(2,1)S(1)} %bitcast.202), custom_call_target="tpu_custom_call" | custom-call | flops 1 | bytes 1 | tf_op jit(solution)/shard_map/output/pallas_call | solution.py:350
  115.4 1.9 collective-permute-done.9
  120.1 2.8 %collective-permute-start.11 = (bf16[192,768]{1,0:T(8,128)(2,1)S(1)}, bf16[192,768]{1,0:T(8,128)(2,1)S(1)}, u32[]{:S(2)}, u32[]{:S(2)}) collective-permute-start(bf16[192,768]{1,0:T(8,128)(2,1)S(1)} %fusion.15), channel_id=1, source_target_pairs={{0,16},{1,17},{2,18},{3,19},{4,20},{5,21},{6,22},{7,23},{8,24},{9,... | collective-permute-start | bytes 884744 | tf_op jit(solution)/shard_map/ppermute | solution.py:656
  123.0 13.6 %self_back.1 = (bf16[2,2,2,2,48,1152]{5,4,3,2,1,0:T(8,128)(2,1)S(1)}, bf16[2,2,2,2,48,1152]{5,4,3,2,1,0:T(8,128)(2,1)S(1)}, bf16[464,768]{1,0:T(8,128)(2,1)}, bf16[464,768]{1,0:T(8,128)(2,1)}, bf16[464,768]{1,0:T(8,128)(2,1)}) custom-call(f32[464,768]{1,0:T(8,128)S(1)} %copy-done.2, bf16[464,768]{1,0:T(8,128)(2,1)S(1)} %copy-done.24, ...), custom_call_target="tpu_custom_call" | custom-call | flops 1 | bytes 1 | tf_op jit(solution)/shard_map/self_back/pallas_call | solution.py:575
  138.2 1.4 collective-permute-start.18
  139.5 1.5 collective-permute-start.19
  141.0 1.6 collective-permute-start.16
  143.1 3.6 %radar.4 = (f32[512,768]{1,0:T(8,128)}, f32[16,768]{1,0:T(8,128)S(1)}) custom-call(bf16[464,768]{1,0:T(8,128)(2,1)S(1)} %copy-done.30, bf16[464,768]{1,0:T(8,128)(2,1)S(1)} %copy-done.28, bf16[464,768]{1,0:T(8,128)(2,1)S(1)} %copy-done.29, bf16[768,2304]{1,0:T(8,128)(2,1)S(1)} %copy-done, f32[464,768]{1,0:T(8,128)S(1)} %copy-done.2, ...), custom_call_target="tpu_custom_call" | custom-call | flops 1 | bytes 1 | tf_op jit(solution)/shard_map/radar/pallas_call | solution.py:645
  146.7 4.2 %collective-permute-done.16 = bf16[2,96,768]{2,1,0:T(8,128)(2,1)S(1)} collective-permute-done((bf16[2,96,768]{2,1,0:T(8,128)(2,1)S(1)}, bf16[2,96,768]{2,1,0:T(8,128)(2,1)S(1)}, u32[]{:S(2)}, u32[]{:S(2)}) %collective-permute-start.16) | collective-permute-done | bytes 294944 | tf_op jit(solution)/shard_map/ppermute | solution.py:656
  150.9 4.8 %collective-permute-done.17 = bf16[192,768]{1,0:T(8,128)(2,1)S(1)} collective-permute-done((bf16[192,768]{1,0:T(8,128)(2,1)S(1)}, bf16[192,768]{1,0:T(8,128)(2,1)S(1)}, u32[]{:S(2)}, u32[]{:S(2)}) %collective-permute-start.17) | collective-permute-done | bytes 294944 | tf_op jit(solution)/shard_map/ppermute | solution.py:656
  160.4 2.6 %collective-permute-start.20 = (bf16[2,96,768]{2,1,0:T(8,128)(2,1)}, bf16[2,96,768]{2,1,0:T(8,128)(2,1)S(1)}, u32[]{:S(2)}, u32[]{:S(2)}) collective-permute-start(bf16[2,96,768]{2,1,0:T(8,128)(2,1)} %fusion.12), channel_id=1, source_target_pairs={{0,16},{1,17},{2,18},{3,19},{4,20},{5,21},{6,22},{7,23},{8,24},{9,... | collective-permute-start | bytes 884744 | tf_op jit(solution)/shard_map/ppermute | solution.py:656
  163.0 1.6 collective-permute-start.23
  166.6 3.9 %optic.3 = f32[512,768]{1,0:T(8,128)} custom-call(bf16[464,768]{1,0:T(8,128)(2,1)} %get-tuple-element.244.dk, bf16[464,768]{1,0:T(8,128)(2,1)} %get-tuple-element.245.dv, bf16[768,1536]{1,0:T(8,128)(2,1)S(1)} %copy-done.1), custom_call_target="tpu_custom_call" | custom-call | flops 1 | bytes 1 | tf_op jit(solution)/shard_map/optic/pallas_call | solution.py:613
  170.5 4.8 %collective-permute-done.20 = bf16[2,96,768]{2,1,0:T(8,128)(2,1)S(1)} collective-permute-done((bf16[2,96,768]{2,1,0:T(8,128)(2,1)}, bf16[2,96,768]{2,1,0:T(8,128)(2,1)S(1)}, u32[]{:S(2)}, u32[]{:S(2)}) %collective-permute-start.20) | collective-permute-done | bytes 294944 | tf_op jit(solution)/shard_map/ppermute | solution.py:656
  175.3 1.8 collective-permute-done.23
  177.1 1.5 fusion.3
  180.5 1.6 collective-permute-start.27
  182.0 1.3 collective-permute-start.26
  183.4 1.7 collective-permute-start.29
  186.2 3.0 %collective-permute-done.30 = f32[16,768]{1,0:T(8,128)S(1)} collective-permute-done((f32[16,768]{1,0:T(8,128)S(1)}, f32[16,768]{1,0:T(8,128)S(1)}, u32[]{:S(2)}, u32[]{:S(2)}) %collective-permute-start.30) | collective-permute-done | bytes 49184 | tf_op jit(solution)/shard_map/ppermute | solution.py:656
  189.7 8.2 %collective-permute-done.25 = bf16[2,48,1152]{2,1,0:T(8,128)(2,1)} collective-permute-done((bf16[2,48,1152]{2,1,0:T(8,128)(2,1)}, bf16[2,48,1152]{2,1,0:T(8,128)(2,1)}, u32[]{:S(2)}, u32[]{:S(2)}) %collective-permute-start.25) | collective-permute-done | bytes 221216 | tf_op jit(solution)/shard_map/ppermute | solution.py:656
  200.4 1.8 collective-permute-start.31
  202.2 1.5 collective-permute-start.32
  204.8 1.7 bitcast_convert_fusion
  206.4 10.0 %collective-permute-done.34 = f32[16,768]{1,0:T(8,128)S(1)} collective-permute-done((f32[16,768]{1,0:T(8,128)S(1)}, f32[16,768]{1,0:T(8,128)S(1)}, u32[]{:S(2)}, u32[]{:S(2)}) %collective-permute-start.34) | collective-permute-done | bytes 49184 | tf_op jit(solution)/shard_map/ppermute | solution.py:656
  216.7 3.4 %collective-permute-start.35 = (bf16[2,48,1152]{2,1,0:T(8,128)(2,1)S(1)}, bf16[2,48,1152]{2,1,0:T(8,128)(2,1)S(1)}, u32[]{:S(2)}, u32[]{:S(2)}) collective-permute-start(bf16[2,48,1152]{2,1,0:T(8,128)(2,1)S(1)} %fusion.20), channel_id=1, source_target_pairs={{0,16},{1,17},{2,18},{3,19},{4,20},{5,21},{6,22},{7,23},{8,24},{9,... | collective-permute-start | bytes 663560 | tf_op jit(solution)/shard_map/ppermute | solution.py:656
  220.1 1.5 collective-permute-start.36
  222.6 1.7 convert_element_type.461
  224.2 3.9 %collective-permute-done.37 = f32[16,768]{1,0:T(8,128)S(1)} collective-permute-done((f32[16,768]{1,0:T(8,128)S(1)}, f32[16,768]{1,0:T(8,128)S(1)}, u32[]{:S(2)}, u32[]{:S(2)}) %collective-permute-start.37) | collective-permute-done | bytes 49184 | tf_op jit(solution)/shard_map/ppermute | solution.py:656
  228.1 7.2 %collective-permute-done.36 = bf16[2,2,48,1920]{3,2,1,0:T(8,128)(2,1)S(1)} collective-permute-done((bf16[2,2,48,1920]{3,2,1,0:T(8,128)(2,1)S(1)}, bf16[2,2,48,1920]{3,2,1,0:T(8,128)(2,1)S(1)}, u32[]{:S(2)}, u32[]{:S(2)}) %collective-permute-start.36) | collective-permute-done | bytes 737312 | tf_op jit(solution)/shard_map/ppermute | solution.py:656
  237.6 1.5 collective-permute-start.38
  239.7 1.4 collective-permute-start.40
  244.5 1.9 collective-permute-done.41
  246.3 1.6 collective-permute-done.40
  249.3 1.3 pad_maximum_fusion
  (251 shorter events, 31.9 us)
Async XLA Ops:
  0.6 38.5 %slice-start.4 = ((s8[4718592]{0:T(1024)(128)(4,1)}), s8[524288]{0:T(1024)(128)(4,1)S(1)}, s32[]{:S(2)}) async-start(s8[4718592]{0:T(1024)(128)(4,1)} %bitcast.203), calls=%async_computation.4 | async-start | bytes 1048576
  1.5 37.6 %slice-start.5 = ((s8[4718592]{0:T(1024)(128)(4,1)}), s8[4194304]{0:T(1024)(128)(4,1)S(1)}, s32[]{:S(2)}) async-start(s8[4718592]{0:T(1024)(128)(4,1)} %bitcast.203), calls=%async_computation.5 | async-start | bytes 8388608
  17.7 19.2 %collective-permute-start = (bf16[464,768]{1,0:T(8,128)(2,1)}, bf16[464,768]{1,0:T(8,128)(2,1)S(1)}, u32[]{:S(2)}, u32[]{:S(2)}) collective-permute-start(bf16[464,768]{1,0:T(8,128)(2,1)} %get-tuple-element.162.gf.refs_4_), channel_id=1, source_target_pairs={{0,4},{1,5},{2,6},{3,7},{4,0},{5,1},{6,2},{7,3},{8,12},{9,13},{10,... | collective-permute-start | bytes 2138120 | tf_op jit(solution)/shard_map/ppermute | solution.py:656
  20.7 16.2 %collective-permute-start.1 = (bf16[464,768]{1,0:T(8,128)(2,1)}, bf16[464,768]{1,0:T(8,128)(2,1)S(1)}, u32[]{:S(2)}, u32[]{:S(2)}) collective-permute-start(bf16[464,768]{1,0:T(8,128)(2,1)} %get-tuple-element.162.gf.refs_4_), channel_id=1, source_target_pairs={{0,1},{1,0},{2,3},{3,2},{4,5},{5,4},{6,7},{7,6},{8,9},{9,8},{10,11... | collective-permute-start | bytes 2138120 | tf_op jit(solution)/shard_map/ppermute | solution.py:656
  33.7 30.6 %copy-start.3 = (f32[464,768]{1,0:T(8,128)}, f32[464,768]{1,0:T(8,128)S(1)}, u32[]{:S(2)}) copy-start(f32[464,768]{1,0:T(8,128)S(1)} %get-tuple-element.164.res2) | copy-start | bytes 4276228
  33.7 30.6 %copy-start.19 = (bf16[464,768]{1,0:T(8,128)(2,1)}, bf16[464,768]{1,0:T(8,128)(2,1)S(1)}, u32[]{:S(2)}) copy-start(bf16[464,768]{1,0:T(8,128)(2,1)S(1)} %get-tuple-element.165.n3.refs_0_) | copy-start | bytes 2138116
  36.8 27.5 %copy-start.46 = (bf16[464,768]{1,0:T(8,128)(2,1)}, bf16[464,768]{1,0:T(8,128)(2,1)S(1)}, u32[]{:S(2)}) copy-start(bf16[464,768]{1,0:T(8,128)(2,1)S(1)} %collective-permute-done.refs_5_) | copy-start | bytes 2138116
  36.8 27.5 %copy-start.47 = (bf16[464,768]{1,0:T(8,128)(2,1)}, bf16[464,768]{1,0:T(8,128)(2,1)S(1)}, u32[]{:S(2)}) copy-start(bf16[464,768]{1,0:T(8,128)(2,1)S(1)} %collective-permute-done.1.refs_6_) | copy-start | bytes 2138116
  36.8 27.6 %collective-permute-start.2 = (bf16[464,768]{1,0:T(8,128)(2,1)S(1)}, bf16[464,768]{1,0:T(8,128)(2,1)}, u32[]{:S(2)}, u32[]{:S(2)}) collective-permute-start(bf16[464,768]{1,0:T(8,128)(2,1)S(1)} %get-tuple-element.165.n3.refs_0_), channel_id=1, source_target_pairs={{0,4},{1,5},{2,6},{3,7},{4,0},{5,1},{6,2},{7,3},{8,12},{9,13},{10,... | collective-permute-start | bytes 2138120 | tf_op jit(solution)/shard_map/ppermute | solution.py:656
  38.6 25.8 %collective-permute-start.3 = (bf16[464,768]{1,0:T(8,128)(2,1)S(1)}, bf16[464,768]{1,0:T(8,128)(2,1)S(1)}, u32[]{:S(2)}, u32[]{:S(2)}) collective-permute-start(bf16[464,768]{1,0:T(8,128)(2,1)S(1)} %get-tuple-element.165.n3.refs_0_), channel_id=1, source_target_pairs={{0,1},{1,0},{2,3},{3,2},{4,5},{5,4},{6,7},{7,6},{8,9},{9,8},{10,11... | collective-permute-start | bytes 2138120 | tf_op jit(solution)/shard_map/ppermute | solution.py:656
  38.6 25.8 %collective-permute-start.4 = (bf16[464,768]{1,0:T(8,128)(2,1)S(1)}, bf16[464,768]{1,0:T(8,128)(2,1)S(1)}, u32[]{:S(2)}, u32[]{:S(2)}) collective-permute-start(bf16[464,768]{1,0:T(8,128)(2,1)S(1)} %collective-permute-done.refs_5_), channel_id=1, source_target_pairs={{0,1},{1,0},{2,3},{3,2},{4,5},{5,4},{6,7},{7,6},{8,9},{9,8},{10,11... | collective-permute-start | bytes 2138120 | tf_op jit(solution)/shard_map/ppermute | solution.py:656
  66.2 2.5 %collective-permute-start.5 = (bf16[464,768]{1,0:T(8,128)(2,1)}, bf16[464,768]{1,0:T(8,128)(2,1)}, u32[]{:S(2)}, u32[]{:S(2)}) collective-permute-start(bf16[464,768]{1,0:T(8,128)(2,1)} %collective-permute-done.2.refs_1_), channel_id=1, source_target_pairs={{0,1},{1,0},{2,3},{3,2},{4,5},{5,4},{6,7},{7,6},{8,9},{9,8},{10,11... | collective-permute-start | bytes 2138120 | tf_op jit(solution)/shard_map/ppermute | solution.py:656
  85.8 21.8 %collective-permute-start.6 = (bf16[2,192,768]{2,1,0:T(8,128)(2,1)S(1)}, bf16[2,192,768]{2,1,0:T(8,128)(2,1)S(1)}, u32[]{:S(2)}, u32[]{:S(2)}) collective-permute-start(bf16[2,192,768]{2,1,0:T(8,128)(2,1)S(1)} %slice_bitcast_fusion), channel_id=1, source_target_pairs={{0,2},{1,3},{2,0},{3,1},{4,6},{5,7},{6,4},{7,5},{8,10},{9,11},{10,... | collective-permute-start | bytes 1769480 | tf_op jit(solution)/shard_map/ppermute | solution.py:656
  87.4 20.2 %collective-permute-start.7 = (bf16[2,96,768]{2,1,0:T(8,128)(2,1)S(1)}, bf16[2,96,768]{2,1,0:T(8,128)(2,1)S(1)}, u32[]{:S(2)}, u32[]{:S(2)}) collective-permute-start(bf16[2,96,768]{2,1,0:T(8,128)(2,1)S(1)} %get-tuple-element.192), channel_id=1, source_target_pairs={{0,2},{1,3},{2,0},{3,1},{4,6},{5,7},{6,4},{7,5},{8,10},{9,11},{10,... | collective-permute-start | bytes 884744 | tf_op jit(solution)/shard_map/ppermute | solution.py:656
  107.8 10.7 %collective-permute-start.8 = (bf16[2,2,2,2,48,1920]{5,4,3,2,1,0:T(8,128)(2,1)S(1)}, bf16[2,2,2,2,48,1920]{5,4,3,2,1,0:T(8,128)(2,1)S(1)}, u32[]{:S(2)}, u32[]{:S(2)}) collective-permute-start(bf16[2,2,2,2,48,1920]{5,4,3,2,1,0:T(8,128)(2,1)S(1)} %get-tuple-element.198), channel_id=1, source_target_pairs={{0,1},{1,0},{2,3},{3,2},{4,5},{5,4},{6,7},{7,6},{8,9},{9,8},{10,11... | collective-permute-start | bytes 8847368 | tf_op jit(solution)/shard_map/ppermute | solution.py:656
  107.9 9.4 %collective-permute-start.9 = (bf16[2,96,768]{2,1,0:T(8,128)(2,1)S(1)}, bf16[2,96,768]{2,1,0:T(8,128)(2,1)S(1)}, u32[]{:S(2)}, u32[]{:S(2)}) collective-permute-start(bf16[2,96,768]{2,1,0:T(8,128)(2,1)S(1)} %get-tuple-element.199), channel_id=1, source_target_pairs={{0,2},{1,3},{2,0},{3,1},{4,6},{5,7},{6,4},{7,5},{8,10},{9,11},{10,... | collective-permute-start | bytes 884744 | tf_op jit(solution)/shard_map/ppermute | solution.py:656
  109.4 9.1 %collective-permute-start.10 = (bf16[192,768]{1,0:T(8,128)(2,1)S(1)}, bf16[192,768]{1,0:T(8,128)(2,1)S(1)}, u32[]{:S(2)}, u32[]{:S(2)}) collective-permute-start(bf16[192,768]{1,0:T(8,128)(2,1)S(1)} %slice_bitcast_fusion.10), channel_id=1, source_target_pairs={{0,8},{1,9},{2,10},{3,11},{4,12},{5,13},{6,14},{7,15},{8,0},{9,1},... | collective-permute-start | bytes 884744 | tf_op jit(solution)/shard_map/ppermute | solution.py:656
  119.2 17.8 %collective-permute-start.12 = (bf16[2,2,48,1920]{3,2,1,0:T(8,128)(2,1)S(1)}, bf16[2,2,48,1920]{3,2,1,0:T(8,128)(2,1)S(1)}, u32[]{:S(2)}, u32[]{:S(2)}) collective-permute-start(bf16[2,2,48,1920]{3,2,1,0:T(8,128)(2,1)S(1)} %get-tuple-element.214), channel_id=1, source_target_pairs={{0,4},{1,5},{2,6},{3,7},{4,0},{5,1},{6,2},{7,3},{8,12},{9,13},{10,... | collective-permute-start | bytes 2211848 | tf_op jit(solution)/shard_map/ppermute | solution.py:656
  119.8 17.4 %collective-permute-start.13 = (bf16[2,2,48,1920]{3,2,1,0:T(8,128)(2,1)S(1)}, bf16[2,2,48,1920]{3,2,1,0:T(8,128)(2,1)S(1)}, u32[]{:S(2)}, u32[]{:S(2)}) collective-permute-start(bf16[2,2,48,1920]{3,2,1,0:T(8,128)(2,1)S(1)} %get-tuple-element.215), channel_id=1, source_target_pairs={{0,2},{1,3},{2,0},{3,1},{4,6},{5,7},{6,4},{7,5},{8,10},{9,11},{10,... | collective-permute-start | bytes 2211848 | tf_op jit(solution)/shard_map/ppermute | solution.py:656
  120.1 16.4 %collective-permute-start.11 = (bf16[192,768]{1,0:T(8,128)(2,1)S(1)}, bf16[192,768]{1,0:T(8,128)(2,1)S(1)}, u32[]{:S(2)}, u32[]{:S(2)}) collective-permute-start(bf16[192,768]{1,0:T(8,128)(2,1)S(1)} %fusion.15), channel_id=1, source_target_pairs={{0,16},{1,17},{2,18},{3,19},{4,20},{5,21},{6,22},{7,23},{8,24},{9,... | collective-permute-start | bytes 884744 | tf_op jit(solution)/shard_map/ppermute | solution.py:656
  122.9 13.7 %collective-permute-start.14 = (bf16[2,96,768]{2,1,0:T(8,128)(2,1)S(1)}, bf16[2,96,768]{2,1,0:T(8,128)(2,1)S(1)}, u32[]{:S(2)}, u32[]{:S(2)}) collective-permute-start(bf16[2,96,768]{2,1,0:T(8,128)(2,1)S(1)} %get-tuple-element.216), channel_id=1, source_target_pairs={{0,1},{1,0},{2,3},{3,2},{4,5},{5,4},{6,7},{7,6},{8,9},{9,8},{10,11... | collective-permute-start | bytes 884744 | tf_op jit(solution)/shard_map/ppermute | solution.py:656
  138.1 17.7 %collective-permute-start.15 = (bf16[2,2,2,2,48,1152]{5,4,3,2,1,0:T(8,128)(2,1)S(1)}, bf16[2,2,2,2,48,1152]{5,4,3,2,1,0:T(8,128)(2,1)S(1)}, u32[]{:S(2)}, u32[]{:S(2)}) collective-permute-start(bf16[2,2,2,2,48,1152]{5,4,3,2,1,0:T(8,128)(2,1)S(1)} %get-tuple-element.232), channel_id=1, source_target_pairs={{0,1},{1,0},{2,3},{3,2},{4,5},{5,4},{6,7},{7,6},{8,9},{9,8},{10,11... | collective-permute-start | bytes 5308424 | tf_op jit(solution)/shard_map/ppermute | solution.py:656
  138.2 17.6 %collective-permute-start.18 = (bf16[2,48,1920]{2,1,0:T(8,128)(2,1)S(1)}, bf16[2,48,1920]{2,1,0:T(8,128)(2,1)S(1)}, u32[]{:S(2)}, u32[]{:S(2)}) collective-permute-start(bf16[2,48,1920]{2,1,0:T(8,128)(2,1)S(1)} %slice_bitcast_fusion.8), channel_id=1, source_target_pairs={{0,2},{1,3},{2,0},{3,1},{4,6},{5,7},{6,4},{7,5},{8,10},{9,11},{10,... | collective-permute-start | bytes 1105928 | tf_op jit(solution)/shard_map/ppermute | solution.py:656
  139.5 16.2 %collective-permute-start.19 = (bf16[2,48,1920]{2,1,0:T(8,128)(2,1)S(1)}, bf16[2,48,1920]{2,1,0:T(8,128)(2,1)S(1)}, u32[]{:S(2)}, u32[]{:S(2)}) collective-permute-start(bf16[2,48,1920]{2,1,0:T(8,128)(2,1)S(1)} %slice_bitcast_fusion.7), channel_id=1, source_target_pairs={{0,4},{1,5},{2,6},{3,7},{4,0},{5,1},{6,2},{7,3},{8,12},{9,13},{10,... | collective-permute-start | bytes 1105928 | tf_op jit(solution)/shard_map/ppermute | solution.py:656
  141.0 9.9 %collective-permute-start.16 = (bf16[2,96,768]{2,1,0:T(8,128)(2,1)S(1)}, bf16[2,96,768]{2,1,0:T(8,128)(2,1)S(1)}, u32[]{:S(2)}, u32[]{:S(2)}) collective-permute-start(bf16[2,96,768]{2,1,0:T(8,128)(2,1)S(1)} %fusion.30), channel_id=1, source_target_pairs={{0,8},{1,9},{2,10},{3,11},{4,12},{5,13},{6,14},{7,15},{8,0},{9,1},... | collective-permute-start | bytes 884744 | tf_op jit(solution)/shard_map/ppermute | solution.py:656
  142.6 13.2 %collective-permute-start.17 = (bf16[192,768]{1,0:T(8,128)(2,1)S(1)}, bf16[192,768]{1,0:T(8,128)(2,1)S(1)}, u32[]{:S(2)}, u32[]{:S(2)}) collective-permute-start(bf16[192,768]{1,0:T(8,128)(2,1)S(1)} %add_convert_fusion.10), channel_id=1, source_target_pairs={{0,8},{1,9},{2,10},{3,11},{4,12},{5,13},{6,14},{7,15},{8,0},{9,1},... | collective-permute-start | bytes 884744 | tf_op jit(solution)/shard_map/ppermute | solution.py:656
  158.8 18.3 %collective-permute-start.21 = (bf16[2,2,48,1152]{3,2,1,0:T(8,128)(2,1)}, bf16[2,2,48,1152]{3,2,1,0:T(8,128)(2,1)}, u32[]{:S(2)}, u32[]{:S(2)}) collective-permute-start(bf16[2,2,48,1152]{3,2,1,0:T(8,128)(2,1)} %get-tuple-element.247), channel_id=1, source_target_pairs={{0,4},{1,5},{2,6},{3,7},{4,0},{5,1},{6,2},{7,3},{8,12},{9,13},{10,... | collective-permute-start | bytes 1327112 | tf_op jit(solution)/shard_map/ppermute | solution.py:656
  159.3 17.8 %collective-permute-start.22 = (bf16[2,2,48,1152]{3,2,1,0:T(8,128)(2,1)}, bf16[2,2,48,1152]{3,2,1,0:T(8,128)(2,1)}, u32[]{:S(2)}, u32[]{:S(2)}) collective-permute-start(bf16[2,2,48,1152]{3,2,1,0:T(8,128)(2,1)} %get-tuple-element.248), channel_id=1, source_target_pairs={{0,2},{1,3},{2,0},{3,1},{4,6},{5,7},{6,4},{7,5},{8,10},{9,11},{10,... | collective-permute-start | bytes 1327112 | tf_op jit(solution)/shard_map/ppermute | solution.py:656
  160.4 14.9 %collective-permute-start.20 = (bf16[2,96,768]{2,1,0:T(8,128)(2,1)}, bf16[2,96,768]{2,1,0:T(8,128)(2,1)S(1)}, u32[]{:S(2)}, u32[]{:S(2)}) collective-permute-start(bf16[2,96,768]{2,1,0:T(8,128)(2,1)} %fusion.12), channel_id=1, source_target_pairs={{0,16},{1,17},{2,18},{3,19},{4,20},{5,21},{6,22},{7,23},{8,24},{9,... | collective-permute-start | bytes 884744 | tf_op jit(solution)/shard_map/ppermute | solution.py:656
  163.0 14.1 %collective-permute-start.23 = (bf16[2,48,1920]{2,1,0:T(8,128)(2,1)}, bf16[2,48,1920]{2,1,0:T(8,128)(2,1)S(1)}, u32[]{:S(2)}, u32[]{:S(2)}) collective-permute-start(bf16[2,48,1920]{2,1,0:T(8,128)(2,1)} %fusion.26), channel_id=1, source_target_pairs={{0,8},{1,9},{2,10},{3,11},{4,12},{5,13},{6,14},{7,15},{8,0},{9,1},... | collective-permute-start | bytes 1105928 | tf_op jit(solution)/shard_map/ppermute | solution.py:656
  164.6 5.9 %collective-permute-start.24 = (f32[16,768]{1,0:T(8,128)S(1)}, f32[16,768]{1,0:T(8,128)S(1)}, u32[]{:S(2)}, u32[]{:S(2)}) collective-permute-start(f32[16,768]{1,0:T(8,128)S(1)} %get-tuple-element.250), channel_id=1, source_target_pairs={{0,1},{1,0},{2,3},{3,2},{4,5},{5,4},{6,7},{7,6},{8,9},{9,8},{10,11... | collective-permute-start | bytes 147464 | tf_op jit(solution)/shard_map/ppermute | solution.py:656
  180.5 17.7 %collective-permute-start.27 = (bf16[2,192,768]{2,1,0:T(8,128)(2,1)}, bf16[2,192,768]{2,1,0:T(8,128)(2,1)S(1)}, u32[]{:S(2)}, u32[]{:S(2)}) collective-permute-start(bf16[2,192,768]{2,1,0:T(8,128)(2,1)} %pad_maximum_fusion.5), channel_id=1, source_target_pairs={{0,4},{1,5},{2,6},{3,7},{4,0},{5,1},{6,2},{7,3},{8,12},{9,13},{10,... | collective-permute-start | bytes 1769480 | tf_op jit(solution)/shard_map/ppermute | solution.py:656
  182.0 16.1 %collective-permute-start.26 = (bf16[2,48,1920]{2,1,0:T(8,128)(2,1)S(1)}, bf16[2,48,1920]{2,1,0:T(8,128)(2,1)S(1)}, u32[]{:S(2)}, u32[]{:S(2)}) collective-permute-start(bf16[2,48,1920]{2,1,0:T(8,128)(2,1)S(1)} %fusion.9), channel_id=1, source_target_pairs={{0,16},{1,17},{2,18},{3,19},{4,20},{5,21},{6,22},{7,23},{8,24},{9,... | collective-permute-start | bytes 1105928 | tf_op jit(solution)/shard_map/ppermute | solution.py:656
  183.4 14.6 %collective-permute-start.29 = (bf16[2,96,768]{2,1,0:T(8,128)(2,1)S(1)}, bf16[2,96,768]{2,1,0:T(8,128)(2,1)S(1)}, u32[]{:S(2)}, u32[]{:S(2)}) collective-permute-start(bf16[2,96,768]{2,1,0:T(8,128)(2,1)S(1)} %add_convert_fusion.9), channel_id=1, source_target_pairs={{0,8},{1,9},{2,10},{3,11},{4,12},{5,13},{6,14},{7,15},{8,0},{9,1},... | collective-permute-start | bytes 884744 | tf_op jit(solution)/shard_map/ppermute | solution.py:656
  185.1 4.1 %collective-permute-start.30 = (f32[16,768]{1,0:T(8,128)S(1)}, f32[16,768]{1,0:T(8,128)S(1)}, u32[]{:S(2)}, u32[]{:S(2)}) collective-permute-start(f32[16,768]{1,0:T(8,128)S(1)} %add.148), channel_id=1, source_target_pairs={{0,2},{1,3},{2,0},{3,1},{4,6},{5,7},{6,4},{7,5},{8,10},{9,11},{10,... | collective-permute-start | bytes 147464 | tf_op jit(solution)/shard_map/ppermute | solution.py:656
  185.6 12.3 %collective-permute-start.25 = (bf16[2,48,1152]{2,1,0:T(8,128)(2,1)}, bf16[2,48,1152]{2,1,0:T(8,128)(2,1)}, u32[]{:S(2)}, u32[]{:S(2)}) collective-permute-start(bf16[2,48,1152]{2,1,0:T(8,128)(2,1)} %slice_bitcast_fusion.20), channel_id=1, source_target_pairs={{0,4},{1,5},{2,6},{3,7},{4,0},{5,1},{6,2},{7,3},{8,12},{9,13},{10,... | collective-permute-start | bytes 663560 | tf_op jit(solution)/shard_map/ppermute | solution.py:656
  189.2 8.8 %collective-permute-start.28 = (bf16[2,48,1152]{2,1,0:T(8,128)(2,1)S(1)}, bf16[2,48,1152]{2,1,0:T(8,128)(2,1)}, u32[]{:S(2)}, u32[]{:S(2)}) collective-permute-start(bf16[2,48,1152]{2,1,0:T(8,128)(2,1)S(1)} %slice_bitcast_fusion.19), channel_id=1, source_target_pairs={{0,2},{1,3},{2,0},{3,1},{4,6},{5,7},{6,4},{7,5},{8,10},{9,11},{10,... | collective-permute-start | bytes 663560 | tf_op jit(solution)/shard_map/ppermute | solution.py:656
  200.4 16.0 %collective-permute-start.31 = (bf16[2,48,1152]{2,1,0:T(8,128)(2,1)S(1)}, bf16[2,48,1152]{2,1,0:T(8,128)(2,1)S(1)}, u32[]{:S(2)}, u32[]{:S(2)}) collective-permute-start(bf16[2,48,1152]{2,1,0:T(8,128)(2,1)S(1)} %fusion.35), channel_id=1, source_target_pairs={{0,8},{1,9},{2,10},{3,11},{4,12},{5,13},{6,14},{7,15},{8,0},{9,1},... | collective-permute-start | bytes 663560 | tf_op jit(solution)/shard_map/ppermute | solution.py:656
  202.2 14.2 %collective-permute-start.32 = (bf16[2,2,96,768]{3,2,1,0:T(8,128)(2,1)S(1)}, bf16[2,2,96,768]{3,2,1,0:T(8,128)(2,1)S(1)}, u32[]{:S(2)}, u32[]{:S(2)}) collective-permute-start(bf16[2,2,96,768]{3,2,1,0:T(8,128)(2,1)S(1)} %pad_maximum_fusion.6), channel_id=1, source_target_pairs={{0,4},{1,5},{2,6},{3,7},{4,0},{5,1},{6,2},{7,3},{8,12},{9,13},{10,... | collective-permute-start | bytes 1769480 | tf_op jit(solution)/shard_map/ppermute | solution.py:656
  203.7 12.7 %collective-permute-start.33 = (bf16[2,48,1920]{2,1,0:T(8,128)(2,1)S(1)}, bf16[2,48,1920]{2,1,0:T(8,128)(2,1)S(1)}, u32[]{:S(2)}, u32[]{:S(2)}) collective-permute-start(bf16[2,48,1920]{2,1,0:T(8,128)(2,1)S(1)} %add_convert_fusion.8), channel_id=1, source_target_pairs={{0,8},{1,9},{2,10},{3,11},{4,12},{5,13},{6,14},{7,15},{8,0},{9,1},... | collective-permute-start | bytes 1105928 | tf_op jit(solution)/shard_map/ppermute | solution.py:656
  203.8 12.6 %collective-permute-start.34 = (f32[16,768]{1,0:T(8,128)S(1)}, f32[16,768]{1,0:T(8,128)S(1)}, u32[]{:S(2)}, u32[]{:S(2)}) collective-permute-start(f32[16,768]{1,0:T(8,128)S(1)} %add.152), channel_id=1, source_target_pairs={{0,4},{1,5},{2,6},{3,7},{4,0},{5,1},{6,2},{7,3},{8,12},{9,13},{10,... | collective-permute-start | bytes 147464 | tf_op jit(solution)/shard_map/ppermute | solution.py:656
  216.7 11.4 %collective-permute-start.35 = (bf16[2,48,1152]{2,1,0:T(8,128)(2,1)S(1)}, bf16[2,48,1152]{2,1,0:T(8,128)(2,1)S(1)}, u32[]{:S(2)}, u32[]{:S(2)}) collective-permute-start(bf16[2,48,1152]{2,1,0:T(8,128)(2,1)S(1)} %fusion.20), channel_id=1, source_target_pairs={{0,16},{1,17},{2,18},{3,19},{4,20},{5,21},{6,22},{7,23},{8,24},{9,... | collective-permute-start | bytes 663560 | tf_op jit(solution)/shard_map/ppermute | solution.py:656
  220.1 15.2 %collective-permute-start.36 = (bf16[2,2,48,1920]{3,2,1,0:T(8,128)(2,1)S(1)}, bf16[2,2,48,1920]{3,2,1,0:T(8,128)(2,1)S(1)}, u32[]{:S(2)}, u32[]{:S(2)}) collective-permute-start(bf16[2,2,48,1920]{3,2,1,0:T(8,128)(2,1)S(1)} %pad_maximum_fusion.2), channel_id=1, source_target_pairs={{0,4},{1,5},{2,6},{3,7},{4,0},{5,1},{6,2},{7,3},{8,12},{9,13},{10,... | collective-permute-start | bytes 2211848 | tf_op jit(solution)/shard_map/ppermute | solution.py:656
  221.6 6.5 %collective-permute-start.37 = (f32[16,768]{1,0:T(8,128)S(1)}, f32[16,768]{1,0:T(8,128)S(1)}, u32[]{:S(2)}, u32[]{:S(2)}) collective-permute-start(f32[16,768]{1,0:T(8,128)S(1)} %add.154), channel_id=1, source_target_pairs={{0,8},{1,9},{2,10},{3,11},{4,12},{5,13},{6,14},{7,15},{8,0},{9,1},... | collective-permute-start | bytes 147464 | tf_op jit(solution)/shard_map/ppermute | solution.py:656
  237.6 8.8 %collective-permute-start.38 = (bf16[2,48,1152]{2,1,0:T(8,128)(2,1)S(1)}, bf16[2,48,1152]{2,1,0:T(8,128)(2,1)S(1)}, u32[]{:S(2)}, u32[]{:S(2)}) collective-permute-start(bf16[2,48,1152]{2,1,0:T(8,128)(2,1)S(1)} %add_convert_fusion.11), channel_id=1, source_target_pairs={{0,4},{1,5},{2,6},{3,7},{4,0},{5,1},{6,2},{7,3},{8,12},{9,13},{10,... | collective-permute-start | bytes 663560 | tf_op jit(solution)/shard_map/ppermute | solution.py:656
  239.0 7.3 %collective-permute-start.39 = (bf16[2,48,1152]{2,1,0:T(8,128)(2,1)S(1)}, bf16[2,48,1152]{2,1,0:T(8,128)(2,1)S(1)}, u32[]{:S(2)}, u32[]{:S(2)}) collective-permute-start(bf16[2,48,1152]{2,1,0:T(8,128)(2,1)S(1)} %add_convert_fusion.11), channel_id=1, source_target_pairs={{0,12},{1,13},{2,14},{3,15},{4,8},{5,9},{6,10},{7,11},{8,4},{9,5},... | collective-permute-start | bytes 663560 | tf_op jit(solution)/shard_map/ppermute | solution.py:656
  239.7 8.2 %collective-permute-start.40 = (bf16[2,48,1152]{2,1,0:T(8,128)(2,1)S(1)}, bf16[2,48,1152]{2,1,0:T(8,128)(2,1)S(1)}, u32[]{:S(2)}, u32[]{:S(2)}) collective-permute-start(bf16[2,48,1152]{2,1,0:T(8,128)(2,1)S(1)} %add_convert_fusion.11), channel_id=1, source_target_pairs={{0,8},{1,9},{2,10},{3,11},{4,12},{5,13},{6,14},{7,15},{8,0},{9,1},... | collective-permute-start | bytes 663560 | tf_op jit(solution)/shard_map/ppermute | solution.py:656
  241.1 5.3 %collective-permute-start.41 = (f32[16,768]{1,0:T(8,128)S(1)}, f32[16,768]{1,0:T(8,128)S(1)}, u32[]{:S(2)}, u32[]{:S(2)}) collective-permute-start(f32[16,768]{1,0:T(8,128)S(1)} %add.156), channel_id=1, source_target_pairs={{0,16},{1,17},{2,18},{3,19},{4,20},{5,21},{6,22},{7,23},{8,24},{9,... | collective-permute-start | bytes 147464 | tf_op jit(solution)/shard_map/ppermute | solution.py:656
  (52 other events, 596.7 us)

commit v4 on v3

--- a/solution.py
+++ b/solution.py
@@ -357,7 +357,7 @@
         compiler_params=params(),
         cost_estimate=cost(2 * rows * d * ff, 2 * d * ff),
         name="output",
-    )(lens, act, res2, biases, wout)
+    )(lens, *far(act), res2, biases, *far(wout))
 
 
 def hidden_grads_kernel(blocks, meta, *refs):
@@ -388,7 +388,7 @@
         for c in range(2):
             for p in range(2):
                 at = ((y * 2 + c) * 2 + p) * piece
-                dwin[y ^ at_y, c ^ at_c, p ^ at_p] = acc_in[at : at + piece].astype(BF16)
+                dwin[p ^ at_p, y ^ at_y, c ^ at_c] = acc_in[at : at + piece].astype(BF16)
 
 
 def hidden_grads(rows, meta, normed, grads, hb, win, wout):
@@ -619,7 +619,7 @@
         compiler_params=params(),
         cost_estimate=cost(4 * rows * d * d, 4 * d * d),
         name="optic",
-    )(*far(dk, dv), weights)
+    )(*far(dk, dv, weights))
 
 
 def radar_kernel(dq, dk, dv, weights, grad_in, radar, gains, hidden_vec, cross_vec, out, vectors):
@@ -651,7 +651,7 @@
         compiler_params=params(),
         cost_estimate=cost(6 * rows * d * d, 6 * d * d),
         name="radar",
-    )(dq, dk, dv, weights, grad_in, tokens, gains, *vectors)
+    )(*far(dq, dk, dv, weights, grad_in, tokens), gains, *vectors)
 def hop(values, perm):
     return lax.ppermute(values, ("grp", "hd"), perm)
 
@@ -693,7 +693,7 @@
 
 
 MOVES = {
-    "C": ACROSS_CORE, "Y": ACROSS_Y, "Z": ACROSS_Y, "X": ACROSS_X, "P": ACROSS_P, "Q": ACROSS_Q,
+    "C": ACROSS_CORE, "Y": ACROSS_Y, "X": ACROSS_X, "P": ACROSS_P, "Q": ACROSS_Q,
     "A": ACROSS_P, "G": ACROSS_X, "D": ACROSS_XP, "W": ACROSS_Y, "V": ACROSS_X,
     "B": ACROSS_P, "H": ACROSS_X,
 }
@@ -728,21 +728,11 @@
 
 class InFlow(Flow):
     def operand(self, stage):
-        if stage in ("Y", "Z"):
-            return self.value[1, 1 if stage == "Y" else 0]
+        return self.value[1] if stage == "C" else super().operand(stage)
+
+    def absorb(self, stage, got):
         if stage == "C":
-            return self.value[1]
-        return self.value[:, 1] if stage == "P" else self.value
-
-    def absorb(self, stage, got):
-        if stage == "Y":
-            self.other = add(self.value[0, 1], got)
-        elif stage == "Z":
-            self.value = [add(self.value[0, 0], got), self.other]
-        elif stage == "C":
             self.value = jnp.stack([self.value[0], got])
-        elif stage == "P":
-            self.value = add(self.value[:, 0], got)
         else:
             super().absorb(stage, got)
 
@@ -869,28 +859,28 @@
         grad_two, dwin, dwout = tie([grad_two, dwin, dwout])
         plan.flows["o"], plan.flows["n"] = Flow(dwout, at_x, at_p), InFlow(dwin, at_x, at_p)
 
-        grad_two = plan.begin(grad_two, "oY", "nY")
+        grad_two = plan.begin(grad_two, "oY", "nP")
         keep, send, dk2, dv2, cross_vec, grad_one = cross_step(grad_two)
-        act = plan.end(tie([act, grad_one])[0], "oY", "nY")
+        act = plan.end(tie([act, grad_one])[0], "oY", "nP")
         plan.flows["a"] = RowFlow(keep, send, at_x, at_p)
 
-        act = plan.begin(act, "aC", "nZ", "oP")
+        act = plan.begin(act, "aC", "nY", "oP")
         layer_output = output(rows, local_rows, tile_lengths, act, res2, proj_biases, hidden_out)
-        grad_one = plan.end(tie([grad_one, layer_output])[0], "aC", "nZ", "oP")
+        grad_one = plan.end(tie([grad_one, layer_output])[0], "aC", "nY", "oP")
 
         grad_one = plan.begin(grad_one, "oQ", "aX", "aW", "nC")
         keep, send, dk1, dv1, dq1 = self_step(grad_one)
         dq1 = plan.end(dq1, "oQ", "aX", "aW", "nC")
         plan.flows["c"] = RowFlow(keep, send, at_x, at_p)
 
-        dq1 = plan.begin(dq1, "cC", "nP", "oB", "aY", "aV")
+        dq1 = plan.begin(dq1, "nQ", "aV", "aY", "cC", "oB")
         radar_grad, small = radar_step(dq1, grad_one)
-        dk2 = plan.end(tie([dk2, radar_grad])[0], "cC", "nP", "oB", "aY", "aV")
+        dk2 = plan.end(tie([dk2, radar_grad])[0], "nQ", "aV", "aY", "cC", "oB")
         plan.flows["s"] = Vectors(small, at_x, at_p)
 
-        dk2 = plan.begin(dk2, "nQ", "cX", "cW", "aP", "sC")
+        dk2 = plan.begin(dk2, "cX", "cW", "aP", "sC")
         optic_grad = optic(local_rows, dk2, dv2, cross_keyval)
-        gate = plan.end(optic_grad, "nQ", "cX", "cW", "aP", "sC")
+        gate = plan.end(optic_grad, "cX", "cW", "aP", "sC")
 
         for stages in (
             ("cV", "aQ", "oH", "cY", "nB", "sY"),
@@ -922,6 +912,7 @@
             for x in range(2):
                 at = jnp.asarray([0, c, x, 0], jnp.int32)
                 dwin, dwout = hidden_grads(rows, at, [n3], [gf], hb, hidden_in, hidden_out)
+                dwin = dwin.transpose(1, 2, 0, 3, 4)
                 into.append(jnp.stack([dwin[:, c], dwin[:, 1 - c]], axis=1).reshape(d, 2, ff // 8))
                 out.append(dwout.reshape(2, ff // 8, d))
         in_part = summed_anywhere(jnp.stack(into, axis=2).reshape(d, ff))

time: 254 us -> 248 us (0.976)
  waiting for transfers between devices: 63.1 us -> 54.6 us
  Pallas kernels: 114 us -> 120 us
  starting transfers between devices: 44.6 us -> 40.5 us
    ppermute x42 -> x41, waiting for transfers between devices: 63.1 us -> 54.6 us  [hop(): return lax.ppermute(values, ('grp', 'hd'), perm)]
    ppermute x42 -> x41, starting transfers between devices: 44.6 us -> 40.5 us  [hop(): return lax.ppermute(values, ('grp', 'hd'), perm)]
    pallas_call x1, Pallas kernels: 3.62 us -> 6.71 us  [radar(): pl.pallas_call(radar_kernel, grid=(1,), in_specs=[full, full, full, whole...]
    convert_element_type x13 -> x14, other arithmetic: 6.01 us -> 5.41 us  [add(): return total.astype(terms[0].dtype)]
  transfers between devices with their start and end apart: 42 -> 41, of which waited for: 19 -> 18; matrix products, arithmetic and copies ran while one was open for 3% -> 4% of each run, Pallas kernels for 32% -> 35%
where the time goes in v4:
time: 248 us; the launch traced here: 245 us
  Pallas kernels  120 us (48%)
  waiting for transfers between devices  54.6 us (22%)
  starting transfers between devices  40.5 us (16%)
  other arithmetic  19.2 us (8%)
  local copies, waits for them, and re-layouts  9.34 us (4%)
    ppermute x41, waiting for transfers between devices, hop(): return lax.ppermute(values, ('grp', 'hd'), perm)  54.6 us
    ppermute x41, starting transfers between devices, hop(): return lax.ppermute(values, ('grp', 'hd'), perm)  40.5 us
    pallas_call x1, Pallas kernels, hidden(): pl.pallas_call(hidden_kernel, grid=(4,), in_specs=[whole((rows, d)), whol...  25.2 us
    pallas_call x1, Pallas kernels, cross_back(): pl.pallas_call(cross_back_kernel, grid=(d // wide,), in_specs=[full, full...  17.2 us
    pallas_call x1, Pallas kernels, hidden_grads(): pl.pallas_call(functools.partial(hidden_grads_kernel, blocks), grid_spec=...  17 us
    pallas_call x1, Pallas kernels, self_forward(): pl.pallas_call(self_forward_kernel, grid=(steps,), in_specs=[smem(), whol...  16.1 us
    pallas_call x1, Pallas kernels, self_back(): pl.pallas_call(self_back_kernel, grid=(d // wide,), in_specs=[full, full,...  14.2 us
    pallas_call x1, Pallas kernels, cross_forward(): pl.pallas_call(cross_forward_kernel, grid=(steps,), in_specs=[smem(), who...  13 us
  transfers between devices with their start and end apart: 41, of which 18 were waited for; matrix products, arithmetic and copies ran while one was open for 4% of the time, Pallas kernels for 35%

profile of v4, /device:TPU:0, one launch (start us, length us, event | category | flops | bytes accessed | tf_op | source)
XLA Modules:
  0.0 245.3 jit_solution(16616043943623646479)
XLA Ops:
  1.5 16.1 %self_forward.1 = (bf16[464,768]{1,0:T(8,128)(2,1)}, bf16[464,768]{1,0:T(8,128)(2,1)}, bf16[464,768]{1,0:T(8,128)(2,1)}, bf16[464,768]{1,0:T(8,128)(2,1)}, bf16[...) custom-call(s32[1,4,3]{2,1,0:T(4,128)S(1)} %copy.31.lens, ...), custom_call_target="tpu_custom_call" | custom-call | flops 1 | bytes 1 | tf_op jit(solution)/shard_map/self_forward/pallas_call | solution.py:232
  17.7 3.0 %collective-permute-start = (bf16[464,768]{1,0:T(8,128)(2,1)}, bf16[464,768]{1,0:T(8,128)(2,1)S(1)}, u32[]{:S(2)}, u32[]{:S(2)}) collective-permute-start(bf16[464,768]{1,0:T(8,128)(2,1)} %get-tuple-element.160.gf.refs_4_), channel_id=1, source_target_pairs={{0,4},{1,5},{2,6},{3,7},{4,0},{5,1},{6,2},{7,3},{8,12},{9,13},{10,... | collective-permute-start | bytes 2138120 | tf_op jit(solution)/shard_map/ppermute | solution.py:656
  20.8 13.0 %cross_forward.1 = (bf16[464,768]{1,0:T(8,128)(2,1)}, bf16[464,768]{1,0:T(8,128)(2,1)}, bf16[464,768]{1,0:T(8,128)(2,1)}, bf16[12,464,464]{2,1,0:T(8,128)(2,1)},...) custom-call(s32[1,4,3]{2,1,0:T(4,128)S(1)} %copy.31.lens, ...), custom_call_target="tpu_custom_call" | custom-call | flops 1 | bytes 1 | tf_op jit(solution)/shard_map/cross_forward/pallas_call | solution.py:261
  33.8 3.1 %collective-permute-done.refs_5_ = bf16[464,768]{1,0:T(8,128)(2,1)S(1)} collective-permute-done((bf16[464,768]{1,0:T(8,128)(2,1)}, bf16[464,768]{1,0:T(8,128)(2,1)S(1)}, u32[]{:S(2)}, u32[]{:S(2)}) %collective-permute-start) | collective-permute-done | bytes 712736 | tf_op jit(solution)/shard_map/ppermute | solution.py:656
  36.8 1.8 collective-permute-start.2
  39.2 25.2 %hidden.1 = (bf16[464,3072]{1,0:T(8,128)(2,1)}, f32[464,768]{1,0:T(8,128)}, f32[8,768]{1,0:T(8,128)}) custom-call(f32[464,768]{1,0:T(8,128)S(1)} %get-tuple-element.162.res2, bf16[464,768]{1,0:T(8,128)(2,1)S(1)} %get-tuple-element.163.n3.refs_0_, bf16[464,768]{1,0:T(8,128)(2,1)} %get-tuple-element.160.gf.refs_4_, f32[3,768]{1,0:T(4,128)S(1)} %copy-done.26, ...), custom_call_target="tpu_custom_call" | custom-call | flops 1 | bytes 1 | tf_op jit(solution)/shard_map/hidden/pallas_call | solution.py:313
  64.7 2.2 collective-permute-done.5.refs_3_
  67.0 17.0 %hidden_grads.1 = (bf16[2,2,2,96,768]{4,3,2,1,0:T(8,128)(2,1)S(1)}, bf16[2,2,192,768]{3,2,1,0:T(8,128)(2,1)S(1)}) custom-call(s32[4]{0:T(128)S(1)} %pad_add_fusion.meta, bf16[464,768]{1,0:T(8,128)(2,1)} %copy-done.16, bf16[464,768]{1,0:T(8,128)(2,1)} %copy-done.40, bf16[464,768]{1,0:T(8,128)(2,1)} %copy-done.41, ...), custom_call_target="tpu_custom_call" | custom-call | flops 1 | bytes 1 | tf_op jit(solution)/shard_map/hidden_grads/pallas_call | solution.py:405
  84.0 1.6 collective-permute-start.6
  85.6 1.6 collective-permute-start.7
  87.3 17.2 %cross_back.1 = (bf16[2,2,2,2,48,1920]{5,4,3,2,1,0:T(8,128)(2,1)S(1)}, bf16[2,2,2,2,48,1920]{5,4,3,2,1,0:T(8,128)(2,1)S(1)}, bf16[464,768]{1,0:T(8,128)(2,1)}, b...) custom-call(f32[464,768]{1,0:T(8,128)S(1)} %copy-done.18, f32[464,768]{1,0:T(8,128)S(1)} %copy-done.5, ...), custom_call_target="tpu_custom_call" | custom-call | flops 1 | bytes 1 | tf_op jit(solution)/shard_map/cross_back/pallas_call | solution.py:547
  106.4 5.8 %output.1 = bf16[512,768]{1,0:T(8,128)(2,1)} custom-call(s32[1,4,3]{2,1,0:T(4,128)S(1)} %copy.31.lens, bf16[464,3072]{1,0:T(8,128)(2,1)} %get-tuple-element.195.act, f32[464,768]{1,0:T(8,128)S(1)} %copy-done.3, f32[3,768]{1,0:T(4,128)S(1)} %copy-done.28, bf16[3072,768]{1,0:T(8,128)(2,1)} %wout.3), custom_call_target="tpu_custom_call" | custom-call | flops 1 | bytes 1 | tf_op jit(solution)/shard_map/output/pallas_call | solution.py:350
  112.2 2.2 collective-permute-done.9
  115.9 1.5 collective-permute-start.13
  117.4 2.6 %collective-permute-start.11 = (bf16[192,768]{1,0:T(8,128)(2,1)S(1)}, bf16[192,768]{1,0:T(8,128)(2,1)S(1)}, u32[]{:S(2)}, u32[]{:S(2)}) collective-permute-start(bf16[192,768]{1,0:T(8,128)(2,1)S(1)} %fusion.14), channel_id=1, source_target_pairs={{0,16},{1,17},{2,18},{3,19},{4,20},{5,21},{6,22},{7,23},{8,24},{9,... | collective-permute-start | bytes 884744 | tf_op jit(solution)/shard_map/ppermute | solution.py:656
  120.0 14.2 %self_back.1 = (bf16[2,2,2,2,48,1152]{5,4,3,2,1,0:T(8,128)(2,1)S(1)}, bf16[2,2,2,2,48,1152]{5,4,3,2,1,0:T(8,128)(2,1)}, bf16[464,768]{1,0:T(8,128)(2,1)}, bf16[464,768]{1,0:T(8,128)(2,1)}, bf16[464,768]{1,0:T(8,128)(2,1)}) custom-call(f32[464,768]{1,0:T(8,128)S(1)} %copy-done.1, bf16[464,768]{1,0:T(8,128)(2,1)S(1)} %copy-done.19, ...), custom_call_target="tpu_custom_call" | custom-call | flops 1 | bytes 1 | tf_op jit(solution)/shard_map/self_back/pallas_call | solution.py:575
  137.8 1.5 collective-permute-start.16
  139.7 2.1 collective-permute-start.15
  142.3 6.7 %radar.4 = (f32[512,768]{1,0:T(8,128)}, f32[16,768]{1,0:T(8,128)S(1)}) custom-call(bf16[464,768]{1,0:T(8,128)(2,1)} %get-tuple-element.222.dq, bf16[464,768]{1,0:T(8,128)(2,1)} %get-tuple-element.223.dk, bf16[464,768]{1,0:T(8,128)(2,1)} %get-tuple-element.224.dv, bf16[768,2304]{1,0:T(8,128)(2,1)} %weights.2, f32[464,768]{1,0:T(8,128)} %get-tuple-element.205.grad_in, ...), custom_call_target="tpu_custom_call" | custom-call | flops 1 | bytes 1 | tf_op jit(solution)/shard_map/radar/pallas_call | solution.py:645
  149.1 6.6 %collective-permute-done.15 = bf16[2,96,768]{2,1,0:T(8,128)(2,1)S(1)} collective-permute-done((bf16[2,96,768]{2,1,0:T(8,128)(2,1)}, bf16[2,96,768]{2,1,0:T(8,128)(2,1)S(1)}, u32[]{:S(2)}, u32[]{:S(2)}) %collective-permute-start.15) | collective-permute-done | bytes 294944 | tf_op jit(solution)/shard_map/ppermute | solution.py:656
  156.7 1.4 fusion.16
  158.0 1.3 fusion.22
  161.4 1.0 select_bitcast_fusion.11
  164.0 4.6 %optic.3 = f32[512,768]{1,0:T(8,128)} custom-call(bf16[464,768]{1,0:T(8,128)(2,1)} %get-tuple-element.241.dk, bf16[464,768]{1,0:T(8,128)(2,1)} %get-tuple-element.242.dv, bf16[768,1536]{1,0:T(8,128)(2,1)} %weights.3), custom_call_target="tpu_custom_call" | custom-call | flops 1 | bytes 1 | tf_op jit(solution)/shard_map/optic/pallas_call | solution.py:613
  168.6 1.8 collective-permute-done.22
  170.7 1.5 fusion.4
  173.1 1.6 collective-permute-start.26
  174.6 2.3 collective-permute-start.28
  178.3 3.1 %collective-permute-done.29 = f32[16,768]{1,0:T(8,128)S(1)} collective-permute-done((f32[16,768]{1,0:T(8,128)S(1)}, f32[16,768]{1,0:T(8,128)S(1)}, u32[]{:S(2)}, u32[]{:S(2)}) %collective-permute-start.29) | collective-permute-done | bytes 49184 | tf_op jit(solution)/shard_map/ppermute | solution.py:656
  182.5 9.3 %collective-permute-done.24 = bf16[2,48,1152]{2,1,0:T(8,128)(2,1)} collective-permute-done((bf16[2,48,1152]{2,1,0:T(8,128)(2,1)S(1)}, bf16[2,48,1152]{2,1,0:T(8,128)(2,1)}, u32[]{:S(2)}, u32[]{:S(2)}) %collective-permute-start.24) | collective-permute-done | bytes 221216 | tf_op jit(solution)/shard_map/ppermute | solution.py:656
  192.0 1.1 fusion.27
  193.1 1.0 fusion.28
  194.6 1.3 collective-permute-start.30
  195.9 1.5 collective-permute-start.31
  198.9 1.7 bitcast_convert_fusion
  200.5 9.5 %collective-permute-done.33 = f32[16,768]{1,0:T(8,128)S(1)} collective-permute-done((f32[16,768]{1,0:T(8,128)S(1)}, f32[16,768]{1,0:T(8,128)S(1)}, u32[]{:S(2)}, u32[]{:S(2)}) %collective-permute-start.33) | collective-permute-done | bytes 49184 | tf_op jit(solution)/shard_map/ppermute | solution.py:656
  210.3 1.8 collective-permute-start.34
  212.1 1.3 collective-permute-start.35
  213.3 1.7 collective-permute-start.36
  215.6 1.7 convert_element_type.445
  217.4 3.1 %collective-permute-done.34 = bf16[2,48,1152]{2,1,0:T(8,128)(2,1)S(1)} collective-permute-done((bf16[2,48,1152]{2,1,0:T(8,128)(2,1)S(1)}, bf16[2,48,1152]{2,1,0:T(8,128)(2,1)S(1)}, u32[]{:S(2)}, u32[]{:S(2)}) %collective-permute-start.34) | collective-permute-done | bytes 221216 | tf_op jit(solution)/shard_map/ppermute | solution.py:656
  220.5 7.8 %collective-permute-done.35 = bf16[2,2,48,1920]{3,2,1,0:T(8,128)(2,1)S(1)} collective-permute-done((bf16[2,2,48,1920]{3,2,1,0:T(8,128)(2,1)S(1)}, bf16[2,2,48,1920]{3,2,1,0:T(8,128)(2,1)S(1)}, u32[]{:S(2)}, u32[]{:S(2)}) %collective-permute-start.35) | collective-permute-done | bytes 737312 | tf_op jit(solution)/shard_map/ppermute | solution.py:656
  229.0 1.2 fusion.32
  230.5 1.2 collective-permute-start.37
  231.7 2.1 collective-permute-start.38
  236.5 1.2 slice.311
  237.7 3.6 %collective-permute-done.40 = f32[16,768]{1,0:T(8,128)S(1)} collective-permute-done((f32[16,768]{1,0:T(8,128)S(1)}, f32[16,768]{1,0:T(8,128)S(1)}, u32[]{:S(2)}, u32[]{:S(2)}) %collective-permute-start.40) | collective-permute-done | bytes 49184 | tf_op jit(solution)/shard_map/ppermute | solution.py:656
  243.2 1.3 pad_maximum_fusion
  (234 shorter events, 26.8 us)
Async XLA Ops:
  0.6 38.5 %slice-start.2 = ((s8[4718592]{0:T(1024)(128)(4,1)}), s8[524288]{0:T(1024)(128)(4,1)S(1)}, s32[]{:S(2)}) async-start(s8[4718592]{0:T(1024)(128)(4,1)} %bitcast.194), calls=%async_computation.2 | async-start | bytes 1048576
  1.5 37.6 %slice-start.3 = ((s8[4718592]{0:T(1024)(128)(4,1)}), s8[4194304]{0:T(1024)(128)(4,1)S(1)}, s32[]{:S(2)}) async-start(s8[4718592]{0:T(1024)(128)(4,1)} %bitcast.194), calls=%async_computation.3 | async-start | bytes 8388608
  17.7 19.2 %collective-permute-start = (bf16[464,768]{1,0:T(8,128)(2,1)}, bf16[464,768]{1,0:T(8,128)(2,1)S(1)}, u32[]{:S(2)}, u32[]{:S(2)}) collective-permute-start(bf16[464,768]{1,0:T(8,128)(2,1)} %get-tuple-element.160.gf.refs_4_), channel_id=1, source_target_pairs={{0,4},{1,5},{2,6},{3,7},{4,0},{5,1},{6,2},{7,3},{8,12},{9,13},{10,... | collective-permute-start | bytes 2138120 | tf_op jit(solution)/shard_map/ppermute | solution.py:656
  20.7 16.2 %collective-permute-start.1 = (bf16[464,768]{1,0:T(8,128)(2,1)}, bf16[464,768]{1,0:T(8,128)(2,1)S(1)}, u32[]{:S(2)}, u32[]{:S(2)}) collective-permute-start(bf16[464,768]{1,0:T(8,128)(2,1)} %get-tuple-element.160.gf.refs_4_), channel_id=1, source_target_pairs={{0,1},{1,0},{2,3},{3,2},{4,5},{5,4},{6,7},{7,6},{8,9},{9,8},{10,11... | collective-permute-start | bytes 2138120 | tf_op jit(solution)/shard_map/ppermute | solution.py:656
  33.8 30.6 %copy-start.2 = (f32[464,768]{1,0:T(8,128)}, f32[464,768]{1,0:T(8,128)S(1)}, u32[]{:S(2)}) copy-start(f32[464,768]{1,0:T(8,128)S(1)} %get-tuple-element.162.res2) | copy-start | bytes 4276228
  33.8 30.6 %copy-start.16 = (bf16[464,768]{1,0:T(8,128)(2,1)}, bf16[464,768]{1,0:T(8,128)(2,1)S(1)}, u32[]{:S(2)}) copy-start(bf16[464,768]{1,0:T(8,128)(2,1)S(1)} %get-tuple-element.163.n3.refs_0_) | copy-start | bytes 2138116
  36.8 27.5 %copy-start.38 = (bf16[464,768]{1,0:T(8,128)(2,1)}, bf16[464,768]{1,0:T(8,128)(2,1)S(1)}, u32[]{:S(2)}) copy-start(bf16[464,768]{1,0:T(8,128)(2,1)S(1)} %collective-permute-done.refs_5_) | copy-start | bytes 2138116
  36.8 27.6 %copy-start.39 = (bf16[464,768]{1,0:T(8,128)(2,1)}, bf16[464,768]{1,0:T(8,128)(2,1)S(1)}, u32[]{:S(2)}) copy-start(bf16[464,768]{1,0:T(8,128)(2,1)S(1)} %collective-permute-done.1.refs_6_) | copy-start | bytes 2138116
  36.8 27.6 %collective-permute-start.2 = (bf16[464,768]{1,0:T(8,128)(2,1)S(1)}, bf16[464,768]{1,0:T(8,128)(2,1)S(1)}, u32[]{:S(2)}, u32[]{:S(2)}) collective-permute-start(bf16[464,768]{1,0:T(8,128)(2,1)S(1)} %get-tuple-element.163.n3.refs_0_), channel_id=1, source_target_pairs={{0,4},{1,5},{2,6},{3,7},{4,0},{5,1},{6,2},{7,3},{8,12},{9,13},{10,... | collective-permute-start | bytes 2138120 | tf_op jit(solution)/shard_map/ppermute | solution.py:656
  38.6 25.8 %collective-permute-start.3 = (bf16[464,768]{1,0:T(8,128)(2,1)S(1)}, bf16[464,768]{1,0:T(8,128)(2,1)S(1)}, u32[]{:S(2)}, u32[]{:S(2)}) collective-permute-start(bf16[464,768]{1,0:T(8,128)(2,1)S(1)} %get-tuple-element.163.n3.refs_0_), channel_id=1, source_target_pairs={{0,1},{1,0},{2,3},{3,2},{4,5},{5,4},{6,7},{7,6},{8,9},{9,8},{10,11... | collective-permute-start | bytes 2138120 | tf_op jit(solution)/shard_map/ppermute | solution.py:656
  38.7 25.8 %collective-permute-start.4 = (bf16[464,768]{1,0:T(8,128)(2,1)S(1)}, bf16[464,768]{1,0:T(8,128)(2,1)S(1)}, u32[]{:S(2)}, u32[]{:S(2)}) collective-permute-start(bf16[464,768]{1,0:T(8,128)(2,1)S(1)} %collective-permute-done.refs_5_), channel_id=1, source_target_pairs={{0,1},{1,0},{2,3},{3,2},{4,5},{5,4},{6,7},{7,6},{8,9},{9,8},{10,11... | collective-permute-start | bytes 2138120 | tf_op jit(solution)/shard_map/ppermute | solution.py:656
  64.5 2.4 collective-permute-start.5
  84.0 20.5 %collective-permute-start.6 = (bf16[2,192,768]{2,1,0:T(8,128)(2,1)S(1)}, bf16[2,192,768]{2,1,0:T(8,128)(2,1)S(1)}, u32[]{:S(2)}, u32[]{:S(2)}) collective-permute-start(bf16[2,192,768]{2,1,0:T(8,128)(2,1)S(1)} %slice_bitcast_fusion.1), channel_id=1, source_target_pairs={{0,2},{1,3},{2,0},{3,1},{4,6},{5,7},{6,4},{7,5},{8,10},{9,11},{10,... | collective-permute-start | bytes 1769480 | tf_op jit(solution)/shard_map/ppermute | solution.py:656
  85.6 18.9 %collective-permute-start.7 = (bf16[2,2,96,768]{3,2,1,0:T(8,128)(2,1)S(1)}, bf16[2,2,96,768]{3,2,1,0:T(8,128)(2,1)S(1)}, u32[]{:S(2)}, u32[]{:S(2)}) collective-permute-start(bf16[2,2,96,768]{3,2,1,0:T(8,128)(2,1)S(1)} %slice_bitcast_fusion), channel_id=1, source_target_pairs={{0,8},{1,9},{2,10},{3,11},{4,12},{5,13},{6,14},{7,15},{8,0},{9,1},... | collective-permute-start | bytes 1769480 | tf_op jit(solution)/shard_map/ppermute | solution.py:656
  104.9 9.7 %collective-permute-start.8 = (bf16[2,2,2,2,48,1920]{5,4,3,2,1,0:T(8,128)(2,1)S(1)}, bf16[2,2,2,2,48,1920]{5,4,3,2,1,0:T(8,128)(2,1)S(1)}, u32[]{:S(2)}, u32[]{:S(2)}) collective-permute-start(bf16[2,2,2,2,48,1920]{5,4,3,2,1,0:T(8,128)(2,1)S(1)} %get-tuple-element.197), channel_id=1, source_target_pairs={{0,1},{1,0},{2,3},{3,2},{4,5},{5,4},{6,7},{7,6},{8,9},{9,8},{10,11... | collective-permute-start | bytes 8847368 | tf_op jit(solution)/shard_map/ppermute | solution.py:656
  105.0 9.4 %collective-permute-start.9 = (bf16[2,96,768]{2,1,0:T(8,128)(2,1)S(1)}, bf16[2,96,768]{2,1,0:T(8,128)(2,1)S(1)}, u32[]{:S(2)}, u32[]{:S(2)}) collective-permute-start(bf16[2,96,768]{2,1,0:T(8,128)(2,1)S(1)} %slice_bitcast_fusion.13), channel_id=1, source_target_pairs={{0,2},{1,3},{2,0},{3,1},{4,6},{5,7},{6,4},{7,5},{8,10},{9,11},{10,... | collective-permute-start | bytes 884744 | tf_op jit(solution)/shard_map/ppermute | solution.py:656
  105.5 9.1 %collective-permute-start.10 = (bf16[192,768]{1,0:T(8,128)(2,1)S(1)}, bf16[192,768]{1,0:T(8,128)(2,1)S(1)}, u32[]{:S(2)}, u32[]{:S(2)}) collective-permute-start(bf16[192,768]{1,0:T(8,128)(2,1)S(1)} %slice_bitcast_fusion.12), channel_id=1, source_target_pairs={{0,8},{1,9},{2,10},{3,11},{4,12},{5,13},{6,14},{7,15},{8,0},{9,1},... | collective-permute-start | bytes 884744 | tf_op jit(solution)/shard_map/ppermute | solution.py:656
  115.3 19.0 %collective-permute-start.12 = (bf16[2,2,48,1920]{3,2,1,0:T(8,128)(2,1)S(1)}, bf16[2,2,48,1920]{3,2,1,0:T(8,128)(2,1)S(1)}, u32[]{:S(2)}, u32[]{:S(2)}) collective-permute-start(bf16[2,2,48,1920]{3,2,1,0:T(8,128)(2,1)S(1)} %get-tuple-element.213), channel_id=1, source_target_pairs={{0,4},{1,5},{2,6},{3,7},{4,0},{5,1},{6,2},{7,3},{8,12},{9,13},{10,... | collective-permute-start | bytes 2211848 | tf_op jit(solution)/shard_map/ppermute | solution.py:656
  115.9 18.4 %collective-permute-start.13 = (bf16[2,2,48,1920]{3,2,1,0:T(8,128)(2,1)S(1)}, bf16[2,2,48,1920]{3,2,1,0:T(8,128)(2,1)S(1)}, u32[]{:S(2)}, u32[]{:S(2)}) collective-permute-start(bf16[2,2,48,1920]{3,2,1,0:T(8,128)(2,1)S(1)} %get-tuple-element.214), channel_id=1, source_target_pairs={{0,2},{1,3},{2,0},{3,1},{4,6},{5,7},{6,4},{7,5},{8,10},{9,11},{10,... | collective-permute-start | bytes 2211848 | tf_op jit(solution)/shard_map/ppermute | solution.py:656
  117.4 16.9 %collective-permute-start.11 = (bf16[192,768]{1,0:T(8,128)(2,1)S(1)}, bf16[192,768]{1,0:T(8,128)(2,1)S(1)}, u32[]{:S(2)}, u32[]{:S(2)}) collective-permute-start(bf16[192,768]{1,0:T(8,128)(2,1)S(1)} %fusion.14), channel_id=1, source_target_pairs={{0,16},{1,17},{2,18},{3,19},{4,20},{5,21},{6,22},{7,23},{8,24},{9,... | collective-permute-start | bytes 884744 | tf_op jit(solution)/shard_map/ppermute | solution.py:656
  120.0 14.3 %collective-permute-start.14 = (bf16[96,768]{1,0:T(8,128)(2,1)S(1)}, bf16[96,768]{1,0:T(8,128)(2,1)S(1)}, u32[]{:S(2)}, u32[]{:S(2)}) collective-permute-start(bf16[96,768]{1,0:T(8,128)(2,1)S(1)} %get-tuple-element.215), channel_id=1, source_target_pairs={{0,1},{1,0},{2,3},{3,2},{4,5},{5,4},{6,7},{7,6},{8,9},{9,8},{10,11... | collective-permute-start | bytes 442376 | tf_op jit(solution)/shard_map/ppermute | solution.py:656
  137.3 19.4 %collective-permute-start.18 = (bf16[2,2,2,2,48,1152]{5,4,3,2,1,0:T(8,128)(2,1)}, bf16[2,2,2,2,48,1152]{5,4,3,2,1,0:T(8,128)(2,1)}, u32[]{:S(2)}, u32[]{:S(2)}) collective-permute-start(bf16[2,2,2,2,48,1152]{5,4,3,2,1,0:T(8,128)(2,1)} %get-tuple-element.233), channel_id=1, source_target_pairs={{0,1},{1,0},{2,3},{3,2},{4,5},{5,4},{6,7},{7,6},{8,9},{9,8},{10,11... | collective-permute-start | bytes 5308424 | tf_op jit(solution)/shard_map/ppermute | solution.py:656
  137.8 18.9 %collective-permute-start.16 = (bf16[2,48,1920]{2,1,0:T(8,128)(2,1)}, bf16[2,48,1920]{2,1,0:T(8,128)(2,1)}, u32[]{:S(2)}, u32[]{:S(2)}) collective-permute-start(bf16[2,48,1920]{2,1,0:T(8,128)(2,1)} %slice_bitcast_fusion.9), channel_id=1, source_target_pairs={{0,4},{1,5},{2,6},{3,7},{4,0},{5,1},{6,2},{7,3},{8,12},{9,13},{10,... | collective-permute-start | bytes 1105928 | tf_op jit(solution)/shard_map/ppermute | solution.py:656
  139.2 17.4 %collective-permute-start.17 = (bf16[2,48,1920]{2,1,0:T(8,128)(2,1)}, bf16[2,48,1920]{2,1,0:T(8,128)(2,1)}, u32[]{:S(2)}, u32[]{:S(2)}) collective-permute-start(bf16[2,48,1920]{2,1,0:T(8,128)(2,1)} %slice_bitcast_fusion.8), channel_id=1, source_target_pairs={{0,2},{1,3},{2,0},{3,1},{4,6},{5,7},{6,4},{7,5},{8,10},{9,11},{10,... | collective-permute-start | bytes 1105928 | tf_op jit(solution)/shard_map/ppermute | solution.py:656
  139.7 16.0 %collective-permute-start.15 = (bf16[2,96,768]{2,1,0:T(8,128)(2,1)}, bf16[2,96,768]{2,1,0:T(8,128)(2,1)S(1)}, u32[]{:S(2)}, u32[]{:S(2)}) collective-permute-start(bf16[2,96,768]{2,1,0:T(8,128)(2,1)} %pad_maximum_fusion.13), channel_id=1, source_target_pairs={{0,16},{1,17},{2,18},{3,19},{4,20},{5,21},{6,22},{7,23},{8,24},{9,... | collective-permute-start | bytes 884744 | tf_op jit(solution)/shard_map/ppermute | solution.py:656
  141.9 14.8 %collective-permute-start.19 = (bf16[192,768]{1,0:T(8,128)(2,1)S(1)}, bf16[192,768]{1,0:T(8,128)(2,1)}, u32[]{:S(2)}, u32[]{:S(2)}) collective-permute-start(bf16[192,768]{1,0:T(8,128)(2,1)S(1)} %add_convert_fusion.10), channel_id=1, source_target_pairs={{0,8},{1,9},{2,10},{3,11},{4,12},{5,13},{6,14},{7,15},{8,0},{9,1},... | collective-permute-start | bytes 884744 | tf_op jit(solution)/shard_map/ppermute | solution.py:656
  159.4 11.1 %collective-permute-start.20 = (bf16[2,2,48,1152]{3,2,1,0:T(8,128)(2,1)S(1)}, bf16[2,2,48,1152]{3,2,1,0:T(8,128)(2,1)S(1)}, u32[]{:S(2)}, u32[]{:S(2)}) collective-permute-start(bf16[2,2,48,1152]{3,2,1,0:T(8,128)(2,1)S(1)} %get-tuple-element.243), channel_id=1, source_target_pairs={{0,4},{1,5},{2,6},{3,7},{4,0},{5,1},{6,2},{7,3},{8,12},{9,13},{10,... | collective-permute-start | bytes 1327112 | tf_op jit(solution)/shard_map/ppermute | solution.py:656
  159.9 10.8 %collective-permute-start.21 = (bf16[2,2,48,1152]{3,2,1,0:T(8,128)(2,1)S(1)}, bf16[2,2,48,1152]{3,2,1,0:T(8,128)(2,1)S(1)}, u32[]{:S(2)}, u32[]{:S(2)}) collective-permute-start(bf16[2,2,48,1152]{3,2,1,0:T(8,128)(2,1)S(1)} %get-tuple-element.244), channel_id=1, source_target_pairs={{0,2},{1,3},{2,0},{3,1},{4,6},{5,7},{6,4},{7,5},{8,10},{9,11},{10,... | collective-permute-start | bytes 1327112 | tf_op jit(solution)/shard_map/ppermute | solution.py:656
  160.8 9.6 %collective-permute-start.22 = (bf16[2,48,1920]{2,1,0:T(8,128)(2,1)S(1)}, bf16[2,48,1920]{2,1,0:T(8,128)(2,1)S(1)}, u32[]{:S(2)}, u32[]{:S(2)}) collective-permute-start(bf16[2,48,1920]{2,1,0:T(8,128)(2,1)S(1)} %fusion.25), channel_id=1, source_target_pairs={{0,8},{1,9},{2,10},{3,11},{4,12},{5,13},{6,14},{7,15},{8,0},{9,1},... | collective-permute-start | bytes 1105928 | tf_op jit(solution)/shard_map/ppermute | solution.py:656
  161.3 7.2 %collective-permute-start.23 = (f32[16,768]{1,0:T(8,128)S(1)}, f32[16,768]{1,0:T(8,128)S(1)}, u32[]{:S(2)}, u32[]{:S(2)}) collective-permute-start(f32[16,768]{1,0:T(8,128)S(1)} %get-tuple-element.246), channel_id=1, source_target_pairs={{0,1},{1,0},{2,3},{3,2},{4,5},{5,4},{6,7},{7,6},{8,9},{9,8},{10,11... | collective-permute-start | bytes 147464 | tf_op jit(solution)/shard_map/ppermute | solution.py:656
  172.2 21.9 %copy-start.37 = (bf16[2,96,768]{2,1,0:T(8,128)(2,1)S(1)}, bf16[2,96,768]{2,1,0:T(8,128)(2,1)}, u32[]{:S(2)}) copy-start(bf16[2,96,768]{2,1,0:T(8,128)(2,1)} %copy-done.36) | copy-start | bytes 884740
  173.1 19.0 %collective-permute-start.26 = (bf16[2,192,768]{2,1,0:T(8,128)(2,1)}, bf16[2,192,768]{2,1,0:T(8,128)(2,1)S(1)}, u32[]{:S(2)}, u32[]{:S(2)}) collective-permute-start(bf16[2,192,768]{2,1,0:T(8,128)(2,1)} %pad_maximum_fusion.5), channel_id=1, source_target_pairs={{0,4},{1,5},{2,6},{3,7},{4,0},{5,1},{6,2},{7,3},{8,12},{9,13},{10,... | collective-permute-start | bytes 1769480 | tf_op jit(solution)/shard_map/ppermute | solution.py:656
  174.6 17.4 %collective-permute-start.25 = (bf16[2,48,1920]{2,1,0:T(8,128)(2,1)S(1)}, bf16[2,48,1920]{2,1,0:T(8,128)(2,1)S(1)}, u32[]{:S(2)}, u32[]{:S(2)}) collective-permute-start(bf16[2,48,1920]{2,1,0:T(8,128)(2,1)S(1)} %fusion.10), channel_id=1, source_target_pairs={{0,16},{1,17},{2,18},{3,19},{4,20},{5,21},{6,22},{7,23},{8,24},{9,... | collective-permute-start | bytes 1105928 | tf_op jit(solution)/shard_map/ppermute | solution.py:656
  174.6 17.2 %collective-permute-start.28 = (bf16[2,96,768]{2,1,0:T(8,128)(2,1)}, bf16[2,96,768]{2,1,0:T(8,128)(2,1)S(1)}, u32[]{:S(2)}, u32[]{:S(2)}) collective-permute-start(bf16[2,96,768]{2,1,0:T(8,128)(2,1)} %add_convert_fusion.9), channel_id=1, source_target_pairs={{0,8},{1,9},{2,10},{3,11},{4,12},{5,13},{6,14},{7,15},{8,0},{9,1},... | collective-permute-start | bytes 884744 | tf_op jit(solution)/shard_map/ppermute | solution.py:656
  176.9 4.4 %collective-permute-start.29 = (f32[16,768]{1,0:T(8,128)S(1)}, f32[16,768]{1,0:T(8,128)S(1)}, u32[]{:S(2)}, u32[]{:S(2)}) collective-permute-start(f32[16,768]{1,0:T(8,128)S(1)} %add.144), channel_id=1, source_target_pairs={{0,2},{1,3},{2,0},{3,1},{4,6},{5,7},{6,4},{7,5},{8,10},{9,11},{10,... | collective-permute-start | bytes 147464 | tf_op jit(solution)/shard_map/ppermute | solution.py:656
  177.6 14.2 %collective-permute-start.24 = (bf16[2,48,1152]{2,1,0:T(8,128)(2,1)S(1)}, bf16[2,48,1152]{2,1,0:T(8,128)(2,1)}, u32[]{:S(2)}, u32[]{:S(2)}) collective-permute-start(bf16[2,48,1152]{2,1,0:T(8,128)(2,1)S(1)} %slice_bitcast_fusion.21), channel_id=1, source_target_pairs={{0,4},{1,5},{2,6},{3,7},{4,0},{5,1},{6,2},{7,3},{8,12},{9,13},{10,... | collective-permute-start | bytes 663560 | tf_op jit(solution)/shard_map/ppermute | solution.py:656
  182.0 9.9 %collective-permute-start.27 = (bf16[2,48,1152]{2,1,0:T(8,128)(2,1)}, bf16[2,48,1152]{2,1,0:T(8,128)(2,1)}, u32[]{:S(2)}, u32[]{:S(2)}) collective-permute-start(bf16[2,48,1152]{2,1,0:T(8,128)(2,1)} %slice_bitcast_fusion.20), channel_id=1, source_target_pairs={{0,2},{1,3},{2,0},{3,1},{4,6},{5,7},{6,4},{7,5},{8,10},{9,11},{10,... | collective-permute-start | bytes 663560 | tf_op jit(solution)/shard_map/ppermute | solution.py:656
  194.6 15.5 %collective-permute-start.30 = (bf16[2,48,1152]{2,1,0:T(8,128)(2,1)S(1)}, bf16[2,48,1152]{2,1,0:T(8,128)(2,1)S(1)}, u32[]{:S(2)}, u32[]{:S(2)}) collective-permute-start(bf16[2,48,1152]{2,1,0:T(8,128)(2,1)S(1)} %fusion.30), channel_id=1, source_target_pairs={{0,8},{1,9},{2,10},{3,11},{4,12},{5,13},{6,14},{7,15},{8,0},{9,1},... | collective-permute-start | bytes 663560 | tf_op jit(solution)/shard_map/ppermute | solution.py:656
  195.9 14.2 %collective-permute-start.31 = (bf16[2,2,96,768]{3,2,1,0:T(8,128)(2,1)S(1)}, bf16[2,2,96,768]{3,2,1,0:T(8,128)(2,1)S(1)}, u32[]{:S(2)}, u32[]{:S(2)}) collective-permute-start(bf16[2,2,96,768]{3,2,1,0:T(8,128)(2,1)S(1)} %pad_maximum_fusion.6), channel_id=1, source_target_pairs={{0,4},{1,5},{2,6},{3,7},{4,0},{5,1},{6,2},{7,3},{8,12},{9,13},{10,... | collective-permute-start | bytes 1769480 | tf_op jit(solution)/shard_map/ppermute | solution.py:656
  197.4 12.7 %collective-permute-start.32 = (bf16[2,48,1920]{2,1,0:T(8,128)(2,1)S(1)}, bf16[2,48,1920]{2,1,0:T(8,128)(2,1)S(1)}, u32[]{:S(2)}, u32[]{:S(2)}) collective-permute-start(bf16[2,48,1920]{2,1,0:T(8,128)(2,1)S(1)} %add_convert_fusion.8), channel_id=1, source_target_pairs={{0,8},{1,9},{2,10},{3,11},{4,12},{5,13},{6,14},{7,15},{8,0},{9,1},... | collective-permute-start | bytes 1105928 | tf_op jit(solution)/shard_map/ppermute | solution.py:656
  197.9 12.1 %collective-permute-start.33 = (f32[16,768]{1,0:T(8,128)S(1)}, f32[16,768]{1,0:T(8,128)S(1)}, u32[]{:S(2)}, u32[]{:S(2)}) collective-permute-start(f32[16,768]{1,0:T(8,128)S(1)} %add.148), channel_id=1, source_target_pairs={{0,4},{1,5},{2,6},{3,7},{4,0},{5,1},{6,2},{7,3},{8,12},{9,13},{10,... | collective-permute-start | bytes 147464 | tf_op jit(solution)/shard_map/ppermute | solution.py:656
  210.3 10.2 %collective-permute-start.34 = (bf16[2,48,1152]{2,1,0:T(8,128)(2,1)S(1)}, bf16[2,48,1152]{2,1,0:T(8,128)(2,1)S(1)}, u32[]{:S(2)}, u32[]{:S(2)}) collective-permute-start(bf16[2,48,1152]{2,1,0:T(8,128)(2,1)S(1)} %fusion.19), channel_id=1, source_target_pairs={{0,16},{1,17},{2,18},{3,19},{4,20},{5,21},{6,22},{7,23},{8,24},{9,... | collective-permute-start | bytes 663560 | tf_op jit(solution)/shard_map/ppermute | solution.py:656
  212.1 16.2 %collective-permute-start.35 = (bf16[2,2,48,1920]{3,2,1,0:T(8,128)(2,1)S(1)}, bf16[2,2,48,1920]{3,2,1,0:T(8,128)(2,1)S(1)}, u32[]{:S(2)}, u32[]{:S(2)}) collective-permute-start(bf16[2,2,48,1920]{3,2,1,0:T(8,128)(2,1)S(1)} %pad_maximum_fusion.2), channel_id=1, source_target_pairs={{0,4},{1,5},{2,6},{3,7},{4,0},{5,1},{6,2},{7,3},{8,12},{9,13},{10,... | collective-permute-start | bytes 2211848 | tf_op jit(solution)/shard_map/ppermute | solution.py:656
  213.3 4.1 %collective-permute-start.36 = (f32[16,768]{1,0:T(8,128)S(1)}, f32[16,768]{1,0:T(8,128)S(1)}, u32[]{:S(2)}, u32[]{:S(2)}) collective-permute-start(f32[16,768]{1,0:T(8,128)S(1)} %add.150), channel_id=1, source_target_pairs={{0,8},{1,9},{2,10},{3,11},{4,12},{5,13},{6,14},{7,15},{8,0},{9,1},... | collective-permute-start | bytes 147464 | tf_op jit(solution)/shard_map/ppermute | solution.py:656
  230.5 10.8 %collective-permute-start.37 = (bf16[2,48,1152]{2,1,0:T(8,128)(2,1)S(1)}, bf16[2,48,1152]{2,1,0:T(8,128)(2,1)S(1)}, u32[]{:S(2)}, u32[]{:S(2)}) collective-permute-start(bf16[2,48,1152]{2,1,0:T(8,128)(2,1)S(1)} %add_convert_fusion.11), channel_id=1, source_target_pairs={{0,4},{1,5},{2,6},{3,7},{4,0},{5,1},{6,2},{7,3},{8,12},{9,13},{10,... | collective-permute-start | bytes 663560 | tf_op jit(solution)/shard_map/ppermute | solution.py:656
  231.7 9.6 %collective-permute-start.38 = (bf16[2,48,1152]{2,1,0:T(8,128)(2,1)S(1)}, bf16[2,48,1152]{2,1,0:T(8,128)(2,1)S(1)}, u32[]{:S(2)}, u32[]{:S(2)}) collective-permute-start(bf16[2,48,1152]{2,1,0:T(8,128)(2,1)S(1)} %add_convert_fusion.11), channel_id=1, source_target_pairs={{0,12},{1,13},{2,14},{3,15},{4,8},{5,9},{6,10},{7,11},{8,4},{9,5},... | collective-permute-start | bytes 663560 | tf_op jit(solution)/shard_map/ppermute | solution.py:656
  233.8 8.0 %collective-permute-start.39 = (bf16[2,48,1152]{2,1,0:T(8,128)(2,1)S(1)}, bf16[2,48,1152]{2,1,0:T(8,128)(2,1)S(1)}, u32[]{:S(2)}, u32[]{:S(2)}) collective-permute-start(bf16[2,48,1152]{2,1,0:T(8,128)(2,1)S(1)} %add_convert_fusion.11), channel_id=1, source_target_pairs={{0,8},{1,9},{2,10},{3,11},{4,12},{5,13},{6,14},{7,15},{8,0},{9,1},... | collective-permute-start | bytes 663560 | tf_op jit(solution)/shard_map/ppermute | solution.py:656
  234.0 7.3 %collective-permute-start.40 = (f32[16,768]{1,0:T(8,128)S(1)}, f32[16,768]{1,0:T(8,128)S(1)}, u32[]{:S(2)}, u32[]{:S(2)}) collective-permute-start(f32[16,768]{1,0:T(8,128)S(1)} %add.152), channel_id=1, source_target_pairs={{0,16},{1,17},{2,18},{3,19},{4,20},{5,21},{6,22},{7,23},{8,24},{9,... | collective-permute-start | bytes 147464 | tf_op jit(solution)/shard_map/ppermute | solution.py:656
  (43 other events, 490.0 us)

commit v5 on v4

--- a/solution.py
+++ b/solution.py
@@ -563,7 +563,7 @@
         compiler_params=params(),
         cost_estimate=cost(18 * rows * d * d + 24 * HEADS * rows * rows * 128, 16 * d * d),
         name="cross_back",
-    )(grad_in, res, xq, xkv, q, k, v, att, att, *far(probs), gains, wo, wq, att_self)
+    )(grad_in, res, xq, xkv, q, k, v, att, att, probs, gains, wo, wq, att_self)
 
 
 def self_back(rows, grad_in, xq, q, k, v, att, probs, wo):
@@ -585,7 +585,7 @@
         compiler_params=params(),
         cost_estimate=cost(18 * rows * d * d + 24 * HEADS * rows * rows * 128, 16 * d * d),
         name="self_back",
-    )(grad_in, xq, q, k, v, att, *far(probs), wo)
+    )(grad_in, xq, q, k, v, att, probs, wo)
 
 
 def through(parts, weights):
@@ -712,13 +712,14 @@
         elif stage == "Q":
             self.value = add(self.value, got)
         elif stage == "B":
-            self.value = jnp.stack(in_order(self.at_p, self.value, got))
+            self.value = jnp.stack([self.value, got])
         else:
             self.ends[stage] = got
 
     def together(self):
         if "H" in self.ends:
-            return in_order(self.at_x, self.value, self.ends["H"])
+            sides = [jnp.stack(in_order(self.at_p, v[0], v[1])) for v in (self.value, self.ends["H"])]
+            return in_order(self.at_x, *sides)
         rows = [
             jnp.stack(in_order(self.at_p, self.value, self.ends["A"])),
             jnp.stack(in_order(self.at_p, self.ends["G"], self.ends["D"])),

time: 248 us -> 239 us (0.964)
  other arithmetic: 19.2 us -> 12.7 us
  waiting for transfers between devices: 54.6 us -> 58.2 us
  Pallas kernels: 120 us -> 117 us
    ppermute x41, waiting for transfers between devices: 54.6 us -> 58.2 us  [hop(): return lax.ppermute(values, ('grp', 'hd'), perm)]
    another operation x3, other arithmetic: 3.38 us -> 0.3 us  [operand(): self.value = jnp.stack(self.parts)]
    convert_element_type x14, other arithmetic: 5.41 us -> 2.4 us  [add(): return total.astype(terms[0].dtype)]
  transfers between devices with their start and end apart: 41 -> 41, of which waited for: 18 -> 20; matrix products, arithmetic and copies ran while one was open for 4% -> 4% of each run, Pallas kernels for 35% -> 35%
where the time goes in v5:
time: 239 us; the launch traced here: 237 us
  Pallas kernels  117 us (49%)
  waiting for transfers between devices  58.2 us (24%)
  starting transfers between devices  39.9 us (17%)
  other arithmetic  12.7 us (5%)
  local copies, waits for them, and re-layouts  7.24 us (3%)
    ppermute x41, waiting for transfers between devices, hop(): return lax.ppermute(values, ('grp', 'hd'), perm)  58.2 us
    ppermute x41, starting transfers between devices, hop(): return lax.ppermute(values, ('grp', 'hd'), perm)  39.9 us
    pallas_call x1, Pallas kernels, hidden(): pl.pallas_call(hidden_kernel, grid=(4,), in_specs=[whole((rows, d)), whol...  25.2 us
    pallas_call x1, Pallas kernels, hidden_grads(): pl.pallas_call(functools.partial(hidden_grads_kernel, blocks), grid_spec=...  17 us
    pallas_call x1, Pallas kernels, self_forward(): pl.pallas_call(self_forward_kernel, grid=(steps,), in_specs=[smem(), whol...  16.1 us
    pallas_call x1, Pallas kernels, cross_back(): pl.pallas_call(cross_back_kernel, grid=(d // wide,), in_specs=[full, full...  15.9 us
    pallas_call x1, Pallas kernels, cross_forward(): pl.pallas_call(cross_forward_kernel, grid=(steps,), in_specs=[smem(), who...  13.1 us
    pallas_call x1, Pallas kernels, self_back(): pl.pallas_call(self_back_kernel, grid=(d // wide,), in_specs=[full, full,...  12.2 us
  transfers between devices with their start and end apart: 41, of which 20 were waited for; matrix products, arithmetic and copies ran while one was open for 4% of the time, Pallas kernels for 35%

profile of v5, /device:TPU:0, one launch (start us, length us, event | category | flops | bytes accessed | tf_op | source)
XLA Modules:
  0.0 237.1 jit_solution(6986279700449137650)
XLA Ops:
  1.5 16.1 %self_forward.1 = (bf16[464,768]{1,0:T(8,128)(2,1)}, bf16[464,768]{1,0:T(8,128)(2,1)}, bf16[464,768]{1,0:T(8,128)(2,1)}, bf16[464,768]{1,0:T(8,128)(2,1)}, bf16[...) custom-call(s32[1,4,3]{2,1,0:T(4,128)S(1)} %copy.31.lens, ...), custom_call_target="tpu_custom_call" | custom-call | flops 1 | bytes 1 | tf_op jit(solution)/shard_map/self_forward/pallas_call | solution.py:232
  17.7 3.0 %collective-permute-start = (bf16[464,768]{1,0:T(8,128)(2,1)}, bf16[464,768]{1,0:T(8,128)(2,1)S(1)}, u32[]{:S(2)}, u32[]{:S(2)}) collective-permute-start(bf16[464,768]{1,0:T(8,128)(2,1)} %get-tuple-element.160.gf.refs_4_), channel_id=1, source_target_pairs={{0,4},{1,5},{2,6},{3,7},{4,0},{5,1},{6,2},{7,3},{8,12},{9,13},{10,... | collective-permute-start | bytes 2138120 | tf_op jit(solution)/shard_map/ppermute | solution.py:656
  20.7 13.1 %cross_forward.1 = (bf16[464,768]{1,0:T(8,128)(2,1)}, bf16[464,768]{1,0:T(8,128)(2,1)}, bf16[464,768]{1,0:T(8,128)(2,1)}, bf16[12,464,464]{2,1,0:T(8,128)(2,1)},...) custom-call(s32[1,4,3]{2,1,0:T(4,128)S(1)} %copy.31.lens, ...), custom_call_target="tpu_custom_call" | custom-call | flops 1 | bytes 1 | tf_op jit(solution)/shard_map/cross_forward/pallas_call | solution.py:261
  33.8 3.0 %collective-permute-done.refs_5_ = bf16[464,768]{1,0:T(8,128)(2,1)S(1)} collective-permute-done((bf16[464,768]{1,0:T(8,128)(2,1)}, bf16[464,768]{1,0:T(8,128)(2,1)S(1)}, u32[]{:S(2)}, u32[]{:S(2)}) %collective-permute-start) | collective-permute-done | bytes 712736 | tf_op jit(solution)/shard_map/ppermute | solution.py:656
  36.8 1.8 collective-permute-start.2
  39.2 25.2 %hidden.1 = (bf16[464,3072]{1,0:T(8,128)(2,1)}, f32[464,768]{1,0:T(8,128)}, f32[8,768]{1,0:T(8,128)}) custom-call(f32[464,768]{1,0:T(8,128)S(1)} %get-tuple-element.162.res2, bf16[464,768]{1,0:T(8,128)(2,1)S(1)} %get-tuple-element.163.n3.refs_0_, bf16[464,768]{1,0:T(8,128)(2,1)} %get-tuple-element.160.gf.refs_4_, f32[3,768]{1,0:T(4,128)S(1)} %copy-done.26, ...), custom_call_target="tpu_custom_call" | custom-call | flops 1 | bytes 1 | tf_op jit(solution)/shard_map/hidden/pallas_call | solution.py:313
  64.7 2.2 collective-permute-done.5.refs_3_
  66.9 17.0 %hidden_grads.1 = (bf16[2,2,2,96,768]{4,3,2,1,0:T(8,128)(2,1)S(1)}, bf16[2,2,192,768]{3,2,1,0:T(8,128)(2,1)S(1)}) custom-call(s32[4]{0:T(128)S(1)} %pad_add_fusion.meta, bf16[464,768]{1,0:T(8,128)(2,1)} %copy-done.16, bf16[464,768]{1,0:T(8,128)(2,1)} %copy-done.35, bf16[464,768]{1,0:T(8,128)(2,1)} %copy-done.36, ...), custom_call_target="tpu_custom_call" | custom-call | flops 1 | bytes 1 | tf_op jit(solution)/shard_map/hidden_grads/pallas_call | solution.py:405
  84.0 1.6 collective-permute-start.6
  85.6 1.6 collective-permute-start.7
  87.3 15.9 %cross_back.1 = (bf16[2,2,2,2,48,1920]{5,4,3,2,1,0:T(8,128)(2,1)S(1)}, bf16[2,2,2,2,48,1920]{5,4,3,2,1,0:T(8,128)(2,1)S(1)}, bf16[464,768]{1,0:T(8,128)(2,1)}, b...) custom-call(f32[464,768]{1,0:T(8,128)S(1)} %copy-done.18, f32[464,768]{1,0:T(8,128)S(1)} %copy-done.5, ...), custom_call_target="tpu_custom_call" | custom-call | flops 1 | bytes 1 | tf_op jit(solution)/shard_map/cross_back/pallas_call | solution.py:547
  105.1 6.2 %output.1 = bf16[512,768]{1,0:T(8,128)(2,1)} custom-call(s32[1,4,3]{2,1,0:T(4,128)S(1)} %copy.31.lens, bf16[464,3072]{1,0:T(8,128)(2,1)} %get-tuple-element.195.act, f32[464,768]{1,0:T(8,128)S(1)} %copy-done.3, f32[3,768]{1,0:T(4,128)S(1)} %copy-done.28, bf16[3072,768]{1,0:T(8,128)(2,1)} %wout.3), custom_call_target="tpu_custom_call" | custom-call | flops 1 | bytes 1 | tf_op jit(solution)/shard_map/output/pallas_call | solution.py:350
  111.3 1.9 collective-permute-done.9
  114.7 1.5 collective-permute-start.13
  116.2 2.6 %collective-permute-start.11 = (bf16[192,768]{1,0:T(8,128)(2,1)S(1)}, bf16[192,768]{1,0:T(8,128)(2,1)S(1)}, u32[]{:S(2)}, u32[]{:S(2)}) collective-permute-start(bf16[192,768]{1,0:T(8,128)(2,1)S(1)} %fusion.14), channel_id=1, source_target_pairs={{0,16},{1,17},{2,18},{3,19},{4,20},{5,21},{6,22},{7,23},{8,24},{9,... | collective-permute-start | bytes 884744 | tf_op jit(solution)/shard_map/ppermute | solution.py:656
  118.8 12.2 %self_back.1 = (bf16[2,2,2,2,48,1152]{5,4,3,2,1,0:T(8,128)(2,1)S(1)}, bf16[2,2,2,2,48,1152]{5,4,3,2,1,0:T(8,128)(2,1)S(1)}, bf16[464,768]{1,0:T(8,128)(2,1)}, bf16[464,768]{1,0:T(8,128)(2,1)}, bf16[464,768]{1,0:T(8,128)(2,1)}) custom-call(f32[464,768]{1,0:T(8,128)S(1)} %copy-done.1, bf16[464,768]{1,0:T(8,128)(2,1)S(1)} %copy-done.19, ...), custom_call_target="tpu_custom_call" | custom-call | flops 1 | bytes 1 | tf_op jit(solution)/shard_map/self_back/pallas_call | solution.py:575
  131.0 0.9 collective-permute-done.12
  133.0 1.6 collective-permute-start.16
  134.6 1.4 collective-permute-start.17
  136.0 2.6 %collective-permute-start.15 = (bf16[2,96,768]{2,1,0:T(8,128)(2,1)S(1)}, bf16[2,96,768]{2,1,0:T(8,128)(2,1)S(1)}, u32[]{:S(2)}, u32[]{:S(2)}) collective-permute-start(bf16[2,96,768]{2,1,0:T(8,128)(2,1)S(1)} %pad_maximum_fusion.19), channel_id=1, source_target_pairs={{0,16},{1,17},{2,18},{3,19},{4,20},{5,21},{6,22},{7,23},{8,24},{9,... | collective-permute-start | bytes 884744 | tf_op jit(solution)/shard_map/ppermute | solution.py:656
  139.1 6.7 %radar.4 = (f32[512,768]{1,0:T(8,128)}, f32[16,768]{1,0:T(8,128)S(1)}) custom-call(bf16[464,768]{1,0:T(8,128)(2,1)} %get-tuple-element.222.dq, bf16[464,768]{1,0:T(8,128)(2,1)} %get-tuple-element.223.dk, bf16[464,768]{1,0:T(8,128)(2,1)} %get-tuple-element.224.dv, bf16[768,2304]{1,0:T(8,128)(2,1)} %weights.2, f32[464,768]{1,0:T(8,128)} %get-tuple-element.205.grad_in, ...), custom_call_target="tpu_custom_call" | custom-call | flops 1 | bytes 1 | tf_op jit(solution)/shard_map/radar/pallas_call | solution.py:645
  145.8 6.2 %collective-permute-done.15 = bf16[2,96,768]{2,1,0:T(8,128)(2,1)S(1)} collective-permute-done((bf16[2,96,768]{2,1,0:T(8,128)(2,1)S(1)}, bf16[2,96,768]{2,1,0:T(8,128)(2,1)S(1)}, u32[]{:S(2)}, u32[]{:S(2)}) %collective-permute-start.15) | collective-permute-done | bytes 294944 | tf_op jit(solution)/shard_map/ppermute | solution.py:656
  152.0 1.3 collective-permute-done.19
  156.4 4.6 %optic.3 = f32[512,768]{1,0:T(8,128)} custom-call(bf16[464,768]{1,0:T(8,128)(2,1)} %get-tuple-element.241.dk, bf16[464,768]{1,0:T(8,128)(2,1)} %get-tuple-element.242.dv, bf16[768,1536]{1,0:T(8,128)(2,1)} %weights.3), custom_call_target="tpu_custom_call" | custom-call | flops 1 | bytes 1 | tf_op jit(solution)/shard_map/optic/pallas_call | solution.py:613
  161.0 2.7 %collective-permute-done.22 = bf16[2,48,1920]{2,1,0:T(8,128)(2,1)S(1)} collective-permute-done((bf16[2,48,1920]{2,1,0:T(8,128)(2,1)S(1)}, bf16[2,48,1920]{2,1,0:T(8,128)(2,1)S(1)}, u32[]{:S(2)}, u32[]{:S(2)}) %collective-permute-start.22) | collective-permute-done | bytes 368672 | tf_op jit(solution)/shard_map/ppermute | solution.py:656
  163.7 1.0 collective-permute-done.20
  166.0 1.5 collective-permute-start.26
  167.5 2.2 collective-permute-start.28
  171.2 3.1 %collective-permute-done.29 = f32[16,768]{1,0:T(8,128)S(1)} collective-permute-done((f32[16,768]{1,0:T(8,128)S(1)}, f32[16,768]{1,0:T(8,128)S(1)}, u32[]{:S(2)}, u32[]{:S(2)}) %collective-permute-start.29) | collective-permute-done | bytes 49184 | tf_op jit(solution)/shard_map/ppermute | solution.py:656
  174.3 0.9 collective-permute-start.27
  175.3 8.4 %collective-permute-done.24 = bf16[2,48,1152]{2,1,0:T(8,128)(2,1)S(1)} collective-permute-done((bf16[2,48,1152]{2,1,0:T(8,128)(2,1)S(1)}, bf16[2,48,1152]{2,1,0:T(8,128)(2,1)S(1)}, u32[]{:S(2)}, u32[]{:S(2)}) %collective-permute-start.24) | collective-permute-done | bytes 221216 | tf_op jit(solution)/shard_map/ppermute | solution.py:656
  184.3 1.1 collective-permute-start.30
  185.4 1.5 collective-permute-start.31
  188.5 1.1 select_bitcast_fusion.3
  189.8 1.7 bitcast_convert_fusion
  191.6 8.4 %collective-permute-done.33 = f32[16,768]{1,0:T(8,128)S(1)} collective-permute-done((f32[16,768]{1,0:T(8,128)S(1)}, f32[16,768]{1,0:T(8,128)S(1)}, u32[]{:S(2)}, u32[]{:S(2)}) %collective-permute-start.33) | collective-permute-done | bytes 49184 | tf_op jit(solution)/shard_map/ppermute | solution.py:656
  200.2 2.6 %collective-permute-start.34 = (bf16[2,48,1152]{2,1,0:T(8,128)(2,1)S(1)}, bf16[2,48,1152]{2,1,0:T(8,128)(2,1)S(1)}, u32[]{:S(2)}, u32[]{:S(2)}) collective-permute-start(bf16[2,48,1152]{2,1,0:T(8,128)(2,1)S(1)} %fusion.19), channel_id=1, source_target_pairs={{0,16},{1,17},{2,18},{3,19},{4,20},{5,21},{6,22},{7,23},{8,24},{9,... | collective-permute-start | bytes 663560 | tf_op jit(solution)/shard_map/ppermute | solution.py:656
  204.5 1.7 convert_element_type.445
  206.1 1.3 collective-permute-done.36
  207.4 4.3 %collective-permute-done.34 = bf16[2,48,1152]{2,1,0:T(8,128)(2,1)S(1)} collective-permute-done((bf16[2,48,1152]{2,1,0:T(8,128)(2,1)S(1)}, bf16[2,48,1152]{2,1,0:T(8,128)(2,1)S(1)}, u32[]{:S(2)}, u32[]{:S(2)}) %collective-permute-start.34) | collective-permute-done | bytes 221216 | tf_op jit(solution)/shard_map/ppermute | solution.py:656
  211.7 7.8 %collective-permute-done.35 = bf16[2,2,48,1920]{3,2,0,1:T(8,128)(2,1)S(1)} collective-permute-done((bf16[2,2,48,1920]{3,2,0,1:T(8,128)(2,1)S(1)}, bf16[2,2,48,1920]{3,2,0,1:T(8,128)(2,1)S(1)}, u32[]{:S(2)}, u32[]{:S(2)}) %collective-permute-start.35) | collective-permute-done | bytes 737312 | tf_op jit(solution)/shard_map/ppermute | solution.py:656
  220.3 1.2 fusion.32
  222.1 1.9 collective-permute-start.38
  223.9 1.3 collective-permute-start.39
  227.5 1.2 slice.335
  228.7 3.3 %collective-permute-done.40 = f32[16,768]{1,0:T(8,128)S(1)} collective-permute-done((f32[16,768]{1,0:T(8,128)S(1)}, f32[16,768]{1,0:T(8,128)S(1)}, u32[]{:S(2)}, u32[]{:S(2)}) %collective-permute-start.40) | collective-permute-done | bytes 49184 | tf_op jit(solution)/shard_map/ppermute | solution.py:656
  232.0 1.5 collective-permute-done.39
  234.9 1.3 pad_maximum_fusion
  (234 shorter events, 22.3 us)
Async XLA Ops:
  0.6 38.5 %slice-start.2 = ((s8[4718592]{0:T(1024)(128)(4,1)}), s8[524288]{0:T(1024)(128)(4,1)S(1)}, s32[]{:S(2)}) async-start(s8[4718592]{0:T(1024)(128)(4,1)} %bitcast.201), calls=%async_computation.2 | async-start | bytes 1048576
  1.5 37.6 %slice-start.3 = ((s8[4718592]{0:T(1024)(128)(4,1)}), s8[4194304]{0:T(1024)(128)(4,1)S(1)}, s32[]{:S(2)}) async-start(s8[4718592]{0:T(1024)(128)(4,1)} %bitcast.201), calls=%async_computation.3 | async-start | bytes 8388608
  17.7 19.2 %collective-permute-start = (bf16[464,768]{1,0:T(8,128)(2,1)}, bf16[464,768]{1,0:T(8,128)(2,1)S(1)}, u32[]{:S(2)}, u32[]{:S(2)}) collective-permute-start(bf16[464,768]{1,0:T(8,128)(2,1)} %get-tuple-element.160.gf.refs_4_), channel_id=1, source_target_pairs={{0,4},{1,5},{2,6},{3,7},{4,0},{5,1},{6,2},{7,3},{8,12},{9,13},{10,... | collective-permute-start | bytes 2138120 | tf_op jit(solution)/shard_map/ppermute | solution.py:656
  20.7 16.2 %collective-permute-start.1 = (bf16[464,768]{1,0:T(8,128)(2,1)}, bf16[464,768]{1,0:T(8,128)(2,1)S(1)}, u32[]{:S(2)}, u32[]{:S(2)}) collective-permute-start(bf16[464,768]{1,0:T(8,128)(2,1)} %get-tuple-element.160.gf.refs_4_), channel_id=1, source_target_pairs={{0,1},{1,0},{2,3},{3,2},{4,5},{5,4},{6,7},{7,6},{8,9},{9,8},{10,11... | collective-permute-start | bytes 2138120 | tf_op jit(solution)/shard_map/ppermute | solution.py:656
  33.8 30.6 %copy-start.2 = (f32[464,768]{1,0:T(8,128)}, f32[464,768]{1,0:T(8,128)S(1)}, u32[]{:S(2)}) copy-start(f32[464,768]{1,0:T(8,128)S(1)} %get-tuple-element.162.res2) | copy-start | bytes 4276228
  33.8 30.6 %copy-start.16 = (bf16[464,768]{1,0:T(8,128)(2,1)}, bf16[464,768]{1,0:T(8,128)(2,1)S(1)}, u32[]{:S(2)}) copy-start(bf16[464,768]{1,0:T(8,128)(2,1)S(1)} %get-tuple-element.163.n3.refs_0_) | copy-start | bytes 2138116
  36.8 27.6 %copy-start.33 = (bf16[464,768]{1,0:T(8,128)(2,1)}, bf16[464,768]{1,0:T(8,128)(2,1)S(1)}, u32[]{:S(2)}) copy-start(bf16[464,768]{1,0:T(8,128)(2,1)S(1)} %collective-permute-done.refs_5_) | copy-start | bytes 2138116
  36.8 27.6 %copy-start.34 = (bf16[464,768]{1,0:T(8,128)(2,1)}, bf16[464,768]{1,0:T(8,128)(2,1)S(1)}, u32[]{:S(2)}) copy-start(bf16[464,768]{1,0:T(8,128)(2,1)S(1)} %collective-permute-done.1.refs_6_) | copy-start | bytes 2138116
  36.8 27.6 %collective-permute-start.2 = (bf16[464,768]{1,0:T(8,128)(2,1)S(1)}, bf16[464,768]{1,0:T(8,128)(2,1)S(1)}, u32[]{:S(2)}, u32[]{:S(2)}) collective-permute-start(bf16[464,768]{1,0:T(8,128)(2,1)S(1)} %get-tuple-element.163.n3.refs_0_), channel_id=1, source_target_pairs={{0,4},{1,5},{2,6},{3,7},{4,0},{5,1},{6,2},{7,3},{8,12},{9,13},{10,... | collective-permute-start | bytes 2138120 | tf_op jit(solution)/shard_map/ppermute | solution.py:656
  38.6 25.8 %collective-permute-start.3 = (bf16[464,768]{1,0:T(8,128)(2,1)S(1)}, bf16[464,768]{1,0:T(8,128)(2,1)S(1)}, u32[]{:S(2)}, u32[]{:S(2)}) collective-permute-start(bf16[464,768]{1,0:T(8,128)(2,1)S(1)} %get-tuple-element.163.n3.refs_0_), channel_id=1, source_target_pairs={{0,1},{1,0},{2,3},{3,2},{4,5},{5,4},{6,7},{7,6},{8,9},{9,8},{10,11... | collective-permute-start | bytes 2138120 | tf_op jit(solution)/shard_map/ppermute | solution.py:656
  38.6 25.8 %collective-permute-start.4 = (bf16[464,768]{1,0:T(8,128)(2,1)S(1)}, bf16[464,768]{1,0:T(8,128)(2,1)S(1)}, u32[]{:S(2)}, u32[]{:S(2)}) collective-permute-start(bf16[464,768]{1,0:T(8,128)(2,1)S(1)} %collective-permute-done.refs_5_), channel_id=1, source_target_pairs={{0,1},{1,0},{2,3},{3,2},{4,5},{5,4},{6,7},{7,6},{8,9},{9,8},{10,11... | collective-permute-start | bytes 2138120 | tf_op jit(solution)/shard_map/ppermute | solution.py:656
  64.5 2.4 %collective-permute-start.5 = (bf16[464,768]{1,0:T(8,128)(2,1)S(1)}, bf16[464,768]{1,0:T(8,128)(2,1)}, u32[]{:S(2)}, u32[]{:S(2)}) collective-permute-start(bf16[464,768]{1,0:T(8,128)(2,1)S(1)} %collective-permute-done.2.refs_1_), channel_id=1, source_target_pairs={{0,1},{1,0},{2,3},{3,2},{4,5},{5,4},{6,7},{7,6},{8,9},{9,8},{10,11... | collective-permute-start | bytes 2138120 | tf_op jit(solution)/shard_map/ppermute | solution.py:656
  64.6 22.6 %slice-start.6 = ((s8[5701632]{0:T(1024)(128)(4,1)}), s8[4194304]{0:T(1024)(128)(4,1)S(1)}, s32[]{:S(2)}) async-start(s8[5701632]{0:T(1024)(128)(4,1)} %bitcast.205), calls=%async_computation.6 | async-start | bytes 8388608
  84.0 19.2 %collective-permute-start.6 = (bf16[2,192,768]{2,1,0:T(8,128)(2,1)S(1)}, bf16[2,192,768]{2,1,0:T(8,128)(2,1)S(1)}, u32[]{:S(2)}, u32[]{:S(2)}) collective-permute-start(bf16[2,192,768]{2,1,0:T(8,128)(2,1)S(1)} %slice_bitcast_fusion.1), channel_id=1, source_target_pairs={{0,2},{1,3},{2,0},{3,1},{4,6},{5,7},{6,4},{7,5},{8,10},{9,11},{10,... | collective-permute-start | bytes 1769480 | tf_op jit(solution)/shard_map/ppermute | solution.py:656
  85.6 17.6 %collective-permute-start.7 = (bf16[2,2,96,768]{3,2,1,0:T(8,128)(2,1)S(1)}, bf16[2,2,96,768]{3,2,1,0:T(8,128)(2,1)S(1)}, u32[]{:S(2)}, u32[]{:S(2)}) collective-permute-start(bf16[2,2,96,768]{3,2,1,0:T(8,128)(2,1)S(1)} %slice_bitcast_fusion), channel_id=1, source_target_pairs={{0,8},{1,9},{2,10},{3,11},{4,12},{5,13},{6,14},{7,15},{8,0},{9,1},... | collective-permute-start | bytes 1769480 | tf_op jit(solution)/shard_map/ppermute | solution.py:656
  103.7 9.7 %collective-permute-start.8 = (bf16[2,2,2,2,48,1920]{5,4,3,2,1,0:T(8,128)(2,1)S(1)}, bf16[2,2,2,2,48,1920]{5,4,3,2,1,0:T(8,128)(2,1)S(1)}, u32[]{:S(2)}, u32[]{:S(2)}) collective-permute-start(bf16[2,2,2,2,48,1920]{5,4,3,2,1,0:T(8,128)(2,1)S(1)} %get-tuple-element.197), channel_id=1, source_target_pairs={{0,1},{1,0},{2,3},{3,2},{4,5},{5,4},{6,7},{7,6},{8,9},{9,8},{10,11... | collective-permute-start | bytes 8847368 | tf_op jit(solution)/shard_map/ppermute | solution.py:656
  103.7 9.4 %collective-permute-start.9 = (bf16[2,96,768]{2,1,0:T(8,128)(2,1)S(1)}, bf16[2,96,768]{2,1,0:T(8,128)(2,1)S(1)}, u32[]{:S(2)}, u32[]{:S(2)}) collective-permute-start(bf16[2,96,768]{2,1,0:T(8,128)(2,1)S(1)} %slice_bitcast_fusion.13), channel_id=1, source_target_pairs={{0,2},{1,3},{2,0},{3,1},{4,6},{5,7},{6,4},{7,5},{8,10},{9,11},{10,... | collective-permute-start | bytes 884744 | tf_op jit(solution)/shard_map/ppermute | solution.py:656
  104.3 9.1 %collective-permute-start.10 = (bf16[192,768]{1,0:T(8,128)(2,1)S(1)}, bf16[192,768]{1,0:T(8,128)(2,1)S(1)}, u32[]{:S(2)}, u32[]{:S(2)}) collective-permute-start(bf16[192,768]{1,0:T(8,128)(2,1)S(1)} %slice_bitcast_fusion.12), channel_id=1, source_target_pairs={{0,8},{1,9},{2,10},{3,11},{4,12},{5,13},{6,14},{7,15},{8,0},{9,1},... | collective-permute-start | bytes 884744 | tf_op jit(solution)/shard_map/ppermute | solution.py:656
  114.1 17.9 %collective-permute-start.12 = (bf16[2,2,48,1920]{3,2,1,0:T(8,128)(2,1)S(1)}, bf16[2,2,48,1920]{3,2,1,0:T(8,128)(2,1)S(1)}, u32[]{:S(2)}, u32[]{:S(2)}) collective-permute-start(bf16[2,2,48,1920]{3,2,1,0:T(8,128)(2,1)S(1)} %get-tuple-element.213), channel_id=1, source_target_pairs={{0,4},{1,5},{2,6},{3,7},{4,0},{5,1},{6,2},{7,3},{8,12},{9,13},{10,... | collective-permute-start | bytes 2211848 | tf_op jit(solution)/shard_map/ppermute | solution.py:656
  114.7 17.5 %collective-permute-start.13 = (bf16[2,2,48,1920]{3,2,1,0:T(8,128)(2,1)S(1)}, bf16[2,2,48,1920]{3,2,1,0:T(8,128)(2,1)S(1)}, u32[]{:S(2)}, u32[]{:S(2)}) collective-permute-start(bf16[2,2,48,1920]{3,2,1,0:T(8,128)(2,1)S(1)} %get-tuple-element.214), channel_id=1, source_target_pairs={{0,2},{1,3},{2,0},{3,1},{4,6},{5,7},{6,4},{7,5},{8,10},{9,11},{10,... | collective-permute-start | bytes 2211848 | tf_op jit(solution)/shard_map/ppermute | solution.py:656
  116.2 14.9 %collective-permute-start.11 = (bf16[192,768]{1,0:T(8,128)(2,1)S(1)}, bf16[192,768]{1,0:T(8,128)(2,1)S(1)}, u32[]{:S(2)}, u32[]{:S(2)}) collective-permute-start(bf16[192,768]{1,0:T(8,128)(2,1)S(1)} %fusion.14), channel_id=1, source_target_pairs={{0,16},{1,17},{2,18},{3,19},{4,20},{5,21},{6,22},{7,23},{8,24},{9,... | collective-permute-start | bytes 884744 | tf_op jit(solution)/shard_map/ppermute | solution.py:656
  118.8 12.3 %collective-permute-start.14 = (bf16[96,768]{1,0:T(8,128)(2,1)S(1)}, bf16[96,768]{1,0:T(8,128)(2,1)S(1)}, u32[]{:S(2)}, u32[]{:S(2)}) collective-permute-start(bf16[96,768]{1,0:T(8,128)(2,1)S(1)} %get-tuple-element.215), channel_id=1, source_target_pairs={{0,1},{1,0},{2,3},{3,2},{4,5},{5,4},{6,7},{7,6},{8,9},{9,8},{10,11... | collective-permute-start | bytes 442376 | tf_op jit(solution)/shard_map/ppermute | solution.py:656
  132.9 20.4 %collective-permute-start.18 = (bf16[2,2,2,2,48,1152]{5,4,3,2,1,0:T(8,128)(2,1)S(1)}, bf16[2,2,2,2,48,1152]{5,4,3,2,1,0:T(8,128)(2,1)S(1)}, u32[]{:S(2)}, u32[]{:S(2)}) collective-permute-start(bf16[2,2,2,2,48,1152]{5,4,3,2,1,0:T(8,128)(2,1)S(1)} %get-tuple-element.233), channel_id=1, source_target_pairs={{0,1},{1,0},{2,3},{3,2},{4,5},{5,4},{6,7},{7,6},{8,9},{9,8},{10,11... | collective-permute-start | bytes 5308424 | tf_op jit(solution)/shard_map/ppermute | solution.py:656
  133.0 20.3 %collective-permute-start.16 = (bf16[2,48,1920]{2,1,0:T(8,128)(2,1)S(1)}, bf16[2,48,1920]{2,1,0:T(8,128)(2,1)S(1)}, u32[]{:S(2)}, u32[]{:S(2)}) collective-permute-start(bf16[2,48,1920]{2,1,0:T(8,128)(2,1)S(1)} %slice_bitcast_fusion.9), channel_id=1, source_target_pairs={{0,4},{1,5},{2,6},{3,7},{4,0},{5,1},{6,2},{7,3},{8,12},{9,13},{10,... | collective-permute-start | bytes 1105928 | tf_op jit(solution)/shard_map/ppermute | solution.py:656
  134.6 18.8 %collective-permute-start.17 = (bf16[2,48,1920]{2,1,0:T(8,128)(2,1)S(1)}, bf16[2,48,1920]{2,1,0:T(8,128)(2,1)S(1)}, u32[]{:S(2)}, u32[]{:S(2)}) collective-permute-start(bf16[2,48,1920]{2,1,0:T(8,128)(2,1)S(1)} %slice_bitcast_fusion.8), channel_id=1, source_target_pairs={{0,2},{1,3},{2,0},{3,1},{4,6},{5,7},{6,4},{7,5},{8,10},{9,11},{10,... | collective-permute-start | bytes 1105928 | tf_op jit(solution)/shard_map/ppermute | solution.py:656
  136.0 16.0 %collective-permute-start.15 = (bf16[2,96,768]{2,1,0:T(8,128)(2,1)S(1)}, bf16[2,96,768]{2,1,0:T(8,128)(2,1)S(1)}, u32[]{:S(2)}, u32[]{:S(2)}) collective-permute-start(bf16[2,96,768]{2,1,0:T(8,128)(2,1)S(1)} %pad_maximum_fusion.19), channel_id=1, source_target_pairs={{0,16},{1,17},{2,18},{3,19},{4,20},{5,21},{6,22},{7,23},{8,24},{9,... | collective-permute-start | bytes 884744 | tf_op jit(solution)/shard_map/ppermute | solution.py:656
  138.6 14.7 %collective-permute-start.19 = (bf16[192,768]{1,0:T(8,128)(2,1)S(1)}, bf16[192,768]{1,0:T(8,128)(2,1)S(1)}, u32[]{:S(2)}, u32[]{:S(2)}) collective-permute-start(bf16[192,768]{1,0:T(8,128)(2,1)S(1)} %add_convert_fusion.10), channel_id=1, source_target_pairs={{0,8},{1,9},{2,10},{3,11},{4,12},{5,13},{6,14},{7,15},{8,0},{9,1},... | collective-permute-start | bytes 884744 | tf_op jit(solution)/shard_map/ppermute | solution.py:656
  153.8 10.8 %collective-permute-start.20 = (bf16[2,2,48,1152]{3,2,1,0:T(8,128)(2,1)S(1)}, bf16[2,2,48,1152]{3,2,1,0:T(8,128)(2,1)S(1)}, u32[]{:S(2)}, u32[]{:S(2)}) collective-permute-start(bf16[2,2,48,1152]{3,2,1,0:T(8,128)(2,1)S(1)} %get-tuple-element.243), channel_id=1, source_target_pairs={{0,4},{1,5},{2,6},{3,7},{4,0},{5,1},{6,2},{7,3},{8,12},{9,13},{10,... | collective-permute-start | bytes 1327112 | tf_op jit(solution)/shard_map/ppermute | solution.py:656
  154.4 10.4 %collective-permute-start.21 = (bf16[2,2,48,1152]{3,2,1,0:T(8,128)(2,1)S(1)}, bf16[2,2,48,1152]{3,2,1,0:T(8,128)(2,1)S(1)}, u32[]{:S(2)}, u32[]{:S(2)}) collective-permute-start(bf16[2,2,48,1152]{3,2,1,0:T(8,128)(2,1)S(1)} %get-tuple-element.244), channel_id=1, source_target_pairs={{0,2},{1,3},{2,0},{3,1},{4,6},{5,7},{6,4},{7,5},{8,10},{9,11},{10,... | collective-permute-start | bytes 1327112 | tf_op jit(solution)/shard_map/ppermute | solution.py:656
  155.0 8.7 %collective-permute-start.22 = (bf16[2,48,1920]{2,1,0:T(8,128)(2,1)S(1)}, bf16[2,48,1920]{2,1,0:T(8,128)(2,1)S(1)}, u32[]{:S(2)}, u32[]{:S(2)}) collective-permute-start(bf16[2,48,1920]{2,1,0:T(8,128)(2,1)S(1)} %fusion.25), channel_id=1, source_target_pairs={{0,8},{1,9},{2,10},{3,11},{4,12},{5,13},{6,14},{7,15},{8,0},{9,1},... | collective-permute-start | bytes 1105928 | tf_op jit(solution)/shard_map/ppermute | solution.py:656
  155.5 5.5 %collective-permute-start.23 = (f32[16,768]{1,0:T(8,128)S(1)}, f32[16,768]{1,0:T(8,128)S(1)}, u32[]{:S(2)}, u32[]{:S(2)}) collective-permute-start(f32[16,768]{1,0:T(8,128)S(1)} %get-tuple-element.246), channel_id=1, source_target_pairs={{0,1},{1,0},{2,3},{3,2},{4,5},{5,4},{6,7},{7,6},{8,9},{9,8},{10,11... | collective-permute-start | bytes 147464 | tf_op jit(solution)/shard_map/ppermute | solution.py:656
  166.0 18.0 %collective-permute-start.26 = (bf16[2,192,768]{2,1,0:T(8,128)(2,1)}, bf16[2,192,768]{2,1,0:T(8,128)(2,1)}, u32[]{:S(2)}, u32[]{:S(2)}) collective-permute-start(bf16[2,192,768]{2,1,0:T(8,128)(2,1)} %pad_maximum_fusion.7), channel_id=1, source_target_pairs={{0,4},{1,5},{2,6},{3,7},{4,0},{5,1},{6,2},{7,3},{8,12},{9,13},{10,... | collective-permute-start | bytes 1769480 | tf_op jit(solution)/shard_map/ppermute | solution.py:656
  167.5 16.5 %collective-permute-start.25 = (bf16[2,48,1920]{2,1,0:T(8,128)(2,1)S(1)}, bf16[2,48,1920]{2,1,0:T(8,128)(2,1)S(1)}, u32[]{:S(2)}, u32[]{:S(2)}) collective-permute-start(bf16[2,48,1920]{2,1,0:T(8,128)(2,1)S(1)} %fusion.10), channel_id=1, source_target_pairs={{0,16},{1,17},{2,18},{3,19},{4,20},{5,21},{6,22},{7,23},{8,24},{9,... | collective-permute-start | bytes 1105928 | tf_op jit(solution)/shard_map/ppermute | solution.py:656
  167.5 16.2 %collective-permute-start.28 = (bf16[2,96,768]{2,1,0:T(8,128)(2,1)S(1)}, bf16[2,96,768]{2,1,0:T(8,128)(2,1)S(1)}, u32[]{:S(2)}, u32[]{:S(2)}) collective-permute-start(bf16[2,96,768]{2,1,0:T(8,128)(2,1)S(1)} %add_convert_fusion.9), channel_id=1, source_target_pairs={{0,8},{1,9},{2,10},{3,11},{4,12},{5,13},{6,14},{7,15},{8,0},{9,1},... | collective-permute-start | bytes 884744 | tf_op jit(solution)/shard_map/ppermute | solution.py:656
  169.8 4.5 %collective-permute-start.29 = (f32[16,768]{1,0:T(8,128)S(1)}, f32[16,768]{1,0:T(8,128)S(1)}, u32[]{:S(2)}, u32[]{:S(2)}) collective-permute-start(f32[16,768]{1,0:T(8,128)S(1)} %add.144), channel_id=1, source_target_pairs={{0,2},{1,3},{2,0},{3,1},{4,6},{5,7},{6,4},{7,5},{8,10},{9,11},{10,... | collective-permute-start | bytes 147464 | tf_op jit(solution)/shard_map/ppermute | solution.py:656
  170.6 13.1 %collective-permute-start.24 = (bf16[2,48,1152]{2,1,0:T(8,128)(2,1)S(1)}, bf16[2,48,1152]{2,1,0:T(8,128)(2,1)S(1)}, u32[]{:S(2)}, u32[]{:S(2)}) collective-permute-start(bf16[2,48,1152]{2,1,0:T(8,128)(2,1)S(1)} %slice_bitcast_fusion.21), channel_id=1, source_target_pairs={{0,4},{1,5},{2,6},{3,7},{4,0},{5,1},{6,2},{7,3},{8,12},{9,13},{10,... | collective-permute-start | bytes 663560 | tf_op jit(solution)/shard_map/ppermute | solution.py:656
  174.3 9.4 %collective-permute-start.27 = (bf16[2,48,1152]{2,1,0:T(8,128)(2,1)}, bf16[2,48,1152]{2,1,0:T(8,128)(2,1)S(1)}, u32[]{:S(2)}, u32[]{:S(2)}) collective-permute-start(bf16[2,48,1152]{2,1,0:T(8,128)(2,1)} %slice_bitcast_fusion.20), channel_id=1, source_target_pairs={{0,2},{1,3},{2,0},{3,1},{4,6},{5,7},{6,4},{7,5},{8,10},{9,11},{10,... | collective-permute-start | bytes 663560 | tf_op jit(solution)/shard_map/ppermute | solution.py:656
  184.3 15.7 %collective-permute-start.30 = (bf16[2,48,1152]{2,1,0:T(8,128)(2,1)S(1)}, bf16[2,48,1152]{2,1,0:T(8,128)(2,1)S(1)}, u32[]{:S(2)}, u32[]{:S(2)}) collective-permute-start(bf16[2,48,1152]{2,1,0:T(8,128)(2,1)S(1)} %fusion.30), channel_id=1, source_target_pairs={{0,8},{1,9},{2,10},{3,11},{4,12},{5,13},{6,14},{7,15},{8,0},{9,1},... | collective-permute-start | bytes 663560 | tf_op jit(solution)/shard_map/ppermute | solution.py:656
  185.4 14.6 %collective-permute-start.31 = (bf16[2,2,96,768]{3,2,1,0:T(8,128)(2,1)S(1)}, bf16[2,2,96,768]{3,2,1,0:T(8,128)(2,1)S(1)}, u32[]{:S(2)}, u32[]{:S(2)}) collective-permute-start(bf16[2,2,96,768]{3,2,1,0:T(8,128)(2,1)S(1)} %pad_maximum_fusion.8), channel_id=1, source_target_pairs={{0,4},{1,5},{2,6},{3,7},{4,0},{5,1},{6,2},{7,3},{8,12},{9,13},{10,... | collective-permute-start | bytes 1769480 | tf_op jit(solution)/shard_map/ppermute | solution.py:656
  186.9 13.2 %collective-permute-start.32 = (bf16[2,48,1920]{2,1,0:T(8,128)(2,1)S(1)}, bf16[2,48,1920]{2,1,0:T(8,128)(2,1)S(1)}, u32[]{:S(2)}, u32[]{:S(2)}) collective-permute-start(bf16[2,48,1920]{2,1,0:T(8,128)(2,1)S(1)} %add_convert_fusion.8), channel_id=1, source_target_pairs={{0,8},{1,9},{2,10},{3,11},{4,12},{5,13},{6,14},{7,15},{8,0},{9,1},... | collective-permute-start | bytes 1105928 | tf_op jit(solution)/shard_map/ppermute | solution.py:656
  187.6 12.4 %collective-permute-start.33 = (f32[16,768]{1,0:T(8,128)S(1)}, f32[16,768]{1,0:T(8,128)S(1)}, u32[]{:S(2)}, u32[]{:S(2)}) collective-permute-start(f32[16,768]{1,0:T(8,128)S(1)} %add.148), channel_id=1, source_target_pairs={{0,4},{1,5},{2,6},{3,7},{4,0},{5,1},{6,2},{7,3},{8,12},{9,13},{10,... | collective-permute-start | bytes 147464 | tf_op jit(solution)/shard_map/ppermute | solution.py:656
  200.2 11.5 %collective-permute-start.34 = (bf16[2,48,1152]{2,1,0:T(8,128)(2,1)S(1)}, bf16[2,48,1152]{2,1,0:T(8,128)(2,1)S(1)}, u32[]{:S(2)}, u32[]{:S(2)}) collective-permute-start(bf16[2,48,1152]{2,1,0:T(8,128)(2,1)S(1)} %fusion.19), channel_id=1, source_target_pairs={{0,16},{1,17},{2,18},{3,19},{4,20},{5,21},{6,22},{7,23},{8,24},{9,... | collective-permute-start | bytes 663560 | tf_op jit(solution)/shard_map/ppermute | solution.py:656
  202.8 16.7 %collective-permute-start.35 = (bf16[2,2,48,1920]{3,2,0,1:T(8,128)(2,1)S(1)}, bf16[2,2,48,1920]{3,2,0,1:T(8,128)(2,1)S(1)}, u32[]{:S(2)}, u32[]{:S(2)}) collective-permute-start(bf16[2,2,48,1920]{3,2,0,1:T(8,128)(2,1)S(1)} %pad_maximum_fusion.2), channel_id=1, source_target_pairs={{0,4},{1,5},{2,6},{3,7},{4,0},{5,1},{6,2},{7,3},{8,12},{9,13},{10,... | collective-permute-start | bytes 2211848 | tf_op jit(solution)/shard_map/ppermute | solution.py:656
  203.3 4.1 %collective-permute-start.36 = (f32[16,768]{1,0:T(8,128)S(1)}, f32[16,768]{1,0:T(8,128)S(1)}, u32[]{:S(2)}, u32[]{:S(2)}) collective-permute-start(f32[16,768]{1,0:T(8,128)S(1)} %add.150), channel_id=1, source_target_pairs={{0,8},{1,9},{2,10},{3,11},{4,12},{5,13},{6,14},{7,15},{8,0},{9,1},... | collective-permute-start | bytes 147464 | tf_op jit(solution)/shard_map/ppermute | solution.py:656
  221.8 10.2 %collective-permute-start.37 = (bf16[2,48,1152]{2,1,0:T(8,128)(2,1)S(1)}, bf16[2,48,1152]{2,1,0:T(8,128)(2,1)S(1)}, u32[]{:S(2)}, u32[]{:S(2)}) collective-permute-start(bf16[2,48,1152]{2,1,0:T(8,128)(2,1)S(1)} %add_convert_fusion.11), channel_id=1, source_target_pairs={{0,4},{1,5},{2,6},{3,7},{4,0},{5,1},{6,2},{7,3},{8,12},{9,13},{10,... | collective-permute-start | bytes 663560 | tf_op jit(solution)/shard_map/ppermute | solution.py:656
  222.1 9.9 %collective-permute-start.38 = (bf16[2,48,1152]{2,1,0:T(8,128)(2,1)S(1)}, bf16[2,48,1152]{2,1,0:T(8,128)(2,1)S(1)}, u32[]{:S(2)}, u32[]{:S(2)}) collective-permute-start(bf16[2,48,1152]{2,1,0:T(8,128)(2,1)S(1)} %add_convert_fusion.11), channel_id=1, source_target_pairs={{0,12},{1,13},{2,14},{3,15},{4,8},{5,9},{6,10},{7,11},{8,4},{9,5},... | collective-permute-start | bytes 663560 | tf_op jit(solution)/shard_map/ppermute | solution.py:656
  223.9 9.5 %collective-permute-start.39 = (bf16[2,48,1152]{2,1,0:T(8,128)(2,1)S(1)}, bf16[2,48,1152]{2,1,0:T(8,128)(2,1)S(1)}, u32[]{:S(2)}, u32[]{:S(2)}) collective-permute-start(bf16[2,48,1152]{2,1,0:T(8,128)(2,1)S(1)} %add_convert_fusion.11), channel_id=1, source_target_pairs={{0,8},{1,9},{2,10},{3,11},{4,12},{5,13},{6,14},{7,15},{8,0},{9,1},... | collective-permute-start | bytes 663560 | tf_op jit(solution)/shard_map/ppermute | solution.py:656
  225.3 6.7 %collective-permute-start.40 = (f32[16,768]{1,0:T(8,128)S(1)}, f32[16,768]{1,0:T(8,128)S(1)}, u32[]{:S(2)}, u32[]{:S(2)}) collective-permute-start(f32[16,768]{1,0:T(8,128)S(1)} %add.152), channel_id=1, source_target_pairs={{0,16},{1,17},{2,18},{3,19},{4,20},{5,21},{6,22},{7,23},{8,24},{9,... | collective-permute-start | bytes 147464 | tf_op jit(solution)/shard_map/ppermute | solution.py:656
  (40 other events, 520.0 us)

commit v6 on v5

--- a/solution.py
+++ b/solution.py
@@ -838,6 +838,12 @@
         n3_c = hop(n3, ACROSS_CORE)
     act, grad_two, hidden_vec = hidden(rows, res2, n3, gf, norm_gains, hb, hidden_in, hidden_out)
 
+    def own_vectors(sums):
+        return (
+            lax.dynamic_slice_in_dim(sums[:9], at_hd * (d // 4), d // 4, 1),
+            lax.dynamic_index_in_dim(sums[9:13], at_hd, 0, keepdims=False),
+        )
+
     def cross_step(grad):
         return cross_back(
             rows, grad, res1, n2, optic_tokens, q2, k2, v2, att2, p2, norm_gains, cross_out, cross_query, att1
@@ -887,12 +893,21 @@
             ("cV", "aQ", "oH", "cY", "nB", "sY"),
             ("cP", "nH", "aB", "sX"),
             ("cQ", "aH", "sP"),
-            ("cG", "cD", "cA", "sQ"),
         ):
             gate = plan.end(plan.begin(gate, *stages), *stages)
+        gate = plan.begin(gate, "cG", "cD", "cA", "sQ")
+        cross = plan.flows["a"]
+        gate, cross.value, cross.ends["H"] = tie([gate, cross.value, cross.ends["H"]])
+        sides = cross.together()
+        gate, cross_a, cross_b = tie(
+            [gate, *[jnp.stack([v[:, i] for v in sides]).reshape(d // 4, -1).astype(F32) for i in range(2)]]
+        )
+        gate = plan.end(gate, "sQ")
+        gate, vectors, hidden_part = tie([gate, *own_vectors(plan.flows["s"].value)])
+        gate = plan.end(gate, "cG", "cD", "cA")
         optic_grad = gate
 
-        done = {name: plan.flows[name].together() for name in "onac"}
+        done = {name: plan.flows[name].together() for name in "onc"}
         out_part = jnp.stack(done["o"]).reshape(-1, d).astype(F32)
         slices = [in_order(at_c, v[:, 0], v[:, 1]) for v in done["n"]]
         half = ff // 8
@@ -903,10 +918,9 @@
             ],
             axis=1,
         ).astype(F32)
-        (cross_a, cross_b), (self_a, self_b) = [
-            [jnp.stack([v[:, i] for v in done[name]]).reshape(d // 4, -1).astype(F32) for i in range(2)] for name in "ac"
+        self_a, self_b = [
+            jnp.stack([v[:, i] for v in done["c"]]).reshape(d // 4, -1).astype(F32) for i in range(2)
         ]
-        small = plan.flows["s"].value
     else:
         into, out = [], []
         for c in range(2):
@@ -926,9 +940,7 @@
         at = (at_y, at_c, at_x, at_p)
         cross_a, cross_b = [summed_anywhere(whole_rows(cross_keep, cross_send, b, at)) for b in range(2)]
         self_a, self_b = [summed_anywhere(whole_rows(self_keep, self_send, b, at)) for b in range(2)]
-        small = lax.psum(small, ("grp", "hd"))
-    vectors = lax.dynamic_slice_in_dim(small[:9], at_hd * (d // 4), d // 4, 1)
-    hidden_part = lax.dynamic_index_in_dim(small[9:13], at_hd, 0, keepdims=False)
+        vectors, hidden_part = own_vectors(lax.psum(small, ("grp", "hd")))
     return (
         layer_output,
         radar_grad,

time: 239 us -> 240 us (level)
  transfers between devices with their start and end apart: 41 -> 41, of which waited for: 20 -> 21; matrix products, arithmetic and copies ran while one was open for 4% -> 3% of each run, Pallas kernels for 35% -> 35%
where the time goes in v6:
time: 240 us; the launch traced here: 237 us
  Pallas kernels  117 us (49%)
  waiting for transfers between devices  57.7 us (24%)
  starting transfers between devices  41.3 us (17%)
  other arithmetic  12.7 us (5%)
  local copies, waits for them, and re-layouts  6.21 us (3%)
    ppermute x41, waiting for transfers between devices, hop(): return lax.ppermute(values, ('grp', 'hd'), perm)  57.7 us
    ppermute x41, starting transfers between devices, hop(): return lax.ppermute(values, ('grp', 'hd'), perm)  41.3 us
    pallas_call x1, Pallas kernels, hidden(): pl.pallas_call(hidden_kernel, grid=(4,), in_specs=[whole((rows, d)), whol...  25.2 us
    pallas_call x1, Pallas kernels, hidden_grads(): pl.pallas_call(functools.partial(hidden_grads_kernel, blocks), grid_spec=...  17 us
    pallas_call x1, Pallas kernels, self_forward(): pl.pallas_call(self_forward_kernel, grid=(steps,), in_specs=[smem(), whol...  16.1 us
    pallas_call x1, Pallas kernels, cross_back(): pl.pallas_call(cross_back_kernel, grid=(d // wide,), in_specs=[full, full...  15.9 us
    pallas_call x1, Pallas kernels, cross_forward(): pl.pallas_call(cross_forward_kernel, grid=(steps,), in_specs=[smem(), who...  13 us
    pallas_call x1, Pallas kernels, self_back(): pl.pallas_call(self_back_kernel, grid=(d // wide,), in_specs=[full, full,...  12.2 us
  transfers between devices with their start and end apart: 41, of which 21 were waited for; matrix products, arithmetic and copies ran while one was open for 3% of the time, Pallas kernels for 35%

profile of v6, /device:TPU:0, one launch (start us, length us, event | category | flops | bytes accessed | tf_op | source)
XLA Modules:
  0.0 236.8 jit_solution(5872385812134946487)
XLA Ops:
  1.5 16.1 %self_forward.1 = (bf16[464,768]{1,0:T(8,128)(2,1)}, bf16[464,768]{1,0:T(8,128)(2,1)}, bf16[464,768]{1,0:T(8,128)(2,1)}, bf16[464,768]{1,0:T(8,128)(2,1)}, bf16[...) custom-call(s32[1,4,3]{2,1,0:T(4,128)S(1)} %copy.31.lens, ...), custom_call_target="tpu_custom_call" | custom-call | flops 1 | bytes 1 | tf_op jit(solution)/shard_map/self_forward/pallas_call | solution.py:232
  18.2 2.6 %collective-permute-start = (bf16[464,768]{1,0:T(8,128)(2,1)}, bf16[464,768]{1,0:T(8,128)(2,1)S(1)}, u32[]{:S(2)}, u32[]{:S(2)}) collective-permute-start(bf16[464,768]{1,0:T(8,128)(2,1)} %get-tuple-element.170.gf.refs_4_), channel_id=1, source_target_pairs={{0,4},{1,5},{2,6},{3,7},{4,0},{5,1},{6,2},{7,3},{8,12},{9,13},{10,... | collective-permute-start | bytes 2138120 | tf_op jit(solution)/shard_map/ppermute | solution.py:656
  20.8 13.0 %cross_forward.1 = (bf16[464,768]{1,0:T(8,128)(2,1)}, bf16[464,768]{1,0:T(8,128)(2,1)}, bf16[464,768]{1,0:T(8,128)(2,1)}, bf16[12,464,464]{2,1,0:T(8,128)(2,1)},...) custom-call(s32[1,4,3]{2,1,0:T(4,128)S(1)} %copy.31.lens, ...), custom_call_target="tpu_custom_call" | custom-call | flops 1 | bytes 1 | tf_op jit(solution)/shard_map/cross_forward/pallas_call | solution.py:261
  33.9 3.6 %collective-permute-done.refs_5_ = bf16[464,768]{1,0:T(8,128)(2,1)S(1)} collective-permute-done((bf16[464,768]{1,0:T(8,128)(2,1)}, bf16[464,768]{1,0:T(8,128)(2,1)S(1)}, u32[]{:S(2)}, u32[]{:S(2)}) %collective-permute-start) | collective-permute-done | bytes 712736 | tf_op jit(solution)/shard_map/ppermute | solution.py:656
  38.0 1.8 collective-permute-start.2
  39.8 25.2 %hidden.1 = (bf16[464,3072]{1,0:T(8,128)(2,1)}, f32[464,768]{1,0:T(8,128)}, f32[8,768]{1,0:T(8,128)}) custom-call(f32[464,768]{1,0:T(8,128)S(1)} %get-tuple-element.172.res2, bf16[464,768]{1,0:T(8,128)(2,1)S(1)} %get-tuple-element.173.n3.refs_0_, bf16[464,768]{1,0:T(8,128)(2,1)} %get-tuple-element.170.gf.refs_4_, f32[3,768]{1,0:T(4,128)S(1)} %copy-done.26, ...), custom_call_target="tpu_custom_call" | custom-call | flops 1 | bytes 1 | tf_op jit(solution)/shard_map/hidden/pallas_call | solution.py:313
  65.3 2.2 collective-permute-done.5.refs_3_
  67.6 17.0 %hidden_grads.1 = (bf16[2,2,2,96,768]{4,3,2,1,0:T(8,128)(2,1)S(1)}, bf16[2,2,192,768]{3,2,1,0:T(8,128)(2,1)S(1)}) custom-call(s32[4]{0:T(128)S(1)} %pad_add_fusion.meta, bf16[464,768]{1,0:T(8,128)(2,1)} %copy-done.16, bf16[464,768]{1,0:T(8,128)(2,1)} %copy-done.36, bf16[464,768]{1,0:T(8,128)(2,1)} %copy-done.35, ...), custom_call_target="tpu_custom_call" | custom-call | flops 1 | bytes 1 | tf_op jit(solution)/shard_map/hidden_grads/pallas_call | solution.py:405
  84.6 1.6 collective-permute-start.6
  86.2 1.6 collective-permute-start.7
  87.9 15.9 %cross_back.1 = (bf16[2,2,2,2,48,1920]{5,4,3,2,1,0:T(8,128)(2,1)S(1)}, bf16[2,2,2,2,48,1920]{5,4,3,2,1,0:T(8,128)(2,1)S(1)}, bf16[464,768]{1,0:T(8,128)(2,1)}, b...) custom-call(f32[464,768]{1,0:T(8,128)S(1)} %copy-done.18, f32[464,768]{1,0:T(8,128)S(1)} %copy-done.5, ...), custom_call_target="tpu_custom_call" | custom-call | flops 1 | bytes 1 | tf_op jit(solution)/shard_map/cross_back/pallas_call | solution.py:547
  105.7 6.2 %output.1 = bf16[512,768]{1,0:T(8,128)(2,1)} custom-call(s32[1,4,3]{2,1,0:T(4,128)S(1)} %copy.31.lens, bf16[464,3072]{1,0:T(8,128)(2,1)} %get-tuple-element.205.act, f32[464,768]{1,0:T(8,128)S(1)} %copy-done.3, f32[3,768]{1,0:T(4,128)S(1)} %copy-done.28, bf16[3072,768]{1,0:T(8,128)(2,1)} %wout.3), custom_call_target="tpu_custom_call" | custom-call | flops 1 | bytes 1 | tf_op jit(solution)/shard_map/output/pallas_call | solution.py:350
  111.9 1.9 collective-permute-done.9
  115.3 1.5 collective-permute-start.13
  116.8 2.6 %collective-permute-start.11 = (bf16[192,768]{1,0:T(8,128)(2,1)S(1)}, bf16[192,768]{1,0:T(8,128)(2,1)S(1)}, u32[]{:S(2)}, u32[]{:S(2)}) collective-permute-start(bf16[192,768]{1,0:T(8,128)(2,1)S(1)} %fusion.14), channel_id=1, source_target_pairs={{0,16},{1,17},{2,18},{3,19},{4,20},{5,21},{6,22},{7,23},{8,24},{9,... | collective-permute-start | bytes 884744 | tf_op jit(solution)/shard_map/ppermute | solution.py:656
  119.5 12.2 %self_back.1 = (bf16[2,2,2,2,48,1152]{5,4,3,2,1,0:T(8,128)(2,1)S(1)}, bf16[2,2,2,2,48,1152]{5,4,3,2,1,0:T(8,128)(2,1)S(1)}, bf16[464,768]{1,0:T(8,128)(2,1)}, bf16[464,768]{1,0:T(8,128)(2,1)}, bf16[464,768]{1,0:T(8,128)(2,1)}) custom-call(f32[464,768]{1,0:T(8,128)S(1)} %copy-done.1, bf16[464,768]{1,0:T(8,128)(2,1)S(1)} %copy-done.19, ...), custom_call_target="tpu_custom_call" | custom-call | flops 1 | bytes 1 | tf_op jit(solution)/shard_map/self_back/pallas_call | solution.py:575
  133.6 1.6 collective-permute-start.16
  135.2 1.4 collective-permute-start.17
  136.6 2.6 %collective-permute-start.15 = (bf16[2,96,768]{2,1,0:T(8,128)(2,1)S(1)}, bf16[2,96,768]{2,1,0:T(8,128)(2,1)S(1)}, u32[]{:S(2)}, u32[]{:S(2)}) collective-permute-start(bf16[2,96,768]{2,1,0:T(8,128)(2,1)S(1)} %pad_maximum_fusion.19), channel_id=1, source_target_pairs={{0,16},{1,17},{2,18},{3,19},{4,20},{5,21},{6,22},{7,23},{8,24},{9,... | collective-permute-start | bytes 884744 | tf_op jit(solution)/shard_map/ppermute | solution.py:656
  139.7 6.7 %radar.4 = (f32[512,768]{1,0:T(8,128)}, f32[16,768]{1,0:T(8,128)S(1)}) custom-call(bf16[464,768]{1,0:T(8,128)(2,1)} %get-tuple-element.232.dq, bf16[464,768]{1,0:T(8,128)(2,1)} %get-tuple-element.233.dk, bf16[464,768]{1,0:T(8,128)(2,1)} %get-tuple-element.234.dv, bf16[768,2304]{1,0:T(8,128)(2,1)} %weights.2, f32[464,768]{1,0:T(8,128)} %get-tuple-element.215.grad_in, ...), custom_call_target="tpu_custom_call" | custom-call | flops 1 | bytes 1 | tf_op jit(solution)/shard_map/radar/pallas_call | solution.py:645
  146.4 6.2 %collective-permute-done.15 = bf16[2,96,768]{2,1,0:T(8,128)(2,1)S(1)} collective-permute-done((bf16[2,96,768]{2,1,0:T(8,128)(2,1)S(1)}, bf16[2,96,768]{2,1,0:T(8,128)(2,1)S(1)}, u32[]{:S(2)}, u32[]{:S(2)}) %collective-permute-start.15) | collective-permute-done | bytes 294944 | tf_op jit(solution)/shard_map/ppermute | solution.py:656
  152.6 1.3 collective-permute-done.19
  156.2 4.6 %optic.3 = f32[512,768]{1,0:T(8,128)} custom-call(bf16[464,768]{1,0:T(8,128)(2,1)} %get-tuple-element.251.dk, bf16[464,768]{1,0:T(8,128)(2,1)} %get-tuple-element.252.dv, bf16[768,1536]{1,0:T(8,128)(2,1)} %weights.3), custom_call_target="tpu_custom_call" | custom-call | flops 1 | bytes 1 | tf_op jit(solution)/shard_map/optic/pallas_call | solution.py:613
  160.8 3.5 %collective-permute-done.22 = bf16[2,48,1920]{2,1,0:T(8,128)(2,1)S(1)} collective-permute-done((bf16[2,48,1920]{2,1,0:T(8,128)(2,1)S(1)}, bf16[2,48,1920]{2,1,0:T(8,128)(2,1)S(1)}, u32[]{:S(2)}, u32[]{:S(2)}) %collective-permute-start.22) | collective-permute-done | bytes 368672 | tf_op jit(solution)/shard_map/ppermute | solution.py:656
  167.3 1.5 collective-permute-start.26
  170.2 1.6 collective-permute-start.25
  172.5 1.1 collective-permute-done.29
  174.2 10.5 %collective-permute-done.24 = bf16[2,48,1152]{2,1,0:T(8,128)(2,1)S(1)} collective-permute-done((bf16[2,48,1152]{2,1,0:T(8,128)(2,1)}, bf16[2,48,1152]{2,1,0:T(8,128)(2,1)S(1)}, u32[]{:S(2)}, u32[]{:S(2)}) %collective-permute-start.24) | collective-permute-done | bytes 221216 | tf_op jit(solution)/shard_map/ppermute | solution.py:656
  184.7 1.8 collective-permute-done.25
  186.8 1.1 select_bitcast_fusion.1
  189.0 1.7 collective-permute-start.32
  190.7 1.5 collective-permute-start.31
  192.4 1.7 bitcast_convert_fusion
  194.2 1.2 collective-permute-done.30
  195.4 3.9 %collective-permute-done.32 = bf16[2,48,1920]{2,1,0:T(8,128)(2,1)S(1)} collective-permute-done((bf16[2,48,1920]{2,1,0:T(8,128)(2,1)S(1)}, bf16[2,48,1920]{2,1,0:T(8,128)(2,1)S(1)}, u32[]{:S(2)}, u32[]{:S(2)}) %collective-permute-start.32) | collective-permute-done | bytes 368672 | tf_op jit(solution)/shard_map/ppermute | solution.py:656
  199.3 2.0 collective-permute-done.31
  201.5 1.7 collective-permute-start.36
  203.2 1.4 collective-permute-start.34
  206.0 1.7 convert_element_type.445
  207.7 4.5 %collective-permute-done.34 = bf16[2,48,1152]{2,1,0:T(8,128)(2,1)S(1)} collective-permute-done((bf16[2,48,1152]{2,1,0:T(8,128)(2,1)S(1)}, bf16[2,48,1152]{2,1,0:T(8,128)(2,1)S(1)}, u32[]{:S(2)}, u32[]{:S(2)}) %collective-permute-start.34) | collective-permute-done | bytes 221216 | tf_op jit(solution)/shard_map/ppermute | solution.py:656
  212.2 6.3 %collective-permute-done.35 = bf16[2,2,48,1920]{3,2,0,1:T(8,128)(2,1)S(1)} collective-permute-done((bf16[2,2,48,1920]{3,2,0,1:T(8,128)(2,1)S(1)}, bf16[2,2,48,1920]{3,2,0,1:T(8,128)(2,1)S(1)}, u32[]{:S(2)}, u32[]{:S(2)}) %collective-permute-start.35) | collective-permute-done | bytes 737312 | tf_op jit(solution)/shard_map/ppermute | solution.py:656
  220.9 1.8 collective-permute-start.37
  223.6 1.2 slice.291
  225.1 1.5 collective-permute-start.39
  226.6 1.7 collective-permute-start.40
  229.6 3.5 %collective-permute-done.38 = bf16[2,48,1152]{2,1,0:T(8,128)(2,1)S(1)} collective-permute-done((bf16[2,48,1152]{2,1,0:T(8,128)(2,1)S(1)}, bf16[2,48,1152]{2,1,0:T(8,128)(2,1)S(1)}, u32[]{:S(2)}, u32[]{:S(2)}) %collective-permute-start.38) | collective-permute-done | bytes 221216 | tf_op jit(solution)/shard_map/ppermute | solution.py:656
  233.1 1.5 collective-permute-done.40
  235.3 1.3 pad_maximum_fusion
  (236 shorter events, 24.4 us)
Async XLA Ops:
  0.6 39.1 %slice-start.2 = ((s8[4718592]{0:T(1024)(128)(4,1)}), s8[524288]{0:T(1024)(128)(4,1)S(1)}, s32[]{:S(2)}) async-start(s8[4718592]{0:T(1024)(128)(4,1)} %bitcast.207), calls=%async_computation.2 | async-start | bytes 1048576
  1.5 38.2 %slice-start.3 = ((s8[4718592]{0:T(1024)(128)(4,1)}), s8[4194304]{0:T(1024)(128)(4,1)S(1)}, s32[]{:S(2)}) async-start(s8[4718592]{0:T(1024)(128)(4,1)} %bitcast.207), calls=%async_computation.3 | async-start | bytes 8388608
  17.6 16.2 %collective-permute-start.1 = (bf16[464,768]{1,0:T(8,128)(2,1)}, bf16[464,768]{1,0:T(8,128)(2,1)S(1)}, u32[]{:S(2)}, u32[]{:S(2)}) collective-permute-start(bf16[464,768]{1,0:T(8,128)(2,1)} %get-tuple-element.170.gf.refs_4_), channel_id=1, source_target_pairs={{0,1},{1,0},{2,3},{3,2},{4,5},{5,4},{6,7},{7,6},{8,9},{9,8},{10,11... | collective-permute-start | bytes 2138120 | tf_op jit(solution)/shard_map/ppermute | solution.py:656
  18.2 19.3 %collective-permute-start = (bf16[464,768]{1,0:T(8,128)(2,1)}, bf16[464,768]{1,0:T(8,128)(2,1)S(1)}, u32[]{:S(2)}, u32[]{:S(2)}) collective-permute-start(bf16[464,768]{1,0:T(8,128)(2,1)} %get-tuple-element.170.gf.refs_4_), channel_id=1, source_target_pairs={{0,4},{1,5},{2,6},{3,7},{4,0},{5,1},{6,2},{7,3},{8,12},{9,13},{10,... | collective-permute-start | bytes 2138120 | tf_op jit(solution)/shard_map/ppermute | solution.py:656
  33.9 31.1 %copy-start.2 = (f32[464,768]{1,0:T(8,128)}, f32[464,768]{1,0:T(8,128)S(1)}, u32[]{:S(2)}) copy-start(f32[464,768]{1,0:T(8,128)S(1)} %get-tuple-element.172.res2) | copy-start | bytes 4276228
  33.9 31.1 %copy-start.16 = (bf16[464,768]{1,0:T(8,128)(2,1)}, bf16[464,768]{1,0:T(8,128)(2,1)S(1)}, u32[]{:S(2)}) copy-start(bf16[464,768]{1,0:T(8,128)(2,1)S(1)} %get-tuple-element.173.n3.refs_0_) | copy-start | bytes 2138116
  33.9 31.1 %copy-start.32 = (bf16[464,768]{1,0:T(8,128)(2,1)}, bf16[464,768]{1,0:T(8,128)(2,1)S(1)}, u32[]{:S(2)}) copy-start(bf16[464,768]{1,0:T(8,128)(2,1)S(1)} %collective-permute-done.1.refs_6_) | copy-start | bytes 2138116
  37.5 27.5 %copy-start.33 = (bf16[464,768]{1,0:T(8,128)(2,1)}, bf16[464,768]{1,0:T(8,128)(2,1)S(1)}, u32[]{:S(2)}) copy-start(bf16[464,768]{1,0:T(8,128)(2,1)S(1)} %collective-permute-done.refs_5_) | copy-start | bytes 2138116
  37.5 27.5 %collective-permute-start.4 = (bf16[464,768]{1,0:T(8,128)(2,1)S(1)}, bf16[464,768]{1,0:T(8,128)(2,1)S(1)}, u32[]{:S(2)}, u32[]{:S(2)}) collective-permute-start(bf16[464,768]{1,0:T(8,128)(2,1)S(1)} %collective-permute-done.refs_5_), channel_id=1, source_target_pairs={{0,1},{1,0},{2,3},{3,2},{4,5},{5,4},{6,7},{7,6},{8,9},{9,8},{10,11... | collective-permute-start | bytes 2138120 | tf_op jit(solution)/shard_map/ppermute | solution.py:656
  37.5 27.5 %collective-permute-start.3 = (bf16[464,768]{1,0:T(8,128)(2,1)S(1)}, bf16[464,768]{1,0:T(8,128)(2,1)S(1)}, u32[]{:S(2)}, u32[]{:S(2)}) collective-permute-start(bf16[464,768]{1,0:T(8,128)(2,1)S(1)} %get-tuple-element.173.n3.refs_0_), channel_id=1, source_target_pairs={{0,1},{1,0},{2,3},{3,2},{4,5},{5,4},{6,7},{7,6},{8,9},{9,8},{10,11... | collective-permute-start | bytes 2138120 | tf_op jit(solution)/shard_map/ppermute | solution.py:656
  38.0 27.0 %collective-permute-start.2 = (bf16[464,768]{1,0:T(8,128)(2,1)S(1)}, bf16[464,768]{1,0:T(8,128)(2,1)S(1)}, u32[]{:S(2)}, u32[]{:S(2)}) collective-permute-start(bf16[464,768]{1,0:T(8,128)(2,1)S(1)} %get-tuple-element.173.n3.refs_0_), channel_id=1, source_target_pairs={{0,4},{1,5},{2,6},{3,7},{4,0},{5,1},{6,2},{7,3},{8,12},{9,13},{10,... | collective-permute-start | bytes 2138120 | tf_op jit(solution)/shard_map/ppermute | solution.py:656
  65.1 2.4 %collective-permute-start.5 = (bf16[464,768]{1,0:T(8,128)(2,1)S(1)}, bf16[464,768]{1,0:T(8,128)(2,1)}, u32[]{:S(2)}, u32[]{:S(2)}) collective-permute-start(bf16[464,768]{1,0:T(8,128)(2,1)S(1)} %collective-permute-done.2.refs_1_), channel_id=1, source_target_pairs={{0,1},{1,0},{2,3},{3,2},{4,5},{5,4},{6,7},{7,6},{8,9},{9,8},{10,11... | collective-permute-start | bytes 2138120 | tf_op jit(solution)/shard_map/ppermute | solution.py:656
  65.2 22.6 %slice-start.6 = ((s8[5701632]{0:T(1024)(128)(4,1)}), s8[4194304]{0:T(1024)(128)(4,1)S(1)}, s32[]{:S(2)}) async-start(s8[5701632]{0:T(1024)(128)(4,1)} %bitcast.211), calls=%async_computation.6 | async-start | bytes 8388608
  84.6 19.2 %collective-permute-start.6 = (bf16[2,192,768]{2,1,0:T(8,128)(2,1)S(1)}, bf16[2,192,768]{2,1,0:T(8,128)(2,1)S(1)}, u32[]{:S(2)}, u32[]{:S(2)}) collective-permute-start(bf16[2,192,768]{2,1,0:T(8,128)(2,1)S(1)} %slice_bitcast_fusion.1), channel_id=1, source_target_pairs={{0,2},{1,3},{2,0},{3,1},{4,6},{5,7},{6,4},{7,5},{8,10},{9,11},{10,... | collective-permute-start | bytes 1769480 | tf_op jit(solution)/shard_map/ppermute | solution.py:656
  86.2 17.6 %collective-permute-start.7 = (bf16[2,2,96,768]{3,2,1,0:T(8,128)(2,1)S(1)}, bf16[2,2,96,768]{3,2,1,0:T(8,128)(2,1)S(1)}, u32[]{:S(2)}, u32[]{:S(2)}) collective-permute-start(bf16[2,2,96,768]{3,2,1,0:T(8,128)(2,1)S(1)} %slice_bitcast_fusion), channel_id=1, source_target_pairs={{0,8},{1,9},{2,10},{3,11},{4,12},{5,13},{6,14},{7,15},{8,0},{9,1},... | collective-permute-start | bytes 1769480 | tf_op jit(solution)/shard_map/ppermute | solution.py:656
  104.3 9.7 %collective-permute-start.8 = (bf16[2,2,2,2,48,1920]{5,4,3,2,1,0:T(8,128)(2,1)S(1)}, bf16[2,2,2,2,48,1920]{5,4,3,2,1,0:T(8,128)(2,1)S(1)}, u32[]{:S(2)}, u32[]{:S(2)}) collective-permute-start(bf16[2,2,2,2,48,1920]{5,4,3,2,1,0:T(8,128)(2,1)S(1)} %get-tuple-element.207), channel_id=1, source_target_pairs={{0,1},{1,0},{2,3},{3,2},{4,5},{5,4},{6,7},{7,6},{8,9},{9,8},{10,11... | collective-permute-start | bytes 8847368 | tf_op jit(solution)/shard_map/ppermute | solution.py:656
  104.3 9.4 %collective-permute-start.9 = (bf16[2,96,768]{2,1,0:T(8,128)(2,1)S(1)}, bf16[2,96,768]{2,1,0:T(8,128)(2,1)S(1)}, u32[]{:S(2)}, u32[]{:S(2)}) collective-permute-start(bf16[2,96,768]{2,1,0:T(8,128)(2,1)S(1)} %slice_bitcast_fusion.13), channel_id=1, source_target_pairs={{0,2},{1,3},{2,0},{3,1},{4,6},{5,7},{6,4},{7,5},{8,10},{9,11},{10,... | collective-permute-start | bytes 884744 | tf_op jit(solution)/shard_map/ppermute | solution.py:656
  104.9 9.1 %collective-permute-start.10 = (bf16[192,768]{1,0:T(8,128)(2,1)S(1)}, bf16[192,768]{1,0:T(8,128)(2,1)S(1)}, u32[]{:S(2)}, u32[]{:S(2)}) collective-permute-start(bf16[192,768]{1,0:T(8,128)(2,1)S(1)} %slice_bitcast_fusion.12), channel_id=1, source_target_pairs={{0,8},{1,9},{2,10},{3,11},{4,12},{5,13},{6,14},{7,15},{8,0},{9,1},... | collective-permute-start | bytes 884744 | tf_op jit(solution)/shard_map/ppermute | solution.py:656
  114.7 17.9 %collective-permute-start.12 = (bf16[2,2,48,1920]{3,2,1,0:T(8,128)(2,1)S(1)}, bf16[2,2,48,1920]{3,2,1,0:T(8,128)(2,1)S(1)}, u32[]{:S(2)}, u32[]{:S(2)}) collective-permute-start(bf16[2,2,48,1920]{3,2,1,0:T(8,128)(2,1)S(1)} %get-tuple-element.223), channel_id=1, source_target_pairs={{0,4},{1,5},{2,6},{3,7},{4,0},{5,1},{6,2},{7,3},{8,12},{9,13},{10,... | collective-permute-start | bytes 2211848 | tf_op jit(solution)/shard_map/ppermute | solution.py:656
  115.3 17.5 %collective-permute-start.13 = (bf16[2,2,48,1920]{3,2,1,0:T(8,128)(2,1)S(1)}, bf16[2,2,48,1920]{3,2,1,0:T(8,128)(2,1)S(1)}, u32[]{:S(2)}, u32[]{:S(2)}) collective-permute-start(bf16[2,2,48,1920]{3,2,1,0:T(8,128)(2,1)S(1)} %get-tuple-element.224), channel_id=1, source_target_pairs={{0,2},{1,3},{2,0},{3,1},{4,6},{5,7},{6,4},{7,5},{8,10},{9,11},{10,... | collective-permute-start | bytes 2211848 | tf_op jit(solution)/shard_map/ppermute | solution.py:656
  116.8 14.9 %collective-permute-start.11 = (bf16[192,768]{1,0:T(8,128)(2,1)S(1)}, bf16[192,768]{1,0:T(8,128)(2,1)S(1)}, u32[]{:S(2)}, u32[]{:S(2)}) collective-permute-start(bf16[192,768]{1,0:T(8,128)(2,1)S(1)} %fusion.14), channel_id=1, source_target_pairs={{0,16},{1,17},{2,18},{3,19},{4,20},{5,21},{6,22},{7,23},{8,24},{9,... | collective-permute-start | bytes 884744 | tf_op jit(solution)/shard_map/ppermute | solution.py:656
  119.4 12.3 %collective-permute-start.14 = (bf16[96,768]{1,0:T(8,128)(2,1)S(1)}, bf16[96,768]{1,0:T(8,128)(2,1)S(1)}, u32[]{:S(2)}, u32[]{:S(2)}) collective-permute-start(bf16[96,768]{1,0:T(8,128)(2,1)S(1)} %get-tuple-element.225), channel_id=1, source_target_pairs={{0,1},{1,0},{2,3},{3,2},{4,5},{5,4},{6,7},{7,6},{8,9},{9,8},{10,11... | collective-permute-start | bytes 442376 | tf_op jit(solution)/shard_map/ppermute | solution.py:656
  133.6 20.4 %collective-permute-start.18 = (bf16[2,2,2,2,48,1152]{5,4,3,2,1,0:T(8,128)(2,1)S(1)}, bf16[2,2,2,2,48,1152]{5,4,3,2,1,0:T(8,128)(2,1)S(1)}, u32[]{:S(2)}, u32[]{:S(2)}) collective-permute-start(bf16[2,2,2,2,48,1152]{5,4,3,2,1,0:T(8,128)(2,1)S(1)} %get-tuple-element.243), channel_id=1, source_target_pairs={{0,1},{1,0},{2,3},{3,2},{4,5},{5,4},{6,7},{7,6},{8,9},{9,8},{10,11... | collective-permute-start | bytes 5308424 | tf_op jit(solution)/shard_map/ppermute | solution.py:656
  133.6 20.3 %collective-permute-start.16 = (bf16[2,48,1920]{2,1,0:T(8,128)(2,1)S(1)}, bf16[2,48,1920]{2,1,0:T(8,128)(2,1)S(1)}, u32[]{:S(2)}, u32[]{:S(2)}) collective-permute-start(bf16[2,48,1920]{2,1,0:T(8,128)(2,1)S(1)} %slice_bitcast_fusion.9), channel_id=1, source_target_pairs={{0,4},{1,5},{2,6},{3,7},{4,0},{5,1},{6,2},{7,3},{8,12},{9,13},{10,... | collective-permute-start | bytes 1105928 | tf_op jit(solution)/shard_map/ppermute | solution.py:656
  135.2 18.8 %collective-permute-start.17 = (bf16[2,48,1920]{2,1,0:T(8,128)(2,1)S(1)}, bf16[2,48,1920]{2,1,0:T(8,128)(2,1)S(1)}, u32[]{:S(2)}, u32[]{:S(2)}) collective-permute-start(bf16[2,48,1920]{2,1,0:T(8,128)(2,1)S(1)} %slice_bitcast_fusion.8), channel_id=1, source_target_pairs={{0,2},{1,3},{2,0},{3,1},{4,6},{5,7},{6,4},{7,5},{8,10},{9,11},{10,... | collective-permute-start | bytes 1105928 | tf_op jit(solution)/shard_map/ppermute | solution.py:656
  136.6 16.0 %collective-permute-start.15 = (bf16[2,96,768]{2,1,0:T(8,128)(2,1)S(1)}, bf16[2,96,768]{2,1,0:T(8,128)(2,1)S(1)}, u32[]{:S(2)}, u32[]{:S(2)}) collective-permute-start(bf16[2,96,768]{2,1,0:T(8,128)(2,1)S(1)} %pad_maximum_fusion.19), channel_id=1, source_target_pairs={{0,16},{1,17},{2,18},{3,19},{4,20},{5,21},{6,22},{7,23},{8,24},{9,... | collective-permute-start | bytes 884744 | tf_op jit(solution)/shard_map/ppermute | solution.py:656
  139.2 14.7 %collective-permute-start.19 = (bf16[192,768]{1,0:T(8,128)(2,1)S(1)}, bf16[192,768]{1,0:T(8,128)(2,1)S(1)}, u32[]{:S(2)}, u32[]{:S(2)}) collective-permute-start(bf16[192,768]{1,0:T(8,128)(2,1)S(1)} %add_convert_fusion.10), channel_id=1, source_target_pairs={{0,8},{1,9},{2,10},{3,11},{4,12},{5,13},{6,14},{7,15},{8,0},{9,1},... | collective-permute-start | bytes 884744 | tf_op jit(solution)/shard_map/ppermute | solution.py:656
  154.4 10.8 %collective-permute-start.20 = (bf16[2,2,48,1152]{3,2,1,0:T(8,128)(2,1)S(1)}, bf16[2,2,48,1152]{3,2,1,0:T(8,128)(2,1)S(1)}, u32[]{:S(2)}, u32[]{:S(2)}) collective-permute-start(bf16[2,2,48,1152]{3,2,1,0:T(8,128)(2,1)S(1)} %get-tuple-element.253), channel_id=1, source_target_pairs={{0,4},{1,5},{2,6},{3,7},{4,0},{5,1},{6,2},{7,3},{8,12},{9,13},{10,... | collective-permute-start | bytes 1327112 | tf_op jit(solution)/shard_map/ppermute | solution.py:656
  155.0 10.4 %collective-permute-start.21 = (bf16[2,2,48,1152]{3,2,1,0:T(8,128)(2,1)S(1)}, bf16[2,2,48,1152]{3,2,1,0:T(8,128)(2,1)S(1)}, u32[]{:S(2)}, u32[]{:S(2)}) collective-permute-start(bf16[2,2,48,1152]{3,2,1,0:T(8,128)(2,1)S(1)} %get-tuple-element.254), channel_id=1, source_target_pairs={{0,2},{1,3},{2,0},{3,1},{4,6},{5,7},{6,4},{7,5},{8,10},{9,11},{10,... | collective-permute-start | bytes 1327112 | tf_op jit(solution)/shard_map/ppermute | solution.py:656
  155.6 8.7 %collective-permute-start.22 = (bf16[2,48,1920]{2,1,0:T(8,128)(2,1)S(1)}, bf16[2,48,1920]{2,1,0:T(8,128)(2,1)S(1)}, u32[]{:S(2)}, u32[]{:S(2)}) collective-permute-start(bf16[2,48,1920]{2,1,0:T(8,128)(2,1)S(1)} %fusion.25), channel_id=1, source_target_pairs={{0,8},{1,9},{2,10},{3,11},{4,12},{5,13},{6,14},{7,15},{8,0},{9,1},... | collective-permute-start | bytes 1105928 | tf_op jit(solution)/shard_map/ppermute | solution.py:656
  156.1 4.7 %collective-permute-start.23 = (f32[16,768]{1,0:T(8,128)S(1)}, f32[16,768]{1,0:T(8,128)S(1)}, u32[]{:S(2)}, u32[]{:S(2)}) collective-permute-start(f32[16,768]{1,0:T(8,128)S(1)} %get-tuple-element.256), channel_id=1, source_target_pairs={{0,1},{1,0},{2,3},{3,2},{4,5},{5,4},{6,7},{7,6},{8,9},{9,8},{10,11... | collective-permute-start | bytes 147464 | tf_op jit(solution)/shard_map/ppermute | solution.py:656
  167.3 19.3 %collective-permute-start.26 = (bf16[2,192,768]{2,1,0:T(8,128)(2,1)S(1)}, bf16[2,192,768]{2,1,0:T(8,128)(2,1)}, u32[]{:S(2)}, u32[]{:S(2)}) collective-permute-start(bf16[2,192,768]{2,1,0:T(8,128)(2,1)S(1)} %pad_maximum_fusion.7), channel_id=1, source_target_pairs={{0,4},{1,5},{2,6},{3,7},{4,0},{5,1},{6,2},{7,3},{8,12},{9,13},{10,... | collective-permute-start | bytes 1769480 | tf_op jit(solution)/shard_map/ppermute | solution.py:656
  168.8 4.8 %collective-permute-start.29 = (f32[16,768]{1,0:T(8,128)}, f32[16,768]{1,0:T(8,128)S(1)}, u32[]{:S(2)}, u32[]{:S(2)}) collective-permute-start(f32[16,768]{1,0:T(8,128)} %add.144), channel_id=1, source_target_pairs={{0,2},{1,3},{2,0},{3,1},{4,6},{5,7},{6,4},{7,5},{8,10},{9,11},{10,... | collective-permute-start | bytes 147464 | tf_op jit(solution)/shard_map/ppermute | solution.py:656
  169.4 15.3 %collective-permute-start.28 = (bf16[2,96,768]{2,1,0:T(8,128)(2,1)S(1)}, bf16[2,96,768]{2,1,0:T(8,128)(2,1)S(1)}, u32[]{:S(2)}, u32[]{:S(2)}) collective-permute-start(bf16[2,96,768]{2,1,0:T(8,128)(2,1)S(1)} %add_convert_fusion.9), channel_id=1, source_target_pairs={{0,8},{1,9},{2,10},{3,11},{4,12},{5,13},{6,14},{7,15},{8,0},{9,1},... | collective-permute-start | bytes 884744 | tf_op jit(solution)/shard_map/ppermute | solution.py:656
  170.2 16.4 %collective-permute-start.25 = (bf16[2,48,1920]{2,1,0:T(8,128)(2,1)S(1)}, bf16[2,48,1920]{2,1,0:T(8,128)(2,1)S(1)}, u32[]{:S(2)}, u32[]{:S(2)}) collective-permute-start(bf16[2,48,1920]{2,1,0:T(8,128)(2,1)S(1)} %fusion.10), channel_id=1, source_target_pairs={{0,16},{1,17},{2,18},{3,19},{4,20},{5,21},{6,22},{7,23},{8,24},{9,... | collective-permute-start | bytes 1105928 | tf_op jit(solution)/shard_map/ppermute | solution.py:656
  171.9 12.9 %collective-permute-start.24 = (bf16[2,48,1152]{2,1,0:T(8,128)(2,1)}, bf16[2,48,1152]{2,1,0:T(8,128)(2,1)S(1)}, u32[]{:S(2)}, u32[]{:S(2)}) collective-permute-start(bf16[2,48,1152]{2,1,0:T(8,128)(2,1)} %slice_bitcast_fusion.21), channel_id=1, source_target_pairs={{0,4},{1,5},{2,6},{3,7},{4,0},{5,1},{6,2},{7,3},{8,12},{9,13},{10,... | collective-permute-start | bytes 663560 | tf_op jit(solution)/shard_map/ppermute | solution.py:656
  173.6 11.2 %collective-permute-start.27 = (bf16[2,48,1152]{2,1,0:T(8,128)(2,1)S(1)}, bf16[2,48,1152]{2,1,0:T(8,128)(2,1)S(1)}, u32[]{:S(2)}, u32[]{:S(2)}) collective-permute-start(bf16[2,48,1152]{2,1,0:T(8,128)(2,1)S(1)} %slice_bitcast_fusion.20), channel_id=1, source_target_pairs={{0,2},{1,3},{2,0},{3,1},{4,6},{5,7},{6,4},{7,5},{8,10},{9,11},{10,... | collective-permute-start | bytes 663560 | tf_op jit(solution)/shard_map/ppermute | solution.py:656
  188.0 6.1 %collective-permute-start.33 = (f32[16,768]{1,0:T(8,128)S(1)}, f32[16,768]{1,0:T(8,128)S(1)}, u32[]{:S(2)}, u32[]{:S(2)}) collective-permute-start(f32[16,768]{1,0:T(8,128)S(1)} %add.148), channel_id=1, source_target_pairs={{0,4},{1,5},{2,6},{3,7},{4,0},{5,1},{6,2},{7,3},{8,12},{9,13},{10,... | collective-permute-start | bytes 147464 | tf_op jit(solution)/shard_map/ppermute | solution.py:656
  188.7 6.7 %collective-permute-start.30 = (bf16[2,48,1152]{2,1,0:T(8,128)(2,1)S(1)}, bf16[2,48,1152]{2,1,0:T(8,128)(2,1)S(1)}, u32[]{:S(2)}, u32[]{:S(2)}) collective-permute-start(bf16[2,48,1152]{2,1,0:T(8,128)(2,1)S(1)} %fusion.31), channel_id=1, source_target_pairs={{0,8},{1,9},{2,10},{3,11},{4,12},{5,13},{6,14},{7,15},{8,0},{9,1},... | collective-permute-start | bytes 663560 | tf_op jit(solution)/shard_map/ppermute | solution.py:656
  189.0 10.3 %collective-permute-start.32 = (bf16[2,48,1920]{2,1,0:T(8,128)(2,1)S(1)}, bf16[2,48,1920]{2,1,0:T(8,128)(2,1)S(1)}, u32[]{:S(2)}, u32[]{:S(2)}) collective-permute-start(bf16[2,48,1920]{2,1,0:T(8,128)(2,1)S(1)} %add_convert_fusion.8), channel_id=1, source_target_pairs={{0,8},{1,9},{2,10},{3,11},{4,12},{5,13},{6,14},{7,15},{8,0},{9,1},... | collective-permute-start | bytes 1105928 | tf_op jit(solution)/shard_map/ppermute | solution.py:656
  190.7 10.6 %collective-permute-start.31 = (bf16[2,2,96,768]{3,2,1,0:T(8,128)(2,1)S(1)}, bf16[2,2,96,768]{3,2,1,0:T(8,128)(2,1)S(1)}, u32[]{:S(2)}, u32[]{:S(2)}) collective-permute-start(bf16[2,2,96,768]{3,2,1,0:T(8,128)(2,1)S(1)} %pad_maximum_fusion.8), channel_id=1, source_target_pairs={{0,4},{1,5},{2,6},{3,7},{4,0},{5,1},{6,2},{7,3},{8,12},{9,13},{10,... | collective-permute-start | bytes 1769480 | tf_op jit(solution)/shard_map/ppermute | solution.py:656
  201.5 6.2 %collective-permute-start.36 = (f32[16,768]{1,0:T(8,128)S(1)}, f32[16,768]{1,0:T(8,128)S(1)}, u32[]{:S(2)}, u32[]{:S(2)}) collective-permute-start(f32[16,768]{1,0:T(8,128)S(1)} %add.150), channel_id=1, source_target_pairs={{0,8},{1,9},{2,10},{3,11},{4,12},{5,13},{6,14},{7,15},{8,0},{9,1},... | collective-permute-start | bytes 147464 | tf_op jit(solution)/shard_map/ppermute | solution.py:656
  203.2 9.0 %collective-permute-start.34 = (bf16[2,48,1152]{2,1,0:T(8,128)(2,1)S(1)}, bf16[2,48,1152]{2,1,0:T(8,128)(2,1)S(1)}, u32[]{:S(2)}, u32[]{:S(2)}) collective-permute-start(bf16[2,48,1152]{2,1,0:T(8,128)(2,1)S(1)} %fusion.19), channel_id=1, source_target_pairs={{0,16},{1,17},{2,18},{3,19},{4,20},{5,21},{6,22},{7,23},{8,24},{9,... | collective-permute-start | bytes 663560 | tf_op jit(solution)/shard_map/ppermute | solution.py:656
  205.1 13.4 %collective-permute-start.35 = (bf16[2,2,48,1920]{3,2,0,1:T(8,128)(2,1)S(1)}, bf16[2,2,48,1920]{3,2,0,1:T(8,128)(2,1)S(1)}, u32[]{:S(2)}, u32[]{:S(2)}) collective-permute-start(bf16[2,2,48,1920]{3,2,0,1:T(8,128)(2,1)S(1)} %copy.34), channel_id=1, source_target_pairs={{0,4},{1,5},{2,6},{3,7},{4,0},{5,1},{6,2},{7,3},{8,12},{9,13},{10,... | collective-permute-start | bytes 2211848 | tf_op jit(solution)/shard_map/ppermute | solution.py:656
  220.9 7.3 %collective-permute-start.37 = (f32[16,768]{1,0:T(8,128)S(1)}, f32[16,768]{1,0:T(8,128)S(1)}, u32[]{:S(2)}, u32[]{:S(2)}) collective-permute-start(f32[16,768]{1,0:T(8,128)S(1)} %add.152), channel_id=1, source_target_pairs={{0,16},{1,17},{2,18},{3,19},{4,20},{5,21},{6,22},{7,23},{8,24},{9,... | collective-permute-start | bytes 147464 | tf_op jit(solution)/shard_map/ppermute | solution.py:656
  224.8 8.3 %collective-permute-start.38 = (bf16[2,48,1152]{2,1,0:T(8,128)(2,1)S(1)}, bf16[2,48,1152]{2,1,0:T(8,128)(2,1)S(1)}, u32[]{:S(2)}, u32[]{:S(2)}) collective-permute-start(bf16[2,48,1152]{2,1,0:T(8,128)(2,1)S(1)} %add_convert_fusion.11), channel_id=1, source_target_pairs={{0,4},{1,5},{2,6},{3,7},{4,0},{5,1},{6,2},{7,3},{8,12},{9,13},{10,... | collective-permute-start | bytes 663560 | tf_op jit(solution)/shard_map/ppermute | solution.py:656
  225.1 8.0 %collective-permute-start.39 = (bf16[2,48,1152]{2,1,0:T(8,128)(2,1)S(1)}, bf16[2,48,1152]{2,1,0:T(8,128)(2,1)S(1)}, u32[]{:S(2)}, u32[]{:S(2)}) collective-permute-start(bf16[2,48,1152]{2,1,0:T(8,128)(2,1)S(1)} %add_convert_fusion.11), channel_id=1, source_target_pairs={{0,12},{1,13},{2,14},{3,15},{4,8},{5,9},{6,10},{7,11},{8,4},{9,5},... | collective-permute-start | bytes 663560 | tf_op jit(solution)/shard_map/ppermute | solution.py:656
  226.6 7.9 %collective-permute-start.40 = (bf16[2,48,1152]{2,1,0:T(8,128)(2,1)S(1)}, bf16[2,48,1152]{2,1,0:T(8,128)(2,1)S(1)}, u32[]{:S(2)}, u32[]{:S(2)}) collective-permute-start(bf16[2,48,1152]{2,1,0:T(8,128)(2,1)S(1)} %add_convert_fusion.11), channel_id=1, source_target_pairs={{0,8},{1,9},{2,10},{3,11},{4,12},{5,13},{6,14},{7,15},{8,0},{9,1},... | collective-permute-start | bytes 663560 | tf_op jit(solution)/shard_map/ppermute | solution.py:656
  (39 other events, 537.4 us)
